TPU v7x, 32 devices: a whole 2x2x4 slice. The times are simulated.
32 devices in a mesh: sys: 2 (over y), row: 4 (over z), col: 4 (over x, core).
Axes of the slice: x: 2, y: 2, z: 4, core: 2. Of those that a mesh axis runs over, the one named last changes fastest.
Arguments:
- a_blocks: bfloat16 [8, 64, 4096], P(('sys', 'row'), 'col'), parts along dimension 0, may hold values from -0.75 to 0.75
- a_index: int32 [2, 8, 64], P(None, ('sys', 'row'), 'col'), parts along dimension 1, may hold values from -1 to 15, as said below
- b_blocks: bfloat16 [128, 16, 4096], P(('sys', 'row'), 'col'), parts along dimension 0, may hold values from -4 to 4
- b_cols: int32 [128, 16], P(('sys', 'row'), 'col'), parts along dimension 0, may hold values from -1 to 15, as said below
- c_cols: int32 [128, 16], P(('sys', 'row'), 'col'), parts along dimension 0, may hold values from 0 to 15, as said below
Outputs:
- c_blocks: float32 [128, 16, 4096], P(('sys', 'row'), 'col'), parts along dimension 0
There are 2 independent parts, one for each index of `sys`. A program takes and returns all parts, laid end to end along the dimension named above; each array names one. Nothing has to cross between parts.
Inputs may be any that keep to these rules, and one draw needn't show every extreme that they name: a_index[0] is -1 for an empty slot; the live slots of one entry (p, g) name distinct blocks; some entry has all 16 slots live and some entry only one. `b_cols`: -1 marks an empty slot; the live entries of one block row within one column group are distinct; some block row has all 4 slots of a column group live and some only one. `c_cols`: the 4 entries of one block row within one column group are distinct.
All inputs are finite; a program needn't handle non-finite values.
Results may differ from a plain program's by a relative error of at most 0.0003.
Values may be sent and summed in bfloat16 or wider, within the bound.
No kernel may reach another device: no remote copies, remote signals or barrier semaphores. Data moves between devices by JAX's collectives and lax.ppermute only.
A program may use at most 64 MiB of HBM per device.

v0:
```python
import functools

import jax
import jax.numpy as jnp
from jax import lax
from jax.experimental import pallas as pl
from jax.experimental.pallas import tpu as pltpu
from jax.sharding import PartitionSpec as P

BS = 64
LANES = 128
ROWS = BS * BS // LANES
CAPACITY = 16
UNROLL = 4
SLOTS = 4
FLAG = 16
IDLE = 63
VMEM = pltpu.VMEM
SMEM = pltpu.SMEM
BF16 = jnp.bfloat16
F32 = jnp.float32
I32 = jnp.int32


def exchanged(block, axis, distance):
    size = lax.axis_size(axis)
    return lax.ppermute(block, axis, [(i, i ^ distance) for i in range(size)])


def describe(a_parts, b_cols, c_cols):
    parts = [part[:, 0, :] for part in a_parts] + [c_cols, b_cols]
    rows = sum(part.shape[0] for part in parts)
    wide = [jnp.pad(p, ((0, 0), (0, LANES - p.shape[1])), constant_values=-1) for p in parts]
    return jnp.concatenate(wide + [jnp.full((-rows % 8, LANES), -1, I32)], axis=0)


def offers(told, cols, row_count):
    start = 2 * cols + SLOTS
    rows = told[pl.ds(start, SLOTS), :]
    lane = iota((1, LANES), 1)
    result = rows[0:1]
    for n in range(1, SLOTS):
        moved = pltpu.roll(rows, n * row_count, 1)[n : n + 1]
        result = jnp.where(lane // row_count == n, moved, result)
    return result


def flatten_kernel(b_ref, flat, wide):
    wide[...] = b_ref[...].astype(F32)
    row_count = b_ref.shape[0]
    for n in range(SLOTS):
        flat[pl.ds(n * row_count, row_count), :] = wide[:, n, :].astype(BF16)


def flatten(b_blocks):
    vmem_spec = pl.BlockSpec(memory_space=VMEM)
    count = b_blocks.shape[0] * b_blocks.shape[1]
    return pl.pallas_call(
        flatten_kernel,
        out_shape=jax.ShapeDtypeStruct((count, BS * BS), BF16),
        in_specs=[vmem_spec],
        out_specs=vmem_spec,
        scratch_shapes=[VMEM(b_blocks.shape, F32)],
        compiler_params=pltpu.CompilerParams(vmem_limit_bytes=24 << 20),
        cost_estimate=pl.CostEstimate(flops=1 << 20, bytes_accessed=8 << 20, transcendentals=0),
        name="flatten",
    )(b_blocks)


def iota(shape, axis):
    return lax.broadcasted_iota(I32, shape, axis)


def turn_to_columns(rows, first, count):
    pick = (iota((count, LANES), 0) + first == iota((count, LANES), 1)).astype(BF16)
    return lax.dot_general(
        pick,
        rows.astype(F32).astype(BF16),
        (((1,), (1,)), ((), ())),
        preferred_element_type=F32,
    )


def matches(receiver, offered, holder, cols, row_count, first_slot, a_slots):
    turned = 2 * (holder ^ lax.axis_index("col"))
    rows = [receiver[pl.ds(turned, 1), :], receiver[pl.ds(turned + 1, 1), :]]
    rows += [receiver[pl.ds(2 * cols, SLOTS), :]]
    rows = jnp.concatenate(rows + [jnp.zeros((8 - 2 - SLOTS, LANES), I32)], axis=0)
    kept_columns = turn_to_columns(rows, 0, row_count)
    if isinstance(first_slot, int) and first_slot == 0 and a_slots == row_count:
        slot_columns = kept_columns
    else:
        slot_columns = turn_to_columns(rows, first_slot, a_slots)
    wanted = offered.astype(F32)
    kept = jnp.zeros((row_count, LANES), F32)
    which = jnp.zeros((row_count, LANES), F32)
    for m in range(SLOTS):
        column = kept_columns[:, 2 + m : 3 + m]
        equal = (column == wanted) & (wanted >= 0)
        kept = jnp.where(equal, 1.0, kept)
        which = jnp.where(equal, float(m), which)
    a_rows = slot_columns[:, 0:1]
    a_columns = slot_columns[:, 1:2]
    shape = (a_slots, row_count)
    by_row = (a_rows == iota(shape, 1).astype(F32)).astype(BF16)
    by_column = a_columns == (iota((a_slots, LANES), 1) % row_count).astype(F32)
    both = jnp.concatenate([kept, which], axis=1).astype(BF16)
    both = jnp.dot(by_row, both, preferred_element_type=F32)
    pairs = jnp.where(by_column & (both[:, :LANES] > 0.5), 1.0, 0.0)
    return pairs, both[:, LANES:], a_rows


def places(needed):
    before = (iota((LANES, LANES), 0) < iota((LANES, LANES), 1)).astype(BF16)
    many = jnp.broadcast_to(needed, (8, LANES)).astype(BF16)
    return jnp.dot(many, before, preferred_element_type=F32)[0:1]


def each(count, body, start):
    if count > 8:
        return lax.fori_loop(0, count, body, start)
    for at in range(count):
        start = body(at, start)
    return start


def pack_kernel(first, peers, cols, a_slots, row_count, *refs):
    refs = list(refs)
    base = 0 if first else refs.pop(0)[0]
    told = refs[:peers]
    flat = refs[peers]
    outs = refs[peers + 1 : 2 * peers]
    most, picks, packed = refs[2 * peers :]
    grid_row = lax.axis_index("row")
    per_col = peers // cols
    offered = offers(told[0], cols, row_count)
    top = jnp.zeros((1, 1), F32)
    first_slot = grid_row % per_col * a_slots if per_col > 1 else 0
    for d in range(1, peers):
        pairs, _, _ = matches(
            told[d], offered, grid_row // per_col, cols, row_count, first_slot, a_slots
        )
        needed = jnp.max(pairs, axis=0, keepdims=True)
        place = jnp.where(needed > 0.5, places(needed), -1.0).astype(I32)
        pick = (place == iota((CAPACITY, LANES), 0) + base).astype(BF16)
        picks[pl.ds((d - 1) * CAPACITY, CAPACITY), :] = pick
        top = jnp.maximum(top, jnp.sum(needed, axis=1, keepdims=True))
    most[...] = jnp.broadcast_to(top, most.shape)
    pick = picks[...][:, : flat.shape[0]]
    for t in range(0, ROWS, 2):
        both = flat[:, pl.ds(t * LANES, 2 * LANES)]
        both = jnp.dot(pick, both, preferred_element_type=F32)
        packed[:, t, :] = both[:, :LANES]
        packed[:, t + 1, :] = both[:, LANES:]
    for d in range(1, peers):
        out = outs[d - 1]
        for x in range(CAPACITY):
            out[pl.ds(x * ROWS, ROWS), :] = packed[(d - 1) * CAPACITY + x].astype(BF16)
        out[pl.ds(CAPACITY * ROWS, FLAG), :] = jnp.broadcast_to(top, (FLAG, LANES)).astype(BF16)


def pack(base, told, flat, cols, row_count, a_slots):
    first = base is None
    peers = len(told)
    smem_spec = pl.BlockSpec(memory_space=SMEM)
    vmem_spec = pl.BlockSpec(memory_space=VMEM)
    given = [] if first else [base]
    results = pl.pallas_call(
        functools.partial(pack_kernel, first, peers, cols, a_slots, row_count),
        out_shape=[jax.ShapeDtypeStruct((CAPACITY * ROWS + FLAG, LANES), BF16)] * (peers - 1)
        + [jax.ShapeDtypeStruct((8, LANES), F32)],
        in_specs=[smem_spec] * len(given) + [vmem_spec] * (peers + 1),
        out_specs=[vmem_spec] * peers,
        scratch_shapes=[
            VMEM(((peers - 1) * CAPACITY, LANES), BF16),
            VMEM(((peers - 1) * CAPACITY, ROWS, LANES), F32),
        ],
        compiler_params=pltpu.CompilerParams(vmem_limit_bytes=32 << 20),
        cost_estimate=pl.CostEstimate(flops=1 << 20, bytes_accessed=4 << 20, transcendentals=0),
        name="pack",
    )(*given, *told, flat)
    return results[:-1], results[-1]


def list_kernel(cols, a_slots, row_count, peers, *refs):
    told = refs[:peers]
    items, starts, words, words_s, sem = refs[peers:]
    grid_row = lax.axis_index("row")
    per_col = peers // cols
    lane = iota((a_slots, LANES), 1)
    slot = iota((a_slots, LANES), 0)
    words[...] = jnp.full(words.shape, IDLE, I32)
    for d in range(peers):
        group = grid_row ^ d
        holder = group // per_col
        first_slot = group % per_col * a_slots if per_col > 1 else 0
        offered = offers(told[d], cols, row_count)
        pairs, which, a_rows = matches(
            told[0], offered, holder, cols, row_count, first_slot, a_slots
        )
        if d == 0:
            place = iota((1, LANES), 1).astype(F32)
        else:
            place = places(jnp.max(pairs, axis=0, keepdims=True))
        stacked = jnp.concatenate([pairs, pairs * place, pairs * which], axis=0).astype(BF16)
        to_slot = iota((LANES, LANES), 1) == iota((LANES, LANES), 0) // row_count + d * SLOTS
        by_slot = jnp.dot(stacked, to_slot.astype(BF16), preferred_element_type=F32)
        hit = by_slot[:a_slots] > 0.5
        at = by_slot[a_slots : 2 * a_slots].astype(I32)
        out = (a_rows * SLOTS + by_slot[2 * a_slots :]).astype(I32)
        a_slot = holder * per_col * a_slots + first_slot + slot
        word = ((a_slot * 64 + out) * 64 + at) * 64 + d
        words[...] = jnp.where(hit & (lane // SLOTS == d), word, words[...])
    fetch([(words, words_s)], sem)

    def one_peer(d, length):
        starts[d] = length
        for n in range(SLOTS):
            for s in range(a_slots):
                word = words_s[s, d * SLOTS + n]
                items[length] = word
                length = length + (word & IDLE != IDLE).astype(I32)
        for u in range(UNROLL):
            items[length + u] = IDLE
        return (length + UNROLL - 1) // UNROLL * UNROLL

    starts[peers] = lax.fori_loop(0, peers, one_peer, jnp.int32(0))


def work_list(told, cols, row_count, a_slots):
    peers = len(told)
    most_items = peers * (a_slots * SLOTS + UNROLL) + UNROLL
    return pl.pallas_call(
        functools.partial(list_kernel, cols, a_slots, row_count, peers),
        out_shape=[
            jax.ShapeDtypeStruct((most_items,), I32),
            jax.ShapeDtypeStruct((peers + 1,), I32),
        ],
        in_specs=[pl.BlockSpec(memory_space=VMEM)] * peers,
        out_specs=[pl.BlockSpec(memory_space=SMEM)] * 2,
        scratch_shapes=[
            VMEM((a_slots, LANES), I32),
            SMEM((a_slots, LANES), I32),
            pltpu.SemaphoreType.DMA((1,)),
        ],
        cost_estimate=pl.CostEstimate(flops=1 << 20, bytes_accessed=1 << 16, transcendentals=0),
        name="work_list",
    )(*told)


def fetch(copies, sems):
    started = [
        pltpu.make_async_copy(source, target, sems.at[at])
        for at, (source, target) in enumerate(copies)
    ]
    for copy in started:
        copy.start()
    for copy in started:
        copy.wait()


def add_products(items, start, stop, a_ref, b_ref, sums, window=None):
    low = iota((ROWS, LANES), 1) < BS
    nothing = jnp.zeros((ROWS, LANES), BF16)
    idle_row = sums.shape[0] - 1

    def some_items(step, carry):
        for u in range(UNROLL):
            word = items[step * UNROLL + u]
            place = (word >> 6) & 63
            target = (word >> 12) & 63
            used = (word & IDLE) != IDLE
            if window is not None:
                place = place - window
                used = used & (place >= 0) & (place < CAPACITY)
                place = jnp.where(used, place, 0)
            a_at = pl.multiple_of((word >> 18) * ROWS, ROWS)
            b_at = pl.multiple_of(place * ROWS, ROWS)
            block = b_ref[pl.ds(b_at, ROWS), :]
            turned = jnp.concatenate([block[:, BS:], block[:, :BS]], axis=1)
            right = jnp.concatenate(
                [
                    jnp.where(low, block, nothing),
                    jnp.where(low, turned, nothing),
                    jnp.where(low, nothing, turned),
                    jnp.where(low, nothing, block),
                ],
                axis=0,
            )
            term = jnp.dot(a_ref[pl.ds(a_at, ROWS), :], right, preferred_element_type=F32)
            i = jnp.where(used, target // SLOTS, idle_row)
            sums[i, pl.ds(target % SLOTS, ROWS, stride=SLOTS), :] += term
        return carry

    lax.fori_loop(start // UNROLL, stop // UNROLL, some_items, 0)


def stage_kernel(cols, *refs):
    a_refs, b_ref, items, starts = refs[:cols], refs[cols], refs[cols + 1], refs[cols + 2]
    a_out, sums, a_wide, b_wide, b_own = refs[cols + 3 :]
    source = iota((LANES, LANES), 0)
    target = iota((LANES, LANES), 1)
    wanted = (target // BS) * BS + 2 * (target % ROWS) + (target // ROWS) % 2
    order = (source == wanted).astype(BF16)
    slots = a_refs[0].shape[1]
    grid_col = lax.axis_index("col")
    for t in range(ROWS):
        pieces = [ref[0, :, pl.ds(t * LANES, LANES)] for ref in a_refs]
        done = jnp.dot(jnp.concatenate(pieces, axis=0), order, preferred_element_type=F32)
        a_wide[:, t, :] = done
    for h in range(cols):
        first = (grid_col ^ h) * slots
        for s in range(slots):
            at = pl.multiple_of((first + s) * ROWS, ROWS)
            a_out[pl.ds(at, ROWS), :] = a_wide[h * slots + s].astype(BF16)
    row_count, slots = b_ref.shape[0], b_ref.shape[1]

    def one_row(k, carry):
        for t in range(ROWS):
            b_wide[pl.ds(t * slots, slots), :] = b_ref[k, :, pl.ds(t * LANES, LANES)].astype(F32)
        for n in range(slots):
            at = pl.multiple_of((n * row_count + k) * ROWS, ROWS)
            b_own[pl.ds(at, ROWS), :] = b_wide[pl.ds(n, ROWS, stride=slots), :].astype(BF16)
        return carry

    lax.fori_loop(0, row_count, one_row, 0)
    sums[...] = jnp.zeros_like(sums)
    add_products(items, 0, starts[1], a_out, b_own, sums)


def stage(a_parts, b_blocks, items, starts):
    cols, slots = len(a_parts), a_parts[0].shape[1]
    row_count, b_slots = b_blocks.shape[0], b_blocks.shape[1]
    vmem_spec = pl.BlockSpec(memory_space=VMEM)
    smem_spec = pl.BlockSpec(memory_space=SMEM)
    return pl.pallas_call(
        functools.partial(stage_kernel, cols),
        out_shape=(
            jax.ShapeDtypeStruct((cols * slots * ROWS, LANES), BF16),
            jax.ShapeDtypeStruct((row_count + 1, ROWS * b_slots, LANES), F32),
        ),
        in_specs=[vmem_spec] * (cols + 1) + [smem_spec] * 2,
        out_specs=(vmem_spec,) * 2,
        scratch_shapes=[
            VMEM((cols * slots, ROWS, LANES), F32),
            VMEM((b_slots * ROWS, LANES), F32),
            VMEM((row_count * b_slots * ROWS, LANES), BF16),
        ],
        compiler_params=pltpu.CompilerParams(vmem_limit_bytes=40 << 20),
        cost_estimate=pl.CostEstimate(flops=1 << 24, bytes_accessed=4 << 20, transcendentals=0),
        name="stage",
    )(*a_parts, b_blocks, items, starts)


def multiply_kernel(first, peers, *refs):
    refs = list(refs)
    base = 0 if first else refs.pop(0)[0]
    items, starts, most, a_ref, sums_in = refs[:5]
    b_refs = refs[5 : 4 + peers]
    out, rounds, sums, rows, sems = refs[4 + peers :]
    width = CAPACITY * ROWS
    needed = jnp.max(most[...])
    for ref in b_refs:
        needed = jnp.maximum(needed, jnp.max(ref[pl.ds(width, FLAG), :].astype(F32)))
    rounds[0] = (needed.astype(I32) + CAPACITY - 1) // CAPACITY
    for d in range(1, peers):
        add_products(items, starts[d], starts[d + 1], a_ref, b_refs[d - 1], sums, window=base)
    row_count, kept = out.shape[0], out.shape[1]
    copies = []
    for i in range(row_count):
        for t in range(ROWS):
            rows[i, :, pl.ds(t * LANES, LANES)] = sums[i, pl.ds(t * kept, kept), :]
        copies.append(pltpu.make_async_copy(rows.at[i], out.at[i], sems.at[i]))
        copies[-1].start()
    for copy in copies:
        copy.wait()


def multiply(base, items, starts, most, a_ready, sums, b_parts, shape):
    first = base is None
    peers = len(b_parts) + 1
    smem_spec = pl.BlockSpec(memory_space=SMEM)
    vmem_spec = pl.BlockSpec(memory_space=VMEM)
    given = [] if first else [base]
    return pl.pallas_call(
        functools.partial(multiply_kernel, first, peers),
        out_shape=[
            jax.ShapeDtypeStruct(shape, F32),
            jax.ShapeDtypeStruct((1,), I32),
            jax.ShapeDtypeStruct(sums.shape, F32),
        ],
        in_specs=[smem_spec] * (len(given) + 2) + [vmem_spec] * (2 + peers),
        out_specs=[pl.BlockSpec(memory_space=pl.ANY), smem_spec, vmem_spec],
        input_output_aliases={len(given) + 4: 2},
        scratch_shapes=[VMEM(shape, F32), pltpu.SemaphoreType.DMA((shape[0],))],
        compiler_params=pltpu.CompilerParams(vmem_limit_bytes=32 << 20),
        cost_estimate=pl.CostEstimate(flops=1 << 26, bytes_accessed=4 << 20, transcendentals=0),
        name="multiply",
    )(*given, items, starts, most, a_ready, sums, *b_parts)


def shards(a_blocks, a_index, b_blocks, b_cols, c_cols):
    rows = lax.axis_size("row")
    cols = lax.axis_size("col")
    a_slots = a_blocks.shape[1] * cols // rows
    row_count = b_blocks.shape[0]

    def send_rows(parts):
        return [exchanged(part, "row", d + 1) for d, part in enumerate(parts)]

    index_parts = [a_index] + [exchanged(a_index, "col", h) for h in range(1, cols)]
    told = describe(index_parts, b_cols.T, c_cols.T)
    told = [told] + send_rows([told] * (rows - 1))
    flat = flatten(b_blocks)
    packed, most = pack(None, told, flat, cols, row_count, a_slots)
    arrived = send_rows(packed)
    items, starts = work_list(told, cols, row_count, a_slots)
    a_late, _ = lax.optimization_barrier((a_blocks, most))
    a_parts = [a_blocks] + [exchanged(a_late, "col", h) for h in range(1, cols)]
    a_ready, sums = stage(a_parts, b_blocks, items, starts)
    shape = (row_count, c_cols.shape[1], BS * BS)
    out, rounds, sums = multiply(None, items, starts, most, a_ready, sums, arrived, shape)

    def more(state):
        return state[0] < rounds[0]

    def one_round(state):
        at, sums, _ = state
        base = jnp.reshape(at * CAPACITY, (1,))
        packed, most = pack(base, told, flat, cols, row_count, a_slots)
        arrived = send_rows(packed)
        out, _, sums = multiply(base, items, starts, most, a_ready, sums, arrived, shape)
        return at + 1, sums, out

    return lax.while_loop(more, one_round, (jnp.int32(1), sums, out))[2]


def solution(mesh):
    return jax.shard_map(
        shards,
        mesh=mesh,
        in_specs=(
            P(("sys", "row"), "col", None),
            P(None, ("sys", "row"), "col"),
            P(("sys", "row"), "col", None),
            P(("sys", "row"), "col"),
            P(("sys", "row"), "col"),
        ),
        out_specs=P(("sys", "row"), "col", None),
        check_vma=False,
    )
```

profile of v0, /device:TPU:16, one launch (start us, length us, event | category | flops | bytes accessed | tf_op | source)
XLA Modules:
  0.0 35.1 jit_solution(11822575626081338721)
XLA Ops:
  0.0 0.0 collective-permute-start.3
  0.0 1.6 %collective-permute-start.5 = (s32[2,1,16]{2,1,0:T(1,128)}, s32[2,1,16]{2,1,0:T(1,128)S(1)}, u32[]{:S(2)}, u32[]{:S(2)}) collective-permute-start(s32[2,1,16]{2,1,0:T(1,128)} %param.8), channel_id=1, source_target_pairs={{0,3},{1,2},{2,1},{3,0},{4,7},{5,6},{6,5},{7,4},{8,11},{9,10},{10,... | collective-permute-start | bytes 392 | tf_op jit(solution)/shard_map/ppermute | solution.py:27
  1.6 0.5 %collective-permute-start.4 = (s32[2,1,16]{2,1,0:T(1,128)}, s32[2,1,16]{2,1,0:T(1,128)S(1)}, u32[]{:S(2)}, u32[]{:S(2)}) collective-permute-start(s32[2,1,16]{2,1,0:T(1,128)} %param.8), channel_id=1, source_target_pairs={{0,2},{1,3},{2,0},{3,1},{4,6},{5,7},{6,4},{7,5},{8,10},{9,11},{10,... | collective-permute-start | bytes 392 | tf_op jit(solution)/shard_map/ppermute | solution.py:27
  2.1 0.7 %pad.20 = s32[2,128]{1,0:T(2,128)S(1)} pad(s32[2,16]{1,0:T(2,128)} %bitcast.13, s32[]{:T(128)} %constant.3.clone.1), padding=0_0x0_112 | pad | bytes 1156 | tf_op jit(solution)/shard_map/jit(_pad)/pad | solution.py:33
  2.9 0.7 %pad.25 = s32[4,128]{1,0:T(4,128)S(1)} pad(s32[4,16]{1,0:T(4,128)} %bitcast.11, s32[]{:T(128)} %constant.3.clone.1), padding=0_0x0_112 | pad | bytes 2308 | tf_op jit(solution)/shard_map/jit(_pad)/pad | solution.py:33
  3.5 0.7 %pad.24 = s32[4,128]{1,0:T(4,128)S(1)} pad(s32[4,16]{1,0:T(4,128)} %bitcast.12, s32[]{:T(128)} %constant.3.clone.1), padding=0_0x0_112 | pad | bytes 2308 | tf_op jit(solution)/shard_map/jit(_pad)/pad | solution.py:33
  4.2 0.0 collective-permute-done.3
  4.2 0.0 collective-permute-done.5
  4.3 1.1 %collective-permute-done.4 = s32[2,1,16]{2,1,0:T(1,128)S(1)} collective-permute-done((s32[2,1,16]{2,1,0:T(1,128)}, s32[2,1,16]{2,1,0:T(1,128)S(1)}, u32[]{:S(2)}, u32[]{:S(2)}) %collective-permute-start.4) | collective-permute-done | bytes 160 | tf_op jit(solution)/shard_map/ppermute | solution.py:27
  5.4 0.5 %collective-permute-start.8 = (s32[16,128]{1,0:T(8,128)S(1)}, s32[16,128]{1,0:T(8,128)S(1)}, u32[]{:S(2)}, u32[]{:S(2)}) collective-permute-start(s32[16,128]{1,0:T(8,128)S(1)} %concatenate.3.refs_0_), channel_id=1, source_target_pairs={{0,12},{4,8},{8,4},{12,0},{1,13},{5,9},{9,5},{13,1},{2,14},{6,10},... | collective-permute-start | bytes 24584 | tf_op jit(solution)/shard_map/ppermute | solution.py:27
  5.9 3.5 %collective-permute-start.7 = (s32[16,128]{1,0:T(8,128)S(1)}, s32[16,128]{1,0:T(8,128)S(1)}, u32[]{:S(2)}, u32[]{:S(2)}) collective-permute-start(s32[16,128]{1,0:T(8,128)S(1)} %concatenate.3.refs_0_), channel_id=1, source_target_pairs={{0,8},{4,12},{8,0},{12,4},{1,9},{5,13},{9,1},{13,5},{2,10},{6,14},... | collective-permute-start | bytes 24584 | tf_op jit(solution)/shard_map/ppermute | solution.py:27
  9.4 0.0 collective-permute-start.6
  9.4 1.0 %copy-done = bf16[16,4,4096]{2,1,0:T(4,128)(2,1)S(1)} copy-done((bf16[16,4,4096]{2,1,0:T(4,128)(2,1)S(1)}, bf16[16,4,4096]{2,1,0:T(4,128)(2,1)}, u32[]{:S(2)}) %copy-start) | copy-done | bytes 524312
  10.5 1.5 %flatten.1.refs_4_ = bf16[64,4096]{1,0:T(8,128)(2,1)S(1)} custom-call(bf16[16,4,4096]{2,1,0:T(4,128)(2,1)S(1)} %copy-done), custom_call_target="tpu_custom_call" | custom-call | flops 1048576 | bytes 8388608 | tf_op jit(solution)/shard_map/flatten/pallas_call | solution.py:58
  12.0 0.0 collective-permute-done.8.refs_3_
  12.0 0.0 collective-permute-done.7.refs_2_
  12.0 1.1 %collective-permute-done.6.refs_1_ = s32[16,128]{1,0:T(8,128)S(1)} collective-permute-done((s32[16,128]{1,0:T(8,128)S(1)}, s32[16,128]{1,0:T(8,128)S(1)}, u32[]{:S(2)}, u32[]{:S(2)}) %collective-permute-start.6) | collective-permute-done | bytes 8224 | tf_op jit(solution)/shard_map/ppermute | solution.py:27
  13.1 1.4 %pack.2 = (bf16[528,128]{1,0:T(8,128)(2,1)S(1)}, bf16[528,128]{1,0:T(8,128)(2,1)S(1)}, bf16[528,128]{1,0:T(8,128)(2,1)S(1)}, f32[8,128]{1,0:T(8,128)S(1)}) custom-call(s32[16,128]{1,0:T(8,128)S(1)} %concatenate.3.refs_0_, s32[16,128]{1,0:T(8,128)S(1)} %collective-permute-done.6.refs_1_, s32[16,128]{1,0:T(8,128)S(1)} %collective-permute-done.7.refs_2_, ...), custom_call_target="tpu_custom_call" | custom-call | flops 1048576 | bytes 4194304 | tf_op jit(solution)/shard_map/pack/pallas_call | solution.py:168
  14.5 0.1 collective-permute-start.11
  14.6 1.0 %collective-permute-start.12 = (bf16[528,128]{1,0:T(8,128)(2,1)S(1)}, bf16[528,128]{1,0:T(8,128)(2,1)S(1)}, u32[]{:S(2)}, u32[]{:S(2)}) collective-permute-start(bf16[528,128]{1,0:T(8,128)(2,1)S(1)} %get-tuple-element.91), channel_id=1, source_target_pairs={{0,4},{4,0},{8,12},{12,8},{1,5},{5,1},{9,13},{13,9},{2,6},{6,2},{1... | collective-permute-start | bytes 405512 | tf_op jit(solution)/shard_map/ppermute | solution.py:27
  15.6 2.5 %collective-permute-start.14 = (bf16[528,128]{1,0:T(8,128)(2,1)S(1)}, bf16[528,128]{1,0:T(8,128)(2,1)S(1)}, u32[]{:S(2)}, u32[]{:S(2)}) collective-permute-start(bf16[528,128]{1,0:T(8,128)(2,1)S(1)} %get-tuple-element.93), channel_id=1, source_target_pairs={{0,12},{4,8},{8,4},{12,0},{1,13},{5,9},{9,5},{13,1},{2,14},{6,10},... | collective-permute-start | bytes 405512 | tf_op jit(solution)/shard_map/ppermute | solution.py:27
  18.1 0.5 %collective-permute-start.10 = (bf16[1,16,4096]{2,1,0:T(8,128)(2,1)S(1)}, bf16[1,16,4096]{2,1,0:T(8,128)(2,1)S(1)}, u32[]{:S(2)}, u32[]{:S(2)}) collective-permute-start(bf16[1,16,4096]{2,1,0:T(8,128)(2,1)S(1)} %copy-done.2), channel_id=1, source_target_pairs={{0,2},{1,3},{2,0},{3,1},{4,6},{5,7},{6,4},{7,5},{8,10},{9,11},{10,... | collective-permute-start | bytes 393224 | tf_op jit(solution)/shard_map/ppermute | solution.py:27
  18.6 0.8 %collective-permute-done.11.refs_3_ = bf16[1,16,4096]{2,1,0:T(8,128)(2,1)S(1)} collective-permute-done((bf16[1,16,4096]{2,1,0:T(8,128)(2,1)S(1)}, bf16[1,16,4096]{2,1,0:T(8,128)(2,1)S(1)}, u32[]{:S(2)}, u32[]{:S(2)}) %collective-permute-start.11) | collective-permute-done | bytes 131104 | tf_op jit(solution)/shard_map/ppermute | solution.py:27
  19.4 0.0 collective-permute-start.9
  19.4 3.5 %work_list.1 = (s32[276]{0:T(512)S(1)}, s32[5]{0:T(128)S(1)}) custom-call(s32[16,128]{1,0:T(8,128)S(1)} %concatenate.3.refs_0_, s32[16,128]{1,0:T(8,128)S(1)} %collective-permute-done.6.refs_1_, s32[16,128]{1,0:T(8,128)S(1)} %collective-permute-done.7.refs_2_, s32[16,128]{1,0:T(8,128)S(1)} %collective-permute-done.8.refs_3_), custom_call_target="tpu_custom_call" | custom-call | flops 1048576 | bytes 65536 | tf_op jit(solution)/shard_map/work_list/pallas_call | solution.py:233
  22.9 0.3 collective-permute-done.10.refs_2_
  23.2 0.0 collective-permute-done.9.refs_1_
  23.2 2.6 %stage.1 = (bf16[2048,128]{1,0:T(8,128)(2,1)S(1)}, f32[17,128,128]{2,1,0:T(8,128)S(1)}) custom-call(bf16[1,16,4096]{2,1,0:T(8,128)(2,1)S(1)} %copy-done.2, bf16[1,16,4096]{2,1,0:T(8,128)(2,1)S(1)} %collective-permute-done.9.refs_1_, bf16[1,16,4096]{2,1,0:T(8,128)(2,1)S(1)} %collective-permute-done.10.refs_2_, ...), custom_call_target="tpu_custom_call" | custom-call | flops 16777216 | bytes 4194304 | tf_op jit(solution)/shard_map/stage/pallas_call | solution.py:336
  25.8 0.0 collective-permute-done.13.refs_6_
  25.8 4.7 %collective-permute-done.14.refs_7_ = bf16[528,128]{1,0:T(8,128)(2,1)S(1)} collective-permute-done((bf16[528,128]{1,0:T(8,128)(2,1)S(1)}, bf16[528,128]{1,0:T(8,128)(2,1)S(1)}, u32[]{:S(2)}, u32[]{:S(2)}) %collective-permute-start.14) | collective-permute-done | bytes 135200 | tf_op jit(solution)/shard_map/ppermute | solution.py:27
  30.6 3.9 %multiply.2 = (f32[16,4,4096]{2,1,0:T(4,128)}, s32[1]{0:T(128)}, f32[17,128,128]{2,1,0:T(8,128)S(1)}) custom-call(s32[276]{0:T(512)S(1)} %get-tuple-element.215.refs_5_.refs_0_, s32[5]{0:T(128)S(1)} %get-tuple-element.216.refs_6_.refs_1_, f32[8,128]{1,0:T(8,128)S(1)} %get-tuple-element.87.refs_2_, ...), custom_call_target="tpu_custom_call", output_to_operand_aliasing={{2}: (4, {})} | custom-call | flops 67108864 | bytes 4194304 | tf_op jit(solution)/shard_map/multiply/pallas_call | solution.py:385
  34.5 0.6 %while.12 = (s32[]{:T(128)}, f32[17,128,128]{2,1,0:T(8,128)S(1)}, f32[16,4,4096]{2,1,0:T(4,128)}, s32[1]{0:T(128)}, s32[16,128]{1,0:T(8,128)S(1)}, /*index=5*/s3...) while((s32[]{:T(128)}, f32[17,128,128]{2,1,0:T(8,128)S(1)}, ...), condition=%wide.region_1.2_spmd, body=%wide.region_0.1_spmd.sunk | while | flops 68157440 | bytes 10010889 | solution.py:435
  (13 shorter events, 0.1 us)
Async XLA Ops:
  0.0 4.2 %collective-permute-start.3 = (s32[2,1,16]{2,1,0:T(1,128)}, s32[2,1,16]{2,1,0:T(1,128)S(1)}, u32[]{:S(2)}, u32[]{:S(2)}) collective-permute-start(s32[2,1,16]{2,1,0:T(1,128)} %param.8), channel_id=1, source_target_pairs={{0,1},{1,0},{2,3},{3,2},{4,5},{5,4},{6,7},{7,6},{8,9},{9,8},{10,11... | collective-permute-start | bytes 392 | tf_op jit(solution)/shard_map/ppermute | solution.py:27
  0.0 4.2 %collective-permute-start.5 = (s32[2,1,16]{2,1,0:T(1,128)}, s32[2,1,16]{2,1,0:T(1,128)S(1)}, u32[]{:S(2)}, u32[]{:S(2)}) collective-permute-start(s32[2,1,16]{2,1,0:T(1,128)} %param.8), channel_id=1, source_target_pairs={{0,3},{1,2},{2,1},{3,0},{4,7},{5,6},{6,5},{7,4},{8,11},{9,10},{10,... | collective-permute-start | bytes 392 | tf_op jit(solution)/shard_map/ppermute | solution.py:27
  1.6 3.8 %collective-permute-start.4 = (s32[2,1,16]{2,1,0:T(1,128)}, s32[2,1,16]{2,1,0:T(1,128)S(1)}, u32[]{:S(2)}, u32[]{:S(2)}) collective-permute-start(s32[2,1,16]{2,1,0:T(1,128)} %param.8), channel_id=1, source_target_pairs={{0,2},{1,3},{2,0},{3,1},{4,6},{5,7},{6,4},{7,5},{8,10},{9,11},{10,... | collective-permute-start | bytes 392 | tf_op jit(solution)/shard_map/ppermute | solution.py:27
  5.4 6.6 %collective-permute-start.8 = (s32[16,128]{1,0:T(8,128)S(1)}, s32[16,128]{1,0:T(8,128)S(1)}, u32[]{:S(2)}, u32[]{:S(2)}) collective-permute-start(s32[16,128]{1,0:T(8,128)S(1)} %concatenate.3.refs_0_), channel_id=1, source_target_pairs={{0,12},{4,8},{8,4},{12,0},{1,13},{5,9},{9,5},{13,1},{2,14},{6,10},... | collective-permute-start | bytes 24584 | tf_op jit(solution)/shard_map/ppermute | solution.py:27
  5.9 6.1 %collective-permute-start.7 = (s32[16,128]{1,0:T(8,128)S(1)}, s32[16,128]{1,0:T(8,128)S(1)}, u32[]{:S(2)}, u32[]{:S(2)}) collective-permute-start(s32[16,128]{1,0:T(8,128)S(1)} %concatenate.3.refs_0_), channel_id=1, source_target_pairs={{0,8},{4,12},{8,0},{12,4},{1,9},{5,13},{9,1},{13,5},{2,10},{6,14},... | collective-permute-start | bytes 24584 | tf_op jit(solution)/shard_map/ppermute | solution.py:27
  9.4 3.7 %collective-permute-start.6 = (s32[16,128]{1,0:T(8,128)S(1)}, s32[16,128]{1,0:T(8,128)S(1)}, u32[]{:S(2)}, u32[]{:S(2)}) collective-permute-start(s32[16,128]{1,0:T(8,128)S(1)} %concatenate.3.refs_0_), channel_id=1, source_target_pairs={{0,4},{4,0},{8,12},{12,8},{1,5},{5,1},{9,13},{13,9},{2,6},{6,2},{1... | collective-permute-start | bytes 24584 | tf_op jit(solution)/shard_map/ppermute | solution.py:27
  9.4 1.0 %copy-start = (bf16[16,4,4096]{2,1,0:T(4,128)(2,1)S(1)}, bf16[16,4,4096]{2,1,0:T(4,128)(2,1)}, u32[]{:S(2)}) copy-start(bf16[16,4,4096]{2,1,0:T(4,128)(2,1)} %refs_4_.1) | copy-start | bytes 1572868
  10.5 4.0 %copy-start.2 = (bf16[1,16,4096]{2,1,0:T(8,128)(2,1)S(1)}, bf16[1,16,4096]{2,1,0:T(8,128)(2,1)}, u32[]{:S(2)}) copy-start(bf16[1,16,4096]{2,1,0:T(8,128)(2,1)} %refs_0_.1) | copy-start | bytes 393220
  10.5 12.8 %copy-start.1 = (bf16[16,4,4096]{2,1,0:T(4,128)(2,1)S(1)}, bf16[16,4,4096]{2,1,0:T(4,128)(2,1)}, u32[]{:S(2)}) copy-start(bf16[16,4,4096]{2,1,0:T(4,128)(2,1)} %refs_4_.1) | copy-start | bytes 1572868
  14.5 5.0 %collective-permute-start.11 = (bf16[1,16,4096]{2,1,0:T(8,128)(2,1)S(1)}, bf16[1,16,4096]{2,1,0:T(8,128)(2,1)S(1)}, u32[]{:S(2)}, u32[]{:S(2)}) collective-permute-start(bf16[1,16,4096]{2,1,0:T(8,128)(2,1)S(1)} %copy-done.2), channel_id=1, source_target_pairs={{0,3},{1,2},{2,1},{3,0},{4,7},{5,6},{6,5},{7,4},{8,11},{9,10},{10,... | collective-permute-start | bytes 393224 | tf_op jit(solution)/shard_map/ppermute | solution.py:27
  14.6 11.3 %collective-permute-start.12 = (bf16[528,128]{1,0:T(8,128)(2,1)S(1)}, bf16[528,128]{1,0:T(8,128)(2,1)S(1)}, u32[]{:S(2)}, u32[]{:S(2)}) collective-permute-start(bf16[528,128]{1,0:T(8,128)(2,1)S(1)} %get-tuple-element.91), channel_id=1, source_target_pairs={{0,4},{4,0},{8,12},{12,8},{1,5},{5,1},{9,13},{13,9},{2,6},{6,2},{1... | collective-permute-start | bytes 405512 | tf_op jit(solution)/shard_map/ppermute | solution.py:27
  15.6 10.2 %collective-permute-start.13 = (bf16[528,128]{1,0:T(8,128)(2,1)S(1)}, bf16[528,128]{1,0:T(8,128)(2,1)S(1)}, u32[]{:S(2)}, u32[]{:S(2)}) collective-permute-start(bf16[528,128]{1,0:T(8,128)(2,1)S(1)} %get-tuple-element.92), channel_id=1, source_target_pairs={{0,8},{4,12},{8,0},{12,4},{1,9},{5,13},{9,1},{13,5},{2,10},{6,14},... | collective-permute-start | bytes 405512 | tf_op jit(solution)/shard_map/ppermute | solution.py:27
  15.6 14.9 %collective-permute-start.14 = (bf16[528,128]{1,0:T(8,128)(2,1)S(1)}, bf16[528,128]{1,0:T(8,128)(2,1)S(1)}, u32[]{:S(2)}, u32[]{:S(2)}) collective-permute-start(bf16[528,128]{1,0:T(8,128)(2,1)S(1)} %get-tuple-element.93), channel_id=1, source_target_pairs={{0,12},{4,8},{8,4},{12,0},{1,13},{5,9},{9,5},{13,1},{2,14},{6,10},... | collective-permute-start | bytes 405512 | tf_op jit(solution)/shard_map/ppermute | solution.py:27
  18.1 5.1 %collective-permute-start.10 = (bf16[1,16,4096]{2,1,0:T(8,128)(2,1)S(1)}, bf16[1,16,4096]{2,1,0:T(8,128)(2,1)S(1)}, u32[]{:S(2)}, u32[]{:S(2)}) collective-permute-start(bf16[1,16,4096]{2,1,0:T(8,128)(2,1)S(1)} %copy-done.2), channel_id=1, source_target_pairs={{0,2},{1,3},{2,0},{3,1},{4,6},{5,7},{6,4},{7,5},{8,10},{9,11},{10,... | collective-permute-start | bytes 393224 | tf_op jit(solution)/shard_map/ppermute | solution.py:27
  19.4 3.8 %collective-permute-start.9 = (bf16[1,16,4096]{2,1,0:T(8,128)(2,1)S(1)}, bf16[1,16,4096]{2,1,0:T(8,128)(2,1)S(1)}, u32[]{:S(2)}, u32[]{:S(2)}) collective-permute-start(bf16[1,16,4096]{2,1,0:T(8,128)(2,1)S(1)} %copy-done.2), channel_id=1, source_target_pairs={{0,1},{1,0},{2,3},{3,2},{4,5},{5,4},{6,7},{7,6},{8,9},{9,8},{10,11... | collective-permute-start | bytes 393224 | tf_op jit(solution)/shard_map/ppermute | solution.py:27
  25.8 8.7 %copy-start.3 = (bf16[2048,128]{1,0:T(8,128)(2,1)}, bf16[2048,128]{1,0:T(8,128)(2,1)S(1)}, u32[]{:S(2)}) copy-start(bf16[2048,128]{1,0:T(8,128)(2,1)S(1)} %get-tuple-element.217.refs_3_) | copy-start | bytes 1572868
where the time goes:
time: 35.2 us; the launch traced here: 35.1 us
  Pallas kernels  12.8 us (36%)
  starting transfers between devices  10.3 us (29%)
  waiting for transfers between devices  8.05 us (23%)
  local copies, waits for them, and re-layouts  3.2 us (9%)
  loops' own time  0.63 us (2%)
    ppermute x12, starting transfers between devices, exchanged(): return lax.ppermute(block, axis, [(i, i ^ distance) for i in range(size)])  10.3 us
    ppermute x12, waiting for transfers between devices, exchanged(): return lax.ppermute(block, axis, [(i, i ^ distance) for i in range(size)])  8.05 us
    pallas_call x1, Pallas kernels, multiply(): pl.pallas_call(functools.partial(multiply_kernel, first, peers), out_shap...  3.9 us
    pallas_call x1, Pallas kernels, work_list(): pl.pallas_call(functools.partial(list_kernel, cols, a_slots, row_count, p...  3.45 us
    pallas_call x1, Pallas kernels, stage(): pl.pallas_call(functools.partial(stage_kernel, cols), out_shape=(jax.Shap...  2.55 us
    pad x6, local copies, waits for them, and re-layouts, describe(): jnp.pad(p, ((0, 0), (0, LANES - p.shape[1])), constant_values=-1)  2.1 us
    pallas_call x1, Pallas kernels, flatten(): pl.pallas_call(flatten_kernel, out_shape=jax.ShapeDtypeStruct((count, BS...  1.51 us
    pallas_call x1, Pallas kernels, pack(): pl.pallas_call(functools.partial(pack_kernel, first, peers, cols, a_slots...  1.38 us
  transfers between devices with their start and end apart: 12, of which 5 were waited for; matrix products, arithmetic and copies ran while one was open for 6% of the time, Pallas kernels for 21%

commit v1 on v0

--- a/solution.py
+++ b/solution.py
@@ -28,10 +28,18 @@
 
 
 def describe(a_parts, b_cols, c_cols):
-    parts = [part[:, 0, :] for part in a_parts] + [c_cols, b_cols]
-    rows = sum(part.shape[0] for part in parts)
-    wide = [jnp.pad(p, ((0, 0), (0, LANES - p.shape[1])), constant_values=-1) for p in parts]
-    return jnp.concatenate(wide + [jnp.full((-rows % 8, LANES), -1, I32)], axis=0)
+    cols = len(a_parts)
+    total = -(-(2 * cols + 2 * SLOTS) // 8) * 8
+
+    def placed(part, at):
+        after = (total - at - part.shape[0], LANES - part.shape[1])
+        return jnp.pad(part, ((at, after[0]), (0, after[1])), constant_values=-1)
+
+    own = jnp.maximum(placed(c_cols, 2 * cols), placed(b_cols, 2 * cols + SLOTS))
+    told = lax.optimization_barrier(jnp.maximum(own, placed(a_parts[0][:, 0, :], 0)))
+    for h in range(1, cols):
+        told = jnp.maximum(told, placed(a_parts[h][:, 0, :], 2 * h))
+    return told
 
 
 def offers(told, cols, row_count):
@@ -46,10 +54,14 @@
 
 
 def flatten_kernel(b_ref, flat, wide):
-    wide[...] = b_ref[...].astype(F32)
     row_count = b_ref.shape[0]
-    for n in range(SLOTS):
-        flat[pl.ds(n * row_count, row_count), :] = wide[:, n, :].astype(BF16)
+    for k in range(row_count):
+        for t in range(ROWS):
+            wide[k, pl.ds(t * SLOTS, SLOTS), :] = b_ref[k, :, pl.ds(t * LANES, LANES)].astype(F32)
+    for t in range(ROWS):
+        for n in range(SLOTS):
+            piece = wide[:, t * SLOTS + n, :].astype(BF16)
+            flat[pl.ds(n * row_count, row_count), pl.ds(t * LANES, LANES)] = piece
 
 
 def flatten(b_blocks):
@@ -60,7 +72,7 @@
         out_shape=jax.ShapeDtypeStruct((count, BS * BS), BF16),
         in_specs=[vmem_spec],
         out_specs=vmem_spec,
-        scratch_shapes=[VMEM(b_blocks.shape, F32)],
+        scratch_shapes=[VMEM((b_blocks.shape[0], b_blocks.shape[1] * ROWS, LANES), F32)],
         compiler_params=pltpu.CompilerParams(vmem_limit_bytes=24 << 20),
         cost_estimate=pl.CostEstimate(flops=1 << 20, bytes_accessed=8 << 20, transcendentals=0),
         name="flatten",
@@ -220,16 +232,16 @@
                 word = words_s[s, d * SLOTS + n]
                 items[length] = word
                 length = length + (word & IDLE != IDLE).astype(I32)
-        for u in range(UNROLL):
-            items[length + u] = IDLE
-        return (length + UNROLL - 1) // UNROLL * UNROLL
-
-    starts[peers] = lax.fori_loop(0, peers, one_peer, jnp.int32(0))
+        return length
+
+    length = lax.fori_loop(0, peers, one_peer, jnp.int32(0))
+    starts[peers] = length
+    items[length] = IDLE
 
 
 def work_list(told, cols, row_count, a_slots):
     peers = len(told)
-    most_items = peers * (a_slots * SLOTS + UNROLL) + UNROLL
+    most_items = peers * a_slots * SLOTS + 1
     return pl.pallas_call(
         functools.partial(list_kernel, cols, a_slots, row_count, peers),
         out_shape=[
@@ -259,40 +271,51 @@
         copy.wait()
 
 
-def add_products(items, start, stop, a_ref, b_ref, sums, window=None):
+def add_products(items, starts, a_ref, peer_refs, sums, window=None):
     low = iota((ROWS, LANES), 1) < BS
     nothing = jnp.zeros((ROWS, LANES), BF16)
     idle_row = sums.shape[0] - 1
 
-    def some_items(step, carry):
-        for u in range(UNROLL):
-            word = items[step * UNROLL + u]
-            place = (word >> 6) & 63
-            target = (word >> 12) & 63
-            used = (word & IDLE) != IDLE
-            if window is not None:
-                place = place - window
-                used = used & (place >= 0) & (place < CAPACITY)
-                place = jnp.where(used, place, 0)
-            a_at = pl.multiple_of((word >> 18) * ROWS, ROWS)
-            b_at = pl.multiple_of(place * ROWS, ROWS)
-            block = b_ref[pl.ds(b_at, ROWS), :]
-            turned = jnp.concatenate([block[:, BS:], block[:, :BS]], axis=1)
-            right = jnp.concatenate(
-                [
-                    jnp.where(low, block, nothing),
-                    jnp.where(low, turned, nothing),
-                    jnp.where(low, nothing, turned),
-                    jnp.where(low, nothing, block),
-                ],
-                axis=0,
-            )
-            term = jnp.dot(a_ref[pl.ds(a_at, ROWS), :], right, preferred_element_type=F32)
-            i = jnp.where(used, target // SLOTS, idle_row)
-            sums[i, pl.ds(target % SLOTS, ROWS, stride=SLOTS), :] += term
-        return carry
-
-    lax.fori_loop(start // UNROLL, stop // UNROLL, some_items, 0)
+    def add_one(word, used, b_ref):
+        place = (word >> 6) & 63
+        target = (word >> 12) & 63
+        used = used & ((word & IDLE) != IDLE)
+        if window is not None:
+            place = place - window
+            used = used & (place >= 0) & (place < CAPACITY)
+        place = jnp.where(used, place, 0)
+        a_at = pl.multiple_of((word >> 18) * ROWS, ROWS)
+        b_at = pl.multiple_of(place * ROWS, ROWS)
+        block = b_ref[pl.ds(b_at, ROWS), :]
+        turned = jnp.concatenate([block[:, BS:], block[:, :BS]], axis=1)
+        right = jnp.concatenate(
+            [
+                jnp.where(low, block, nothing),
+                jnp.where(low, turned, nothing),
+                jnp.where(low, nothing, turned),
+                jnp.where(low, nothing, block),
+            ],
+            axis=0,
+        )
+        term = jnp.dot(a_ref[pl.ds(a_at, ROWS), :], right, preferred_element_type=F32)
+        i = jnp.where(used, target // SLOTS, idle_row)
+        sums[i, pl.ds(target % SLOTS, ROWS, stride=SLOTS), :] += term
+
+    for at in range(0, len(peer_refs), 3):
+        chosen = peer_refs[at : at + 3]
+        bounds = [(starts[d], starts[d + 1]) for d, _ in chosen]
+        longest = functools.reduce(jnp.maximum, [stop - start for start, stop in bounds])
+        width = UNROLL if len(chosen) < 3 else UNROLL - 1
+
+        def some_items(step, carry, chosen=chosen, bounds=bounds, width=width):
+            for u in range(width):
+                for (_, b_ref), (start, stop) in zip(chosen, bounds):
+                    y = start + step * width + u
+                    used = y < stop
+                    add_one(items[jnp.where(used, y, start)], used, b_ref)
+            return carry
+
+        lax.fori_loop(0, (longest + width - 1) // width, some_items, 0)
 
 
 def stage_kernel(cols, *refs):
@@ -325,7 +348,7 @@
 
     lax.fori_loop(0, row_count, one_row, 0)
     sums[...] = jnp.zeros_like(sums)
-    add_products(items, 0, starts[1], a_out, b_own, sums)
+    add_products(items, starts, a_out, [(0, b_own)], sums)
 
 
 def stage(a_parts, b_blocks, items, starts):
@@ -355,16 +378,10 @@
 def multiply_kernel(first, peers, *refs):
     refs = list(refs)
     base = 0 if first else refs.pop(0)[0]
-    items, starts, most, a_ref, sums_in = refs[:5]
-    b_refs = refs[5 : 4 + peers]
+    items, starts, most, a_ref = refs[:4]
+    b_refs = refs[5 : 4 + peers][::-1]
     out, rounds, sums, rows, sems = refs[4 + peers :]
-    width = CAPACITY * ROWS
-    needed = jnp.max(most[...])
-    for ref in b_refs:
-        needed = jnp.maximum(needed, jnp.max(ref[pl.ds(width, FLAG), :].astype(F32)))
-    rounds[0] = (needed.astype(I32) + CAPACITY - 1) // CAPACITY
-    for d in range(1, peers):
-        add_products(items, starts[d], starts[d + 1], a_ref, b_refs[d - 1], sums, window=base)
+    add_products(items, starts, a_ref, list(enumerate(b_refs, 1)), sums, window=base)
     row_count, kept = out.shape[0], out.shape[1]
     copies = []
     for i in range(row_count):
@@ -372,6 +389,11 @@
             rows[i, :, pl.ds(t * LANES, LANES)] = sums[i, pl.ds(t * kept, kept), :]
         copies.append(pltpu.make_async_copy(rows.at[i], out.at[i], sems.at[i]))
         copies[-1].start()
+    flags = most[...]
+    for ref in b_refs:
+        flag = ref[pl.ds(CAPACITY * ROWS, FLAG), :].astype(F32)
+        flags = jnp.maximum(flags, jnp.max(flag, axis=0, keepdims=True))
+    rounds[0] = (jnp.max(flags).astype(I32) + CAPACITY - 1) // CAPACITY
     for copy in copies:
         copy.wait()
 
@@ -396,7 +418,7 @@
         compiler_params=pltpu.CompilerParams(vmem_limit_bytes=32 << 20),
         cost_estimate=pl.CostEstimate(flops=1 << 26, bytes_accessed=4 << 20, transcendentals=0),
         name="multiply",
-    )(*given, items, starts, most, a_ready, sums, *b_parts)
+    )(*given, items, starts, most, a_ready, sums, *b_parts[::-1])
 
 
 def shards(a_blocks, a_index, b_blocks, b_cols, c_cols):
@@ -406,20 +428,26 @@
     row_count = b_blocks.shape[0]
 
     def send_rows(parts):
-        return [exchanged(part, "row", d + 1) for d, part in enumerate(parts)]
-
+        far_first = range(len(parts), 0, -1)
+        return [exchanged(parts[d - 1], "row", d) for d in far_first][::-1]
+
+    def finish(base, most, sums, arrived):
+        return multiply(base, items, starts, most, a_ready, sums, arrived, shape)
+
+    shape = (row_count, c_cols.shape[1], BS * BS)
     index_parts = [a_index] + [exchanged(a_index, "col", h) for h in range(1, cols)]
     told = describe(index_parts, b_cols.T, c_cols.T)
+    a_soon, _ = lax.optimization_barrier((a_blocks, told))
     told = [told] + send_rows([told] * (rows - 1))
     flat = flatten(b_blocks)
     packed, most = pack(None, told, flat, cols, row_count, a_slots)
     arrived = send_rows(packed)
     items, starts = work_list(told, cols, row_count, a_slots)
     a_late, _ = lax.optimization_barrier((a_blocks, most))
-    a_parts = [a_blocks] + [exchanged(a_late, "col", h) for h in range(1, cols)]
+    a_parts = [a_blocks, exchanged(a_soon, "col", 1)]
+    a_parts += [exchanged(a_late, "col", h) for h in range(2, cols)]
     a_ready, sums = stage(a_parts, b_blocks, items, starts)
-    shape = (row_count, c_cols.shape[1], BS * BS)
-    out, rounds, sums = multiply(None, items, starts, most, a_ready, sums, arrived, shape)
+    out, rounds, sums = finish(None, most, sums, arrived)
 
     def more(state):
         return state[0] < rounds[0]
@@ -428,8 +456,7 @@
         at, sums, _ = state
         base = jnp.reshape(at * CAPACITY, (1,))
         packed, most = pack(base, told, flat, cols, row_count, a_slots)
-        arrived = send_rows(packed)
-        out, _, sums = multiply(base, items, starts, most, a_ready, sums, arrived, shape)
+        out, _, sums = finish(base, most, sums, send_rows(packed))
         return at + 1, sums, out
 
     return lax.while_loop(more, one_round, (jnp.int32(1), sums, out))[2]

time: 35.2 us -> 34.7 us (0.986)
  the two profiles are of different devices: /device:TPU:16 before, /device:TPU:1 now
where the time goes in v1:
time: 34.7 us; the launch traced here: 34.4 us
  starting transfers between devices  15.4 us (44%)
  Pallas kernels  11.4 us (33%)
  waiting for transfers between devices  5.17 us (15%)
  local copies, waits for them, and re-layouts  1.05 us (3%)
  other arithmetic  0.73 us (2%)
  loops' own time  0.63 us (2%)
    ppermute x12, starting transfers between devices, exchanged(): return lax.ppermute(block, axis, [(i, i ^ distance) for i in range(size)])  15.4 us
    ppermute x12, waiting for transfers between devices, exchanged(): return lax.ppermute(block, axis, [(i, i ^ distance) for i in range(size)])  5.17 us
    pallas_call x1, Pallas kernels, work_list(): pl.pallas_call(functools.partial(list_kernel, cols, a_slots, row_count, p...  3.42 us
    pallas_call x1, Pallas kernels, multiply(): pl.pallas_call(functools.partial(multiply_kernel, first, peers), out_shap...  3.07 us
    pallas_call x1, Pallas kernels, stage(): pl.pallas_call(functools.partial(stage_kernel, cols), out_shape=(jax.Shap...  2.33 us
    pallas_call x1, Pallas kernels, pack(): pl.pallas_call(functools.partial(pack_kernel, first, peers, cols, a_slots...  1.38 us
    pallas_call x1, Pallas kernels, flatten(): pl.pallas_call(flatten_kernel, out_shape=jax.ShapeDtypeStruct((count, BS...  1.16 us
    unnamed x8, local copies, waits for them, and re-layouts  1.05 us
  transfers between devices with their start and end apart: 12, of which 4 were waited for; matrix products, arithmetic and copies ran while one was open for 2% of the time, Pallas kernels for 24%

profile of v1, /device:TPU:1, one launch (start us, length us, event | category | flops | bytes accessed | tf_op | source)
XLA Modules:
  0.0 34.4 jit_solution(8655173234070750424)
XLA Ops:
  0.0 0.1 collective-permute-start.3
  0.1 2.5 %collective-permute-start.5 = (s32[2,1,16]{2,1,0:T(1,128)}, s32[2,1,16]{2,1,0:T(1,128)S(1)}, u32[]{:S(2)}, u32[]{:S(2)}) collective-permute-start(s32[2,1,16]{2,1,0:T(1,128)} %param.8), channel_id=1, source_target_pairs={{0,3},{1,2},{2,1},{3,0},{4,7},{5,6},{6,5},{7,4},{8,11},{9,10},{10,... | collective-permute-start | bytes 392 | tf_op jit(solution)/shard_map/ppermute | solution.py:27
  2.6 0.1 collective-permute-start.4
  2.8 0.7 %pad_maximum_fusion.1 = s32[16,128]{1,0:T(8,128)S(1)} fusion(s32[2,16]{1,0:T(2,128)} %bitcast.16, s32[4,16]{1,0:T(4,128)} %bitcast.11, s32[4,16]{1,0:T(4,128)} %bitcast.12), kind=kLoop, calls=%fused_computation.1 | loop fusion | flops 4096 | bytes 8832 | tf_op jit(solution)/shard_map/max | solution.py:39
  3.5 0.0 collective-permute-done.3
  3.5 0.7 %collective-permute-done.5 = s32[2,1,16]{2,1,0:T(1,128)S(1)} collective-permute-done((s32[2,1,16]{2,1,0:T(1,128)}, s32[2,1,16]{2,1,0:T(1,128)S(1)}, u32[]{:S(2)}, u32[]{:S(2)}) %collective-permute-start.5) | collective-permute-done | bytes 160 | tf_op jit(solution)/shard_map/ppermute | solution.py:27
  4.2 1.1 %collective-permute-done.4 = s32[2,1,16]{2,1,0:T(1,128)S(1)} collective-permute-done((s32[2,1,16]{2,1,0:T(1,128)}, s32[2,1,16]{2,1,0:T(1,128)S(1)}, u32[]{:S(2)}, u32[]{:S(2)}) %collective-permute-start.4) | collective-permute-done | bytes 160 | tf_op jit(solution)/shard_map/ppermute | solution.py:27
  5.2 1.7 %collective-permute-start.9 = (bf16[1,16,4096]{2,1,0:T(8,128)(2,1)}, bf16[1,16,4096]{2,1,0:T(8,128)(2,1)S(1)}, u32[]{:S(2)}, u32[]{:S(2)}) collective-permute-start(bf16[1,16,4096]{2,1,0:T(8,128)(2,1)} %refs_0_.1), channel_id=1, source_target_pairs={{0,1},{1,0},{2,3},{3,2},{4,5},{5,4},{6,7},{7,6},{8,9},{9,8},{10,11... | collective-permute-start | bytes 393224 | tf_op jit(solution)/shard_map/ppermute | solution.py:27
  7.0 3.3 %collective-permute-start.8 = (s32[16,128]{1,0:T(8,128)S(1)}, s32[16,128]{1,0:T(8,128)S(1)}, u32[]{:S(2)}, u32[]{:S(2)}) collective-permute-start(s32[16,128]{1,0:T(8,128)S(1)} %pad_maximum_fusion.refs_0_), channel_id=1, source_target_pairs={{0,12},{4,8},{8,4},{12,0},{1,13},{5,9},{9,5},{13,1},{2,14},{6,10},... | collective-permute-start | bytes 24584 | tf_op jit(solution)/shard_map/ppermute | solution.py:27
  10.3 0.0 collective-permute-start.7
  10.3 0.3 collective-permute-start.6
  10.6 1.0 %copy-done = bf16[16,4,4096]{2,1,0:T(4,128)(2,1)S(1)} copy-done((bf16[16,4,4096]{2,1,0:T(4,128)(2,1)S(1)}, bf16[16,4,4096]{2,1,0:T(4,128)(2,1)}, u32[]{:S(2)}) %copy-start) | copy-done | bytes 524312
  11.6 1.2 %flatten.1.refs_4_ = bf16[64,4096]{1,0:T(8,128)(2,1)S(1)} custom-call(bf16[16,4,4096]{2,1,0:T(4,128)(2,1)S(1)} %copy-done), custom_call_target="tpu_custom_call" | custom-call | flops 1048576 | bytes 8388608 | tf_op jit(solution)/shard_map/flatten/pallas_call | solution.py:70
  12.8 0.0 collective-permute-done.8.refs_3_
  12.8 0.9 %collective-permute-done.7.refs_2_ = s32[16,128]{1,0:T(8,128)S(1)} collective-permute-done((s32[16,128]{1,0:T(8,128)S(1)}, s32[16,128]{1,0:T(8,128)S(1)}, u32[]{:S(2)}, u32[]{:S(2)}) %collective-permute-start.7) | collective-permute-done | bytes 8224 | tf_op jit(solution)/shard_map/ppermute | solution.py:27
  13.7 0.0 collective-permute-done.6.refs_1_
  13.7 1.4 %pack.2 = (bf16[528,128]{1,0:T(8,128)(2,1)S(1)}, bf16[528,128]{1,0:T(8,128)(2,1)S(1)}, bf16[528,128]{1,0:T(8,128)(2,1)S(1)}, f32[8,128]{1,0:T(8,128)S(1)}) custom-call(s32[16,128]{1,0:T(8,128)S(1)} %pad_maximum_fusion.refs_0_, s32[16,128]{1,0:T(8,128)S(1)} %collective-permute-done.6.refs_1_, s32[16,128]{1,0:T(8,128)S(1)} %collective-permute-done.7.refs_2_, ...), custom_call_target="tpu_custom_call" | custom-call | flops 1048576 | bytes 4194304 | tf_op jit(solution)/shard_map/pack/pallas_call | solution.py:180
  15.1 2.5 %collective-permute-start.12 = (bf16[528,128]{1,0:T(8,128)(2,1)S(1)}, bf16[528,128]{1,0:T(8,128)(2,1)S(1)}, u32[]{:S(2)}, u32[]{:S(2)}) collective-permute-start(bf16[528,128]{1,0:T(8,128)(2,1)S(1)} %get-tuple-element.93), channel_id=1, source_target_pairs={{0,12},{4,8},{8,4},{12,0},{1,13},{5,9},{9,5},{13,1},{2,14},{6,10},... | collective-permute-start | bytes 405512 | tf_op jit(solution)/shard_map/ppermute | solution.py:27
  17.6 0.0 collective-permute-start.13
  17.6 1.1 %collective-permute-start.14 = (bf16[528,128]{1,0:T(8,128)(2,1)S(1)}, bf16[528,128]{1,0:T(8,128)(2,1)S(1)}, u32[]{:S(2)}, u32[]{:S(2)}) collective-permute-start(bf16[528,128]{1,0:T(8,128)(2,1)S(1)} %get-tuple-element.95), channel_id=1, source_target_pairs={{0,4},{4,0},{8,12},{12,8},{1,5},{5,1},{9,13},{13,9},{2,6},{6,2},{1... | collective-permute-start | bytes 405512 | tf_op jit(solution)/shard_map/ppermute | solution.py:27
  18.7 2.5 %collective-permute-start.11 = (bf16[1,16,4096]{2,1,0:T(8,128)(2,1)S(1)}, bf16[1,16,4096]{2,1,0:T(8,128)(2,1)S(1)}, u32[]{:S(2)}, u32[]{:S(2)}) collective-permute-start(bf16[1,16,4096]{2,1,0:T(8,128)(2,1)S(1)} %copy-done.2), channel_id=1, source_target_pairs={{0,3},{1,2},{2,1},{3,0},{4,7},{5,6},{6,5},{7,4},{8,11},{9,10},{10,... | collective-permute-start | bytes 393224 | tf_op jit(solution)/shard_map/ppermute | solution.py:27
  21.2 0.0 collective-permute-done.9.refs_1_
  21.2 1.2 %collective-permute-start.10 = (bf16[1,16,4096]{2,1,0:T(8,128)(2,1)S(1)}, bf16[1,16,4096]{2,1,0:T(8,128)(2,1)S(1)}, u32[]{:S(2)}, u32[]{:S(2)}) collective-permute-start(bf16[1,16,4096]{2,1,0:T(8,128)(2,1)S(1)} %copy-done.2), channel_id=1, source_target_pairs={{0,2},{1,3},{2,0},{3,1},{4,6},{5,7},{6,4},{7,5},{8,10},{9,11},{10,... | collective-permute-start | bytes 393224 | tf_op jit(solution)/shard_map/ppermute | solution.py:27
  22.4 3.4 %work_list.1 = (s32[257]{0:T(512)S(1)}, s32[5]{0:T(128)S(1)}) custom-call(s32[16,128]{1,0:T(8,128)S(1)} %pad_maximum_fusion.refs_0_, s32[16,128]{1,0:T(8,128)S(1)} %collective-permute-done.6.refs_1_, s32[16,128]{1,0:T(8,128)S(1)} %collective-permute-done.7.refs_2_, s32[16,128]{1,0:T(8,128)S(1)} %collective-permute-done.8.refs_3_), custom_call_target="tpu_custom_call" | custom-call | flops 1048576 | bytes 65536 | tf_op jit(solution)/shard_map/work_list/pallas_call | solution.py:245
  25.8 0.0 collective-permute-done.11.refs_3_
  25.8 2.5 %collective-permute-done.10.refs_2_ = bf16[1,16,4096]{2,1,0:T(8,128)(2,1)S(1)} collective-permute-done((bf16[1,16,4096]{2,1,0:T(8,128)(2,1)S(1)}, bf16[1,16,4096]{2,1,0:T(8,128)(2,1)S(1)}, u32[]{:S(2)}, u32[]{:S(2)}) %collective-permute-start.10) | collective-permute-done | bytes 131104 | tf_op jit(solution)/shard_map/ppermute | solution.py:27
  28.4 2.3 %stage.1 = (bf16[2048,128]{1,0:T(8,128)(2,1)S(1)}, f32[17,128,128]{2,1,0:T(8,128)S(1)}) custom-call(bf16[1,16,4096]{2,1,0:T(8,128)(2,1)S(1)} %copy-done.2, bf16[1,16,4096]{2,1,0:T(8,128)(2,1)S(1)} %collective-permute-done.9.refs_1_, bf16[1,16,4096]{2,1,0:T(8,128)(2,1)S(1)} %collective-permute-done.10.refs_2_, ...), custom_call_target="tpu_custom_call" | custom-call | flops 16777216 | bytes 4194304 | tf_op jit(solution)/shard_map/stage/pallas_call | solution.py:359
  30.7 0.0 collective-permute-done.12.refs_5_
  30.7 0.0 collective-permute-done.13.refs_6_
  30.7 0.0 collective-permute-done.14.refs_7_
  30.7 3.1 %multiply.2 = (f32[16,4,4096]{2,1,0:T(4,128)}, s32[1]{0:T(128)}, f32[17,128,128]{2,1,0:T(8,128)S(1)}) custom-call(s32[257]{0:T(512)S(1)} %get-tuple-element.217.refs_5_.refs_0_, s32[5]{0:T(128)S(1)} %get-tuple-element.218.refs_6_.refs_1_, f32[8,128]{1,0:T(8,128)S(1)} %get-tuple-element.88.refs_2_, ...), custom_call_target="tpu_custom_call", output_to_operand_aliasing={{2}: (4, {})} | custom-call | flops 67108864 | bytes 4194304 | tf_op jit(solution)/shard_map/multiply/pallas_call | solution.py:407
  33.8 0.6 %while.12 = (s32[]{:T(128)}, f32[17,128,128]{2,1,0:T(8,128)S(1)}, f32[16,4,4096]{2,1,0:T(4,128)}, s32[1]{0:T(128)}, s32[16,128]{1,0:T(8,128)S(1)}, /*index=5*/s3...) while((s32[]{:T(128)}, f32[17,128,128]{2,1,0:T(8,128)S(1)}, ...), condition=%wide.region_1.2_spmd, body=%wide.region_0.1_spmd.sunk | while | flops 68157440 | bytes 10010889 | solution.py:462
  (8 shorter events, 0.0 us)
Async XLA Ops:
  0.0 3.5 %collective-permute-start.3 = (s32[2,1,16]{2,1,0:T(1,128)}, s32[2,1,16]{2,1,0:T(1,128)S(1)}, u32[]{:S(2)}, u32[]{:S(2)}) collective-permute-start(s32[2,1,16]{2,1,0:T(1,128)} %param.8), channel_id=1, source_target_pairs={{0,1},{1,0},{2,3},{3,2},{4,5},{5,4},{6,7},{7,6},{8,9},{9,8},{10,11... | collective-permute-start | bytes 392 | tf_op jit(solution)/shard_map/ppermute | solution.py:27
  0.1 4.1 %collective-permute-start.5 = (s32[2,1,16]{2,1,0:T(1,128)}, s32[2,1,16]{2,1,0:T(1,128)S(1)}, u32[]{:S(2)}, u32[]{:S(2)}) collective-permute-start(s32[2,1,16]{2,1,0:T(1,128)} %param.8), channel_id=1, source_target_pairs={{0,3},{1,2},{2,1},{3,0},{4,7},{5,6},{6,5},{7,4},{8,11},{9,10},{10,... | collective-permute-start | bytes 392 | tf_op jit(solution)/shard_map/ppermute | solution.py:27
  2.6 2.6 %collective-permute-start.4 = (s32[2,1,16]{2,1,0:T(1,128)}, s32[2,1,16]{2,1,0:T(1,128)S(1)}, u32[]{:S(2)}, u32[]{:S(2)}) collective-permute-start(s32[2,1,16]{2,1,0:T(1,128)} %param.8), channel_id=1, source_target_pairs={{0,2},{1,3},{2,0},{3,1},{4,6},{5,7},{6,4},{7,5},{8,10},{9,11},{10,... | collective-permute-start | bytes 392 | tf_op jit(solution)/shard_map/ppermute | solution.py:27
  5.2 15.9 %collective-permute-start.9 = (bf16[1,16,4096]{2,1,0:T(8,128)(2,1)}, bf16[1,16,4096]{2,1,0:T(8,128)(2,1)S(1)}, u32[]{:S(2)}, u32[]{:S(2)}) collective-permute-start(bf16[1,16,4096]{2,1,0:T(8,128)(2,1)} %refs_0_.1), channel_id=1, source_target_pairs={{0,1},{1,0},{2,3},{3,2},{4,5},{5,4},{6,7},{7,6},{8,9},{9,8},{10,11... | collective-permute-start | bytes 393224 | tf_op jit(solution)/shard_map/ppermute | solution.py:27
  7.0 5.8 %collective-permute-start.8 = (s32[16,128]{1,0:T(8,128)S(1)}, s32[16,128]{1,0:T(8,128)S(1)}, u32[]{:S(2)}, u32[]{:S(2)}) collective-permute-start(s32[16,128]{1,0:T(8,128)S(1)} %pad_maximum_fusion.refs_0_), channel_id=1, source_target_pairs={{0,12},{4,8},{8,4},{12,0},{1,13},{5,9},{9,5},{13,1},{2,14},{6,10},... | collective-permute-start | bytes 24584 | tf_op jit(solution)/shard_map/ppermute | solution.py:27
  10.3 3.4 %collective-permute-start.7 = (s32[16,128]{1,0:T(8,128)S(1)}, s32[16,128]{1,0:T(8,128)S(1)}, u32[]{:S(2)}, u32[]{:S(2)}) collective-permute-start(s32[16,128]{1,0:T(8,128)S(1)} %pad_maximum_fusion.refs_0_), channel_id=1, source_target_pairs={{0,8},{4,12},{8,0},{12,4},{1,9},{5,13},{9,1},{13,5},{2,10},{6,14},... | collective-permute-start | bytes 24584 | tf_op jit(solution)/shard_map/ppermute | solution.py:27
  10.3 3.4 %collective-permute-start.6 = (s32[16,128]{1,0:T(8,128)S(1)}, s32[16,128]{1,0:T(8,128)S(1)}, u32[]{:S(2)}, u32[]{:S(2)}) collective-permute-start(s32[16,128]{1,0:T(8,128)S(1)} %pad_maximum_fusion.refs_0_), channel_id=1, source_target_pairs={{0,4},{4,0},{8,12},{12,8},{1,5},{5,1},{9,13},{13,9},{2,6},{6,2},{1... | collective-permute-start | bytes 24584 | tf_op jit(solution)/shard_map/ppermute | solution.py:27
  10.6 1.0 %copy-start = (bf16[16,4,4096]{2,1,0:T(4,128)(2,1)S(1)}, bf16[16,4,4096]{2,1,0:T(4,128)(2,1)}, u32[]{:S(2)}) copy-start(bf16[16,4,4096]{2,1,0:T(4,128)(2,1)} %refs_4_.1) | copy-start | bytes 1572868
  11.6 7.1 %copy-start.2 = (bf16[1,16,4096]{2,1,0:T(8,128)(2,1)S(1)}, bf16[1,16,4096]{2,1,0:T(8,128)(2,1)}, u32[]{:S(2)}) copy-start(bf16[1,16,4096]{2,1,0:T(8,128)(2,1)} %refs_0_.1) | copy-start | bytes 393220
  11.6 16.7 %copy-start.1 = (bf16[16,4,4096]{2,1,0:T(4,128)(2,1)S(1)}, bf16[16,4,4096]{2,1,0:T(4,128)(2,1)}, u32[]{:S(2)}) copy-start(bf16[16,4,4096]{2,1,0:T(4,128)(2,1)} %refs_4_.1) | copy-start | bytes 1572868
  15.1 15.6 %collective-permute-start.12 = (bf16[528,128]{1,0:T(8,128)(2,1)S(1)}, bf16[528,128]{1,0:T(8,128)(2,1)S(1)}, u32[]{:S(2)}, u32[]{:S(2)}) collective-permute-start(bf16[528,128]{1,0:T(8,128)(2,1)S(1)} %get-tuple-element.93), channel_id=1, source_target_pairs={{0,12},{4,8},{8,4},{12,0},{1,13},{5,9},{9,5},{13,1},{2,14},{6,10},... | collective-permute-start | bytes 405512 | tf_op jit(solution)/shard_map/ppermute | solution.py:27
  17.6 13.1 %collective-permute-start.13 = (bf16[528,128]{1,0:T(8,128)(2,1)S(1)}, bf16[528,128]{1,0:T(8,128)(2,1)S(1)}, u32[]{:S(2)}, u32[]{:S(2)}) collective-permute-start(bf16[528,128]{1,0:T(8,128)(2,1)S(1)} %get-tuple-element.94), channel_id=1, source_target_pairs={{0,8},{4,12},{8,0},{12,4},{1,9},{5,13},{9,1},{13,5},{2,10},{6,14},... | collective-permute-start | bytes 405512 | tf_op jit(solution)/shard_map/ppermute | solution.py:27
  17.6 13.2 %collective-permute-start.14 = (bf16[528,128]{1,0:T(8,128)(2,1)S(1)}, bf16[528,128]{1,0:T(8,128)(2,1)S(1)}, u32[]{:S(2)}, u32[]{:S(2)}) collective-permute-start(bf16[528,128]{1,0:T(8,128)(2,1)S(1)} %get-tuple-element.95), channel_id=1, source_target_pairs={{0,4},{4,0},{8,12},{12,8},{1,5},{5,1},{9,13},{13,9},{2,6},{6,2},{1... | collective-permute-start | bytes 405512 | tf_op jit(solution)/shard_map/ppermute | solution.py:27
  18.7 7.1 %collective-permute-start.11 = (bf16[1,16,4096]{2,1,0:T(8,128)(2,1)S(1)}, bf16[1,16,4096]{2,1,0:T(8,128)(2,1)S(1)}, u32[]{:S(2)}, u32[]{:S(2)}) collective-permute-start(bf16[1,16,4096]{2,1,0:T(8,128)(2,1)S(1)} %copy-done.2), channel_id=1, source_target_pairs={{0,3},{1,2},{2,1},{3,0},{4,7},{5,6},{6,5},{7,4},{8,11},{9,10},{10,... | collective-permute-start | bytes 393224 | tf_op jit(solution)/shard_map/ppermute | solution.py:27
  21.2 7.2 %collective-permute-start.10 = (bf16[1,16,4096]{2,1,0:T(8,128)(2,1)S(1)}, bf16[1,16,4096]{2,1,0:T(8,128)(2,1)S(1)}, u32[]{:S(2)}, u32[]{:S(2)}) collective-permute-start(bf16[1,16,4096]{2,1,0:T(8,128)(2,1)S(1)} %copy-done.2), channel_id=1, source_target_pairs={{0,2},{1,3},{2,0},{3,1},{4,6},{5,7},{6,4},{7,5},{8,10},{9,11},{10,... | collective-permute-start | bytes 393224 | tf_op jit(solution)/shard_map/ppermute | solution.py:27
  30.7 3.1 %copy-start.3 = (bf16[2048,128]{1,0:T(8,128)(2,1)}, bf16[2048,128]{1,0:T(8,128)(2,1)S(1)}, u32[]{:S(2)}) copy-start(bf16[2048,128]{1,0:T(8,128)(2,1)S(1)} %get-tuple-element.219.refs_3_) | copy-start | bytes 1572868

commit v2 on v1

--- a/solution.py
+++ b/solution.py
@@ -27,8 +27,7 @@
     return lax.ppermute(block, axis, [(i, i ^ distance) for i in range(size)])
 
 
-def describe(a_parts, b_cols, c_cols):
-    cols = len(a_parts)
+def describe(a_index, b_cols, c_cols, cols):
     total = -(-(2 * cols + 2 * SLOTS) // 8) * 8
 
     def placed(part, at):
@@ -36,10 +35,33 @@
         return jnp.pad(part, ((at, after[0]), (0, after[1])), constant_values=-1)
 
     own = jnp.maximum(placed(c_cols, 2 * cols), placed(b_cols, 2 * cols + SLOTS))
-    told = lax.optimization_barrier(jnp.maximum(own, placed(a_parts[0][:, 0, :], 0)))
-    for h in range(1, cols):
-        told = jnp.maximum(told, placed(a_parts[h][:, 0, :], 2 * h))
+    told = lax.optimization_barrier(jnp.maximum(own, placed(a_index[:, 0, :], 0)))
+    h = 1
+    while h < cols:
+        if h == 1:
+            came = exchanged(a_index, "col", 1)[:, 0, :]
+        else:
+            came = exchanged(told, "col", h)[: 2 * h]
+        told = jnp.maximum(told, placed(came, 2 * h))
+        h = 2 * h
     return told
+
+
+def tell_rows(told):
+    parts = [told]
+    d = 1
+    while d < lax.axis_size("row"):
+        known = parts[0] if d == 1 else jnp.concatenate(parts, axis=0)
+        parts.append(exchanged(known, "row", d))
+        d = 2 * d
+    return parts
+
+
+def told_views(refs):
+    height = refs[0].shape[0]
+    return [
+        ref.at[pl.ds(at, height), :] for ref in refs for at in range(0, ref.shape[0], height)
+    ]
 
 
 def offers(told, cols, row_count):
@@ -51,32 +73,6 @@
         moved = pltpu.roll(rows, n * row_count, 1)[n : n + 1]
         result = jnp.where(lane // row_count == n, moved, result)
     return result
-
-
-def flatten_kernel(b_ref, flat, wide):
-    row_count = b_ref.shape[0]
-    for k in range(row_count):
-        for t in range(ROWS):
-            wide[k, pl.ds(t * SLOTS, SLOTS), :] = b_ref[k, :, pl.ds(t * LANES, LANES)].astype(F32)
-    for t in range(ROWS):
-        for n in range(SLOTS):
-            piece = wide[:, t * SLOTS + n, :].astype(BF16)
-            flat[pl.ds(n * row_count, row_count), pl.ds(t * LANES, LANES)] = piece
-
-
-def flatten(b_blocks):
-    vmem_spec = pl.BlockSpec(memory_space=VMEM)
-    count = b_blocks.shape[0] * b_blocks.shape[1]
-    return pl.pallas_call(
-        flatten_kernel,
-        out_shape=jax.ShapeDtypeStruct((count, BS * BS), BF16),
-        in_specs=[vmem_spec],
-        out_specs=vmem_spec,
-        scratch_shapes=[VMEM((b_blocks.shape[0], b_blocks.shape[1] * ROWS, LANES), F32)],
-        compiler_params=pltpu.CompilerParams(vmem_limit_bytes=24 << 20),
-        cost_estimate=pl.CostEstimate(flops=1 << 20, bytes_accessed=8 << 20, transcendentals=0),
-        name="flatten",
-    )(b_blocks)
 
 
 def iota(shape, axis):
@@ -136,13 +132,16 @@
     return start
 
 
-def pack_kernel(first, peers, cols, a_slots, row_count, *refs):
+def pack_kernel(first, peers, cols, a_slots, tellers, *refs):
     refs = list(refs)
     base = 0 if first else refs.pop(0)[0]
-    told = refs[:peers]
-    flat = refs[peers]
-    outs = refs[peers + 1 : 2 * peers]
-    most, picks, packed = refs[2 * peers :]
+    told = told_views(refs[:tellers])
+    b_any = refs[tellers]
+    outs = refs[tellers + 1 : tellers + peers]
+    most, b_ref, picks, wide, packed, sem = refs[tellers + peers :]
+    loading = pltpu.make_async_copy(b_any, b_ref, sem.at[0])
+    loading.start()
+    row_count = b_ref.shape[0]
     grid_row = lax.axis_index("row")
     per_col = peers // cols
     offered = offers(told[0], cols, row_count)
@@ -158,9 +157,17 @@
         picks[pl.ds((d - 1) * CAPACITY, CAPACITY), :] = pick
         top = jnp.maximum(top, jnp.sum(needed, axis=1, keepdims=True))
     most[...] = jnp.broadcast_to(top, most.shape)
-    pick = picks[...][:, : flat.shape[0]]
+    loading.wait()
+    for k in range(row_count):
+        for t in range(ROWS):
+            wide[k, pl.ds(t * SLOTS, SLOTS), :] = b_ref[k, :, pl.ds(t * LANES, LANES)].astype(F32)
+    pick = picks[...][:, : row_count * SLOTS]
     for t in range(0, ROWS, 2):
-        both = flat[:, pl.ds(t * LANES, 2 * LANES)]
+        pair = [
+            jnp.concatenate([wide[:, at * SLOTS + n, :] for n in range(SLOTS)], axis=0)
+            for at in (t, t + 1)
+        ]
+        both = jnp.concatenate(pair, axis=1).astype(BF16)
         both = jnp.dot(pick, both, preferred_element_type=F32)
         packed[:, t, :] = both[:, :LANES]
         packed[:, t + 1, :] = both[:, LANES:]
@@ -171,32 +178,36 @@
         out[pl.ds(CAPACITY * ROWS, FLAG), :] = jnp.broadcast_to(top, (FLAG, LANES)).astype(BF16)
 
 
-def pack(base, told, flat, cols, row_count, a_slots):
+def pack(base, told, b_blocks, peers, cols, a_slots):
     first = base is None
-    peers = len(told)
     smem_spec = pl.BlockSpec(memory_space=SMEM)
     vmem_spec = pl.BlockSpec(memory_space=VMEM)
     given = [] if first else [base]
     results = pl.pallas_call(
-        functools.partial(pack_kernel, first, peers, cols, a_slots, row_count),
+        functools.partial(pack_kernel, first, peers, cols, a_slots, len(told)),
         out_shape=[jax.ShapeDtypeStruct((CAPACITY * ROWS + FLAG, LANES), BF16)] * (peers - 1)
         + [jax.ShapeDtypeStruct((8, LANES), F32)],
-        in_specs=[smem_spec] * len(given) + [vmem_spec] * (peers + 1),
+        in_specs=[smem_spec] * len(given)
+        + [vmem_spec] * len(told)
+        + [pl.BlockSpec(memory_space=pl.ANY)],
         out_specs=[vmem_spec] * peers,
         scratch_shapes=[
+            VMEM(b_blocks.shape, BF16),
             VMEM(((peers - 1) * CAPACITY, LANES), BF16),
+            VMEM((b_blocks.shape[0], SLOTS * ROWS, LANES), F32),
             VMEM(((peers - 1) * CAPACITY, ROWS, LANES), F32),
+            pltpu.SemaphoreType.DMA((1,)),
         ],
         compiler_params=pltpu.CompilerParams(vmem_limit_bytes=32 << 20),
         cost_estimate=pl.CostEstimate(flops=1 << 20, bytes_accessed=4 << 20, transcendentals=0),
         name="pack",
-    )(*given, *told, flat)
+    )(*given, *told, b_blocks)
     return results[:-1], results[-1]
 
 
-def list_kernel(cols, a_slots, row_count, peers, *refs):
-    told = refs[:peers]
-    items, starts, words, words_s, sem = refs[peers:]
+def list_kernel(cols, a_slots, row_count, peers, tellers, *refs):
+    told = told_views(refs[:tellers])
+    items, starts, words, words_s, sem = refs[tellers:]
     grid_row = lax.axis_index("row")
     per_col = peers // cols
     lane = iota((a_slots, LANES), 1)
@@ -239,16 +250,15 @@
     items[length] = IDLE
 
 
-def work_list(told, cols, row_count, a_slots):
-    peers = len(told)
+def work_list(told, peers, cols, row_count, a_slots):
     most_items = peers * a_slots * SLOTS + 1
     return pl.pallas_call(
-        functools.partial(list_kernel, cols, a_slots, row_count, peers),
+        functools.partial(list_kernel, cols, a_slots, row_count, peers, len(told)),
         out_shape=[
             jax.ShapeDtypeStruct((most_items,), I32),
             jax.ShapeDtypeStruct((peers + 1,), I32),
         ],
-        in_specs=[pl.BlockSpec(memory_space=VMEM)] * peers,
+        in_specs=[pl.BlockSpec(memory_space=VMEM)] * len(told),
         out_specs=[pl.BlockSpec(memory_space=SMEM)] * 2,
         scratch_shapes=[
             VMEM((a_slots, LANES), I32),
@@ -319,14 +329,23 @@
 
 
 def stage_kernel(cols, *refs):
-    a_refs, b_ref, items, starts = refs[:cols], refs[cols], refs[cols + 1], refs[cols + 2]
-    a_out, sums, a_wide, b_wide, b_own = refs[cols + 3 :]
+    a_refs, b_any, items, starts = list(refs[:cols]), refs[cols], refs[cols + 1], refs[cols + 2]
+    a_out, sums, a_ref, b_ref, a_wide, b_wide, b_own, sems = refs[cols + 3 :]
+    loading = [
+        pltpu.make_async_copy(a_refs[0], a_ref, sems.at[0]),
+        pltpu.make_async_copy(b_any, b_ref, sems.at[1]),
+    ]
+    for copy in loading:
+        copy.start()
+    a_refs[0] = a_ref
+    sums[...] = jnp.zeros_like(sums)
     source = iota((LANES, LANES), 0)
     target = iota((LANES, LANES), 1)
     wanted = (target // BS) * BS + 2 * (target % ROWS) + (target // ROWS) % 2
     order = (source == wanted).astype(BF16)
     slots = a_refs[0].shape[1]
     grid_col = lax.axis_index("col")
+    loading[0].wait()
     for t in range(ROWS):
         pieces = [ref[0, :, pl.ds(t * LANES, LANES)] for ref in a_refs]
         done = jnp.dot(jnp.concatenate(pieces, axis=0), order, preferred_element_type=F32)
@@ -346,14 +365,15 @@
             b_own[pl.ds(at, ROWS), :] = b_wide[pl.ds(n, ROWS, stride=slots), :].astype(BF16)
         return carry
 
+    loading[1].wait()
     lax.fori_loop(0, row_count, one_row, 0)
-    sums[...] = jnp.zeros_like(sums)
     add_products(items, starts, a_out, [(0, b_own)], sums)
 
 
 def stage(a_parts, b_blocks, items, starts):
     cols, slots = len(a_parts), a_parts[0].shape[1]
     row_count, b_slots = b_blocks.shape[0], b_blocks.shape[1]
+    any_spec = pl.BlockSpec(memory_space=pl.ANY)
     vmem_spec = pl.BlockSpec(memory_space=VMEM)
     smem_spec = pl.BlockSpec(memory_space=SMEM)
     return pl.pallas_call(
@@ -362,12 +382,15 @@
             jax.ShapeDtypeStruct((cols * slots * ROWS, LANES), BF16),
             jax.ShapeDtypeStruct((row_count + 1, ROWS * b_slots, LANES), F32),
         ),
-        in_specs=[vmem_spec] * (cols + 1) + [smem_spec] * 2,
+        in_specs=[any_spec] + [vmem_spec] * (cols - 1) + [any_spec] + [smem_spec] * 2,
         out_specs=(vmem_spec,) * 2,
         scratch_shapes=[
+            VMEM(a_parts[0].shape, BF16),
+            VMEM(b_blocks.shape, BF16),
             VMEM((cols * slots, ROWS, LANES), F32),
             VMEM((b_slots * ROWS, LANES), F32),
             VMEM((row_count * b_slots * ROWS, LANES), BF16),
+            pltpu.SemaphoreType.DMA((2,)),
         ],
         compiler_params=pltpu.CompilerParams(vmem_limit_bytes=40 << 20),
         cost_estimate=pl.CostEstimate(flops=1 << 24, bytes_accessed=4 << 20, transcendentals=0),
@@ -435,17 +458,16 @@
         return multiply(base, items, starts, most, a_ready, sums, arrived, shape)
 
     shape = (row_count, c_cols.shape[1], BS * BS)
-    index_parts = [a_index] + [exchanged(a_index, "col", h) for h in range(1, cols)]
-    told = describe(index_parts, b_cols.T, c_cols.T)
-    a_soon, _ = lax.optimization_barrier((a_blocks, told))
-    told = [told] + send_rows([told] * (rows - 1))
-    flat = flatten(b_blocks)
-    packed, most = pack(None, told, flat, cols, row_count, a_slots)
+    told = tell_rows(describe(a_index, b_cols.T, c_cols.T, cols))
+    packed, most = pack(None, told, b_blocks, rows, cols, a_slots)
     arrived = send_rows(packed)
-    items, starts = work_list(told, cols, row_count, a_slots)
+    items, starts = work_list(told, rows, cols, row_count, a_slots)
     a_late, _ = lax.optimization_barrier((a_blocks, most))
-    a_parts = [a_blocks, exchanged(a_soon, "col", 1)]
-    a_parts += [exchanged(a_late, "col", h) for h in range(2, cols)]
+    a_parts = [a_blocks, exchanged(a_late, "col", 1)]
+    a_soon, _ = lax.optimization_barrier((a_blocks, told[1]))
+    for h in range(2, cols, 2):
+        far = exchanged(a_soon, "col", h)
+        a_parts += [far, exchanged(far, "col", 1)]
     a_ready, sums = stage(a_parts, b_blocks, items, starts)
     out, rounds, sums = finish(None, most, sums, arrived)
 
@@ -455,7 +477,7 @@
     def one_round(state):
         at, sums, _ = state
         base = jnp.reshape(at * CAPACITY, (1,))
-        packed, most = pack(base, told, flat, cols, row_count, a_slots)
+        packed, most = pack(base, told, b_blocks, rows, cols, a_slots)
         out, _, sums = finish(base, most, sums, send_rows(packed))
         return at + 1, sums, out
 

time: 34.7 us -> 34.5 us (level)
  the two profiles are of different devices: /device:TPU:1 before, /device:TPU:0 now
where the time goes in v2:
time: 34.5 us; the launch traced here: 34.1 us
  starting transfers between devices  15 us (43%)
  Pallas kernels  11.1 us (32%)
  waiting for transfers between devices  5.63 us (16%)
  local copies, waits for them, and re-layouts  0.91 us (3%)
  other arithmetic  0.74 us (2%)
  loops' own time  0.63 us (2%)
    ppermute x10, starting transfers between devices, exchanged(): return lax.ppermute(block, axis, [(i, i ^ distance) for i in range(size)])  15 us
    ppermute x10, waiting for transfers between devices, exchanged(): return lax.ppermute(block, axis, [(i, i ^ distance) for i in range(size)])  5.63 us
    pallas_call x1, Pallas kernels, work_list(): pl.pallas_call(functools.partial(list_kernel, cols, a_slots, row_count, p...  3.42 us
    pallas_call x1, Pallas kernels, multiply(): pl.pallas_call(functools.partial(multiply_kernel, first, peers), out_shap...  2.78 us
    pallas_call x1, Pallas kernels, stage(): pl.pallas_call(functools.partial(stage_kernel, cols), out_shape=(jax.Shap...  2.56 us
    pallas_call x1, Pallas kernels, pack(): pl.pallas_call(functools.partial(pack_kernel, first, peers, cols, a_slots...  2.38 us
    unnamed x4, local copies, waits for them, and re-layouts  0.91 us
    max x1, other arithmetic, describe(): jnp.maximum(own, placed(a_index[:, 0, :], 0))  0.72 us
  transfers between devices with their start and end apart: 10, of which 4 were waited for; matrix products, arithmetic and copies ran while one was open for 2% of the time, Pallas kernels for 25%

profile of v2, /device:TPU:0, one launch (start us, length us, event | category | flops | bytes accessed | tf_op | source)
XLA Modules:
  0.0 34.1 jit_solution(5550523888019359956)
XLA Ops:
  0.0 0.5 %collective-permute-start.3 = (s32[2,1,16]{2,1,0:T(1,128)}, s32[2,1,16]{2,1,0:T(1,128)S(1)}, u32[]{:S(2)}, u32[]{:S(2)}) collective-permute-start(s32[2,1,16]{2,1,0:T(1,128)} %param.8), channel_id=1, source_target_pairs={{0,1},{1,0},{2,3},{3,2},{4,5},{5,4},{6,7},{7,6},{8,9},{9,8},{10,11... | collective-permute-start | bytes 392 | tf_op jit(solution)/shard_map/ppermute | solution.py:27
  0.5 0.7 %pad_maximum_fusion.2 = s32[16,128]{1,0:T(8,128)S(1)} fusion(s32[2,16]{1,0:T(2,128)} %bitcast.12, s32[4,16]{1,0:T(4,128)} %bitcast.9, s32[4,16]{1,0:T(4,128)} %bitcast.10), kind=kLoop, calls=%fused_computation.3 | loop fusion | flops 4096 | bytes 8832 | tf_op jit(solution)/shard_map/max | solution.py:38
  1.2 0.3 collective-permute-done.3
  1.5 2.9 %collective-permute-start.4 = (s32[16,128]{1,0:T(8,128)S(1)}, s32[16,128]{1,0:T(8,128)S(1)}, u32[]{:S(2)}, u32[]{:S(2)}) collective-permute-start(s32[16,128]{1,0:T(8,128)S(1)} %pad_maximum_fusion.1), channel_id=1, source_target_pairs={{0,2},{1,3},{2,0},{3,1},{4,6},{5,7},{6,4},{7,5},{8,10},{9,11},{10,... | collective-permute-start | bytes 24584 | tf_op jit(solution)/shard_map/ppermute | solution.py:27
  4.4 1.6 %collective-permute-done.4 = s32[16,128]{1,0:T(8,128)S(1)} collective-permute-done((s32[16,128]{1,0:T(8,128)S(1)}, s32[16,128]{1,0:T(8,128)S(1)}, u32[]{:S(2)}, u32[]{:S(2)}) %collective-permute-start.4) | collective-permute-done | bytes 8224 | tf_op jit(solution)/shard_map/ppermute | solution.py:27
  6.0 2.2 %collective-permute-start.5 = (s32[16,128]{1,0:T(8,128)S(1)}, s32[16,128]{1,0:T(8,128)S(1)}, u32[]{:S(2)}, u32[]{:S(2)}) collective-permute-start(s32[16,128]{1,0:T(8,128)S(1)} %pad_maximum_fusion.refs_0_), channel_id=1, source_target_pairs={{0,4},{4,0},{8,12},{12,8},{1,5},{5,1},{9,13},{13,9},{2,6},{6,2},{1... | collective-permute-start | bytes 24584 | tf_op jit(solution)/shard_map/ppermute | solution.py:27
  8.2 1.6 %collective-permute-done.5.refs_1_ = s32[16,128]{1,0:T(8,128)S(1)} collective-permute-done((s32[16,128]{1,0:T(8,128)S(1)}, s32[16,128]{1,0:T(8,128)S(1)}, u32[]{:S(2)}, u32[]{:S(2)}) %collective-permute-start.5) | collective-permute-done | bytes 8224 | tf_op jit(solution)/shard_map/ppermute | solution.py:27
  9.8 1.9 %collective-permute-start.8 = (bf16[1,16,4096]{2,1,0:T(8,128)(2,1)}, bf16[1,16,4096]{2,1,0:T(8,128)(2,1)S(1)}, u32[]{:S(2)}, u32[]{:S(2)}) collective-permute-start(bf16[1,16,4096]{2,1,0:T(8,128)(2,1)} %refs_0_.1), channel_id=1, source_target_pairs={{0,2},{1,3},{2,0},{3,1},{4,6},{5,7},{6,4},{7,5},{8,10},{9,11},{10,... | collective-permute-start | bytes 393224 | tf_op jit(solution)/shard_map/ppermute | solution.py:27
  11.7 2.6 %collective-permute-start.6 = (s32[32,128]{1,0:T(8,128)S(1)}, s32[32,128]{1,0:T(8,128)S(1)}, u32[]{:S(2)}, u32[]{:S(2)}) collective-permute-start(s32[32,128]{1,0:T(8,128)S(1)} %pad_add_fusion), channel_id=1, source_target_pairs={{0,8},{4,12},{8,0},{12,4},{1,9},{5,13},{9,1},{13,5},{2,10},{6,14},... | collective-permute-start | bytes 49160 | tf_op jit(solution)/shard_map/ppermute | solution.py:27
  14.3 2.0 %collective-permute-done.6.refs_2_ = s32[32,128]{1,0:T(8,128)S(1)} collective-permute-done((s32[32,128]{1,0:T(8,128)S(1)}, s32[32,128]{1,0:T(8,128)S(1)}, u32[]{:S(2)}, u32[]{:S(2)}) %collective-permute-start.6) | collective-permute-done | bytes 16416 | tf_op jit(solution)/shard_map/ppermute | solution.py:27
  16.4 2.4 %pack.2 = (bf16[528,128]{1,0:T(8,128)(2,1)S(1)}, bf16[528,128]{1,0:T(8,128)(2,1)S(1)}, bf16[528,128]{1,0:T(8,128)(2,1)S(1)}, f32[8,128]{1,0:T(8,128)S(1)}) custom-call(s32[16,128]{1,0:T(8,128)S(1)} %pad_maximum_fusion.refs_0_, s32[16,128]{1,0:T(8,128)S(1)} %collective-permute-done.5.refs_1_, s32[32,128]{1,0:T(8,128)S(1)} %collective-permute-done.6.refs_2_, ...), custom_call_target="tpu_custom_call" | custom-call | flops 1048576 | bytes 4194304 | tf_op jit(solution)/shard_map/pack/pallas_call | solution.py:186
  18.8 3.7 %collective-permute-start.10 = (bf16[528,128]{1,0:T(8,128)(2,1)S(1)}, bf16[528,128]{1,0:T(8,128)(2,1)S(1)}, u32[]{:S(2)}, u32[]{:S(2)}) collective-permute-start(bf16[528,128]{1,0:T(8,128)(2,1)S(1)} %get-tuple-element.88), channel_id=1, source_target_pairs={{0,12},{4,8},{8,4},{12,0},{1,13},{5,9},{9,5},{13,1},{2,14},{6,10},... | collective-permute-start | bytes 405512 | tf_op jit(solution)/shard_map/ppermute | solution.py:27
  22.5 0.0 collective-permute-start.11
  22.5 0.7 %collective-permute-start.12 = (bf16[528,128]{1,0:T(8,128)(2,1)S(1)}, bf16[528,128]{1,0:T(8,128)(2,1)S(1)}, u32[]{:S(2)}, u32[]{:S(2)}) collective-permute-start(bf16[528,128]{1,0:T(8,128)(2,1)S(1)} %get-tuple-element.90), channel_id=1, source_target_pairs={{0,4},{4,0},{8,12},{12,8},{1,5},{5,1},{9,13},{13,9},{2,6},{6,2},{1... | collective-permute-start | bytes 405512 | tf_op jit(solution)/shard_map/ppermute | solution.py:27
  23.2 0.0 collective-permute-start.7
  23.2 0.0 collective-permute-done.8.refs_2_
  23.2 0.5 %collective-permute-start.9 = (bf16[1,16,4096]{2,1,0:T(8,128)(2,1)S(1)}, bf16[1,16,4096]{2,1,0:T(8,128)(2,1)S(1)}, u32[]{:S(2)}, u32[]{:S(2)}) collective-permute-start(bf16[1,16,4096]{2,1,0:T(8,128)(2,1)S(1)} %collective-permute-done.8.refs_2_), channel_id=1, source_target_pairs={{0,1},{1,0},{2,3},{3,2},{4,5},{5,4},{6,7},{7,6},{8,9},{9,8},{10,11... | collective-permute-start | bytes 393224 | tf_op jit(solution)/shard_map/ppermute | solution.py:27
  23.7 3.4 %work_list.1 = (s32[257]{0:T(512)S(1)}, s32[5]{0:T(128)S(1)}) custom-call(s32[16,128]{1,0:T(8,128)S(1)} %pad_maximum_fusion.refs_0_, s32[16,128]{1,0:T(8,128)S(1)} %collective-permute-done.5.refs_1_, s32[32,128]{1,0:T(8,128)S(1)} %collective-permute-done.6.refs_2_), custom_call_target="tpu_custom_call" | custom-call | flops 1048576 | bytes 65536 | tf_op jit(solution)/shard_map/work_list/pallas_call | solution.py:255
  27.2 0.0 collective-permute-done.7.refs_1_
  27.2 0.0 collective-permute-done.9.refs_3_
  27.2 0.0 copy-start
  27.2 0.9 %copy-done = bf16[1,16,4096]{2,1,0:T(8,128)(2,1)S(1)} copy-done((bf16[1,16,4096]{2,1,0:T(8,128)(2,1)S(1)}, bf16[1,16,4096]{2,1,0:T(8,128)(2,1)}, u32[]{:S(2)}) %copy-start) | copy-done | bytes 131096
  28.1 2.6 %stage.1 = (bf16[2048,128]{1,0:T(8,128)(2,1)S(1)}, f32[17,128,128]{2,1,0:T(8,128)S(1)}) custom-call(bf16[1,16,4096]{2,1,0:T(8,128)(2,1)S(1)} %copy-done, bf16[1,16,4096]{2,1,0:T(8,128)(2,1)S(1)} %collective-permute-done.7.refs_1_, bf16[1,16,4096]{2,1,0:T(8,128)(2,1)S(1)} %collective-permute-done.8.refs_2_, ...), custom_call_target="tpu_custom_call" | custom-call | flops 16777216 | bytes 4194304 | tf_op jit(solution)/shard_map/stage/pallas_call | solution.py:379
  30.7 0.0 copy-start.1
  30.7 0.0 collective-permute-done.10.refs_5_
  30.7 0.0 collective-permute-done.11.refs_6_
  30.7 0.0 collective-permute-done.12.refs_7_
  30.7 2.8 %multiply.2 = (f32[16,4,4096]{2,1,0:T(4,128)}, s32[1]{0:T(128)}, f32[17,128,128]{2,1,0:T(8,128)S(1)}) custom-call(s32[257]{0:T(512)S(1)} %get-tuple-element.203.refs_5_.refs_0_, s32[5]{0:T(128)S(1)} %get-tuple-element.204.refs_6_.refs_1_, f32[8,128]{1,0:T(8,128)S(1)} %get-tuple-element.83.refs_2_, ...), custom_call_target="tpu_custom_call", output_to_operand_aliasing={{2}: (4, {})} | custom-call | flops 67108864 | bytes 4194304 | tf_op jit(solution)/shard_map/multiply/pallas_call | solution.py:430
  33.5 0.0 copy-done.1
  33.5 0.6 %while.12 = (s32[]{:T(128)}, f32[17,128,128]{2,1,0:T(8,128)S(1)}, f32[16,4,4096]{2,1,0:T(4,128)}, s32[1]{0:T(128)}, s32[16,128]{1,0:T(8,128)S(1)}, /*index=5*/s3...) while((s32[]{:T(128)}, f32[17,128,128]{2,1,0:T(8,128)S(1)}, ...), condition=%wide.region_1.2_spmd, body=%wide.region_0.1_spmd.sunk | while | flops 68157440 | bytes 10010881 | solution.py:484
  (4 shorter events, 0.0 us)
Async XLA Ops:
  0.0 1.5 %collective-permute-start.3 = (s32[2,1,16]{2,1,0:T(1,128)}, s32[2,1,16]{2,1,0:T(1,128)S(1)}, u32[]{:S(2)}, u32[]{:S(2)}) collective-permute-start(s32[2,1,16]{2,1,0:T(1,128)} %param.8), channel_id=1, source_target_pairs={{0,1},{1,0},{2,3},{3,2},{4,5},{5,4},{6,7},{7,6},{8,9},{9,8},{10,11... | collective-permute-start | bytes 392 | tf_op jit(solution)/shard_map/ppermute | solution.py:27
  1.5 4.5 %collective-permute-start.4 = (s32[16,128]{1,0:T(8,128)S(1)}, s32[16,128]{1,0:T(8,128)S(1)}, u32[]{:S(2)}, u32[]{:S(2)}) collective-permute-start(s32[16,128]{1,0:T(8,128)S(1)} %pad_maximum_fusion.1), channel_id=1, source_target_pairs={{0,2},{1,3},{2,0},{3,1},{4,6},{5,7},{6,4},{7,5},{8,10},{9,11},{10,... | collective-permute-start | bytes 24584 | tf_op jit(solution)/shard_map/ppermute | solution.py:27
  6.0 3.8 %collective-permute-start.5 = (s32[16,128]{1,0:T(8,128)S(1)}, s32[16,128]{1,0:T(8,128)S(1)}, u32[]{:S(2)}, u32[]{:S(2)}) collective-permute-start(s32[16,128]{1,0:T(8,128)S(1)} %pad_maximum_fusion.refs_0_), channel_id=1, source_target_pairs={{0,4},{4,0},{8,12},{12,8},{1,5},{5,1},{9,13},{13,9},{2,6},{6,2},{1... | collective-permute-start | bytes 24584 | tf_op jit(solution)/shard_map/ppermute | solution.py:27
  9.8 13.4 %collective-permute-start.8 = (bf16[1,16,4096]{2,1,0:T(8,128)(2,1)}, bf16[1,16,4096]{2,1,0:T(8,128)(2,1)S(1)}, u32[]{:S(2)}, u32[]{:S(2)}) collective-permute-start(bf16[1,16,4096]{2,1,0:T(8,128)(2,1)} %refs_0_.1), channel_id=1, source_target_pairs={{0,2},{1,3},{2,0},{3,1},{4,6},{5,7},{6,4},{7,5},{8,10},{9,11},{10,... | collective-permute-start | bytes 393224 | tf_op jit(solution)/shard_map/ppermute | solution.py:27
  11.7 4.6 %collective-permute-start.6 = (s32[32,128]{1,0:T(8,128)S(1)}, s32[32,128]{1,0:T(8,128)S(1)}, u32[]{:S(2)}, u32[]{:S(2)}) collective-permute-start(s32[32,128]{1,0:T(8,128)S(1)} %pad_add_fusion), channel_id=1, source_target_pairs={{0,8},{4,12},{8,0},{12,4},{1,9},{5,13},{9,1},{13,5},{2,10},{6,14},... | collective-permute-start | bytes 49160 | tf_op jit(solution)/shard_map/ppermute | solution.py:27
  18.8 11.9 %collective-permute-start.10 = (bf16[528,128]{1,0:T(8,128)(2,1)S(1)}, bf16[528,128]{1,0:T(8,128)(2,1)S(1)}, u32[]{:S(2)}, u32[]{:S(2)}) collective-permute-start(bf16[528,128]{1,0:T(8,128)(2,1)S(1)} %get-tuple-element.88), channel_id=1, source_target_pairs={{0,12},{4,8},{8,4},{12,0},{1,13},{5,9},{9,5},{13,1},{2,14},{6,10},... | collective-permute-start | bytes 405512 | tf_op jit(solution)/shard_map/ppermute | solution.py:27
  22.5 8.2 %collective-permute-start.11 = (bf16[528,128]{1,0:T(8,128)(2,1)S(1)}, bf16[528,128]{1,0:T(8,128)(2,1)S(1)}, u32[]{:S(2)}, u32[]{:S(2)}) collective-permute-start(bf16[528,128]{1,0:T(8,128)(2,1)S(1)} %get-tuple-element.89), channel_id=1, source_target_pairs={{0,8},{4,12},{8,0},{12,4},{1,9},{5,13},{9,1},{13,5},{2,10},{6,14},... | collective-permute-start | bytes 405512 | tf_op jit(solution)/shard_map/ppermute | solution.py:27
  22.5 8.2 %collective-permute-start.12 = (bf16[528,128]{1,0:T(8,128)(2,1)S(1)}, bf16[528,128]{1,0:T(8,128)(2,1)S(1)}, u32[]{:S(2)}, u32[]{:S(2)}) collective-permute-start(bf16[528,128]{1,0:T(8,128)(2,1)S(1)} %get-tuple-element.90), channel_id=1, source_target_pairs={{0,4},{4,0},{8,12},{12,8},{1,5},{5,1},{9,13},{13,9},{2,6},{6,2},{1... | collective-permute-start | bytes 405512 | tf_op jit(solution)/shard_map/ppermute | solution.py:27
  23.2 4.0 %collective-permute-start.7 = (bf16[1,16,4096]{2,1,0:T(8,128)(2,1)}, bf16[1,16,4096]{2,1,0:T(8,128)(2,1)S(1)}, u32[]{:S(2)}, u32[]{:S(2)}) collective-permute-start(bf16[1,16,4096]{2,1,0:T(8,128)(2,1)} %refs_0_.1), channel_id=1, source_target_pairs={{0,1},{1,0},{2,3},{3,2},{4,5},{5,4},{6,7},{7,6},{8,9},{9,8},{10,11... | collective-permute-start | bytes 393224 | tf_op jit(solution)/shard_map/ppermute | solution.py:27
  23.2 4.0 %collective-permute-start.9 = (bf16[1,16,4096]{2,1,0:T(8,128)(2,1)S(1)}, bf16[1,16,4096]{2,1,0:T(8,128)(2,1)S(1)}, u32[]{:S(2)}, u32[]{:S(2)}) collective-permute-start(bf16[1,16,4096]{2,1,0:T(8,128)(2,1)S(1)} %collective-permute-done.8.refs_2_), channel_id=1, source_target_pairs={{0,1},{1,0},{2,3},{3,2},{4,5},{5,4},{6,7},{7,6},{8,9},{9,8},{10,11... | collective-permute-start | bytes 393224 | tf_op jit(solution)/shard_map/ppermute | solution.py:27
  27.2 0.9 %copy-start = (bf16[1,16,4096]{2,1,0:T(8,128)(2,1)S(1)}, bf16[1,16,4096]{2,1,0:T(8,128)(2,1)}, u32[]{:S(2)}) copy-start(bf16[1,16,4096]{2,1,0:T(8,128)(2,1)} %refs_0_.1) | copy-start | bytes 393220
  30.7 2.8 %copy-start.1 = (bf16[16,4,4096]{2,1,0:T(4,128)(2,1)S(1)}, bf16[16,4,4096]{2,1,0:T(4,128)(2,1)}, u32[]{:S(2)}) copy-start(bf16[16,4,4096]{2,1,0:T(4,128)(2,1)} %refs_4_.1) | copy-start | bytes 1572868

commit v3 on v1

--- a/solution.py
+++ b/solution.py
@@ -255,7 +255,7 @@
             SMEM((a_slots, LANES), I32),
             pltpu.SemaphoreType.DMA((1,)),
         ],
-        cost_estimate=pl.CostEstimate(flops=1 << 20, bytes_accessed=1 << 16, transcendentals=0),
+        cost_estimate=pl.CostEstimate(flops=1 << 33, bytes_accessed=1 << 16, transcendentals=0),
         name="work_list",
     )(*told)
 
@@ -437,15 +437,16 @@
     shape = (row_count, c_cols.shape[1], BS * BS)
     index_parts = [a_index] + [exchanged(a_index, "col", h) for h in range(1, cols)]
     told = describe(index_parts, b_cols.T, c_cols.T)
-    a_soon, _ = lax.optimization_barrier((a_blocks, told))
     told = [told] + send_rows([told] * (rows - 1))
     flat = flatten(b_blocks)
     packed, most = pack(None, told, flat, cols, row_count, a_slots)
     arrived = send_rows(packed)
     items, starts = work_list(told, cols, row_count, a_slots)
     a_late, _ = lax.optimization_barrier((a_blocks, most))
-    a_parts = [a_blocks, exchanged(a_soon, "col", 1)]
-    a_parts += [exchanged(a_late, "col", h) for h in range(2, cols)]
+    a_parts = [a_blocks, exchanged(a_late, "col", 1)]
+    for h in range(2, cols, 2):
+        far = exchanged(a_late, "col", h)
+        a_parts += [far, exchanged(lax.optimization_barrier((far, items))[0], "col", 1)]
     a_ready, sums = stage(a_parts, b_blocks, items, starts)
     out, rounds, sums = finish(None, most, sums, arrived)
 

time: 34.7 us -> 33.3 us (0.960)
  the two profiles are of different devices: /device:TPU:1 before, /device:TPU:0 now
where the time goes in v3:
time: 33.3 us; the launch traced here: 33.2 us
  starting transfers between devices  13.1 us (39%)
  Pallas kernels  11.6 us (35%)
  waiting for transfers between devices  5.91 us (18%)
  local copies, waits for them, and re-layouts  1.05 us (3%)
  other arithmetic  0.77 us (2%)
  loops' own time  0.63 us (2%)
    ppermute x12, starting transfers between devices, exchanged(): return lax.ppermute(block, axis, [(i, i ^ distance) for i in range(size)])  13.1 us
    ppermute x12, waiting for transfers between devices, exchanged(): return lax.ppermute(block, axis, [(i, i ^ distance) for i in range(size)])  5.91 us
    pallas_call x1, Pallas kernels, work_list(): pl.pallas_call(functools.partial(list_kernel, cols, a_slots, row_count, p...  3.42 us
    pallas_call x1, Pallas kernels, multiply(): pl.pallas_call(functools.partial(multiply_kernel, first, peers), out_shap...  3.35 us
    pallas_call x1, Pallas kernels, stage(): pl.pallas_call(functools.partial(stage_kernel, cols), out_shape=(jax.Shap...  2.33 us
    pallas_call x1, Pallas kernels, pack(): pl.pallas_call(functools.partial(pack_kernel, first, peers, cols, a_slots...  1.38 us
    pallas_call x1, Pallas kernels, flatten(): pl.pallas_call(flatten_kernel, out_shape=jax.ShapeDtypeStruct((count, BS...  1.16 us
    unnamed x8, local copies, waits for them, and re-layouts  1.05 us
  transfers between devices with their start and end apart: 12, of which 6 were waited for; matrix products, arithmetic and copies ran while one was open for 2% of the time, Pallas kernels for 21%

profile of v3, /device:TPU:0, one launch (start us, length us, event | category | flops | bytes accessed | tf_op | source)
XLA Modules:
  0.0 33.2 jit_solution(15656770083879891920)
XLA Ops:
  0.0 0.5 %collective-permute-start.3 = (s32[2,1,16]{2,1,0:T(1,128)}, s32[2,1,16]{2,1,0:T(1,128)S(1)}, u32[]{:S(2)}, u32[]{:S(2)}) collective-permute-start(s32[2,1,16]{2,1,0:T(1,128)} %param.8), channel_id=1, source_target_pairs={{0,1},{1,0},{2,3},{3,2},{4,5},{5,4},{6,7},{7,6},{8,9},{9,8},{10,11... | collective-permute-start | bytes 392 | tf_op jit(solution)/shard_map/ppermute | solution.py:27
  0.5 2.6 %collective-permute-start.5 = (s32[2,1,16]{2,1,0:T(1,128)}, s32[2,1,16]{2,1,0:T(1,128)S(1)}, u32[]{:S(2)}, u32[]{:S(2)}) collective-permute-start(s32[2,1,16]{2,1,0:T(1,128)} %param.8), channel_id=1, source_target_pairs={{0,3},{1,2},{2,1},{3,0},{4,7},{5,6},{6,5},{7,4},{8,11},{9,10},{10,... | collective-permute-start | bytes 392 | tf_op jit(solution)/shard_map/ppermute | solution.py:27
  3.1 0.0 collective-permute-start.4
  3.1 0.8 %pad_maximum_fusion.1 = s32[16,128]{1,0:T(8,128)S(1)} fusion(s32[2,16]{1,0:T(2,128)} %bitcast.16, s32[4,16]{1,0:T(4,128)} %bitcast.11, s32[4,16]{1,0:T(4,128)} %bitcast.12), kind=kLoop, calls=%fused_computation.1 | loop fusion | flops 4096 | bytes 8832 | tf_op jit(solution)/shard_map/max | solution.py:39
  3.8 0.0 collective-permute-done.3
  3.8 0.7 %collective-permute-done.5 = s32[2,1,16]{2,1,0:T(1,128)S(1)} collective-permute-done((s32[2,1,16]{2,1,0:T(1,128)}, s32[2,1,16]{2,1,0:T(1,128)S(1)}, u32[]{:S(2)}, u32[]{:S(2)}) %collective-permute-start.5) | collective-permute-done | bytes 160 | tf_op jit(solution)/shard_map/ppermute | solution.py:27
  4.6 2.3 %collective-permute-done.4 = s32[2,1,16]{2,1,0:T(1,128)S(1)} collective-permute-done((s32[2,1,16]{2,1,0:T(1,128)}, s32[2,1,16]{2,1,0:T(1,128)S(1)}, u32[]{:S(2)}, u32[]{:S(2)}) %collective-permute-start.4) | collective-permute-done | bytes 160 | tf_op jit(solution)/shard_map/ppermute | solution.py:27
  6.8 3.7 %collective-permute-start.8 = (s32[16,128]{1,0:T(8,128)S(1)}, s32[16,128]{1,0:T(8,128)S(1)}, u32[]{:S(2)}, u32[]{:S(2)}) collective-permute-start(s32[16,128]{1,0:T(8,128)S(1)} %pad_maximum_fusion.refs_0_), channel_id=1, source_target_pairs={{0,12},{4,8},{8,4},{12,0},{1,13},{5,9},{9,5},{13,1},{2,14},{6,10},... | collective-permute-start | bytes 24584 | tf_op jit(solution)/shard_map/ppermute | solution.py:27
  10.5 0.0 collective-permute-start.7
  10.5 0.8 %collective-permute-start.6 = (s32[16,128]{1,0:T(8,128)S(1)}, s32[16,128]{1,0:T(8,128)S(1)}, u32[]{:S(2)}, u32[]{:S(2)}) collective-permute-start(s32[16,128]{1,0:T(8,128)S(1)} %pad_maximum_fusion.refs_0_), channel_id=1, source_target_pairs={{0,4},{4,0},{8,12},{12,8},{1,5},{5,1},{9,13},{13,9},{2,6},{6,2},{1... | collective-permute-start | bytes 24584 | tf_op jit(solution)/shard_map/ppermute | solution.py:27
  11.3 1.0 %copy-done = bf16[16,4,4096]{2,1,0:T(4,128)(2,1)S(1)} copy-done((bf16[16,4,4096]{2,1,0:T(4,128)(2,1)S(1)}, bf16[16,4,4096]{2,1,0:T(4,128)(2,1)}, u32[]{:S(2)}) %copy-start) | copy-done | bytes 524312
  12.3 1.2 %flatten.1.refs_4_ = bf16[64,4096]{1,0:T(8,128)(2,1)S(1)} custom-call(bf16[16,4,4096]{2,1,0:T(4,128)(2,1)S(1)} %copy-done), custom_call_target="tpu_custom_call" | custom-call | flops 1048576 | bytes 8388608 | tf_op jit(solution)/shard_map/flatten/pallas_call | solution.py:70
  13.5 0.0 collective-permute-done.8.refs_3_
  13.5 1.5 %collective-permute-done.7.refs_2_ = s32[16,128]{1,0:T(8,128)S(1)} collective-permute-done((s32[16,128]{1,0:T(8,128)S(1)}, s32[16,128]{1,0:T(8,128)S(1)}, u32[]{:S(2)}, u32[]{:S(2)}) %collective-permute-start.7) | collective-permute-done | bytes 8224 | tf_op jit(solution)/shard_map/ppermute | solution.py:27
  15.1 0.0 collective-permute-done.6.refs_1_
  15.1 1.4 %pack.2 = (bf16[528,128]{1,0:T(8,128)(2,1)S(1)}, bf16[528,128]{1,0:T(8,128)(2,1)S(1)}, bf16[528,128]{1,0:T(8,128)(2,1)S(1)}, f32[8,128]{1,0:T(8,128)S(1)}) custom-call(s32[16,128]{1,0:T(8,128)S(1)} %pad_maximum_fusion.refs_0_, s32[16,128]{1,0:T(8,128)S(1)} %collective-permute-done.6.refs_1_, s32[16,128]{1,0:T(8,128)S(1)} %collective-permute-done.7.refs_2_, ...), custom_call_target="tpu_custom_call" | custom-call | flops 1048576 | bytes 4194304 | tf_op jit(solution)/shard_map/pack/pallas_call | solution.py:180
  16.5 0.6 %collective-permute-start.10 = (bf16[1,16,4096]{2,1,0:T(8,128)(2,1)S(1)}, bf16[1,16,4096]{2,1,0:T(8,128)(2,1)S(1)}, u32[]{:S(2)}, u32[]{:S(2)}) collective-permute-start(bf16[1,16,4096]{2,1,0:T(8,128)(2,1)S(1)} %copy-done.2), channel_id=1, source_target_pairs={{0,2},{1,3},{2,0},{3,1},{4,6},{5,7},{6,4},{7,5},{8,10},{9,11},{10,... | collective-permute-start | bytes 393224 | tf_op jit(solution)/shard_map/ppermute | solution.py:27
  17.1 2.1 %collective-permute-start.12 = (bf16[528,128]{1,0:T(8,128)(2,1)S(1)}, bf16[528,128]{1,0:T(8,128)(2,1)S(1)}, u32[]{:S(2)}, u32[]{:S(2)}) collective-permute-start(bf16[528,128]{1,0:T(8,128)(2,1)S(1)} %get-tuple-element.93), channel_id=1, source_target_pairs={{0,12},{4,8},{8,4},{12,0},{1,13},{5,9},{9,5},{13,1},{2,14},{6,10},... | collective-permute-start | bytes 405512 | tf_op jit(solution)/shard_map/ppermute | solution.py:27
  19.1 0.0 collective-permute-start.13
  19.2 2.3 %collective-permute-start.14 = (bf16[528,128]{1,0:T(8,128)(2,1)S(1)}, bf16[528,128]{1,0:T(8,128)(2,1)S(1)}, u32[]{:S(2)}, u32[]{:S(2)}) collective-permute-start(bf16[528,128]{1,0:T(8,128)(2,1)S(1)} %get-tuple-element.95), channel_id=1, source_target_pairs={{0,4},{4,0},{8,12},{12,8},{1,5},{5,1},{9,13},{13,9},{2,6},{6,2},{1... | collective-permute-start | bytes 405512 | tf_op jit(solution)/shard_map/ppermute | solution.py:27
  21.5 3.4 %work_list.1 = (s32[257]{0:T(512)S(1)}, s32[5]{0:T(128)S(1)}) custom-call(s32[16,128]{1,0:T(8,128)S(1)} %pad_maximum_fusion.refs_0_, s32[16,128]{1,0:T(8,128)S(1)} %collective-permute-done.6.refs_1_, s32[16,128]{1,0:T(8,128)S(1)} %collective-permute-done.7.refs_2_, s32[16,128]{1,0:T(8,128)S(1)} %collective-permute-done.8.refs_3_), custom_call_target="tpu_custom_call" | custom-call | flops 8589934592 | bytes 65536 | tf_op jit(solution)/shard_map/work_list/pallas_call | solution.py:245
  24.9 0.1 collective-permute-start.9
  25.0 0.0 collective-permute-done.10.refs_2_
  25.0 0.5 %collective-permute-start.11 = (bf16[1,16,4096]{2,1,0:T(8,128)(2,1)S(1)}, bf16[1,16,4096]{2,1,0:T(8,128)(2,1)S(1)}, u32[]{:S(2)}, u32[]{:S(2)}) collective-permute-start(bf16[1,16,4096]{2,1,0:T(8,128)(2,1)S(1)} %collective-permute-done.10.refs_2_), channel_id=1, source_target_pairs={{0,1},{1,0},{2,3},{3,2},{4,5},{5,4},{6,7},{7,6},{8,9},{9,8},{10,11... | collective-permute-start | bytes 393224 | tf_op jit(solution)/shard_map/ppermute | solution.py:27
  25.5 0.8 %collective-permute-done.9.refs_1_ = bf16[1,16,4096]{2,1,0:T(8,128)(2,1)S(1)} collective-permute-done((bf16[1,16,4096]{2,1,0:T(8,128)(2,1)S(1)}, bf16[1,16,4096]{2,1,0:T(8,128)(2,1)S(1)}, u32[]{:S(2)}, u32[]{:S(2)}) %collective-permute-start.9) | collective-permute-done | bytes 131104 | tf_op jit(solution)/shard_map/ppermute | solution.py:27
  26.3 0.2 collective-permute-done.11.refs_3_
  26.5 2.3 %stage.1 = (bf16[2048,128]{1,0:T(8,128)(2,1)S(1)}, f32[17,128,128]{2,1,0:T(8,128)S(1)}) custom-call(bf16[1,16,4096]{2,1,0:T(8,128)(2,1)S(1)} %copy-done.2, bf16[1,16,4096]{2,1,0:T(8,128)(2,1)S(1)} %collective-permute-done.9.refs_1_, bf16[1,16,4096]{2,1,0:T(8,128)(2,1)S(1)} %collective-permute-done.10.refs_2_, ...), custom_call_target="tpu_custom_call" | custom-call | flops 16777216 | bytes 4194304 | tf_op jit(solution)/shard_map/stage/pallas_call | solution.py:359
  28.8 0.0 collective-permute-done.12.refs_5_
  28.8 0.3 collective-permute-done.13.refs_6_
  29.2 0.0 collective-permute-done.14.refs_7_
  29.2 3.3 %multiply.2 = (f32[16,4,4096]{2,1,0:T(4,128)}, s32[1]{0:T(128)}, f32[17,128,128]{2,1,0:T(8,128)S(1)}) custom-call(s32[257]{0:T(512)S(1)} %get-tuple-element.217.refs_5_.refs_0_, s32[5]{0:T(128)S(1)} %get-tuple-element.218.refs_6_.refs_1_, f32[8,128]{1,0:T(8,128)S(1)} %get-tuple-element.88.refs_2_, ...), custom_call_target="tpu_custom_call", output_to_operand_aliasing={{2}: (4, {})} | custom-call | flops 67108864 | bytes 4194304 | tf_op jit(solution)/shard_map/multiply/pallas_call | solution.py:407
  32.5 0.6 %while.12 = (s32[]{:T(128)}, f32[17,128,128]{2,1,0:T(8,128)S(1)}, f32[16,4,4096]{2,1,0:T(4,128)}, s32[1]{0:T(128)}, s32[16,128]{1,0:T(8,128)S(1)}, /*index=5*/s3...) while((s32[]{:T(128)}, f32[17,128,128]{2,1,0:T(8,128)S(1)}, ...), condition=%wide.region_1.2_spmd, body=%wide.region_0.1_spmd.sunk | while | flops 68157440 | bytes 10010889 | solution.py:463
  (8 shorter events, 0.0 us)
Async XLA Ops:
  0.0 3.8 %collective-permute-start.3 = (s32[2,1,16]{2,1,0:T(1,128)}, s32[2,1,16]{2,1,0:T(1,128)S(1)}, u32[]{:S(2)}, u32[]{:S(2)}) collective-permute-start(s32[2,1,16]{2,1,0:T(1,128)} %param.8), channel_id=1, source_target_pairs={{0,1},{1,0},{2,3},{3,2},{4,5},{5,4},{6,7},{7,6},{8,9},{9,8},{10,11... | collective-permute-start | bytes 392 | tf_op jit(solution)/shard_map/ppermute | solution.py:27
  0.5 4.1 %collective-permute-start.5 = (s32[2,1,16]{2,1,0:T(1,128)}, s32[2,1,16]{2,1,0:T(1,128)S(1)}, u32[]{:S(2)}, u32[]{:S(2)}) collective-permute-start(s32[2,1,16]{2,1,0:T(1,128)} %param.8), channel_id=1, source_target_pairs={{0,3},{1,2},{2,1},{3,0},{4,7},{5,6},{6,5},{7,4},{8,11},{9,10},{10,... | collective-permute-start | bytes 392 | tf_op jit(solution)/shard_map/ppermute | solution.py:27
  3.1 3.8 %collective-permute-start.4 = (s32[2,1,16]{2,1,0:T(1,128)}, s32[2,1,16]{2,1,0:T(1,128)S(1)}, u32[]{:S(2)}, u32[]{:S(2)}) collective-permute-start(s32[2,1,16]{2,1,0:T(1,128)} %param.8), channel_id=1, source_target_pairs={{0,2},{1,3},{2,0},{3,1},{4,6},{5,7},{6,4},{7,5},{8,10},{9,11},{10,... | collective-permute-start | bytes 392 | tf_op jit(solution)/shard_map/ppermute | solution.py:27
  6.8 6.7 %collective-permute-start.8 = (s32[16,128]{1,0:T(8,128)S(1)}, s32[16,128]{1,0:T(8,128)S(1)}, u32[]{:S(2)}, u32[]{:S(2)}) collective-permute-start(s32[16,128]{1,0:T(8,128)S(1)} %pad_maximum_fusion.refs_0_), channel_id=1, source_target_pairs={{0,12},{4,8},{8,4},{12,0},{1,13},{5,9},{9,5},{13,1},{2,14},{6,10},... | collective-permute-start | bytes 24584 | tf_op jit(solution)/shard_map/ppermute | solution.py:27
  10.5 4.5 %collective-permute-start.7 = (s32[16,128]{1,0:T(8,128)S(1)}, s32[16,128]{1,0:T(8,128)S(1)}, u32[]{:S(2)}, u32[]{:S(2)}) collective-permute-start(s32[16,128]{1,0:T(8,128)S(1)} %pad_maximum_fusion.refs_0_), channel_id=1, source_target_pairs={{0,8},{4,12},{8,0},{12,4},{1,9},{5,13},{9,1},{13,5},{2,10},{6,14},... | collective-permute-start | bytes 24584 | tf_op jit(solution)/shard_map/ppermute | solution.py:27
  10.5 4.5 %collective-permute-start.6 = (s32[16,128]{1,0:T(8,128)S(1)}, s32[16,128]{1,0:T(8,128)S(1)}, u32[]{:S(2)}, u32[]{:S(2)}) collective-permute-start(s32[16,128]{1,0:T(8,128)S(1)} %pad_maximum_fusion.refs_0_), channel_id=1, source_target_pairs={{0,4},{4,0},{8,12},{12,8},{1,5},{5,1},{9,13},{13,9},{2,6},{6,2},{1... | collective-permute-start | bytes 24584 | tf_op jit(solution)/shard_map/ppermute | solution.py:27
  11.3 1.0 %copy-start = (bf16[16,4,4096]{2,1,0:T(4,128)(2,1)S(1)}, bf16[16,4,4096]{2,1,0:T(4,128)(2,1)}, u32[]{:S(2)}) copy-start(bf16[16,4,4096]{2,1,0:T(4,128)(2,1)} %refs_4_.1) | copy-start | bytes 1572868
  12.3 4.1 %copy-start.2 = (bf16[1,16,4096]{2,1,0:T(8,128)(2,1)S(1)}, bf16[1,16,4096]{2,1,0:T(8,128)(2,1)}, u32[]{:S(2)}) copy-start(bf16[1,16,4096]{2,1,0:T(8,128)(2,1)} %refs_0_.1) | copy-start | bytes 393220
  16.5 8.5 %collective-permute-start.10 = (bf16[1,16,4096]{2,1,0:T(8,128)(2,1)S(1)}, bf16[1,16,4096]{2,1,0:T(8,128)(2,1)S(1)}, u32[]{:S(2)}, u32[]{:S(2)}) collective-permute-start(bf16[1,16,4096]{2,1,0:T(8,128)(2,1)S(1)} %copy-done.2), channel_id=1, source_target_pairs={{0,2},{1,3},{2,0},{3,1},{4,6},{5,7},{6,4},{7,5},{8,10},{9,11},{10,... | collective-permute-start | bytes 393224 | tf_op jit(solution)/shard_map/ppermute | solution.py:27
  17.1 11.8 %collective-permute-start.12 = (bf16[528,128]{1,0:T(8,128)(2,1)S(1)}, bf16[528,128]{1,0:T(8,128)(2,1)S(1)}, u32[]{:S(2)}, u32[]{:S(2)}) collective-permute-start(bf16[528,128]{1,0:T(8,128)(2,1)S(1)} %get-tuple-element.93), channel_id=1, source_target_pairs={{0,12},{4,8},{8,4},{12,0},{1,13},{5,9},{9,5},{13,1},{2,14},{6,10},... | collective-permute-start | bytes 405512 | tf_op jit(solution)/shard_map/ppermute | solution.py:27
  19.1 10.0 %collective-permute-start.13 = (bf16[528,128]{1,0:T(8,128)(2,1)S(1)}, bf16[528,128]{1,0:T(8,128)(2,1)S(1)}, u32[]{:S(2)}, u32[]{:S(2)}) collective-permute-start(bf16[528,128]{1,0:T(8,128)(2,1)S(1)} %get-tuple-element.94), channel_id=1, source_target_pairs={{0,8},{4,12},{8,0},{12,4},{1,9},{5,13},{9,1},{13,5},{2,10},{6,14},... | collective-permute-start | bytes 405512 | tf_op jit(solution)/shard_map/ppermute | solution.py:27
  19.2 7.3 %copy-start.1 = (bf16[16,4,4096]{2,1,0:T(4,128)(2,1)S(1)}, bf16[16,4,4096]{2,1,0:T(4,128)(2,1)}, u32[]{:S(2)}) copy-start(bf16[16,4,4096]{2,1,0:T(4,128)(2,1)} %refs_4_.1) | copy-start | bytes 1572868
  19.2 10.0 %collective-permute-start.14 = (bf16[528,128]{1,0:T(8,128)(2,1)S(1)}, bf16[528,128]{1,0:T(8,128)(2,1)S(1)}, u32[]{:S(2)}, u32[]{:S(2)}) collective-permute-start(bf16[528,128]{1,0:T(8,128)(2,1)S(1)} %get-tuple-element.95), channel_id=1, source_target_pairs={{0,4},{4,0},{8,12},{12,8},{1,5},{5,1},{9,13},{13,9},{2,6},{6,2},{1... | collective-permute-start | bytes 405512 | tf_op jit(solution)/shard_map/ppermute | solution.py:27
  24.9 1.4 %collective-permute-start.9 = (bf16[1,16,4096]{2,1,0:T(8,128)(2,1)S(1)}, bf16[1,16,4096]{2,1,0:T(8,128)(2,1)S(1)}, u32[]{:S(2)}, u32[]{:S(2)}) collective-permute-start(bf16[1,16,4096]{2,1,0:T(8,128)(2,1)S(1)} %copy-done.2), channel_id=1, source_target_pairs={{0,1},{1,0},{2,3},{3,2},{4,5},{5,4},{6,7},{7,6},{8,9},{9,8},{10,11... | collective-permute-start | bytes 393224 | tf_op jit(solution)/shard_map/ppermute | solution.py:27
  25.0 1.5 %collective-permute-start.11 = (bf16[1,16,4096]{2,1,0:T(8,128)(2,1)S(1)}, bf16[1,16,4096]{2,1,0:T(8,128)(2,1)S(1)}, u32[]{:S(2)}, u32[]{:S(2)}) collective-permute-start(bf16[1,16,4096]{2,1,0:T(8,128)(2,1)S(1)} %collective-permute-done.10.refs_2_), channel_id=1, source_target_pairs={{0,1},{1,0},{2,3},{3,2},{4,5},{5,4},{6,7},{7,6},{8,9},{9,8},{10,11... | collective-permute-start | bytes 393224 | tf_op jit(solution)/shard_map/ppermute | solution.py:27
  28.8 3.7 %copy-start.3 = (bf16[2048,128]{1,0:T(8,128)(2,1)}, bf16[2048,128]{1,0:T(8,128)(2,1)S(1)}, u32[]{:S(2)}) copy-start(bf16[2048,128]{1,0:T(8,128)(2,1)S(1)} %get-tuple-element.219.refs_3_) | copy-start | bytes 1572868

commit v4 on v3

--- a/solution.py
+++ b/solution.py
@@ -4,6 +4,7 @@
 import jax.numpy as jnp
 from jax import lax
 from jax.experimental import pallas as pl
+from jax.experimental.layout import Layout, with_layout_constraint
 from jax.experimental.pallas import tpu as pltpu
 from jax.sharding import PartitionSpec as P
 
@@ -27,6 +28,20 @@
     return lax.ppermute(block, axis, [(i, i ^ distance) for i in range(size)])
 
 
+def seen_by_rows(blocks):
+    count = blocks.shape[0]
+    parted = blocks.reshape(count, SLOTS, ROWS, LANES)
+    parted = with_layout_constraint(parted, Layout(major_to_minor=(0, 2, 1, 3)))
+    return parted.transpose(0, 2, 1, 3).reshape(count, ROWS * SLOTS, LANES)
+
+
+def seen_by_blocks(rows):
+    count = rows.shape[0]
+    parted = rows.reshape(count, ROWS, SLOTS, LANES).transpose(0, 2, 1, 3)
+    parted = with_layout_constraint(parted, Layout(major_to_minor=(0, 2, 1, 3)))
+    return parted.reshape(count, SLOTS, BS * BS)
+
+
 def describe(a_parts, b_cols, c_cols):
     cols = len(a_parts)
     total = -(-(2 * cols + 2 * SLOTS) // 8) * 8
@@ -53,30 +68,37 @@
     return result
 
 
-def flatten_kernel(b_ref, flat, wide):
+def flatten_kernel(b_ref, flat, own, sums, wide):
     row_count = b_ref.shape[0]
-    for k in range(row_count):
-        for t in range(ROWS):
-            wide[k, pl.ds(t * SLOTS, SLOTS), :] = b_ref[k, :, pl.ds(t * LANES, LANES)].astype(F32)
+    wide[...] = b_ref[...].astype(F32)
     for t in range(ROWS):
         for n in range(SLOTS):
             piece = wide[:, t * SLOTS + n, :].astype(BF16)
             flat[pl.ds(n * row_count, row_count), pl.ds(t * LANES, LANES)] = piece
-
-
-def flatten(b_blocks):
+    for n in range(SLOTS):
+        for k in range(row_count):
+            block = wide[k, pl.ds(n, ROWS, stride=SLOTS), :].astype(BF16)
+            own[pl.ds((n * row_count + k) * ROWS, ROWS), :] = block
+    sums[...] = jnp.zeros_like(sums)
+
+
+def flatten(b_rows):
     vmem_spec = pl.BlockSpec(memory_space=VMEM)
-    count = b_blocks.shape[0] * b_blocks.shape[1]
+    row_count = b_rows.shape[0]
     return pl.pallas_call(
         flatten_kernel,
-        out_shape=jax.ShapeDtypeStruct((count, BS * BS), BF16),
+        out_shape=(
+            jax.ShapeDtypeStruct((row_count * SLOTS, BS * BS), BF16),
+            jax.ShapeDtypeStruct((row_count * SLOTS * ROWS, LANES), BF16),
+            jax.ShapeDtypeStruct(b_rows.shape, F32),
+        ),
         in_specs=[vmem_spec],
-        out_specs=vmem_spec,
-        scratch_shapes=[VMEM((b_blocks.shape[0], b_blocks.shape[1] * ROWS, LANES), F32)],
+        out_specs=(vmem_spec,) * 3,
+        scratch_shapes=[VMEM(b_rows.shape, F32)],
         compiler_params=pltpu.CompilerParams(vmem_limit_bytes=24 << 20),
         cost_estimate=pl.CostEstimate(flops=1 << 20, bytes_accessed=8 << 20, transcendentals=0),
         name="flatten",
-    )(b_blocks)
+    )(b_rows)
 
 
 def iota(shape, axis):
@@ -255,7 +277,7 @@
             SMEM((a_slots, LANES), I32),
             pltpu.SemaphoreType.DMA((1,)),
         ],
-        cost_estimate=pl.CostEstimate(flops=1 << 33, bytes_accessed=1 << 16, transcendentals=0),
+        cost_estimate=pl.CostEstimate(flops=1 << 10, bytes_accessed=1 << 10, transcendentals=0),
         name="work_list",
     )(*told)
 
@@ -274,7 +296,6 @@
 def add_products(items, starts, a_ref, peer_refs, sums, window=None):
     low = iota((ROWS, LANES), 1) < BS
     nothing = jnp.zeros((ROWS, LANES), BF16)
-    idle_row = sums.shape[0] - 1
 
     def add_one(word, used, b_ref):
         place = (word >> 6) & 63
@@ -286,7 +307,7 @@
         place = jnp.where(used, place, 0)
         a_at = pl.multiple_of((word >> 18) * ROWS, ROWS)
         b_at = pl.multiple_of(place * ROWS, ROWS)
-        block = b_ref[pl.ds(b_at, ROWS), :]
+        block = jnp.where(used, b_ref[pl.ds(b_at, ROWS), :], nothing)
         turned = jnp.concatenate([block[:, BS:], block[:, :BS]], axis=1)
         right = jnp.concatenate(
             [
@@ -298,8 +319,7 @@
             axis=0,
         )
         term = jnp.dot(a_ref[pl.ds(a_at, ROWS), :], right, preferred_element_type=F32)
-        i = jnp.where(used, target // SLOTS, idle_row)
-        sums[i, pl.ds(target % SLOTS, ROWS, stride=SLOTS), :] += term
+        sums[target // SLOTS, pl.ds(target % SLOTS, ROWS, stride=SLOTS), :] += term
 
     for at in range(0, len(peer_refs), 3):
         chosen = peer_refs[at : at + 3]
@@ -319,8 +339,8 @@
 
 
 def stage_kernel(cols, *refs):
-    a_refs, b_ref, items, starts = refs[:cols], refs[cols], refs[cols + 1], refs[cols + 2]
-    a_out, sums, a_wide, b_wide, b_own = refs[cols + 3 :]
+    a_refs, own, items, starts = refs[:cols], refs[cols], refs[cols + 1], refs[cols + 2]
+    a_out, sums, a_wide = refs[cols + 4 :]
     source = iota((LANES, LANES), 0)
     target = iota((LANES, LANES), 1)
     wanted = (target // BS) * BS + 2 * (target % ROWS) + (target // ROWS) % 2
@@ -336,43 +356,27 @@
         for s in range(slots):
             at = pl.multiple_of((first + s) * ROWS, ROWS)
             a_out[pl.ds(at, ROWS), :] = a_wide[h * slots + s].astype(BF16)
-    row_count, slots = b_ref.shape[0], b_ref.shape[1]
-
-    def one_row(k, carry):
-        for t in range(ROWS):
-            b_wide[pl.ds(t * slots, slots), :] = b_ref[k, :, pl.ds(t * LANES, LANES)].astype(F32)
-        for n in range(slots):
-            at = pl.multiple_of((n * row_count + k) * ROWS, ROWS)
-            b_own[pl.ds(at, ROWS), :] = b_wide[pl.ds(n, ROWS, stride=slots), :].astype(BF16)
-        return carry
-
-    lax.fori_loop(0, row_count, one_row, 0)
-    sums[...] = jnp.zeros_like(sums)
-    add_products(items, starts, a_out, [(0, b_own)], sums)
-
-
-def stage(a_parts, b_blocks, items, starts):
+    add_products(items, starts, a_out, [(0, own)], sums)
+
+
+def stage(a_parts, own, sums, items, starts):
     cols, slots = len(a_parts), a_parts[0].shape[1]
-    row_count, b_slots = b_blocks.shape[0], b_blocks.shape[1]
     vmem_spec = pl.BlockSpec(memory_space=VMEM)
     smem_spec = pl.BlockSpec(memory_space=SMEM)
     return pl.pallas_call(
         functools.partial(stage_kernel, cols),
         out_shape=(
             jax.ShapeDtypeStruct((cols * slots * ROWS, LANES), BF16),
-            jax.ShapeDtypeStruct((row_count + 1, ROWS * b_slots, LANES), F32),
+            jax.ShapeDtypeStruct(sums.shape, F32),
         ),
-        in_specs=[vmem_spec] * (cols + 1) + [smem_spec] * 2,
+        in_specs=[vmem_spec] * (cols + 1) + [smem_spec] * 2 + [vmem_spec],
         out_specs=(vmem_spec,) * 2,
-        scratch_shapes=[
-            VMEM((cols * slots, ROWS, LANES), F32),
-            VMEM((b_slots * ROWS, LANES), F32),
-            VMEM((row_count * b_slots * ROWS, LANES), BF16),
-        ],
+        input_output_aliases={cols + 3: 1},
+        scratch_shapes=[VMEM((cols * slots, ROWS, LANES), F32)],
         compiler_params=pltpu.CompilerParams(vmem_limit_bytes=40 << 20),
-        cost_estimate=pl.CostEstimate(flops=1 << 24, bytes_accessed=4 << 20, transcendentals=0),
+        cost_estimate=pl.CostEstimate(flops=1 << 10, bytes_accessed=1 << 10, transcendentals=0),
         name="stage",
-    )(*a_parts, b_blocks, items, starts)
+    )(*a_parts, own, items, starts, sums)
 
 
 def multiply_kernel(first, peers, *refs):
@@ -380,25 +384,19 @@
     base = 0 if first else refs.pop(0)[0]
     items, starts, most, a_ref = refs[:4]
     b_refs = refs[5 : 4 + peers][::-1]
-    out, rounds, sums, rows, sems = refs[4 + peers :]
+    out, rounds, sums, sem = refs[4 + peers :]
     add_products(items, starts, a_ref, list(enumerate(b_refs, 1)), sums, window=base)
-    row_count, kept = out.shape[0], out.shape[1]
-    copies = []
-    for i in range(row_count):
-        for t in range(ROWS):
-            rows[i, :, pl.ds(t * LANES, LANES)] = sums[i, pl.ds(t * kept, kept), :]
-        copies.append(pltpu.make_async_copy(rows.at[i], out.at[i], sems.at[i]))
-        copies[-1].start()
+    copy = pltpu.make_async_copy(sums, out, sem.at[0])
+    copy.start()
     flags = most[...]
     for ref in b_refs:
         flag = ref[pl.ds(CAPACITY * ROWS, FLAG), :].astype(F32)
         flags = jnp.maximum(flags, jnp.max(flag, axis=0, keepdims=True))
     rounds[0] = (jnp.max(flags).astype(I32) + CAPACITY - 1) // CAPACITY
-    for copy in copies:
-        copy.wait()
-
-
-def multiply(base, items, starts, most, a_ready, sums, b_parts, shape):
+    copy.wait()
+
+
+def multiply(base, items, starts, most, a_ready, sums, b_parts):
     first = base is None
     peers = len(b_parts) + 1
     smem_spec = pl.BlockSpec(memory_space=SMEM)
@@ -407,14 +405,14 @@
     return pl.pallas_call(
         functools.partial(multiply_kernel, first, peers),
         out_shape=[
-            jax.ShapeDtypeStruct(shape, F32),
+            jax.ShapeDtypeStruct(sums.shape, F32),
             jax.ShapeDtypeStruct((1,), I32),
             jax.ShapeDtypeStruct(sums.shape, F32),
         ],
         in_specs=[smem_spec] * (len(given) + 2) + [vmem_spec] * (2 + peers),
         out_specs=[pl.BlockSpec(memory_space=pl.ANY), smem_spec, vmem_spec],
         input_output_aliases={len(given) + 4: 2},
-        scratch_shapes=[VMEM(shape, F32), pltpu.SemaphoreType.DMA((shape[0],))],
+        scratch_shapes=[pltpu.SemaphoreType.DMA((1,))],
         compiler_params=pltpu.CompilerParams(vmem_limit_bytes=32 << 20),
         cost_estimate=pl.CostEstimate(flops=1 << 26, bytes_accessed=4 << 20, transcendentals=0),
         name="multiply",
@@ -431,24 +429,20 @@
         far_first = range(len(parts), 0, -1)
         return [exchanged(parts[d - 1], "row", d) for d in far_first][::-1]
 
-    def finish(base, most, sums, arrived):
-        return multiply(base, items, starts, most, a_ready, sums, arrived, shape)
-
-    shape = (row_count, c_cols.shape[1], BS * BS)
-    index_parts = [a_index] + [exchanged(a_index, "col", h) for h in range(1, cols)]
-    told = describe(index_parts, b_cols.T, c_cols.T)
+    told = describe([a_index] + [exchanged(a_index, "col", h) for h in range(1, cols)],
+                    b_cols.T, c_cols.T)
     told = [told] + send_rows([told] * (rows - 1))
-    flat = flatten(b_blocks)
+    flat, own, sums = flatten(seen_by_rows(b_blocks))
     packed, most = pack(None, told, flat, cols, row_count, a_slots)
     arrived = send_rows(packed)
     items, starts = work_list(told, cols, row_count, a_slots)
     a_late, _ = lax.optimization_barrier((a_blocks, most))
+    a_far = [exchanged(a_late, "col", h) for h in range(2, cols, 2)]
     a_parts = [a_blocks, exchanged(a_late, "col", 1)]
-    for h in range(2, cols, 2):
-        far = exchanged(a_late, "col", h)
+    for far in a_far:
         a_parts += [far, exchanged(lax.optimization_barrier((far, items))[0], "col", 1)]
-    a_ready, sums = stage(a_parts, b_blocks, items, starts)
-    out, rounds, sums = finish(None, most, sums, arrived)
+    a_ready, sums = stage(a_parts, own, sums, items, starts)
+    out, rounds, sums = multiply(None, items, starts, most, a_ready, sums, arrived)
 
     def more(state):
         return state[0] < rounds[0]
@@ -457,10 +451,11 @@
         at, sums, _ = state
         base = jnp.reshape(at * CAPACITY, (1,))
         packed, most = pack(base, told, flat, cols, row_count, a_slots)
-        out, _, sums = finish(base, most, sums, send_rows(packed))
+        arrived = send_rows(packed)
+        out, _, sums = multiply(base, items, starts, most, a_ready, sums, arrived)
         return at + 1, sums, out
 
-    return lax.while_loop(more, one_round, (jnp.int32(1), sums, out))[2]
+    return seen_by_blocks(lax.while_loop(more, one_round, (jnp.int32(1), sums, out))[2])
 
 
 def solution(mesh):

time: 33.3 us -> 33.1 us (level); the launches traced: 33.2 us -> 33.3 us
  other arithmetic: 0.77 us -> 0.02 us
  local copies, waits for them, and re-layouts: 1.05 us -> 1.79 us
  waiting for transfers between devices: 5.91 us -> 6.25 us
    max x1, other arithmetic: 0.75 us -> 0.01 us  [describe(): jnp.maximum(own, placed(a_parts[0][:, 0, :], 0))]
    unnamed x8 -> x12, local copies, waits for them, and re-layouts: 1.05 us -> 1.79 us
    pallas_call x1, Pallas kernels: 2.33 us -> 1.91 us  [stage(): pl.pallas_call(functools.partial(stage_kernel, cols), out_shape=(jax.Shap...]
    ppermute x12, waiting for transfers between devices: 5.91 us -> 6.25 us  [exchanged(): return lax.ppermute(block, axis, [(i, i ^ distance) for i in range(size)])]
  transfers between devices with their start and end apart: 12 -> 12, of which waited for: 6 -> 6; matrix products, arithmetic and copies ran while one was open for 2% -> 0% of each run, Pallas kernels for 21% -> 20%
where the time goes in v4:
time: 33.1 us; the launch traced here: 33.3 us
  starting transfers between devices  13.1 us (40%)
  Pallas kernels  11.5 us (35%)
  waiting for transfers between devices  6.25 us (19%)
  local copies, waits for them, and re-layouts  1.79 us (5%)
  loops' own time  0.56 us (2%)
    ppermute x12, starting transfers between devices, exchanged(): return lax.ppermute(block, axis, [(i, i ^ distance) for i in range(size)])  13.1 us
    ppermute x12, waiting for transfers between devices, exchanged(): return lax.ppermute(block, axis, [(i, i ^ distance) for i in range(size)])  6.25 us
    pallas_call x1, Pallas kernels, multiply(): pl.pallas_call(functools.partial(multiply_kernel, first, peers), out_shap...  3.55 us
    pallas_call x1, Pallas kernels, work_list(): pl.pallas_call(functools.partial(list_kernel, cols, a_slots, row_count, p...  3.42 us
    pallas_call x1, Pallas kernels, stage(): pl.pallas_call(functools.partial(stage_kernel, cols), out_shape=(jax.Shap...  1.91 us
    unnamed x12, local copies, waits for them, and re-layouts  1.79 us
    pallas_call x1, Pallas kernels, pack(): pl.pallas_call(functools.partial(pack_kernel, first, peers, cols, a_slots...  1.38 us
    pallas_call x1, Pallas kernels, flatten(): pl.pallas_call(flatten_kernel, out_shape=(jax.ShapeDtypeStruct((row_count...  1.24 us
  transfers between devices with their start and end apart: 12, of which 6 were waited for; matrix products, arithmetic and copies ran while one was open for 0% of the time, Pallas kernels for 20%

profile of v4, /device:TPU:0, one launch (start us, length us, event | category | flops | bytes accessed | tf_op | source)
XLA Modules:
  0.0 33.3 jit_solution(9337080961383442241)
XLA Ops:
  0.0 0.5 %collective-permute-start.3 = (s32[2,1,16]{2,1,0:T(1,128)}, s32[2,1,16]{2,1,0:T(1,128)S(1)}, u32[]{:S(2)}, u32[]{:S(2)}) collective-permute-start(s32[2,1,16]{2,1,0:T(1,128)} %param.8), channel_id=1, source_target_pairs={{0,1},{1,0},{2,3},{3,2},{4,5},{5,4},{6,7},{7,6},{8,9},{9,8},{10,11... | collective-permute-start | bytes 392 | tf_op jit(solution)/shard_map/ppermute | solution.py:28
  0.5 2.6 %collective-permute-start.5 = (s32[2,1,16]{2,1,0:T(1,128)}, s32[2,1,16]{2,1,0:T(1,128)S(1)}, u32[]{:S(2)}, u32[]{:S(2)}) collective-permute-start(s32[2,1,16]{2,1,0:T(1,128)} %param.8), channel_id=1, source_target_pairs={{0,3},{1,2},{2,1},{3,0},{4,7},{5,6},{6,5},{7,4},{8,11},{9,10},{10,... | collective-permute-start | bytes 392 | tf_op jit(solution)/shard_map/ppermute | solution.py:28
  3.1 0.0 collective-permute-start.4
  3.1 0.7 %copy-done.5 = s32[16,4]{0,1:T(4,128)S(1)} copy-done((s32[16,4]{0,1:T(4,128)S(1)}, s32[16,4]{0,1:T(4,128)}, u32[]{:S(2)}) %copy-start.5) | copy-done | bytes 280
  3.7 0.0 copy-done.4
  3.8 0.0 copy-done.6
  3.8 0.0 collective-permute-done.3
  3.8 0.7 %collective-permute-done.5 = s32[2,1,16]{2,1,0:T(1,128)S(1)} collective-permute-done((s32[2,1,16]{2,1,0:T(1,128)}, s32[2,1,16]{2,1,0:T(1,128)S(1)}, u32[]{:S(2)}, u32[]{:S(2)}) %collective-permute-start.5) | collective-permute-done | bytes 160 | tf_op jit(solution)/shard_map/ppermute | solution.py:28
  4.6 2.3 %collective-permute-done.4 = s32[2,1,16]{2,1,0:T(1,128)S(1)} collective-permute-done((s32[2,1,16]{2,1,0:T(1,128)}, s32[2,1,16]{2,1,0:T(1,128)S(1)}, u32[]{:S(2)}, u32[]{:S(2)}) %collective-permute-start.4) | collective-permute-done | bytes 160 | tf_op jit(solution)/shard_map/ppermute | solution.py:28
  6.8 3.7 %collective-permute-start.8 = (s32[16,128]{1,0:T(8,128)S(1)}, s32[16,128]{1,0:T(8,128)S(1)}, u32[]{:S(2)}, u32[]{:S(2)}) collective-permute-start(s32[16,128]{1,0:T(8,128)S(1)} %pad_maximum_fusion.refs_0_), channel_id=1, source_target_pairs={{0,12},{4,8},{8,4},{12,0},{1,13},{5,9},{9,5},{13,1},{2,14},{6,10},... | collective-permute-start | bytes 24584 | tf_op jit(solution)/shard_map/ppermute | solution.py:28
  10.5 0.0 collective-permute-start.7
  10.5 0.8 %collective-permute-start.6 = (s32[16,128]{1,0:T(8,128)S(1)}, s32[16,128]{1,0:T(8,128)S(1)}, u32[]{:S(2)}, u32[]{:S(2)}) collective-permute-start(s32[16,128]{1,0:T(8,128)S(1)} %pad_maximum_fusion.refs_0_), channel_id=1, source_target_pairs={{0,4},{4,0},{8,12},{12,8},{1,5},{5,1},{9,13},{13,9},{2,6},{6,2},{1... | collective-permute-start | bytes 24584 | tf_op jit(solution)/shard_map/ppermute | solution.py:28
  11.3 1.0 %copy-done = bf16[16,4,4096]{2,1,0:T(4,128)(2,1)S(1)} copy-done((bf16[16,4,4096]{2,1,0:T(4,128)(2,1)S(1)}, bf16[16,4,4096]{2,1,0:T(4,128)(2,1)}, u32[]{:S(2)}) %copy-start) | copy-done | bytes 524312
  12.3 1.2 %flatten.1 = (bf16[64,4096]{1,0:T(8,128)(2,1)S(1)}, bf16[2048,128]{1,0:T(8,128)(2,1)S(1)}, f32[16,128,128]{2,1,0:T(8,128)S(1)}) custom-call(bf16[16,128,128]{2,1,0:T(8,128)(2,1)S(1)} %bitcast.21), custom_call_target="tpu_custom_call" | custom-call | flops 1048576 | bytes 8388608 | tf_op jit(solution)/shard_map/flatten/pallas_call | solution.py:88
  13.6 0.0 collective-permute-done.8.refs_3_
  13.6 1.5 %collective-permute-done.7.refs_2_ = s32[16,128]{1,0:T(8,128)S(1)} collective-permute-done((s32[16,128]{1,0:T(8,128)S(1)}, s32[16,128]{1,0:T(8,128)S(1)}, u32[]{:S(2)}, u32[]{:S(2)}) %collective-permute-start.7) | collective-permute-done | bytes 8224 | tf_op jit(solution)/shard_map/ppermute | solution.py:28
  15.1 1.4 %pack.2 = (bf16[528,128]{1,0:T(8,128)(2,1)S(1)}, bf16[528,128]{1,0:T(8,128)(2,1)S(1)}, bf16[528,128]{1,0:T(8,128)(2,1)S(1)}, f32[8,128]{1,0:T(8,128)S(1)}) custom-call(s32[16,128]{1,0:T(8,128)S(1)} %pad_maximum_fusion.refs_0_, s32[16,128]{1,0:T(8,128)S(1)} %collective-permute-done.6.refs_1_, s32[16,128]{1,0:T(8,128)S(1)} %collective-permute-done.7.refs_2_, ...), custom_call_target="tpu_custom_call" | custom-call | flops 1048576 | bytes 4194304 | tf_op jit(solution)/shard_map/pack/pallas_call | solution.py:202
  16.5 0.6 %collective-permute-start.10 = (bf16[1,16,4096]{2,1,0:T(8,128)(2,1)S(1)}, bf16[1,16,4096]{2,1,0:T(8,128)(2,1)S(1)}, u32[]{:S(2)}, u32[]{:S(2)}) collective-permute-start(bf16[1,16,4096]{2,1,0:T(8,128)(2,1)S(1)} %copy-done.1), channel_id=1, source_target_pairs={{0,2},{1,3},{2,0},{3,1},{4,6},{5,7},{6,4},{7,5},{8,10},{9,11},{10,... | collective-permute-start | bytes 393224 | tf_op jit(solution)/shard_map/ppermute | solution.py:28
  17.1 2.2 %collective-permute-start.12 = (bf16[528,128]{1,0:T(8,128)(2,1)S(1)}, bf16[528,128]{1,0:T(8,128)(2,1)S(1)}, u32[]{:S(2)}, u32[]{:S(2)}) collective-permute-start(bf16[528,128]{1,0:T(8,128)(2,1)S(1)} %get-tuple-element.99), channel_id=1, source_target_pairs={{0,12},{4,8},{8,4},{12,0},{1,13},{5,9},{9,5},{13,1},{2,14},{6,10},... | collective-permute-start | bytes 405512 | tf_op jit(solution)/shard_map/ppermute | solution.py:28
  19.2 2.2 %collective-permute-start.14 = (bf16[528,128]{1,0:T(8,128)(2,1)S(1)}, bf16[528,128]{1,0:T(8,128)(2,1)S(1)}, u32[]{:S(2)}, u32[]{:S(2)}) collective-permute-start(bf16[528,128]{1,0:T(8,128)(2,1)S(1)} %get-tuple-element.101), channel_id=1, source_target_pairs={{0,4},{4,0},{8,12},{12,8},{1,5},{5,1},{9,13},{13,9},{2,6},{6,2},{1... | collective-permute-start | bytes 405512 | tf_op jit(solution)/shard_map/ppermute | solution.py:28
  21.5 3.4 %work_list.1 = (s32[257]{0:T(512)S(1)}, s32[5]{0:T(128)S(1)}) custom-call(s32[16,128]{1,0:T(8,128)S(1)} %pad_maximum_fusion.refs_0_, s32[16,128]{1,0:T(8,128)S(1)} %collective-permute-done.6.refs_1_, s32[16,128]{1,0:T(8,128)S(1)} %collective-permute-done.7.refs_2_, s32[16,128]{1,0:T(8,128)S(1)} %collective-permute-done.8.refs_3_), custom_call_target="tpu_custom_call" | custom-call | flops 1024 | bytes 1024 | tf_op jit(solution)/shard_map/work_list/pallas_call | solution.py:267
  24.9 0.1 collective-permute-start.9
  25.0 0.0 collective-permute-done.10.refs_2_
  25.0 0.5 %collective-permute-start.11 = (bf16[1,16,4096]{2,1,0:T(8,128)(2,1)S(1)}, bf16[1,16,4096]{2,1,0:T(8,128)(2,1)S(1)}, u32[]{:S(2)}, u32[]{:S(2)}) collective-permute-start(bf16[1,16,4096]{2,1,0:T(8,128)(2,1)S(1)} %collective-permute-done.10.refs_2_), channel_id=1, source_target_pairs={{0,1},{1,0},{2,3},{3,2},{4,5},{5,4},{6,7},{7,6},{8,9},{9,8},{10,11... | collective-permute-start | bytes 393224 | tf_op jit(solution)/shard_map/ppermute | solution.py:28
  25.5 0.8 %collective-permute-done.9.refs_1_ = bf16[1,16,4096]{2,1,0:T(8,128)(2,1)S(1)} collective-permute-done((bf16[1,16,4096]{2,1,0:T(8,128)(2,1)S(1)}, bf16[1,16,4096]{2,1,0:T(8,128)(2,1)S(1)}, u32[]{:S(2)}, u32[]{:S(2)}) %collective-permute-start.9) | collective-permute-done | bytes 131104 | tf_op jit(solution)/shard_map/ppermute | solution.py:28
  26.3 0.2 collective-permute-done.11.refs_3_
  26.5 1.9 %stage.1 = (bf16[2048,128]{1,0:T(8,128)(2,1)S(1)}, f32[16,128,128]{2,1,0:T(8,128)S(1)}) custom-call(bf16[1,16,4096]{2,1,0:T(8,128)(2,1)S(1)} %copy-done.1, bf16[1,16,4096]{2,1,0:T(8,128)(2,1)S(1)} %collective-permute-done.9.refs_1_, bf16[1,16,4096]{2,1,0:T(8,128)(2,1)S(1)} %collective-permute-done.10.refs_2_, ...), custom_call_target="tpu_custom_call", output_to_operand_aliasing={{1}: (7, {})} | custom-call | flops 1024 | bytes 1024 | tf_op jit(solution)/shard_map/stage/pallas_call | solution.py:366
  28.4 0.0 collective-permute-done.12.refs_5_
  28.4 0.7 %collective-permute-done.13.refs_6_ = bf16[528,128]{1,0:T(8,128)(2,1)S(1)} collective-permute-done((bf16[528,128]{1,0:T(8,128)(2,1)S(1)}, bf16[528,128]{1,0:T(8,128)(2,1)S(1)}, u32[]{:S(2)}, u32[]{:S(2)}) %collective-permute-start.13) | collective-permute-done | bytes 135200 | tf_op jit(solution)/shard_map/ppermute | solution.py:28
  29.2 0.0 collective-permute-done.14.refs_7_
  29.2 3.6 %multiply.2 = (f32[16,128,128]{2,1,0:T(8,128)}, s32[1]{0:T(128)}, f32[16,128,128]{2,1,0:T(8,128)S(1)}) custom-call(s32[257]{0:T(512)S(1)} %get-tuple-element.223.refs_5_.refs_0_, s32[5]{0:T(128)S(1)} %get-tuple-element.224.refs_6_.refs_1_, f32[8,128]{1,0:T(8,128)S(1)} %get-tuple-element.92.refs_2_, ...), custom_call_target="tpu_custom_call", output_to_operand_aliasing={{2}: (4, {})} | custom-call | flops 67108864 | bytes 4194304 | tf_op jit(solution)/shard_map/multiply/pallas_call | solution.py:405
  32.8 0.6 %while.12 = (s32[]{:T(128)}, f32[16,128,128]{2,1,0:T(8,128)S(1)}, f32[16,128,128]{2,1,0:T(8,128)}, s32[1]{0:T(128)}, s32[16,128]{1,0:T(8,128)S(1)}, /*index=5*/s...) while((s32[]{:T(128)}, f32[16,128,128]{2,1,0:T(8,128)S(1)}, ...), condition=%wide.region_1.2_spmd, body=%wide.region_0.1_spmd.sunk | while | flops 68157440 | bytes 12108069 | solution.py:458
  (12 shorter events, 0.0 us)
Async XLA Ops:
  0.0 3.8 %collective-permute-start.3 = (s32[2,1,16]{2,1,0:T(1,128)}, s32[2,1,16]{2,1,0:T(1,128)S(1)}, u32[]{:S(2)}, u32[]{:S(2)}) collective-permute-start(s32[2,1,16]{2,1,0:T(1,128)} %param.8), channel_id=1, source_target_pairs={{0,1},{1,0},{2,3},{3,2},{4,5},{5,4},{6,7},{7,6},{8,9},{9,8},{10,11... | collective-permute-start | bytes 392 | tf_op jit(solution)/shard_map/ppermute | solution.py:28
  0.5 4.1 %collective-permute-start.5 = (s32[2,1,16]{2,1,0:T(1,128)}, s32[2,1,16]{2,1,0:T(1,128)S(1)}, u32[]{:S(2)}, u32[]{:S(2)}) collective-permute-start(s32[2,1,16]{2,1,0:T(1,128)} %param.8), channel_id=1, source_target_pairs={{0,3},{1,2},{2,1},{3,0},{4,7},{5,6},{6,5},{7,4},{8,11},{9,10},{10,... | collective-permute-start | bytes 392 | tf_op jit(solution)/shard_map/ppermute | solution.py:28
  3.1 3.8 %collective-permute-start.4 = (s32[2,1,16]{2,1,0:T(1,128)}, s32[2,1,16]{2,1,0:T(1,128)S(1)}, u32[]{:S(2)}, u32[]{:S(2)}) collective-permute-start(s32[2,1,16]{2,1,0:T(1,128)} %param.8), channel_id=1, source_target_pairs={{0,2},{1,3},{2,0},{3,1},{4,6},{5,7},{6,4},{7,5},{8,10},{9,11},{10,... | collective-permute-start | bytes 392 | tf_op jit(solution)/shard_map/ppermute | solution.py:28
  3.1 0.7 %copy-start.5 = (s32[16,4]{0,1:T(4,128)S(1)}, s32[16,4]{0,1:T(4,128)}, u32[]{:S(2)}) copy-start(s32[16,4]{0,1:T(4,128)} %param.11) | copy-start | bytes 772
  3.1 0.7 %copy-start.4 = (s32[16,4]{0,1:T(4,128)S(1)}, s32[16,4]{0,1:T(4,128)}, u32[]{:S(2)}) copy-start(s32[16,4]{0,1:T(4,128)} %param.10) | copy-start | bytes 772
  3.1 0.7 %copy-start.6 = (s32[2,1,16]{2,1,0:T(1,128)S(1)}, s32[2,1,16]{2,1,0:T(1,128)}, u32[]{:S(2)}) copy-start(s32[2,1,16]{2,1,0:T(1,128)} %param.8) | copy-start | bytes 388
  6.8 6.7 %collective-permute-start.8 = (s32[16,128]{1,0:T(8,128)S(1)}, s32[16,128]{1,0:T(8,128)S(1)}, u32[]{:S(2)}, u32[]{:S(2)}) collective-permute-start(s32[16,128]{1,0:T(8,128)S(1)} %pad_maximum_fusion.refs_0_), channel_id=1, source_target_pairs={{0,12},{4,8},{8,4},{12,0},{1,13},{5,9},{9,5},{13,1},{2,14},{6,10},... | collective-permute-start | bytes 24584 | tf_op jit(solution)/shard_map/ppermute | solution.py:28
  10.5 4.5 %collective-permute-start.7 = (s32[16,128]{1,0:T(8,128)S(1)}, s32[16,128]{1,0:T(8,128)S(1)}, u32[]{:S(2)}, u32[]{:S(2)}) collective-permute-start(s32[16,128]{1,0:T(8,128)S(1)} %pad_maximum_fusion.refs_0_), channel_id=1, source_target_pairs={{0,8},{4,12},{8,0},{12,4},{1,9},{5,13},{9,1},{13,5},{2,10},{6,14},... | collective-permute-start | bytes 24584 | tf_op jit(solution)/shard_map/ppermute | solution.py:28
  10.5 4.5 %collective-permute-start.6 = (s32[16,128]{1,0:T(8,128)S(1)}, s32[16,128]{1,0:T(8,128)S(1)}, u32[]{:S(2)}, u32[]{:S(2)}) collective-permute-start(s32[16,128]{1,0:T(8,128)S(1)} %pad_maximum_fusion.refs_0_), channel_id=1, source_target_pairs={{0,4},{4,0},{8,12},{12,8},{1,5},{5,1},{9,13},{13,9},{2,6},{6,2},{1... | collective-permute-start | bytes 24584 | tf_op jit(solution)/shard_map/ppermute | solution.py:28
  11.3 1.0 %copy-start = (bf16[16,4,4096]{2,1,0:T(4,128)(2,1)S(1)}, bf16[16,4,4096]{2,1,0:T(4,128)(2,1)}, u32[]{:S(2)}) copy-start(bf16[16,4,4096]{2,1,0:T(4,128)(2,1)} %param.9) | copy-start | bytes 1572868
  15.1 1.4 %copy-start.1 = (bf16[1,16,4096]{2,1,0:T(8,128)(2,1)S(1)}, bf16[1,16,4096]{2,1,0:T(8,128)(2,1)}, u32[]{:S(2)}) copy-start(bf16[1,16,4096]{2,1,0:T(8,128)(2,1)} %refs_0_.1) | copy-start | bytes 393220
  16.5 8.5 %collective-permute-start.10 = (bf16[1,16,4096]{2,1,0:T(8,128)(2,1)S(1)}, bf16[1,16,4096]{2,1,0:T(8,128)(2,1)S(1)}, u32[]{:S(2)}, u32[]{:S(2)}) collective-permute-start(bf16[1,16,4096]{2,1,0:T(8,128)(2,1)S(1)} %copy-done.1), channel_id=1, source_target_pairs={{0,2},{1,3},{2,0},{3,1},{4,6},{5,7},{6,4},{7,5},{8,10},{9,11},{10,... | collective-permute-start | bytes 393224 | tf_op jit(solution)/shard_map/ppermute | solution.py:28
  17.1 11.4 %collective-permute-start.12 = (bf16[528,128]{1,0:T(8,128)(2,1)S(1)}, bf16[528,128]{1,0:T(8,128)(2,1)S(1)}, u32[]{:S(2)}, u32[]{:S(2)}) collective-permute-start(bf16[528,128]{1,0:T(8,128)(2,1)S(1)} %get-tuple-element.99), channel_id=1, source_target_pairs={{0,12},{4,8},{8,4},{12,0},{1,13},{5,9},{9,5},{13,1},{2,14},{6,10},... | collective-permute-start | bytes 405512 | tf_op jit(solution)/shard_map/ppermute | solution.py:28
  19.2 9.9 %collective-permute-start.13 = (bf16[528,128]{1,0:T(8,128)(2,1)S(1)}, bf16[528,128]{1,0:T(8,128)(2,1)S(1)}, u32[]{:S(2)}, u32[]{:S(2)}) collective-permute-start(bf16[528,128]{1,0:T(8,128)(2,1)S(1)} %get-tuple-element.100), channel_id=1, source_target_pairs={{0,8},{4,12},{8,0},{12,4},{1,9},{5,13},{9,1},{13,5},{2,10},{6,14},... | collective-permute-start | bytes 405512 | tf_op jit(solution)/shard_map/ppermute | solution.py:28
  19.2 9.9 %collective-permute-start.14 = (bf16[528,128]{1,0:T(8,128)(2,1)S(1)}, bf16[528,128]{1,0:T(8,128)(2,1)S(1)}, u32[]{:S(2)}, u32[]{:S(2)}) collective-permute-start(bf16[528,128]{1,0:T(8,128)(2,1)S(1)} %get-tuple-element.101), channel_id=1, source_target_pairs={{0,4},{4,0},{8,12},{12,8},{1,5},{5,1},{9,13},{13,9},{2,6},{6,2},{1... | collective-permute-start | bytes 405512 | tf_op jit(solution)/shard_map/ppermute | solution.py:28
  24.9 1.4 %collective-permute-start.9 = (bf16[1,16,4096]{2,1,0:T(8,128)(2,1)S(1)}, bf16[1,16,4096]{2,1,0:T(8,128)(2,1)S(1)}, u32[]{:S(2)}, u32[]{:S(2)}) collective-permute-start(bf16[1,16,4096]{2,1,0:T(8,128)(2,1)S(1)} %copy-done.1), channel_id=1, source_target_pairs={{0,1},{1,0},{2,3},{3,2},{4,5},{5,4},{6,7},{7,6},{8,9},{9,8},{10,11... | collective-permute-start | bytes 393224 | tf_op jit(solution)/shard_map/ppermute | solution.py:28
  25.0 1.5 %collective-permute-start.11 = (bf16[1,16,4096]{2,1,0:T(8,128)(2,1)S(1)}, bf16[1,16,4096]{2,1,0:T(8,128)(2,1)S(1)}, u32[]{:S(2)}, u32[]{:S(2)}) collective-permute-start(bf16[1,16,4096]{2,1,0:T(8,128)(2,1)S(1)} %collective-permute-done.10.refs_2_), channel_id=1, source_target_pairs={{0,1},{1,0},{2,3},{3,2},{4,5},{5,4},{6,7},{7,6},{8,9},{9,8},{10,11... | collective-permute-start | bytes 393224 | tf_op jit(solution)/shard_map/ppermute | solution.py:28
  28.4 4.3 %copy-start.2 = (bf16[2048,128]{1,0:T(8,128)(2,1)}, bf16[2048,128]{1,0:T(8,128)(2,1)S(1)}, u32[]{:S(2)}) copy-start(bf16[2048,128]{1,0:T(8,128)(2,1)S(1)} %get-tuple-element.225.refs_3_) | copy-start | bytes 1572868

commit v5 on v4

--- a/solution.py
+++ b/solution.py
@@ -14,8 +14,6 @@
 CAPACITY = 16
 UNROLL = 4
 SLOTS = 4
-FLAG = 16
-IDLE = 63
 VMEM = pltpu.VMEM
 SMEM = pltpu.SMEM
 BF16 = jnp.bfloat16
@@ -103,6 +101,12 @@
 
 def iota(shape, axis):
     return lax.broadcasted_iota(I32, shape, axis)
+
+
+def along_lanes(left, right):
+    return lax.dot_general(
+        left.astype(BF16), right.astype(BF16), (((1,), (1,)), ((), ())), preferred_element_type=F32
+    )
 
 
 def turn_to_columns(rows, first, count):
@@ -150,25 +154,16 @@
     return jnp.dot(many, before, preferred_element_type=F32)[0:1]
 
 
-def each(count, body, start):
-    if count > 8:
-        return lax.fori_loop(0, count, body, start)
-    for at in range(count):
-        start = body(at, start)
-    return start
-
-
 def pack_kernel(first, peers, cols, a_slots, row_count, *refs):
     refs = list(refs)
     base = 0 if first else refs.pop(0)[0]
     told = refs[:peers]
     flat = refs[peers]
     outs = refs[peers + 1 : 2 * peers]
-    most, picks, packed = refs[2 * peers :]
+    picks, packed = refs[2 * peers :]
     grid_row = lax.axis_index("row")
     per_col = peers // cols
     offered = offers(told[0], cols, row_count)
-    top = jnp.zeros((1, 1), F32)
     first_slot = grid_row % per_col * a_slots if per_col > 1 else 0
     for d in range(1, peers):
         pairs, _, _ = matches(
@@ -178,8 +173,6 @@
         place = jnp.where(needed > 0.5, places(needed), -1.0).astype(I32)
         pick = (place == iota((CAPACITY, LANES), 0) + base).astype(BF16)
         picks[pl.ds((d - 1) * CAPACITY, CAPACITY), :] = pick
-        top = jnp.maximum(top, jnp.sum(needed, axis=1, keepdims=True))
-    most[...] = jnp.broadcast_to(top, most.shape)
     pick = picks[...][:, : flat.shape[0]]
     for t in range(0, ROWS, 2):
         both = flat[:, pl.ds(t * LANES, 2 * LANES)]
@@ -190,7 +183,6 @@
         out = outs[d - 1]
         for x in range(CAPACITY):
             out[pl.ds(x * ROWS, ROWS), :] = packed[(d - 1) * CAPACITY + x].astype(BF16)
-        out[pl.ds(CAPACITY * ROWS, FLAG), :] = jnp.broadcast_to(top, (FLAG, LANES)).astype(BF16)
 
 
 def pack(base, told, flat, cols, row_count, a_slots):
@@ -199,12 +191,11 @@
     smem_spec = pl.BlockSpec(memory_space=SMEM)
     vmem_spec = pl.BlockSpec(memory_space=VMEM)
     given = [] if first else [base]
-    results = pl.pallas_call(
+    return pl.pallas_call(
         functools.partial(pack_kernel, first, peers, cols, a_slots, row_count),
-        out_shape=[jax.ShapeDtypeStruct((CAPACITY * ROWS + FLAG, LANES), BF16)] * (peers - 1)
-        + [jax.ShapeDtypeStruct((8, LANES), F32)],
+        out_shape=[jax.ShapeDtypeStruct((CAPACITY * ROWS, LANES), BF16)] * (peers - 1),
         in_specs=[smem_spec] * len(given) + [vmem_spec] * (peers + 1),
-        out_specs=[vmem_spec] * peers,
+        out_specs=[vmem_spec] * (peers - 1),
         scratch_shapes=[
             VMEM(((peers - 1) * CAPACITY, LANES), BF16),
             VMEM(((peers - 1) * CAPACITY, ROWS, LANES), F32),
@@ -213,99 +204,147 @@
         cost_estimate=pl.CostEstimate(flops=1 << 20, bytes_accessed=4 << 20, transcendentals=0),
         name="pack",
     )(*given, *told, flat)
-    return results[:-1], results[-1]
 
 
 def list_kernel(cols, a_slots, row_count, peers, *refs):
-    told = refs[:peers]
-    items, starts, words, words_s, sem = refs[peers:]
+    told, items = refs[:peers], refs[peers]
     grid_row = lax.axis_index("row")
+    grid_col = lax.axis_index("col")
     per_col = peers // cols
-    lane = iota((a_slots, LANES), 1)
-    slot = iota((a_slots, LANES), 0)
-    words[...] = jnp.full(words.shape, IDLE, I32)
+    blocks = row_count * SLOTS
+    lane = iota((1, LANES), 1)
+    spot = iota((blocks, LANES), 0)
+    before = (iota((LANES, LANES), 0) < iota((LANES, LANES), 1)).astype(BF16)
+    below = (iota((blocks, blocks), 1) < iota((blocks, blocks), 0)).astype(BF16)
+    same_slot = spot // row_count == iota((blocks, LANES), 1) // a_slots
     for d in range(peers):
         group = grid_row ^ d
         holder = group // per_col
         first_slot = group % per_col * a_slots if per_col > 1 else 0
-        offered = offers(told[d], cols, row_count)
-        pairs, which, a_rows = matches(
-            told[0], offered, holder, cols, row_count, first_slot, a_slots
-        )
+        at = 2 * (holder ^ grid_col)
+        slots = []
+        for row in (told[0][pl.ds(at, 1), :], told[0][pl.ds(at + 1, 1), :]):
+            if per_col > 1:
+                row = pltpu.roll(row, (LANES - first_slot) % LANES, 1)
+            spread = row
+            for n in range(1, SLOTS):
+                spread = jnp.where(lane // a_slots == n, pltpu.roll(row, n * a_slots, 1), spread)
+            slots.append(jnp.where(lane < SLOTS * a_slots, spread, -1))
+        a_rows, a_columns = slots
+        offered = turn_to_columns(
+            jnp.broadcast_to(offers(told[d], cols, row_count), (8, LANES)), 0, blocks
+        )[:, 0:1]
+        kept = jnp.zeros((blocks, LANES), F32)
+        which = jnp.zeros((blocks, LANES), F32)
+        for m in range(SLOTS):
+            column = told[0][pl.ds(2 * cols + m, 1), :].astype(F32)
+            equal = (column == offered) & (offered >= 0)
+            kept = jnp.where(equal, 1.0, kept)
+            which = jnp.where(equal, float(m), which)
+        by_row = (a_rows == iota((row_count, LANES), 0)).astype(BF16)
+        both = jnp.concatenate([kept, which], axis=0)[:, :row_count].astype(BF16)
+        both = jnp.dot(both, by_row, preferred_element_type=F32)
+        meets = (both[:blocks] > 0.5) & (a_columns == spot % row_count) & same_slot
+        pairs = jnp.where(meets, 1.0, 0.0)
         if d == 0:
-            place = iota((1, LANES), 1).astype(F32)
+            place = spot.astype(F32)
         else:
-            place = places(jnp.max(pairs, axis=0, keepdims=True))
-        stacked = jnp.concatenate([pairs, pairs * place, pairs * which], axis=0).astype(BF16)
-        to_slot = iota((LANES, LANES), 1) == iota((LANES, LANES), 0) // row_count + d * SLOTS
-        by_slot = jnp.dot(stacked, to_slot.astype(BF16), preferred_element_type=F32)
-        hit = by_slot[:a_slots] > 0.5
-        at = by_slot[a_slots : 2 * a_slots].astype(I32)
-        out = (a_rows * SLOTS + by_slot[2 * a_slots :]).astype(I32)
-        a_slot = holder * per_col * a_slots + first_slot + slot
-        word = ((a_slot * 64 + out) * 64 + at) * 64 + d
-        words[...] = jnp.where(hit & (lane // SLOTS == d), word, words[...])
-    fetch([(words, words_s)], sem)
-
-    def one_peer(d, length):
-        starts[d] = length
-        for n in range(SLOTS):
-            for s in range(a_slots):
-                word = words_s[s, d * SLOTS + n]
-                items[length] = word
-                length = length + (word & IDLE != IDLE).astype(I32)
-        return length
-
-    length = lax.fori_loop(0, peers, one_peer, jnp.int32(0))
-    starts[peers] = length
-    items[length] = IDLE
+            needed = jnp.max(pairs, axis=1, keepdims=True)
+            many = jnp.broadcast_to(needed, (blocks, LANES)).astype(BF16)
+            place = jnp.dot(below, many, preferred_element_type=F32)
+        hit = jnp.sum(pairs, axis=0, keepdims=True)
+        place = jnp.sum(pairs * place, axis=0, keepdims=True)
+        out = jnp.sum(pairs * both[blocks:], axis=0, keepdims=True)
+        out = out + a_rows.astype(F32) * SLOTS * hit
+        rank = jnp.dot(
+            jnp.broadcast_to(hit, (8, LANES)).astype(BF16), before, preferred_element_type=F32
+        )[0:1]
+        rank = jnp.where(hit > 0.5, rank, -1.0).astype(I32)
+        chosen = rank == iota((LANES, LANES), 0)
+        zero = jnp.zeros((1, LANES), F32)
+        values = [(lane % a_slots).astype(F32) * hit, out, place] + [zero] * 5
+        listed = along_lanes(jnp.concatenate(values, axis=0), chosen.astype(F32)).astype(I32)
+        a_slot = holder * per_col * a_slots + first_slot + listed[0:1]
+        word = (a_slot * 64 + listed[1:2]) * 64 + listed[2:3]
+        total = jnp.sum(hit, axis=1, keepdims=True).astype(I32)
+        items[pl.ds(d, 1), :] = jnp.where(lane == LANES - 1, total, word)
 
 
 def work_list(told, cols, row_count, a_slots):
     peers = len(told)
-    most_items = peers * a_slots * SLOTS + 1
     return pl.pallas_call(
         functools.partial(list_kernel, cols, a_slots, row_count, peers),
-        out_shape=[
-            jax.ShapeDtypeStruct((most_items,), I32),
-            jax.ShapeDtypeStruct((peers + 1,), I32),
-        ],
+        out_shape=jax.ShapeDtypeStruct((-(-peers // 8) * 8, LANES), I32),
         in_specs=[pl.BlockSpec(memory_space=VMEM)] * peers,
-        out_specs=[pl.BlockSpec(memory_space=SMEM)] * 2,
-        scratch_shapes=[
-            VMEM((a_slots, LANES), I32),
-            SMEM((a_slots, LANES), I32),
-            pltpu.SemaphoreType.DMA((1,)),
-        ],
+        out_specs=pl.BlockSpec(memory_space=VMEM),
         cost_estimate=pl.CostEstimate(flops=1 << 10, bytes_accessed=1 << 10, transcendentals=0),
         name="work_list",
     )(*told)
 
 
-def fetch(copies, sems):
-    started = [
-        pltpu.make_async_copy(source, target, sems.at[at])
-        for at, (source, target) in enumerate(copies)
-    ]
-    for copy in started:
-        copy.start()
-    for copy in started:
-        copy.wait()
-
-
-def add_products(items, starts, a_ref, peer_refs, sums, window=None):
+def rounds_kernel(cols, a_slots, row_count, peers, *refs):
+    told_refs, rounds, told = refs[:peers], refs[peers], refs[peers + 1]
+    for d, ref in enumerate(told_refs):
+        told[d, :, :] = ref[...]
+    grid_row = lax.axis_index("row")
+    per_col = peers // cols
+
+    def one_pair(receiver, d, most):
+        group = grid_row ^ receiver ^ d
+        sender = receiver ^ d
+        first_slot = group % per_col * a_slots if per_col > 1 else 0
+        pairs, _, _ = matches(
+            told.at[receiver],
+            offers(told.at[sender], cols, row_count),
+            group // per_col,
+            cols,
+            row_count,
+            first_slot,
+            a_slots,
+        )
+        needed = jnp.max(pairs, axis=0, keepdims=True)
+        return jnp.maximum(most, jnp.sum(needed, axis=1, keepdims=True))
+
+    most = jnp.zeros((1, 1), F32)
+    if peers <= 4:
+        for receiver in range(peers):
+            for d in range(1, peers):
+                most = one_pair(receiver, d, most)
+    else:
+
+        def step(at, most):
+            return one_pair(at // (peers - 1), at % (peers - 1) + 1, most)
+
+        most = lax.fori_loop(0, peers * (peers - 1), step, most)
+    rounds[0] = (jnp.max(most).astype(I32) + CAPACITY - 1) // CAPACITY
+
+
+def count_rounds(told, cols, row_count, a_slots):
+    peers = len(told)
+    return pl.pallas_call(
+        functools.partial(rounds_kernel, cols, a_slots, row_count, peers),
+        out_shape=jax.ShapeDtypeStruct((1,), I32),
+        in_specs=[pl.BlockSpec(memory_space=VMEM)] * peers,
+        out_specs=pl.BlockSpec(memory_space=SMEM),
+        scratch_shapes=[VMEM((peers,) + told[0].shape, I32)],
+        cost_estimate=pl.CostEstimate(flops=1 << 10, bytes_accessed=1 << 10, transcendentals=0),
+        name="count_rounds",
+    )(*told)
+
+
+def add_products(items, a_ref, peer_refs, sums, window=None):
     low = iota((ROWS, LANES), 1) < BS
     nothing = jnp.zeros((ROWS, LANES), BF16)
 
     def add_one(word, used, b_ref):
-        place = (word >> 6) & 63
-        target = (word >> 12) & 63
-        used = used & ((word & IDLE) != IDLE)
+        word = jnp.where(used, word, 0)
+        place = word & 63
+        target = (word >> 6) & 63
         if window is not None:
             place = place - window
             used = used & (place >= 0) & (place < CAPACITY)
-        place = jnp.where(used, place, 0)
-        a_at = pl.multiple_of((word >> 18) * ROWS, ROWS)
+            place = jnp.where(used, place, 0)
+        a_at = pl.multiple_of((word >> 12) * ROWS, ROWS)
         b_at = pl.multiple_of(place * ROWS, ROWS)
         block = jnp.where(used, b_ref[pl.ds(b_at, ROWS), :], nothing)
         turned = jnp.concatenate([block[:, BS:], block[:, :BS]], axis=1)
@@ -323,24 +362,23 @@
 
     for at in range(0, len(peer_refs), 3):
         chosen = peer_refs[at : at + 3]
-        bounds = [(starts[d], starts[d + 1]) for d, _ in chosen]
-        longest = functools.reduce(jnp.maximum, [stop - start for start, stop in bounds])
+        totals = [items[d, LANES - 1] for d, _ in chosen]
+        longest = functools.reduce(jnp.maximum, totals)
         width = UNROLL if len(chosen) < 3 else UNROLL - 1
 
-        def some_items(step, carry, chosen=chosen, bounds=bounds, width=width):
+        def some_items(step, carry, chosen=chosen, totals=totals, width=width):
             for u in range(width):
-                for (_, b_ref), (start, stop) in zip(chosen, bounds):
-                    y = start + step * width + u
-                    used = y < stop
-                    add_one(items[jnp.where(used, y, start)], used, b_ref)
+                for (d, b_ref), total in zip(chosen, totals):
+                    y = step * width + u
+                    add_one(items[d, y], y < total, b_ref)
             return carry
 
         lax.fori_loop(0, (longest + width - 1) // width, some_items, 0)
 
 
 def stage_kernel(cols, *refs):
-    a_refs, own, items, starts = refs[:cols], refs[cols], refs[cols + 1], refs[cols + 2]
-    a_out, sums, a_wide = refs[cols + 4 :]
+    a_refs, own, items = refs[:cols], refs[cols], refs[cols + 1]
+    a_out, sums, a_wide = refs[cols + 3 :]
     source = iota((LANES, LANES), 0)
     target = iota((LANES, LANES), 1)
     wanted = (target // BS) * BS + 2 * (target % ROWS) + (target // ROWS) % 2
@@ -356,10 +394,10 @@
         for s in range(slots):
             at = pl.multiple_of((first + s) * ROWS, ROWS)
             a_out[pl.ds(at, ROWS), :] = a_wide[h * slots + s].astype(BF16)
-    add_products(items, starts, a_out, [(0, own)], sums)
-
-
-def stage(a_parts, own, sums, items, starts):
+    add_products(items, a_out, [(0, own)], sums)
+
+
+def stage(a_parts, own, sums, items):
     cols, slots = len(a_parts), a_parts[0].shape[1]
     vmem_spec = pl.BlockSpec(memory_space=VMEM)
     smem_spec = pl.BlockSpec(memory_space=SMEM)
@@ -369,34 +407,29 @@
             jax.ShapeDtypeStruct((cols * slots * ROWS, LANES), BF16),
             jax.ShapeDtypeStruct(sums.shape, F32),
         ),
-        in_specs=[vmem_spec] * (cols + 1) + [smem_spec] * 2 + [vmem_spec],
+        in_specs=[vmem_spec] * (cols + 1) + [smem_spec] + [vmem_spec],
         out_specs=(vmem_spec,) * 2,
-        input_output_aliases={cols + 3: 1},
+        input_output_aliases={cols + 2: 1},
         scratch_shapes=[VMEM((cols * slots, ROWS, LANES), F32)],
         compiler_params=pltpu.CompilerParams(vmem_limit_bytes=40 << 20),
         cost_estimate=pl.CostEstimate(flops=1 << 10, bytes_accessed=1 << 10, transcendentals=0),
         name="stage",
-    )(*a_parts, own, items, starts, sums)
+    )(*a_parts, own, items, sums)
 
 
 def multiply_kernel(first, peers, *refs):
     refs = list(refs)
     base = 0 if first else refs.pop(0)[0]
-    items, starts, most, a_ref = refs[:4]
-    b_refs = refs[5 : 4 + peers][::-1]
-    out, rounds, sums, sem = refs[4 + peers :]
-    add_products(items, starts, a_ref, list(enumerate(b_refs, 1)), sums, window=base)
+    items, a_ref = refs[:2]
+    b_refs = refs[3 : 2 + peers][::-1]
+    sums, out, sem = refs[2 + peers :]
+    add_products(items, a_ref, list(enumerate(b_refs, 1)), sums, window=base)
     copy = pltpu.make_async_copy(sums, out, sem.at[0])
     copy.start()
-    flags = most[...]
-    for ref in b_refs:
-        flag = ref[pl.ds(CAPACITY * ROWS, FLAG), :].astype(F32)
-        flags = jnp.maximum(flags, jnp.max(flag, axis=0, keepdims=True))
-    rounds[0] = (jnp.max(flags).astype(I32) + CAPACITY - 1) // CAPACITY
     copy.wait()
 
 
-def multiply(base, items, starts, most, a_ready, sums, b_parts):
+def multiply(base, items, a_ready, sums, b_parts):
     first = base is None
     peers = len(b_parts) + 1
     smem_spec = pl.BlockSpec(memory_space=SMEM)
@@ -404,19 +437,15 @@
     given = [] if first else [base]
     return pl.pallas_call(
         functools.partial(multiply_kernel, first, peers),
-        out_shape=[
-            jax.ShapeDtypeStruct(sums.shape, F32),
-            jax.ShapeDtypeStruct((1,), I32),
-            jax.ShapeDtypeStruct(sums.shape, F32),
-        ],
-        in_specs=[smem_spec] * (len(given) + 2) + [vmem_spec] * (2 + peers),
-        out_specs=[pl.BlockSpec(memory_space=pl.ANY), smem_spec, vmem_spec],
-        input_output_aliases={len(given) + 4: 2},
+        out_shape=[jax.ShapeDtypeStruct(sums.shape, F32)] * 2,
+        in_specs=[smem_spec] * (len(given) + 1) + [vmem_spec] * (1 + peers),
+        out_specs=[vmem_spec, pl.BlockSpec(memory_space=pl.ANY)],
+        input_output_aliases={len(given) + 2: 0},
         scratch_shapes=[pltpu.SemaphoreType.DMA((1,))],
         compiler_params=pltpu.CompilerParams(vmem_limit_bytes=32 << 20),
         cost_estimate=pl.CostEstimate(flops=1 << 26, bytes_accessed=4 << 20, transcendentals=0),
         name="multiply",
-    )(*given, items, starts, most, a_ready, sums, *b_parts[::-1])
+    )(*given, items, a_ready, sums, *b_parts[::-1])
 
 
 def shards(a_blocks, a_index, b_blocks, b_cols, c_cols):
@@ -429,20 +458,20 @@
         far_first = range(len(parts), 0, -1)
         return [exchanged(parts[d - 1], "row", d) for d in far_first][::-1]
 
-    told = describe([a_index] + [exchanged(a_index, "col", h) for h in range(1, cols)],
-                    b_cols.T, c_cols.T)
+    index_parts = [a_index] + [exchanged(a_index, "col", h) for h in range(1, cols)]
+    told = describe(index_parts, b_cols.T, c_cols.T)
+    a_parts = [exchanged(a_blocks, "col", h) for h in range(1, cols)]
+    told, a_parts[0] = lax.optimization_barrier((told, a_parts[0]))
     told = [told] + send_rows([told] * (rows - 1))
     flat, own, sums = flatten(seen_by_rows(b_blocks))
-    packed, most = pack(None, told, flat, cols, row_count, a_slots)
+    flat, *a_parts = lax.optimization_barrier((flat, *a_parts))
+    packed = pack(None, told, flat, cols, row_count, a_slots)
     arrived = send_rows(packed)
-    items, starts = work_list(told, cols, row_count, a_slots)
-    a_late, _ = lax.optimization_barrier((a_blocks, most))
-    a_far = [exchanged(a_late, "col", h) for h in range(2, cols, 2)]
-    a_parts = [a_blocks, exchanged(a_late, "col", 1)]
-    for far in a_far:
-        a_parts += [far, exchanged(lax.optimization_barrier((far, items))[0], "col", 1)]
-    a_ready, sums = stage(a_parts, own, sums, items, starts)
-    out, rounds, sums = multiply(None, items, starts, most, a_ready, sums, arrived)
+    told_late = lax.optimization_barrier((told, packed[0]))[0]
+    items = work_list(told_late, cols, row_count, a_slots)
+    rounds = count_rounds(told_late, cols, row_count, a_slots)
+    a_ready, sums = stage([a_blocks] + a_parts, own, sums, items)
+    sums, out = multiply(None, items, a_ready, sums, arrived)
 
     def more(state):
         return state[0] < rounds[0]
@@ -450,10 +479,8 @@
     def one_round(state):
         at, sums, _ = state
         base = jnp.reshape(at * CAPACITY, (1,))
-        packed, most = pack(base, told, flat, cols, row_count, a_slots)
-        arrived = send_rows(packed)
-        out, _, sums = multiply(base, items, starts, most, a_ready, sums, arrived)
-        return at + 1, sums, out
+        arrived = send_rows(pack(base, told, flat, cols, row_count, a_slots))
+        return at + 1, *multiply(base, items, a_ready, sums, arrived)
 
     return seen_by_blocks(lax.while_loop(more, one_round, (jnp.int32(1), sums, out))[2])
 

time: 33.1 us -> 33 us (level); the launches traced: 33.3 us -> 32.9 us
  Pallas kernels: 11.5 us -> 9.8 us
  starting transfers between devices: 13.1 us -> 14.1 us
    pallas_call x1, Pallas kernels: 3.42 us -> 1.91 us  [work_list(): pl.pallas_call(functools.partial(list_kernel, cols, a_slots, row_count, p...]
    pallas_call x1, Pallas kernels: 3.55 us -> 2.19 us  [multiply(): pl.pallas_call(functools.partial(multiply_kernel, first, peers), out_shap...]
    pallas_call x0 -> x1, Pallas kernels: none -> 1.35 us  [count_rounds(): pl.pallas_call(functools.partial(rounds_kernel, cols, a_slots, row_count,...]
    ppermute x12, starting transfers between devices: 13.1 us -> 14.1 us  [exchanged(): return lax.ppermute(block, axis, [(i, i ^ distance) for i in range(size)])]
  transfers between devices with their start and end apart: 12 -> 12, of which waited for: 6 -> 4; matrix products, arithmetic and copies ran while one was open for 0% -> 0% of each run, Pallas kernels for 20% -> 19%
where the time goes in v5:
time: 33 us; the launch traced here: 32.9 us
  starting transfers between devices  14.1 us (43%)
  Pallas kernels  9.8 us (30%)
  waiting for transfers between devices  6.36 us (19%)
  local copies, waits for them, and re-layouts  1.76 us (5%)
  loops' own time  0.68 us (2%)
    ppermute x12, starting transfers between devices, exchanged(): return lax.ppermute(block, axis, [(i, i ^ distance) for i in range(size)])  14.1 us
    ppermute x12, waiting for transfers between devices, exchanged(): return lax.ppermute(block, axis, [(i, i ^ distance) for i in range(size)])  6.36 us
    pallas_call x1, Pallas kernels, multiply(): pl.pallas_call(functools.partial(multiply_kernel, first, peers), out_shap...  2.19 us
    pallas_call x1, Pallas kernels, work_list(): pl.pallas_call(functools.partial(list_kernel, cols, a_slots, row_count, p...  1.91 us
    unnamed x12, local copies, waits for them, and re-layouts  1.76 us
    pallas_call x1, Pallas kernels, stage(): pl.pallas_call(functools.partial(stage_kernel, cols), out_shape=(jax.Shap...  1.74 us
    pallas_call x1, Pallas kernels, pack(): pl.pallas_call(functools.partial(pack_kernel, first, peers, cols, a_slots...  1.38 us
    pallas_call x1, Pallas kernels, count_rounds(): pl.pallas_call(functools.partial(rounds_kernel, cols, a_slots, row_count,...  1.35 us
  transfers between devices with their start and end apart: 12, of which 4 were waited for; matrix products, arithmetic and copies ran while one was open for 0% of the time, Pallas kernels for 19%

profile of v5, /device:TPU:0, one launch (start us, length us, event | category | flops | bytes accessed | tf_op | source)
XLA Modules:
  0.0 32.9 jit_solution(10078148689052805220)
XLA Ops:
  0.0 0.5 %collective-permute-start.3 = (s32[2,1,16]{2,1,0:T(1,128)}, s32[2,1,16]{2,1,0:T(1,128)S(1)}, u32[]{:S(2)}, u32[]{:S(2)}) collective-permute-start(s32[2,1,16]{2,1,0:T(1,128)} %param.8), channel_id=1, source_target_pairs={{0,1},{1,0},{2,3},{3,2},{4,5},{5,4},{6,7},{7,6},{8,9},{9,8},{10,11... | collective-permute-start | bytes 392 | tf_op jit(solution)/shard_map/ppermute | solution.py:26
  0.5 2.6 %collective-permute-start.5 = (s32[2,1,16]{2,1,0:T(1,128)}, s32[2,1,16]{2,1,0:T(1,128)S(1)}, u32[]{:S(2)}, u32[]{:S(2)}) collective-permute-start(s32[2,1,16]{2,1,0:T(1,128)} %param.8), channel_id=1, source_target_pairs={{0,3},{1,2},{2,1},{3,0},{4,7},{5,6},{6,5},{7,4},{8,11},{9,10},{10,... | collective-permute-start | bytes 392 | tf_op jit(solution)/shard_map/ppermute | solution.py:26
  3.1 0.0 collective-permute-start.4
  3.1 2.0 %collective-permute-start.10 = (bf16[1,16,4096]{2,1,0:T(8,128)(2,1)}, bf16[1,16,4096]{2,1,0:T(8,128)(2,1)S(1)}, u32[]{:S(2)}, u32[]{:S(2)}) collective-permute-start(bf16[1,16,4096]{2,1,0:T(8,128)(2,1)} %refs_0_.1), channel_id=1, source_target_pairs={{0,2},{1,3},{2,0},{3,1},{4,6},{5,7},{6,4},{7,5},{8,10},{9,11},{10,... | collective-permute-start | bytes 393224 | tf_op jit(solution)/shard_map/ppermute | solution.py:26
  5.1 0.7 %copy-done.4 = s32[16,4]{0,1:T(4,128)S(1)} copy-done((s32[16,4]{0,1:T(4,128)S(1)}, s32[16,4]{0,1:T(4,128)}, u32[]{:S(2)}) %copy-start.4) | copy-done | bytes 280
  5.8 0.0 copy-done.3
  5.8 0.0 copy-done.5
  5.8 0.1 collective-permute-start.6
  5.9 0.1 collective-permute-start.11
  6.0 0.0 collective-permute-done.5
  6.0 0.8 %collective-permute-done.4 = s32[2,1,16]{2,1,0:T(1,128)S(1)} collective-permute-done((s32[2,1,16]{2,1,0:T(1,128)}, s32[2,1,16]{2,1,0:T(1,128)S(1)}, u32[]{:S(2)}, u32[]{:S(2)}) %collective-permute-start.4) | collective-permute-done | bytes 160 | tf_op jit(solution)/shard_map/ppermute | solution.py:26
  6.9 0.6 %collective-permute-done.6.refs_1_ = bf16[1,16,4096]{2,1,0:T(8,128)(2,1)S(1)} collective-permute-done((bf16[1,16,4096]{2,1,0:T(8,128)(2,1)}, bf16[1,16,4096]{2,1,0:T(8,128)(2,1)S(1)}, u32[]{:S(2)}, u32[]{:S(2)}) %collective-permute-start.6) | collective-permute-done | bytes 131104 | tf_op jit(solution)/shard_map/ppermute | solution.py:26
  7.4 3.6 %collective-permute-start.9 = (s32[16,128]{1,0:T(8,128)S(1)}, s32[16,128]{1,0:T(8,128)S(1)}, u32[]{:S(2)}, u32[]{:S(2)}) collective-permute-start(s32[16,128]{1,0:T(8,128)S(1)} %pad_maximum_fusion.refs_0_), channel_id=1, source_target_pairs={{0,12},{4,8},{8,4},{12,0},{1,13},{5,9},{9,5},{13,1},{2,14},{6,10},... | collective-permute-start | bytes 24584 | tf_op jit(solution)/shard_map/ppermute | solution.py:26
  11.0 0.0 collective-permute-start.8
  11.0 0.8 %collective-permute-start.7 = (s32[16,128]{1,0:T(8,128)S(1)}, s32[16,128]{1,0:T(8,128)S(1)}, u32[]{:S(2)}, u32[]{:S(2)}) collective-permute-start(s32[16,128]{1,0:T(8,128)S(1)} %pad_maximum_fusion.refs_0_), channel_id=1, source_target_pairs={{0,4},{4,0},{8,12},{12,8},{1,5},{5,1},{9,13},{13,9},{2,6},{6,2},{1... | collective-permute-start | bytes 24584 | tf_op jit(solution)/shard_map/ppermute | solution.py:26
  11.8 1.0 %copy-done = bf16[16,4,4096]{2,1,0:T(4,128)(2,1)S(1)} copy-done((bf16[16,4,4096]{2,1,0:T(4,128)(2,1)S(1)}, bf16[16,4,4096]{2,1,0:T(4,128)(2,1)}, u32[]{:S(2)}) %copy-start) | copy-done | bytes 524312
  12.9 1.2 %flatten.1 = (bf16[64,4096]{1,0:T(8,128)(2,1)S(1)}, bf16[2048,128]{1,0:T(8,128)(2,1)S(1)}, f32[16,128,128]{2,1,0:T(8,128)S(1)}) custom-call(bf16[16,128,128]{2,1,0:T(8,128)(2,1)S(1)} %bitcast.21), custom_call_target="tpu_custom_call" | custom-call | flops 1048576 | bytes 8388608 | tf_op jit(solution)/shard_map/flatten/pallas_call | solution.py:86
  14.1 0.0 collective-permute-done.10.refs_2_
  14.1 0.0 collective-permute-done.11.refs_3_
  14.1 1.4 %collective-permute-done.8.refs_2_ = s32[16,128]{1,0:T(8,128)S(1)} collective-permute-done((s32[16,128]{1,0:T(8,128)S(1)}, s32[16,128]{1,0:T(8,128)S(1)}, u32[]{:S(2)}, u32[]{:S(2)}) %collective-permute-start.8) | collective-permute-done | bytes 8224 | tf_op jit(solution)/shard_map/ppermute | solution.py:26
  15.6 1.4 %pack.2 = (bf16[512,128]{1,0:T(8,128)(2,1)S(1)}, bf16[512,128]{1,0:T(8,128)(2,1)S(1)}, bf16[512,128]{1,0:T(8,128)(2,1)S(1)}) custom-call(s32[16,128]{1,0:T(8,128)S(1)} %pad_maximum_fusion.refs_0_, s32[16,128]{1,0:T(8,128)S(1)} %collective-permute-done.7.refs_1_, s32[16,128]{1,0:T(8,128)S(1)} %collective-permute-done.8.refs_2_, ...), custom_call_target="tpu_custom_call" | custom-call | flops 1048576 | bytes 4194304 | tf_op jit(solution)/shard_map/pack/pallas_call | solution.py:194
  17.0 2.3 %collective-permute-start.12 = (bf16[512,128]{1,0:T(8,128)(2,1)S(1)}, bf16[512,128]{1,0:T(8,128)(2,1)S(1)}, u32[]{:S(2)}, u32[]{:S(2)}) collective-permute-start(bf16[512,128]{1,0:T(8,128)(2,1)S(1)} %get-tuple-element.103), channel_id=1, source_target_pairs={{0,12},{4,8},{8,4},{12,0},{1,13},{5,9},{9,5},{13,1},{2,14},{6,10},... | collective-permute-start | bytes 393224 | tf_op jit(solution)/shard_map/ppermute | solution.py:26
  19.2 0.0 collective-permute-start.13
  19.2 2.2 %collective-permute-start.14 = (bf16[512,128]{1,0:T(8,128)(2,1)S(1)}, bf16[512,128]{1,0:T(8,128)(2,1)S(1)}, u32[]{:S(2)}, u32[]{:S(2)}) collective-permute-start(bf16[512,128]{1,0:T(8,128)(2,1)S(1)} %get-tuple-element.91), channel_id=1, source_target_pairs={{0,4},{4,0},{8,12},{12,8},{1,5},{5,1},{9,13},{13,9},{2,6},{6,2},{1... | collective-permute-start | bytes 393224 | tf_op jit(solution)/shard_map/ppermute | solution.py:26
  21.4 1.4 %count_rounds.1 = s32[1]{0:T(128)} custom-call(s32[16,128]{1,0:T(8,128)S(1)} %pad_maximum_fusion.refs_0_, s32[16,128]{1,0:T(8,128)S(1)} %collective-permute-done.7.refs_1_, s32[16,128]{1,0:T(8,128)S(1)} %collective-permute-done.8.refs_2_, s32[16,128]{1,0:T(8,128)S(1)} %collective-permute-done.9.refs_3_), custom_call_target="tpu_custom_call" | custom-call | flops 1024 | bytes 1024 | tf_op jit(solution)/shard_map/count_rounds/pallas_call | solution.py:324
  22.8 1.9 %work_list.1.refs_5_.refs_0_ = s32[8,128]{1,0:T(8,128)S(1)} custom-call(s32[16,128]{1,0:T(8,128)S(1)} %pad_maximum_fusion.refs_0_, s32[16,128]{1,0:T(8,128)S(1)} %collective-permute-done.7.refs_1_, s32[16,128]{1,0:T(8,128)S(1)} %collective-permute-done.8.refs_2_, s32[16,128]{1,0:T(8,128)S(1)} %collective-permute-done.9.refs_3_), custom_call_target="tpu_custom_call" | custom-call | flops 1024 | bytes 1024 | tf_op jit(solution)/shard_map/work_list/pallas_call | solution.py:275
  24.7 1.7 %stage.1 = (bf16[2048,128]{1,0:T(8,128)(2,1)S(1)}, f32[16,128,128]{2,1,0:T(8,128)S(1)}) custom-call(bf16[1,16,4096]{2,1,0:T(8,128)(2,1)S(1)} %copy-done.1, bf16[1,16,4096]{2,1,0:T(8,128)(2,1)S(1)} %collective-permute-done.6.refs_1_, bf16[1,16,4096]{2,1,0:T(8,128)(2,1)S(1)} %collective-permute-done.10.refs_2_, ...), custom_call_target="tpu_custom_call", output_to_operand_aliasing={{1}: (6, {})} | custom-call | flops 1024 | bytes 1024 | tf_op jit(solution)/shard_map/stage/pallas_call | solution.py:404
  26.4 0.0 collective-permute-done.12.refs_3_
  26.4 3.5 %collective-permute-done.13.refs_4_ = bf16[512,128]{1,0:T(8,128)(2,1)S(1)} collective-permute-done((bf16[512,128]{1,0:T(8,128)(2,1)S(1)}, bf16[512,128]{1,0:T(8,128)(2,1)S(1)}, u32[]{:S(2)}, u32[]{:S(2)}) %collective-permute-start.13) | collective-permute-done | bytes 131104 | tf_op jit(solution)/shard_map/ppermute | solution.py:26
  30.0 0.0 collective-permute-done.14.refs_5_
  30.0 2.2 %multiply.2 = (f32[16,128,128]{2,1,0:T(8,128)S(1)}, f32[16,128,128]{2,1,0:T(8,128)}) custom-call(s32[8,128]{1,0:T(8,128)S(1)} %work_list.1.refs_5_.refs_0_, bf16[2048,128]{1,0:T(8,128)(2,1)S(1)} %get-tuple-element.216.refs_1_, f32[16,128,128]{2,1,0:T(8,128)S(1)} %get-tuple-element.102.refs_2_, ...), custom_call_target="tpu_custom_call", output_to_operand_aliasing={{0}: (2, {})} | custom-call | flops 67108864 | bytes 4194304 | tf_op jit(solution)/shard_map/multiply/pallas_call | solution.py:438
  32.2 0.7 %while.12 = (s32[]{:T(128)}, f32[16,128,128]{2,1,0:T(8,128)S(1)}, f32[16,128,128]{2,1,0:T(8,128)}, s32[1]{0:T(128)}, s32[16,128]{1,0:T(8,128)S(1)}, /*index=5*/s...) while((s32[]{:T(128)}, f32[16,128,128]{2,1,0:T(8,128)S(1)}, ...), condition=%wide.region_1.2_spmd, body=%wide.region_0.1_spmd.sunk | while | flops 68157440 | bytes 9961729 | solution.py:485
  (13 shorter events, 0.0 us)
Async XLA Ops:
  0.0 5.9 %collective-permute-start.3 = (s32[2,1,16]{2,1,0:T(1,128)}, s32[2,1,16]{2,1,0:T(1,128)S(1)}, u32[]{:S(2)}, u32[]{:S(2)}) collective-permute-start(s32[2,1,16]{2,1,0:T(1,128)} %param.8), channel_id=1, source_target_pairs={{0,1},{1,0},{2,3},{3,2},{4,5},{5,4},{6,7},{7,6},{8,9},{9,8},{10,11... | collective-permute-start | bytes 392 | tf_op jit(solution)/shard_map/ppermute | solution.py:26
  0.5 5.6 %collective-permute-start.5 = (s32[2,1,16]{2,1,0:T(1,128)}, s32[2,1,16]{2,1,0:T(1,128)S(1)}, u32[]{:S(2)}, u32[]{:S(2)}) collective-permute-start(s32[2,1,16]{2,1,0:T(1,128)} %param.8), channel_id=1, source_target_pairs={{0,3},{1,2},{2,1},{3,0},{4,7},{5,6},{6,5},{7,4},{8,11},{9,10},{10,... | collective-permute-start | bytes 392 | tf_op jit(solution)/shard_map/ppermute | solution.py:26
  3.1 3.8 %collective-permute-start.4 = (s32[2,1,16]{2,1,0:T(1,128)}, s32[2,1,16]{2,1,0:T(1,128)S(1)}, u32[]{:S(2)}, u32[]{:S(2)}) collective-permute-start(s32[2,1,16]{2,1,0:T(1,128)} %param.8), channel_id=1, source_target_pairs={{0,2},{1,3},{2,0},{3,1},{4,6},{5,7},{6,4},{7,5},{8,10},{9,11},{10,... | collective-permute-start | bytes 392 | tf_op jit(solution)/shard_map/ppermute | solution.py:26
  3.1 11.1 %collective-permute-start.10 = (bf16[1,16,4096]{2,1,0:T(8,128)(2,1)}, bf16[1,16,4096]{2,1,0:T(8,128)(2,1)S(1)}, u32[]{:S(2)}, u32[]{:S(2)}) collective-permute-start(bf16[1,16,4096]{2,1,0:T(8,128)(2,1)} %refs_0_.1), channel_id=1, source_target_pairs={{0,2},{1,3},{2,0},{3,1},{4,6},{5,7},{6,4},{7,5},{8,10},{9,11},{10,... | collective-permute-start | bytes 393224 | tf_op jit(solution)/shard_map/ppermute | solution.py:26
  5.1 0.7 %copy-start.4 = (s32[16,4]{0,1:T(4,128)S(1)}, s32[16,4]{0,1:T(4,128)}, u32[]{:S(2)}) copy-start(s32[16,4]{0,1:T(4,128)} %param.11) | copy-start | bytes 772
  5.1 0.7 %copy-start.3 = (s32[16,4]{0,1:T(4,128)S(1)}, s32[16,4]{0,1:T(4,128)}, u32[]{:S(2)}) copy-start(s32[16,4]{0,1:T(4,128)} %param.10) | copy-start | bytes 772
  5.1 0.7 %copy-start.5 = (s32[2,1,16]{2,1,0:T(1,128)S(1)}, s32[2,1,16]{2,1,0:T(1,128)}, u32[]{:S(2)}) copy-start(s32[2,1,16]{2,1,0:T(1,128)} %param.8) | copy-start | bytes 388
  5.8 1.6 %collective-permute-start.6 = (bf16[1,16,4096]{2,1,0:T(8,128)(2,1)}, bf16[1,16,4096]{2,1,0:T(8,128)(2,1)S(1)}, u32[]{:S(2)}, u32[]{:S(2)}) collective-permute-start(bf16[1,16,4096]{2,1,0:T(8,128)(2,1)} %refs_0_.1), channel_id=1, source_target_pairs={{0,1},{1,0},{2,3},{3,2},{4,5},{5,4},{6,7},{7,6},{8,9},{9,8},{10,11... | collective-permute-start | bytes 393224 | tf_op jit(solution)/shard_map/ppermute | solution.py:26
  5.9 8.2 %collective-permute-start.11 = (bf16[1,16,4096]{2,1,0:T(8,128)(2,1)}, bf16[1,16,4096]{2,1,0:T(8,128)(2,1)S(1)}, u32[]{:S(2)}, u32[]{:S(2)}) collective-permute-start(bf16[1,16,4096]{2,1,0:T(8,128)(2,1)} %refs_0_.1), channel_id=1, source_target_pairs={{0,3},{1,2},{2,1},{3,0},{4,7},{5,6},{6,5},{7,4},{8,11},{9,10},{10,... | collective-permute-start | bytes 393224 | tf_op jit(solution)/shard_map/ppermute | solution.py:26
  7.4 6.7 %collective-permute-start.9 = (s32[16,128]{1,0:T(8,128)S(1)}, s32[16,128]{1,0:T(8,128)S(1)}, u32[]{:S(2)}, u32[]{:S(2)}) collective-permute-start(s32[16,128]{1,0:T(8,128)S(1)} %pad_maximum_fusion.refs_0_), channel_id=1, source_target_pairs={{0,12},{4,8},{8,4},{12,0},{1,13},{5,9},{9,5},{13,1},{2,14},{6,10},... | collective-permute-start | bytes 24584 | tf_op jit(solution)/shard_map/ppermute | solution.py:26
  11.0 4.5 %collective-permute-start.8 = (s32[16,128]{1,0:T(8,128)S(1)}, s32[16,128]{1,0:T(8,128)S(1)}, u32[]{:S(2)}, u32[]{:S(2)}) collective-permute-start(s32[16,128]{1,0:T(8,128)S(1)} %pad_maximum_fusion.refs_0_), channel_id=1, source_target_pairs={{0,8},{4,12},{8,0},{12,4},{1,9},{5,13},{9,1},{13,5},{2,10},{6,14},... | collective-permute-start | bytes 24584 | tf_op jit(solution)/shard_map/ppermute | solution.py:26
  11.0 4.5 %collective-permute-start.7 = (s32[16,128]{1,0:T(8,128)S(1)}, s32[16,128]{1,0:T(8,128)S(1)}, u32[]{:S(2)}, u32[]{:S(2)}) collective-permute-start(s32[16,128]{1,0:T(8,128)S(1)} %pad_maximum_fusion.refs_0_), channel_id=1, source_target_pairs={{0,4},{4,0},{8,12},{12,8},{1,5},{5,1},{9,13},{13,9},{2,6},{6,2},{1... | collective-permute-start | bytes 24584 | tf_op jit(solution)/shard_map/ppermute | solution.py:26
  11.8 1.0 %copy-start = (bf16[16,4,4096]{2,1,0:T(4,128)(2,1)S(1)}, bf16[16,4,4096]{2,1,0:T(4,128)(2,1)}, u32[]{:S(2)}) copy-start(bf16[16,4,4096]{2,1,0:T(4,128)(2,1)} %param.9) | copy-start | bytes 1572868
  14.1 5.1 %copy-start.2 = (bf16[64,4096]{1,0:T(8,128)(2,1)}, bf16[64,4096]{1,0:T(8,128)(2,1)S(1)}, u32[]{:S(2)}) copy-start(bf16[64,4096]{1,0:T(8,128)(2,1)S(1)} %get-tuple-element.214.refs_4_) | copy-start | bytes 1572868
  15.6 9.1 %copy-start.1 = (bf16[1,16,4096]{2,1,0:T(8,128)(2,1)S(1)}, bf16[1,16,4096]{2,1,0:T(8,128)(2,1)}, u32[]{:S(2)}) copy-start(bf16[1,16,4096]{2,1,0:T(8,128)(2,1)} %refs_0_.1) | copy-start | bytes 393220
  17.0 9.5 %collective-permute-start.12 = (bf16[512,128]{1,0:T(8,128)(2,1)S(1)}, bf16[512,128]{1,0:T(8,128)(2,1)S(1)}, u32[]{:S(2)}, u32[]{:S(2)}) collective-permute-start(bf16[512,128]{1,0:T(8,128)(2,1)S(1)} %get-tuple-element.103), channel_id=1, source_target_pairs={{0,12},{4,8},{8,4},{12,0},{1,13},{5,9},{9,5},{13,1},{2,14},{6,10},... | collective-permute-start | bytes 393224 | tf_op jit(solution)/shard_map/ppermute | solution.py:26
  19.2 10.7 %collective-permute-start.13 = (bf16[512,128]{1,0:T(8,128)(2,1)S(1)}, bf16[512,128]{1,0:T(8,128)(2,1)S(1)}, u32[]{:S(2)}, u32[]{:S(2)}) collective-permute-start(bf16[512,128]{1,0:T(8,128)(2,1)S(1)} %get-tuple-element.104), channel_id=1, source_target_pairs={{0,8},{4,12},{8,0},{12,4},{1,9},{5,13},{9,1},{13,5},{2,10},{6,14},... | collective-permute-start | bytes 393224 | tf_op jit(solution)/shard_map/ppermute | solution.py:26
  19.2 10.7 %collective-permute-start.14 = (bf16[512,128]{1,0:T(8,128)(2,1)S(1)}, bf16[512,128]{1,0:T(8,128)(2,1)S(1)}, u32[]{:S(2)}, u32[]{:S(2)}) collective-permute-start(bf16[512,128]{1,0:T(8,128)(2,1)S(1)} %get-tuple-element.91), channel_id=1, source_target_pairs={{0,4},{4,0},{8,12},{12,8},{1,5},{5,1},{9,13},{13,9},{2,6},{6,2},{1... | collective-permute-start | bytes 393224 | tf_op jit(solution)/shard_map/ppermute | solution.py:26

commit v6 on v5

--- a/solution.py
+++ b/solution.py
@@ -157,11 +157,11 @@
 def pack_kernel(first, peers, cols, a_slots, row_count, *refs):
     refs = list(refs)
     base = 0 if first else refs.pop(0)[0]
-    told = refs[:peers]
-    flat = refs[peers]
-    outs = refs[peers + 1 : 2 * peers]
-    picks, packed = refs[2 * peers :]
     grid_row = lax.axis_index("row")
+    told = [refs[0].at[grid_row ^ d] for d in range(peers)]
+    flat = refs[1]
+    outs = refs[2 : 1 + peers]
+    picks, packed = refs[1 + peers :]
     per_col = peers // cols
     offered = offers(told[0], cols, row_count)
     first_slot = grid_row % per_col * a_slots if per_col > 1 else 0
@@ -187,14 +187,14 @@
 
 def pack(base, told, flat, cols, row_count, a_slots):
     first = base is None
-    peers = len(told)
+    peers = told.shape[0]
     smem_spec = pl.BlockSpec(memory_space=SMEM)
     vmem_spec = pl.BlockSpec(memory_space=VMEM)
     given = [] if first else [base]
     return pl.pallas_call(
         functools.partial(pack_kernel, first, peers, cols, a_slots, row_count),
         out_shape=[jax.ShapeDtypeStruct((CAPACITY * ROWS, LANES), BF16)] * (peers - 1),
-        in_specs=[smem_spec] * len(given) + [vmem_spec] * (peers + 1),
+        in_specs=[smem_spec] * len(given) + [vmem_spec] * 2,
         out_specs=[vmem_spec] * (peers - 1),
         scratch_shapes=[
             VMEM(((peers - 1) * CAPACITY, LANES), BF16),
@@ -203,12 +203,12 @@
         compiler_params=pltpu.CompilerParams(vmem_limit_bytes=32 << 20),
         cost_estimate=pl.CostEstimate(flops=1 << 20, bytes_accessed=4 << 20, transcendentals=0),
         name="pack",
-    )(*given, *told, flat)
+    )(*given, told, flat)
 
 
 def list_kernel(cols, a_slots, row_count, peers, *refs):
-    told, items = refs[:peers], refs[peers]
     grid_row = lax.axis_index("row")
+    told, items = [refs[0].at[grid_row ^ d] for d in range(peers)], refs[1]
     grid_col = lax.axis_index("col")
     per_col = peers // cols
     blocks = row_count * SLOTS
@@ -271,27 +271,22 @@
 
 
 def work_list(told, cols, row_count, a_slots):
-    peers = len(told)
+    peers = told.shape[0]
     return pl.pallas_call(
         functools.partial(list_kernel, cols, a_slots, row_count, peers),
         out_shape=jax.ShapeDtypeStruct((-(-peers // 8) * 8, LANES), I32),
-        in_specs=[pl.BlockSpec(memory_space=VMEM)] * peers,
+        in_specs=[pl.BlockSpec(memory_space=VMEM)],
         out_specs=pl.BlockSpec(memory_space=VMEM),
         cost_estimate=pl.CostEstimate(flops=1 << 10, bytes_accessed=1 << 10, transcendentals=0),
         name="work_list",
-    )(*told)
-
-
-def rounds_kernel(cols, a_slots, row_count, peers, *refs):
-    told_refs, rounds, told = refs[:peers], refs[peers], refs[peers + 1]
-    for d, ref in enumerate(told_refs):
-        told[d, :, :] = ref[...]
-    grid_row = lax.axis_index("row")
+    )(told)
+
+
+def rounds_kernel(cols, a_slots, row_count, peers, told, rounds):
     per_col = peers // cols
 
     def one_pair(receiver, d, most):
-        group = grid_row ^ receiver ^ d
-        sender = receiver ^ d
+        group = sender = receiver ^ d
         first_slot = group % per_col * a_slots if per_col > 1 else 0
         pairs, _, _ = matches(
             told.at[receiver],
@@ -320,16 +315,15 @@
 
 
 def count_rounds(told, cols, row_count, a_slots):
-    peers = len(told)
+    peers = told.shape[0]
     return pl.pallas_call(
         functools.partial(rounds_kernel, cols, a_slots, row_count, peers),
         out_shape=jax.ShapeDtypeStruct((1,), I32),
-        in_specs=[pl.BlockSpec(memory_space=VMEM)] * peers,
+        in_specs=[pl.BlockSpec(memory_space=VMEM)],
         out_specs=pl.BlockSpec(memory_space=SMEM),
-        scratch_shapes=[VMEM((peers,) + told[0].shape, I32)],
         cost_estimate=pl.CostEstimate(flops=1 << 10, bytes_accessed=1 << 10, transcendentals=0),
         name="count_rounds",
-    )(*told)
+    )(told)
 
 
 def add_products(items, a_ref, peer_refs, sums, window=None):
@@ -462,7 +456,8 @@
     told = describe(index_parts, b_cols.T, c_cols.T)
     a_parts = [exchanged(a_blocks, "col", h) for h in range(1, cols)]
     told, a_parts[0] = lax.optimization_barrier((told, a_parts[0]))
-    told = [told] + send_rows([told] * (rows - 1))
+    told = jnp.broadcast_to(told[None], (rows,) + told.shape)
+    told = lax.all_to_all(told, "row", 0, 0)
     flat, own, sums = flatten(seen_by_rows(b_blocks))
     flat, *a_parts = lax.optimization_barrier((flat, *a_parts))
     packed = pack(None, told, flat, cols, row_count, a_slots)

time: 33 us -> 36.8 us (1.12)
  waiting for transfers between devices: 6.36 us -> 8.24 us
  local copies, waits for them, and re-layouts: 1.76 us -> 2.38 us
  Pallas kernels: 9.8 us -> 10.4 us
  starting transfers between devices: 14.1 us -> 14.6 us
    all_to_all x0 -> x1, starting transfers between devices: none -> 4.87 us  [shards(): told = lax.all_to_all(told, 'row', 0, 0)]
    ppermute x12 -> x9, starting transfers between devices: 14.1 us -> 9.75 us  [exchanged(): return lax.ppermute(block, axis, [(i, i ^ distance) for i in range(size)])]
    all_to_all x0 -> x1, waiting for transfers between devices: none -> 3.34 us  [shards(): told = lax.all_to_all(told, 'row', 0, 0)]
    ppermute x12 -> x9, waiting for transfers between devices: 6.36 us -> 4.91 us  [exchanged(): return lax.ppermute(block, axis, [(i, i ^ distance) for i in range(size)])]
    broadcast_in_dim x0 -> x1, local copies, waits for them, and re-layouts: none -> 0.62 us  [shards(): told = jnp.broadcast_to(told[None], (rows,) + told.shape)]
    pallas_call x1, Pallas kernels: 2.19 us -> 2.77 us  [multiply(): pl.pallas_call(functools.partial(multiply_kernel, first, peers), out_shap...]
  transfers between devices with their start and end apart: 12 -> 10, of which waited for: 4 -> 4; matrix products, arithmetic and copies ran while one was open for 0% -> 2% of each run, Pallas kernels for 19% -> 17%
where the time goes in v6:
time: 36.8 us; the launch traced here: 36.4 us
  starting transfers between devices  14.6 us (40%)
  Pallas kernels  10.4 us (28%)
  waiting for transfers between devices  8.24 us (22%)
  local copies, waits for them, and re-layouts  2.38 us (6%)
  loops' own time  0.64 us (2%)
    ppermute x9, starting transfers between devices, exchanged(): return lax.ppermute(block, axis, [(i, i ^ distance) for i in range(size)])  9.75 us
    ppermute x9, waiting for transfers between devices, exchanged(): return lax.ppermute(block, axis, [(i, i ^ distance) for i in range(size)])  4.91 us
    all_to_all x1, starting transfers between devices, shards(): told = lax.all_to_all(told, 'row', 0, 0)  4.87 us
    all_to_all x1, waiting for transfers between devices, shards(): told = lax.all_to_all(told, 'row', 0, 0)  3.34 us
    pallas_call x1, Pallas kernels, multiply(): pl.pallas_call(functools.partial(multiply_kernel, first, peers), out_shap...  2.77 us
    pallas_call x1, Pallas kernels, work_list(): pl.pallas_call(functools.partial(list_kernel, cols, a_slots, row_count, p...  1.92 us
    unnamed x12, local copies, waits for them, and re-layouts  1.76 us
    pallas_call x1, Pallas kernels, stage(): pl.pallas_call(functools.partial(stage_kernel, cols), out_shape=(jax.Shap...  1.73 us
  transfers between devices with their start and end apart: 10, of which 4 were waited for; matrix products, arithmetic and copies ran while one was open for 2% of the time, Pallas kernels for 17%

profile of v6, /device:TPU:0, one launch (start us, length us, event | category | flops | bytes accessed | tf_op | source)
XLA Modules:
  0.0 36.4 jit_solution(5470718518215297608)
XLA Ops:
  0.0 0.5 %collective-permute-start.3 = (s32[2,1,16]{2,1,0:T(1,128)}, s32[2,1,16]{2,1,0:T(1,128)S(1)}, u32[]{:S(2)}, u32[]{:S(2)}) collective-permute-start(s32[2,1,16]{2,1,0:T(1,128)} %param.8), channel_id=1, source_target_pairs={{0,1},{1,0},{2,3},{3,2},{4,5},{5,4},{6,7},{7,6},{8,9},{9,8},{10,11... | collective-permute-start | bytes 392 | tf_op jit(solution)/shard_map/ppermute | solution.py:26
  0.5 2.6 %collective-permute-start.5 = (s32[2,1,16]{2,1,0:T(1,128)}, s32[2,1,16]{2,1,0:T(1,128)S(1)}, u32[]{:S(2)}, u32[]{:S(2)}) collective-permute-start(s32[2,1,16]{2,1,0:T(1,128)} %param.8), channel_id=1, source_target_pairs={{0,3},{1,2},{2,1},{3,0},{4,7},{5,6},{6,5},{7,4},{8,11},{9,10},{10,... | collective-permute-start | bytes 392 | tf_op jit(solution)/shard_map/ppermute | solution.py:26
  3.1 0.0 collective-permute-start.4
  3.1 2.0 %collective-permute-start.7 = (bf16[1,16,4096]{2,1,0:T(8,128)(2,1)}, bf16[1,16,4096]{2,1,0:T(8,128)(2,1)S(1)}, u32[]{:S(2)}, u32[]{:S(2)}) collective-permute-start(bf16[1,16,4096]{2,1,0:T(8,128)(2,1)} %refs_0_.1), channel_id=1, source_target_pairs={{0,2},{1,3},{2,0},{3,1},{4,6},{5,7},{6,4},{7,5},{8,10},{9,11},{10,... | collective-permute-start | bytes 393224 | tf_op jit(solution)/shard_map/ppermute | solution.py:26
  5.1 0.7 %copy-done.4 = s32[16,4]{0,1:T(4,128)S(1)} copy-done((s32[16,4]{0,1:T(4,128)S(1)}, s32[16,4]{0,1:T(4,128)}, u32[]{:S(2)}) %copy-start.4) | copy-done | bytes 280
  5.8 0.0 copy-done.3
  5.8 0.0 copy-done.5
  5.8 0.1 collective-permute-start.6
  5.9 0.0 collective-permute-done.3
  5.9 0.1 collective-permute-start.8
  6.0 0.0 collective-permute-done.5
  6.0 0.8 %collective-permute-done.4 = s32[2,1,16]{2,1,0:T(1,128)S(1)} collective-permute-done((s32[2,1,16]{2,1,0:T(1,128)}, s32[2,1,16]{2,1,0:T(1,128)S(1)}, u32[]{:S(2)}, u32[]{:S(2)}) %collective-permute-start.4) | collective-permute-done | bytes 160 | tf_op jit(solution)/shard_map/ppermute | solution.py:26
  6.9 0.6 %collective-permute-done.6.refs_1_ = bf16[1,16,4096]{2,1,0:T(8,128)(2,1)S(1)} collective-permute-done((bf16[1,16,4096]{2,1,0:T(8,128)(2,1)}, bf16[1,16,4096]{2,1,0:T(8,128)(2,1)S(1)}, u32[]{:S(2)}, u32[]{:S(2)}) %collective-permute-start.6) | collective-permute-done | bytes 131104 | tf_op jit(solution)/shard_map/ppermute | solution.py:26
  7.4 0.6 %broadcast_in_dim.2 = s32[4,16,128]{2,1,0:T(8,128)} broadcast(s32[16,128]{1,0:T(8,128)S(1)} %pad_maximum_fusion), dimensions={1,2} | broadcast | bytes 40960 | tf_op jit(solution)/shard_map/broadcast_in_dim | solution.py:459
  8.0 4.9 %all-to-all-start = ((s32[4,16,128]{2,1,0:T(8,128)}), s32[4,16,128]{2,1,0:T(8,128)S(1)}, u32[]{:S(2)}, u32[]{:S(2)}) async-start(s32[4,16,128]{2,1,0:T(8,128)} %broadcast_in_dim.2), calls=%async_computation | async-start | bytes 65536 | tf_op jit(solution)/shard_map/all_to_all | solution.py:460
  12.9 1.0 %copy-done = bf16[16,4,4096]{2,1,0:T(4,128)(2,1)S(1)} copy-done((bf16[16,4,4096]{2,1,0:T(4,128)(2,1)S(1)}, bf16[16,4,4096]{2,1,0:T(4,128)(2,1)}, u32[]{:S(2)}) %copy-start) | copy-done | bytes 524312
  14.0 1.2 %flatten.1 = (bf16[64,4096]{1,0:T(8,128)(2,1)S(1)}, bf16[2048,128]{1,0:T(8,128)(2,1)S(1)}, f32[16,128,128]{2,1,0:T(8,128)S(1)}) custom-call(bf16[16,128,128]{2,1,0:T(8,128)(2,1)S(1)} %bitcast.21), custom_call_target="tpu_custom_call" | custom-call | flops 1048576 | bytes 8388608 | tf_op jit(solution)/shard_map/flatten/pallas_call | solution.py:86
  15.2 0.0 collective-permute-done.8.refs_3_
  15.2 3.3 %all-to-all-done.refs_0_.told = s32[4,16,128]{2,1,0:T(8,128)S(1)} async-done(((s32[4,16,128]{2,1,0:T(8,128)}), s32[4,16,128]{2,1,0:T(8,128)S(1)}, u32[]{:S(2)}, u32[]{:S(2)}) %all-to-all-start) | async-done | bytes 32800 | tf_op jit(solution)/shard_map/all_to_all | solution.py:460
  18.6 1.4 %pack.2 = (bf16[512,128]{1,0:T(8,128)(2,1)S(1)}, bf16[512,128]{1,0:T(8,128)(2,1)S(1)}, bf16[512,128]{1,0:T(8,128)(2,1)S(1)}) custom-call(s32[4,16,128]{2,1,0:T(8,128)S(1)} %all-to-all-done.refs_0_.told, bf16[64,4096]{1,0:T(8,128)(2,1)S(1)} %get-tuple-element.166.refs_1_), custom_call_target="tpu_custom_call" | custom-call | flops 1048576 | bytes 4194304 | tf_op jit(solution)/shard_map/pack/pallas_call | solution.py:194
  20.0 0.7 %collective-permute-start.9 = (bf16[512,128]{1,0:T(8,128)(2,1)S(1)}, bf16[512,128]{1,0:T(8,128)(2,1)S(1)}, u32[]{:S(2)}, u32[]{:S(2)}) collective-permute-start(bf16[512,128]{1,0:T(8,128)(2,1)S(1)} %get-tuple-element.82), channel_id=1, source_target_pairs={{0,12},{4,8},{8,4},{12,0},{1,13},{5,9},{9,5},{13,1},{2,14},{6,10},... | collective-permute-start | bytes 393224 | tf_op jit(solution)/shard_map/ppermute | solution.py:26
  20.7 1.6 %collective-permute-start.10 = (bf16[512,128]{1,0:T(8,128)(2,1)S(1)}, bf16[512,128]{1,0:T(8,128)(2,1)S(1)}, u32[]{:S(2)}, u32[]{:S(2)}) collective-permute-start(bf16[512,128]{1,0:T(8,128)(2,1)S(1)} %get-tuple-element.83), channel_id=1, source_target_pairs={{0,8},{4,12},{8,0},{12,4},{1,9},{5,13},{9,1},{13,5},{2,10},{6,14},... | collective-permute-start | bytes 393224 | tf_op jit(solution)/shard_map/ppermute | solution.py:26
  22.2 2.2 %collective-permute-start.11 = (bf16[512,128]{1,0:T(8,128)(2,1)S(1)}, bf16[512,128]{1,0:T(8,128)(2,1)S(1)}, u32[]{:S(2)}, u32[]{:S(2)}) collective-permute-start(bf16[512,128]{1,0:T(8,128)(2,1)S(1)} %get-tuple-element.73), channel_id=1, source_target_pairs={{0,4},{4,0},{8,12},{12,8},{1,5},{5,1},{9,13},{13,9},{2,6},{6,2},{1... | collective-permute-start | bytes 393224 | tf_op jit(solution)/shard_map/ppermute | solution.py:26
  24.4 1.3 %count_rounds.1 = s32[1]{0:T(128)} custom-call(s32[4,16,128]{2,1,0:T(8,128)S(1)} %all-to-all-done.refs_0_.told), custom_call_target="tpu_custom_call" | custom-call | flops 1024 | bytes 1024 | tf_op jit(solution)/shard_map/count_rounds/pallas_call | solution.py:319
  25.8 1.9 %work_list.1.refs_5_.refs_0_ = s32[8,128]{1,0:T(8,128)S(1)} custom-call(s32[4,16,128]{2,1,0:T(8,128)S(1)} %all-to-all-done.refs_0_.told), custom_call_target="tpu_custom_call" | custom-call | flops 1024 | bytes 1024 | tf_op jit(solution)/shard_map/work_list/pallas_call | solution.py:275
  27.7 0.0 copy-done.1
  27.7 1.7 %stage.1 = (bf16[2048,128]{1,0:T(8,128)(2,1)S(1)}, f32[16,128,128]{2,1,0:T(8,128)S(1)}) custom-call(bf16[1,16,4096]{2,1,0:T(8,128)(2,1)S(1)} %copy-done.1, bf16[1,16,4096]{2,1,0:T(8,128)(2,1)S(1)} %collective-permute-done.6.refs_1_, bf16[1,16,4096]{2,1,0:T(8,128)(2,1)S(1)} %collective-permute-done.7.refs_2_, ...), custom_call_target="tpu_custom_call", output_to_operand_aliasing={{1}: (6, {})} | custom-call | flops 1024 | bytes 1024 | tf_op jit(solution)/shard_map/stage/pallas_call | solution.py:398
  29.4 0.0 collective-permute-done.9.refs_3_
  29.4 3.5 %collective-permute-done.10.refs_4_ = bf16[512,128]{1,0:T(8,128)(2,1)S(1)} collective-permute-done((bf16[512,128]{1,0:T(8,128)(2,1)S(1)}, bf16[512,128]{1,0:T(8,128)(2,1)S(1)}, u32[]{:S(2)}, u32[]{:S(2)}) %collective-permute-start.10) | collective-permute-done | bytes 131104 | tf_op jit(solution)/shard_map/ppermute | solution.py:26
  33.0 0.0 collective-permute-done.11.refs_5_
  33.0 2.8 %multiply.2 = (f32[16,128,128]{2,1,0:T(8,128)S(1)}, f32[16,128,128]{2,1,0:T(8,128)}) custom-call(s32[8,128]{1,0:T(8,128)S(1)} %work_list.1.refs_5_.refs_0_, bf16[2048,128]{1,0:T(8,128)(2,1)S(1)} %get-tuple-element.168.refs_1_, f32[16,128,128]{2,1,0:T(8,128)S(1)} %get-tuple-element.81.refs_2_, ...), custom_call_target="tpu_custom_call", output_to_operand_aliasing={{0}: (2, {})} | custom-call | flops 67108864 | bytes 4194304 | tf_op jit(solution)/shard_map/multiply/pallas_call | solution.py:432
  35.7 0.6 %while.12 = (s32[]{:T(128)}, f32[16,128,128]{2,1,0:T(8,128)S(1)}, f32[16,128,128]{2,1,0:T(8,128)}, s32[1]{0:T(128)}, s32[4,16,128]{2,1,0:T(8,128)S(1)}, /*index=...) while((s32[]{:T(128)}, f32[16,128,128]{2,1,0:T(8,128)S(1)}, ...), condition=%wide.region_1.2_spmd, body=%wide.region_0.1_spmd.sunk | while | flops 68157440 | bytes 9961705 | solution.py:480
  (10 shorter events, 0.0 us)
Async XLA Ops:
  0.0 5.9 %collective-permute-start.3 = (s32[2,1,16]{2,1,0:T(1,128)}, s32[2,1,16]{2,1,0:T(1,128)S(1)}, u32[]{:S(2)}, u32[]{:S(2)}) collective-permute-start(s32[2,1,16]{2,1,0:T(1,128)} %param.8), channel_id=1, source_target_pairs={{0,1},{1,0},{2,3},{3,2},{4,5},{5,4},{6,7},{7,6},{8,9},{9,8},{10,11... | collective-permute-start | bytes 392 | tf_op jit(solution)/shard_map/ppermute | solution.py:26
  0.5 5.6 %collective-permute-start.5 = (s32[2,1,16]{2,1,0:T(1,128)}, s32[2,1,16]{2,1,0:T(1,128)S(1)}, u32[]{:S(2)}, u32[]{:S(2)}) collective-permute-start(s32[2,1,16]{2,1,0:T(1,128)} %param.8), channel_id=1, source_target_pairs={{0,3},{1,2},{2,1},{3,0},{4,7},{5,6},{6,5},{7,4},{8,11},{9,10},{10,... | collective-permute-start | bytes 392 | tf_op jit(solution)/shard_map/ppermute | solution.py:26
  3.1 3.8 %collective-permute-start.4 = (s32[2,1,16]{2,1,0:T(1,128)}, s32[2,1,16]{2,1,0:T(1,128)S(1)}, u32[]{:S(2)}, u32[]{:S(2)}) collective-permute-start(s32[2,1,16]{2,1,0:T(1,128)} %param.8), channel_id=1, source_target_pairs={{0,2},{1,3},{2,0},{3,1},{4,6},{5,7},{6,4},{7,5},{8,10},{9,11},{10,... | collective-permute-start | bytes 392 | tf_op jit(solution)/shard_map/ppermute | solution.py:26
  3.1 12.2 %collective-permute-start.7 = (bf16[1,16,4096]{2,1,0:T(8,128)(2,1)}, bf16[1,16,4096]{2,1,0:T(8,128)(2,1)S(1)}, u32[]{:S(2)}, u32[]{:S(2)}) collective-permute-start(bf16[1,16,4096]{2,1,0:T(8,128)(2,1)} %refs_0_.1), channel_id=1, source_target_pairs={{0,2},{1,3},{2,0},{3,1},{4,6},{5,7},{6,4},{7,5},{8,10},{9,11},{10,... | collective-permute-start | bytes 393224 | tf_op jit(solution)/shard_map/ppermute | solution.py:26
  5.1 0.7 %copy-start.4 = (s32[16,4]{0,1:T(4,128)S(1)}, s32[16,4]{0,1:T(4,128)}, u32[]{:S(2)}) copy-start(s32[16,4]{0,1:T(4,128)} %param.11) | copy-start | bytes 772
  5.1 0.7 %copy-start.3 = (s32[16,4]{0,1:T(4,128)S(1)}, s32[16,4]{0,1:T(4,128)}, u32[]{:S(2)}) copy-start(s32[16,4]{0,1:T(4,128)} %param.10) | copy-start | bytes 772
  5.1 0.7 %copy-start.5 = (s32[2,1,16]{2,1,0:T(1,128)S(1)}, s32[2,1,16]{2,1,0:T(1,128)}, u32[]{:S(2)}) copy-start(s32[2,1,16]{2,1,0:T(1,128)} %param.8) | copy-start | bytes 388
  5.8 1.6 %collective-permute-start.6 = (bf16[1,16,4096]{2,1,0:T(8,128)(2,1)}, bf16[1,16,4096]{2,1,0:T(8,128)(2,1)S(1)}, u32[]{:S(2)}, u32[]{:S(2)}) collective-permute-start(bf16[1,16,4096]{2,1,0:T(8,128)(2,1)} %refs_0_.1), channel_id=1, source_target_pairs={{0,1},{1,0},{2,3},{3,2},{4,5},{5,4},{6,7},{7,6},{8,9},{9,8},{10,11... | collective-permute-start | bytes 393224 | tf_op jit(solution)/shard_map/ppermute | solution.py:26
  5.9 9.3 %collective-permute-start.8 = (bf16[1,16,4096]{2,1,0:T(8,128)(2,1)}, bf16[1,16,4096]{2,1,0:T(8,128)(2,1)S(1)}, u32[]{:S(2)}, u32[]{:S(2)}) collective-permute-start(bf16[1,16,4096]{2,1,0:T(8,128)(2,1)} %refs_0_.1), channel_id=1, source_target_pairs={{0,3},{1,2},{2,1},{3,0},{4,7},{5,6},{6,5},{7,4},{8,11},{9,10},{10,... | collective-permute-start | bytes 393224 | tf_op jit(solution)/shard_map/ppermute | solution.py:26
  8.0 10.5 %all-to-all-start = ((s32[4,16,128]{2,1,0:T(8,128)}), s32[4,16,128]{2,1,0:T(8,128)S(1)}, u32[]{:S(2)}, u32[]{:S(2)}) async-start(s32[4,16,128]{2,1,0:T(8,128)} %broadcast_in_dim.2), calls=%async_computation | async-start | bytes 65536 | tf_op jit(solution)/shard_map/all_to_all | solution.py:460
  12.9 1.0 %copy-start = (bf16[16,4,4096]{2,1,0:T(4,128)(2,1)S(1)}, bf16[16,4,4096]{2,1,0:T(4,128)(2,1)}, u32[]{:S(2)}) copy-start(bf16[16,4,4096]{2,1,0:T(4,128)(2,1)} %param.9) | copy-start | bytes 1572868
  15.2 12.5 %copy-start.2 = (bf16[64,4096]{1,0:T(8,128)(2,1)}, bf16[64,4096]{1,0:T(8,128)(2,1)S(1)}, u32[]{:S(2)}) copy-start(bf16[64,4096]{1,0:T(8,128)(2,1)S(1)} %get-tuple-element.166.refs_1_) | copy-start | bytes 1572868
  18.6 9.1 %copy-start.1 = (bf16[1,16,4096]{2,1,0:T(8,128)(2,1)S(1)}, bf16[1,16,4096]{2,1,0:T(8,128)(2,1)}, u32[]{:S(2)}) copy-start(bf16[1,16,4096]{2,1,0:T(8,128)(2,1)} %refs_0_.1) | copy-start | bytes 393220
  20.0 9.5 %collective-permute-start.9 = (bf16[512,128]{1,0:T(8,128)(2,1)S(1)}, bf16[512,128]{1,0:T(8,128)(2,1)S(1)}, u32[]{:S(2)}, u32[]{:S(2)}) collective-permute-start(bf16[512,128]{1,0:T(8,128)(2,1)S(1)} %get-tuple-element.82), channel_id=1, source_target_pairs={{0,12},{4,8},{8,4},{12,0},{1,13},{5,9},{9,5},{13,1},{2,14},{6,10},... | collective-permute-start | bytes 393224 | tf_op jit(solution)/shard_map/ppermute | solution.py:26
  20.7 12.3 %collective-permute-start.10 = (bf16[512,128]{1,0:T(8,128)(2,1)S(1)}, bf16[512,128]{1,0:T(8,128)(2,1)S(1)}, u32[]{:S(2)}, u32[]{:S(2)}) collective-permute-start(bf16[512,128]{1,0:T(8,128)(2,1)S(1)} %get-tuple-element.83), channel_id=1, source_target_pairs={{0,8},{4,12},{8,0},{12,4},{1,9},{5,13},{9,1},{13,5},{2,10},{6,14},... | collective-permute-start | bytes 393224 | tf_op jit(solution)/shard_map/ppermute | solution.py:26
  22.2 10.7 %collective-permute-start.11 = (bf16[512,128]{1,0:T(8,128)(2,1)S(1)}, bf16[512,128]{1,0:T(8,128)(2,1)S(1)}, u32[]{:S(2)}, u32[]{:S(2)}) collective-permute-start(bf16[512,128]{1,0:T(8,128)(2,1)S(1)} %get-tuple-element.73), channel_id=1, source_target_pairs={{0,4},{4,0},{8,12},{12,8},{1,5},{5,1},{9,13},{13,9},{2,6},{6,2},{1... | collective-permute-start | bytes 393224 | tf_op jit(solution)/shard_map/ppermute | solution.py:26

commit v7 on v5

--- a/solution.py
+++ b/solution.py
@@ -460,21 +460,24 @@
 
     index_parts = [a_index] + [exchanged(a_index, "col", h) for h in range(1, cols)]
     told = describe(index_parts, b_cols.T, c_cols.T)
-    a_parts = [exchanged(a_blocks, "col", h) for h in range(1, cols)]
-    told, a_parts[0] = lax.optimization_barrier((told, a_parts[0]))
+    a_far = [exchanged(a_blocks, "col", h) for h in range(2, cols, 2)]
     told = [told] + send_rows([told] * (rows - 1))
     flat, own, sums = flatten(seen_by_rows(b_blocks))
-    flat, *a_parts = lax.optimization_barrier((flat, *a_parts))
+    flat, *a_far = lax.optimization_barrier((flat, *a_far))
     packed = pack(None, told, flat, cols, row_count, a_slots)
     arrived = send_rows(packed)
-    told_late = lax.optimization_barrier((told, packed[0]))[0]
+    told_late, a_late, *a_far = lax.optimization_barrier((told, a_blocks, *a_far, packed[0]))[:-1]
     items = work_list(told_late, cols, row_count, a_slots)
-    rounds = count_rounds(told_late, cols, row_count, a_slots)
-    a_ready, sums = stage([a_blocks] + a_parts, own, sums, items)
+    rounds = jnp.minimum(count_rounds(told_late, cols, row_count, a_slots)[0], LANES)
+    a_parts = [a_blocks, exchanged(a_late, "col", 1)]
+    for far in a_far:
+        a_parts += [far, exchanged(far, "col", 1)]
+    a_ready, sums = stage(a_parts, own, sums, items)
+    sums, rounds = lax.optimization_barrier((sums, rounds))
     sums, out = multiply(None, items, a_ready, sums, arrived)
 
     def more(state):
-        return state[0] < rounds[0]
+        return state[0] < rounds
 
     def one_round(state):
         at, sums, _ = state

time: 33 us -> 34.1 us (1.033)
  between operations: 0.1 us -> 0.8 us
  Pallas kernels: 9.8 us -> 10.5 us
  loops' own time: 0.68 us -> 0.01 us
  starting transfers between devices: 14.1 us -> 14.5 us
    another operation x1, loops' own time: 0.68 us -> 0.01 us  [shards(): lax.while_loop(more, one_round, (jnp.int32(1), sums, out))[2]]
    pallas_call x1, Pallas kernels: 1.74 us -> 2.17 us  [stage(): pl.pallas_call(functools.partial(stage_kernel, cols), out_shape=(jax.Shap...]
    ppermute x12, starting transfers between devices: 14.1 us -> 14.5 us  [exchanged(): return lax.ppermute(block, axis, [(i, i ^ distance) for i in range(size)])]
  transfers between devices with their start and end apart: 12 -> 12, of which waited for: 4 -> 3; matrix products, arithmetic and copies ran while one was open for 0% -> 0% of each run, Pallas kernels for 19% -> 20%
where the time goes in v7:
time: 34.1 us; the launch traced here: 33.7 us
  starting transfers between devices  14.5 us (43%)
  Pallas kernels  10.5 us (31%)
  waiting for transfers between devices  6.13 us (18%)
  local copies, waits for them, and re-layouts  1.76 us (5%)
  between operations  0.8 us (2%)
    ppermute x12, starting transfers between devices, exchanged(): return lax.ppermute(block, axis, [(i, i ^ distance) for i in range(size)])  14.5 us
    ppermute x12, waiting for transfers between devices, exchanged(): return lax.ppermute(block, axis, [(i, i ^ distance) for i in range(size)])  6.13 us
    pallas_call x1, Pallas kernels, multiply(): pl.pallas_call(functools.partial(multiply_kernel, first, peers), out_shap...  2.48 us
    pallas_call x1, Pallas kernels, stage(): pl.pallas_call(functools.partial(stage_kernel, cols), out_shape=(jax.Shap...  2.17 us
    pallas_call x1, Pallas kernels, work_list(): pl.pallas_call(functools.partial(list_kernel, cols, a_slots, row_count, p...  1.91 us
    unnamed x12, local copies, waits for them, and re-layouts  1.76 us
    pallas_call x1, Pallas kernels, pack(): pl.pallas_call(functools.partial(pack_kernel, first, peers, cols, a_slots...  1.38 us
    pallas_call x1, Pallas kernels, count_rounds(): pl.pallas_call(functools.partial(rounds_kernel, cols, a_slots, row_count,...  1.35 us
  transfers between devices with their start and end apart: 12, of which 3 were waited for; matrix products, arithmetic and copies ran while one was open for 0% of the time, Pallas kernels for 20%

profile of v7, /device:TPU:0, one launch (start us, length us, event | category | flops | bytes accessed | tf_op | source)
XLA Modules:
  0.0 33.7 jit_solution(14655624207868756572)
XLA Ops:
  0.0 0.5 %collective-permute-start.3 = (s32[2,1,16]{2,1,0:T(1,128)}, s32[2,1,16]{2,1,0:T(1,128)S(1)}, u32[]{:S(2)}, u32[]{:S(2)}) collective-permute-start(s32[2,1,16]{2,1,0:T(1,128)} %param.8), channel_id=1, source_target_pairs={{0,1},{1,0},{2,3},{3,2},{4,5},{5,4},{6,7},{7,6},{8,9},{9,8},{10,11... | collective-permute-start | bytes 392 | tf_op jit(solution)/shard_map/ppermute | solution.py:26
  0.5 2.6 %collective-permute-start.5 = (s32[2,1,16]{2,1,0:T(1,128)}, s32[2,1,16]{2,1,0:T(1,128)S(1)}, u32[]{:S(2)}, u32[]{:S(2)}) collective-permute-start(s32[2,1,16]{2,1,0:T(1,128)} %param.8), channel_id=1, source_target_pairs={{0,3},{1,2},{2,1},{3,0},{4,7},{5,6},{6,5},{7,4},{8,11},{9,10},{10,... | collective-permute-start | bytes 392 | tf_op jit(solution)/shard_map/ppermute | solution.py:26
  3.1 0.0 collective-permute-start.4
  3.1 2.0 %collective-permute-start.9 = (bf16[1,16,4096]{2,1,0:T(8,128)(2,1)}, bf16[1,16,4096]{2,1,0:T(8,128)(2,1)S(1)}, u32[]{:S(2)}, u32[]{:S(2)}) collective-permute-start(bf16[1,16,4096]{2,1,0:T(8,128)(2,1)} %refs_0_.1), channel_id=1, source_target_pairs={{0,2},{1,3},{2,0},{3,1},{4,6},{5,7},{6,4},{7,5},{8,10},{9,11},{10,... | collective-permute-start | bytes 393224 | tf_op jit(solution)/shard_map/ppermute | solution.py:26
  5.1 0.7 %copy-done.4 = s32[16,4]{0,1:T(4,128)S(1)} copy-done((s32[16,4]{0,1:T(4,128)S(1)}, s32[16,4]{0,1:T(4,128)}, u32[]{:S(2)}) %copy-start.4) | copy-done | bytes 280
  5.8 0.0 copy-done.3
  5.8 0.0 copy-done.5
  5.8 0.0 collective-permute-done.3
  5.8 0.0 collective-permute-done.5
  5.8 1.0 %collective-permute-done.4 = s32[2,1,16]{2,1,0:T(1,128)S(1)} collective-permute-done((s32[2,1,16]{2,1,0:T(1,128)}, s32[2,1,16]{2,1,0:T(1,128)S(1)}, u32[]{:S(2)}, u32[]{:S(2)}) %collective-permute-start.4) | collective-permute-done | bytes 160 | tf_op jit(solution)/shard_map/ppermute | solution.py:26
  6.9 3.7 %collective-permute-start.8 = (s32[16,128]{1,0:T(8,128)S(1)}, s32[16,128]{1,0:T(8,128)S(1)}, u32[]{:S(2)}, u32[]{:S(2)}) collective-permute-start(s32[16,128]{1,0:T(8,128)S(1)} %pad_maximum_fusion.refs_0_), channel_id=1, source_target_pairs={{0,12},{4,8},{8,4},{12,0},{1,13},{5,9},{9,5},{13,1},{2,14},{6,10},... | collective-permute-start | bytes 24584 | tf_op jit(solution)/shard_map/ppermute | solution.py:26
  10.5 0.0 collective-permute-start.7
  10.5 0.8 %collective-permute-start.6 = (s32[16,128]{1,0:T(8,128)S(1)}, s32[16,128]{1,0:T(8,128)S(1)}, u32[]{:S(2)}, u32[]{:S(2)}) collective-permute-start(s32[16,128]{1,0:T(8,128)S(1)} %pad_maximum_fusion.refs_0_), channel_id=1, source_target_pairs={{0,4},{4,0},{8,12},{12,8},{1,5},{5,1},{9,13},{13,9},{2,6},{6,2},{1... | collective-permute-start | bytes 24584 | tf_op jit(solution)/shard_map/ppermute | solution.py:26
  11.3 1.0 %copy-done = bf16[16,4,4096]{2,1,0:T(4,128)(2,1)S(1)} copy-done((bf16[16,4,4096]{2,1,0:T(4,128)(2,1)S(1)}, bf16[16,4,4096]{2,1,0:T(4,128)(2,1)}, u32[]{:S(2)}) %copy-start) | copy-done | bytes 524312
  12.3 1.2 %flatten.1 = (bf16[64,4096]{1,0:T(8,128)(2,1)S(1)}, bf16[2048,128]{1,0:T(8,128)(2,1)S(1)}, f32[16,128,128]{2,1,0:T(8,128)S(1)}) custom-call(bf16[16,128,128]{2,1,0:T(8,128)(2,1)S(1)} %bitcast.20), custom_call_target="tpu_custom_call" | custom-call | flops 1048576 | bytes 8388608 | tf_op jit(solution)/shard_map/flatten/pallas_call | solution.py:86
  13.6 0.0 collective-permute-done.9.refs_2_
  13.6 0.0 copy-start.1
  13.6 0.0 collective-permute-done.8.refs_3_
  13.6 1.4 %collective-permute-done.7.refs_2_ = s32[16,128]{1,0:T(8,128)S(1)} collective-permute-done((s32[16,128]{1,0:T(8,128)S(1)}, s32[16,128]{1,0:T(8,128)S(1)}, u32[]{:S(2)}, u32[]{:S(2)}) %collective-permute-start.7) | collective-permute-done | bytes 8224 | tf_op jit(solution)/shard_map/ppermute | solution.py:26
  15.1 0.0 collective-permute-done.6.refs_1_
  15.1 1.4 %pack.2 = (bf16[512,128]{1,0:T(8,128)(2,1)S(1)}, bf16[512,128]{1,0:T(8,128)(2,1)S(1)}, bf16[512,128]{1,0:T(8,128)(2,1)S(1)}) custom-call(s32[16,128]{1,0:T(8,128)S(1)} %pad_maximum_fusion.refs_0_, s32[16,128]{1,0:T(8,128)S(1)} %collective-permute-done.6.refs_1_, s32[16,128]{1,0:T(8,128)S(1)} %collective-permute-done.7.refs_2_, ...), custom_call_target="tpu_custom_call" | custom-call | flops 1048576 | bytes 4194304 | tf_op jit(solution)/shard_map/pack/pallas_call | solution.py:194
  16.5 0.1 collective-permute-start.10
  16.5 0.5 %collective-permute-start.11 = (bf16[1,16,4096]{2,1,0:T(8,128)(2,1)S(1)}, bf16[1,16,4096]{2,1,0:T(8,128)(2,1)S(1)}, u32[]{:S(2)}, u32[]{:S(2)}) collective-permute-start(bf16[1,16,4096]{2,1,0:T(8,128)(2,1)S(1)} %collective-permute-done.9.refs_2_), channel_id=1, source_target_pairs={{0,1},{1,0},{2,3},{3,2},{4,5},{5,4},{6,7},{7,6},{8,9},{9,8},{10,11... | collective-permute-start | bytes 393224 | tf_op jit(solution)/shard_map/ppermute | solution.py:26
  17.0 2.2 %collective-permute-start.12 = (bf16[512,128]{1,0:T(8,128)(2,1)S(1)}, bf16[512,128]{1,0:T(8,128)(2,1)S(1)}, u32[]{:S(2)}, u32[]{:S(2)}) collective-permute-start(bf16[512,128]{1,0:T(8,128)(2,1)S(1)} %get-tuple-element.102), channel_id=1, source_target_pairs={{0,12},{4,8},{8,4},{12,0},{1,13},{5,9},{9,5},{13,1},{2,14},{6,10},... | collective-permute-start | bytes 393224 | tf_op jit(solution)/shard_map/ppermute | solution.py:26
  19.2 2.2 %collective-permute-start.14 = (bf16[512,128]{1,0:T(8,128)(2,1)S(1)}, bf16[512,128]{1,0:T(8,128)(2,1)S(1)}, u32[]{:S(2)}, u32[]{:S(2)}) collective-permute-start(bf16[512,128]{1,0:T(8,128)(2,1)S(1)} %get-tuple-element.90), channel_id=1, source_target_pairs={{0,4},{4,0},{8,12},{12,8},{1,5},{5,1},{9,13},{13,9},{2,6},{6,2},{1... | collective-permute-start | bytes 393224 | tf_op jit(solution)/shard_map/ppermute | solution.py:26
  21.4 1.4 %count_rounds.1 = s32[1]{0:T(128)} custom-call(s32[16,128]{1,0:T(8,128)S(1)} %pad_maximum_fusion.refs_0_, s32[16,128]{1,0:T(8,128)S(1)} %collective-permute-done.6.refs_1_, s32[16,128]{1,0:T(8,128)S(1)} %collective-permute-done.7.refs_2_, s32[16,128]{1,0:T(8,128)S(1)} %collective-permute-done.8.refs_3_), custom_call_target="tpu_custom_call" | custom-call | flops 1024 | bytes 1024 | tf_op jit(solution)/shard_map/count_rounds/pallas_call | solution.py:324
  22.8 1.9 %work_list.1.refs_5_.refs_0_ = s32[8,128]{1,0:T(8,128)S(1)} custom-call(s32[16,128]{1,0:T(8,128)S(1)} %pad_maximum_fusion.refs_0_, s32[16,128]{1,0:T(8,128)S(1)} %collective-permute-done.6.refs_1_, s32[16,128]{1,0:T(8,128)S(1)} %collective-permute-done.7.refs_2_, s32[16,128]{1,0:T(8,128)S(1)} %collective-permute-done.8.refs_3_), custom_call_target="tpu_custom_call" | custom-call | flops 1024 | bytes 1024 | tf_op jit(solution)/shard_map/work_list/pallas_call | solution.py:275
  25.4 0.0 collective-permute-done.10.refs_1_
  25.4 2.2 %stage.1 = (bf16[2048,128]{1,0:T(8,128)(2,1)S(1)}, f32[16,128,128]{2,1,0:T(8,128)S(1)}) custom-call(bf16[1,16,4096]{2,1,0:T(8,128)(2,1)S(1)} %copy-done.1, bf16[1,16,4096]{2,1,0:T(8,128)(2,1)S(1)} %collective-permute-done.10.refs_1_, bf16[1,16,4096]{2,1,0:T(8,128)(2,1)S(1)} %collective-permute-done.9.refs_2_, ...), custom_call_target="tpu_custom_call", output_to_operand_aliasing={{1}: (6, {})} | custom-call | flops 1024 | bytes 1024 | tf_op jit(solution)/shard_map/stage/pallas_call | solution.py:404
  27.6 3.7 %collective-permute-done.13.refs_4_ = bf16[512,128]{1,0:T(8,128)(2,1)S(1)} collective-permute-done((bf16[512,128]{1,0:T(8,128)(2,1)S(1)}, bf16[512,128]{1,0:T(8,128)(2,1)S(1)}, u32[]{:S(2)}, u32[]{:S(2)}) %collective-permute-start.13) | collective-permute-done | bytes 131104 | tf_op jit(solution)/shard_map/ppermute | solution.py:26
  31.2 0.0 collective-permute-done.14.refs_5_
  31.2 2.5 %multiply.2 = (f32[16,128,128]{2,1,0:T(8,128)S(1)}, f32[16,128,128]{2,1,0:T(8,128)}) custom-call(s32[8,128]{1,0:T(8,128)S(1)} %work_list.1.refs_5_.refs_0_, bf16[2048,128]{1,0:T(8,128)(2,1)S(1)} %get-tuple-element.216.refs_1_, f32[16,128,128]{2,1,0:T(8,128)S(1)} %get-tuple-element.101.refs_2_, ...), custom_call_target="tpu_custom_call", output_to_operand_aliasing={{0}: (2, {})} | custom-call | flops 67108864 | bytes 4194304 | tf_op jit(solution)/shard_map/multiply/pallas_call | solution.py:438
  (13 shorter events, 0.1 us)
Async XLA Ops:
  0.0 5.8 %collective-permute-start.3 = (s32[2,1,16]{2,1,0:T(1,128)}, s32[2,1,16]{2,1,0:T(1,128)S(1)}, u32[]{:S(2)}, u32[]{:S(2)}) collective-permute-start(s32[2,1,16]{2,1,0:T(1,128)} %param.8), channel_id=1, source_target_pairs={{0,1},{1,0},{2,3},{3,2},{4,5},{5,4},{6,7},{7,6},{8,9},{9,8},{10,11... | collective-permute-start | bytes 392 | tf_op jit(solution)/shard_map/ppermute | solution.py:26
  0.5 5.4 %collective-permute-start.5 = (s32[2,1,16]{2,1,0:T(1,128)}, s32[2,1,16]{2,1,0:T(1,128)S(1)}, u32[]{:S(2)}, u32[]{:S(2)}) collective-permute-start(s32[2,1,16]{2,1,0:T(1,128)} %param.8), channel_id=1, source_target_pairs={{0,3},{1,2},{2,1},{3,0},{4,7},{5,6},{6,5},{7,4},{8,11},{9,10},{10,... | collective-permute-start | bytes 392 | tf_op jit(solution)/shard_map/ppermute | solution.py:26
  3.1 3.8 %collective-permute-start.4 = (s32[2,1,16]{2,1,0:T(1,128)}, s32[2,1,16]{2,1,0:T(1,128)S(1)}, u32[]{:S(2)}, u32[]{:S(2)}) collective-permute-start(s32[2,1,16]{2,1,0:T(1,128)} %param.8), channel_id=1, source_target_pairs={{0,2},{1,3},{2,0},{3,1},{4,6},{5,7},{6,4},{7,5},{8,10},{9,11},{10,... | collective-permute-start | bytes 392 | tf_op jit(solution)/shard_map/ppermute | solution.py:26
  3.1 10.5 %collective-permute-start.9 = (bf16[1,16,4096]{2,1,0:T(8,128)(2,1)}, bf16[1,16,4096]{2,1,0:T(8,128)(2,1)S(1)}, u32[]{:S(2)}, u32[]{:S(2)}) collective-permute-start(bf16[1,16,4096]{2,1,0:T(8,128)(2,1)} %refs_0_.1), channel_id=1, source_target_pairs={{0,2},{1,3},{2,0},{3,1},{4,6},{5,7},{6,4},{7,5},{8,10},{9,11},{10,... | collective-permute-start | bytes 393224 | tf_op jit(solution)/shard_map/ppermute | solution.py:26
  5.1 0.7 %copy-start.4 = (s32[16,4]{0,1:T(4,128)S(1)}, s32[16,4]{0,1:T(4,128)}, u32[]{:S(2)}) copy-start(s32[16,4]{0,1:T(4,128)} %param.11) | copy-start | bytes 772
  5.1 0.7 %copy-start.3 = (s32[16,4]{0,1:T(4,128)S(1)}, s32[16,4]{0,1:T(4,128)}, u32[]{:S(2)}) copy-start(s32[16,4]{0,1:T(4,128)} %param.10) | copy-start | bytes 772
  5.1 0.7 %copy-start.5 = (s32[2,1,16]{2,1,0:T(1,128)S(1)}, s32[2,1,16]{2,1,0:T(1,128)}, u32[]{:S(2)}) copy-start(s32[2,1,16]{2,1,0:T(1,128)} %param.8) | copy-start | bytes 388
  6.9 6.8 %collective-permute-start.8 = (s32[16,128]{1,0:T(8,128)S(1)}, s32[16,128]{1,0:T(8,128)S(1)}, u32[]{:S(2)}, u32[]{:S(2)}) collective-permute-start(s32[16,128]{1,0:T(8,128)S(1)} %pad_maximum_fusion.refs_0_), channel_id=1, source_target_pairs={{0,12},{4,8},{8,4},{12,0},{1,13},{5,9},{9,5},{13,1},{2,14},{6,10},... | collective-permute-start | bytes 24584 | tf_op jit(solution)/shard_map/ppermute | solution.py:26
  10.5 4.5 %collective-permute-start.7 = (s32[16,128]{1,0:T(8,128)S(1)}, s32[16,128]{1,0:T(8,128)S(1)}, u32[]{:S(2)}, u32[]{:S(2)}) collective-permute-start(s32[16,128]{1,0:T(8,128)S(1)} %pad_maximum_fusion.refs_0_), channel_id=1, source_target_pairs={{0,8},{4,12},{8,0},{12,4},{1,9},{5,13},{9,1},{13,5},{2,10},{6,14},... | collective-permute-start | bytes 24584 | tf_op jit(solution)/shard_map/ppermute | solution.py:26
  10.5 4.5 %collective-permute-start.6 = (s32[16,128]{1,0:T(8,128)S(1)}, s32[16,128]{1,0:T(8,128)S(1)}, u32[]{:S(2)}, u32[]{:S(2)}) collective-permute-start(s32[16,128]{1,0:T(8,128)S(1)} %pad_maximum_fusion.refs_0_), channel_id=1, source_target_pairs={{0,4},{4,0},{8,12},{12,8},{1,5},{5,1},{9,13},{13,9},{2,6},{6,2},{1... | collective-permute-start | bytes 24584 | tf_op jit(solution)/shard_map/ppermute | solution.py:26
  11.3 1.0 %copy-start = (bf16[16,4,4096]{2,1,0:T(4,128)(2,1)S(1)}, bf16[16,4,4096]{2,1,0:T(4,128)(2,1)}, u32[]{:S(2)}) copy-start(bf16[16,4,4096]{2,1,0:T(4,128)(2,1)} %param.9) | copy-start | bytes 1572868
  13.6 5.6 %copy-start.2 = (bf16[64,4096]{1,0:T(8,128)(2,1)}, bf16[64,4096]{1,0:T(8,128)(2,1)S(1)}, u32[]{:S(2)}) copy-start(bf16[64,4096]{1,0:T(8,128)(2,1)S(1)} %get-tuple-element.214.refs_4_) | copy-start | bytes 1572868
  13.6 2.8 %copy-start.1 = (bf16[1,16,4096]{2,1,0:T(8,128)(2,1)S(1)}, bf16[1,16,4096]{2,1,0:T(8,128)(2,1)}, u32[]{:S(2)}) copy-start(bf16[1,16,4096]{2,1,0:T(8,128)(2,1)} %refs_0_.1) | copy-start | bytes 393220
  16.5 8.9 %collective-permute-start.10 = (bf16[1,16,4096]{2,1,0:T(8,128)(2,1)S(1)}, bf16[1,16,4096]{2,1,0:T(8,128)(2,1)S(1)}, u32[]{:S(2)}, u32[]{:S(2)}) collective-permute-start(bf16[1,16,4096]{2,1,0:T(8,128)(2,1)S(1)} %copy-done.1), channel_id=1, source_target_pairs={{0,1},{1,0},{2,3},{3,2},{4,5},{5,4},{6,7},{7,6},{8,9},{9,8},{10,11... | collective-permute-start | bytes 393224 | tf_op jit(solution)/shard_map/ppermute | solution.py:26
  16.5 8.8 %collective-permute-start.11 = (bf16[1,16,4096]{2,1,0:T(8,128)(2,1)S(1)}, bf16[1,16,4096]{2,1,0:T(8,128)(2,1)S(1)}, u32[]{:S(2)}, u32[]{:S(2)}) collective-permute-start(bf16[1,16,4096]{2,1,0:T(8,128)(2,1)S(1)} %collective-permute-done.9.refs_2_), channel_id=1, source_target_pairs={{0,1},{1,0},{2,3},{3,2},{4,5},{5,4},{6,7},{7,6},{8,9},{9,8},{10,11... | collective-permute-start | bytes 393224 | tf_op jit(solution)/shard_map/ppermute | solution.py:26
  17.0 10.5 %collective-permute-start.12 = (bf16[512,128]{1,0:T(8,128)(2,1)S(1)}, bf16[512,128]{1,0:T(8,128)(2,1)S(1)}, u32[]{:S(2)}, u32[]{:S(2)}) collective-permute-start(bf16[512,128]{1,0:T(8,128)(2,1)S(1)} %get-tuple-element.102), channel_id=1, source_target_pairs={{0,12},{4,8},{8,4},{12,0},{1,13},{5,9},{9,5},{13,1},{2,14},{6,10},... | collective-permute-start | bytes 393224 | tf_op jit(solution)/shard_map/ppermute | solution.py:26
  19.2 12.0 %collective-permute-start.13 = (bf16[512,128]{1,0:T(8,128)(2,1)S(1)}, bf16[512,128]{1,0:T(8,128)(2,1)S(1)}, u32[]{:S(2)}, u32[]{:S(2)}) collective-permute-start(bf16[512,128]{1,0:T(8,128)(2,1)S(1)} %get-tuple-element.103), channel_id=1, source_target_pairs={{0,8},{4,12},{8,0},{12,4},{1,9},{5,13},{9,1},{13,5},{2,10},{6,14},... | collective-permute-start | bytes 393224 | tf_op jit(solution)/shard_map/ppermute | solution.py:26
  19.2 12.0 %collective-permute-start.14 = (bf16[512,128]{1,0:T(8,128)(2,1)S(1)}, bf16[512,128]{1,0:T(8,128)(2,1)S(1)}, u32[]{:S(2)}, u32[]{:S(2)}) collective-permute-start(bf16[512,128]{1,0:T(8,128)(2,1)S(1)} %get-tuple-element.90), channel_id=1, source_target_pairs={{0,4},{4,0},{8,12},{12,8},{1,5},{5,1},{9,13},{13,9},{2,6},{6,2},{1... | collective-permute-start | bytes 393224 | tf_op jit(solution)/shard_map/ppermute | solution.py:26

commit v8 on v5

--- a/solution.py
+++ b/solution.py
@@ -417,35 +417,59 @@
     )(*a_parts, own, items, sums)
 
 
-def multiply_kernel(first, peers, *refs):
+def near_kernel(first, chosen, *refs):
     refs = list(refs)
     base = 0 if first else refs.pop(0)[0]
     items, a_ref = refs[:2]
-    b_refs = refs[3 : 2 + peers][::-1]
-    sums, out, sem = refs[2 + peers :]
-    add_products(items, a_ref, list(enumerate(b_refs, 1)), sums, window=base)
+    b_refs, sums = refs[3:-1], refs[-1]
+    add_products(items, a_ref, list(zip(chosen, b_refs)), sums, window=base)
+
+
+def near_products(base, chosen, items, a_ready, sums, b_parts):
+    first = base is None
+    smem_spec = pl.BlockSpec(memory_space=SMEM)
+    vmem_spec = pl.BlockSpec(memory_space=VMEM)
+    given = [] if first else [base]
+    return pl.pallas_call(
+        functools.partial(near_kernel, first, chosen),
+        out_shape=jax.ShapeDtypeStruct(sums.shape, F32),
+        in_specs=[smem_spec] * (len(given) + 1) + [vmem_spec] * (2 + len(chosen)),
+        out_specs=vmem_spec,
+        input_output_aliases={len(given) + 2: 0},
+        compiler_params=pltpu.CompilerParams(vmem_limit_bytes=32 << 20),
+        cost_estimate=pl.CostEstimate(flops=1 << 10, bytes_accessed=1 << 10, transcendentals=0),
+        name="near_products",
+    )(*given, items, a_ready, sums, *b_parts)
+
+
+def multiply_kernel(first, chosen, *refs):
+    refs = list(refs)
+    base = 0 if first else refs.pop(0)[0]
+    items, a_ref = refs[:2]
+    b_refs = refs[3 : 3 + len(chosen)]
+    sums, out, sem = refs[3 + len(chosen) :]
+    add_products(items, a_ref, list(zip(chosen, b_refs)), sums, window=base)
     copy = pltpu.make_async_copy(sums, out, sem.at[0])
     copy.start()
     copy.wait()
 
 
-def multiply(base, items, a_ready, sums, b_parts):
+def multiply(base, chosen, items, a_ready, sums, b_parts):
     first = base is None
-    peers = len(b_parts) + 1
     smem_spec = pl.BlockSpec(memory_space=SMEM)
     vmem_spec = pl.BlockSpec(memory_space=VMEM)
     given = [] if first else [base]
     return pl.pallas_call(
-        functools.partial(multiply_kernel, first, peers),
+        functools.partial(multiply_kernel, first, chosen),
         out_shape=[jax.ShapeDtypeStruct(sums.shape, F32)] * 2,
-        in_specs=[smem_spec] * (len(given) + 1) + [vmem_spec] * (1 + peers),
+        in_specs=[smem_spec] * (len(given) + 1) + [vmem_spec] * (2 + len(chosen)),
         out_specs=[vmem_spec, pl.BlockSpec(memory_space=pl.ANY)],
         input_output_aliases={len(given) + 2: 0},
         scratch_shapes=[pltpu.SemaphoreType.DMA((1,))],
         compiler_params=pltpu.CompilerParams(vmem_limit_bytes=32 << 20),
         cost_estimate=pl.CostEstimate(flops=1 << 26, bytes_accessed=4 << 20, transcendentals=0),
         name="multiply",
-    )(*given, items, a_ready, sums, *b_parts[::-1])
+    )(*given, items, a_ready, sums, *b_parts)
 
 
 def shards(a_blocks, a_index, b_blocks, b_cols, c_cols):
@@ -458,10 +482,19 @@
         far_first = range(len(parts), 0, -1)
         return [exchanged(parts[d - 1], "row", d) for d in far_first][::-1]
 
+    def finish(base, sums, arrived):
+        split = max(rows - 1, 1) - 1
+        near, last = list(range(split + 1, rows)), list(range(split, 0, -1))
+        sums = near_products(base, near, items, a_ready, sums, [arrived[d - 1] for d in near])
+        return multiply(base, last, items, a_ready, sums, [arrived[d - 1] for d in last])
+
     index_parts = [a_index] + [exchanged(a_index, "col", h) for h in range(1, cols)]
     told = describe(index_parts, b_cols.T, c_cols.T)
-    a_parts = [exchanged(a_blocks, "col", h) for h in range(1, cols)]
+    a_parts = [exchanged(a_blocks, "col", 1)]
     told, a_parts[0] = lax.optimization_barrier((told, a_parts[0]))
+    for h in range(2, cols, 2):
+        far = exchanged(a_blocks, "col", h)
+        a_parts += [far, exchanged(a_blocks, "col", h + 1)]
     told = [told] + send_rows([told] * (rows - 1))
     flat, own, sums = flatten(seen_by_rows(b_blocks))
     flat, *a_parts = lax.optimization_barrier((flat, *a_parts))
@@ -469,18 +502,19 @@
     arrived = send_rows(packed)
     told_late = lax.optimization_barrier((told, packed[0]))[0]
     items = work_list(told_late, cols, row_count, a_slots)
-    rounds = count_rounds(told_late, cols, row_count, a_slots)
+    rounds = jnp.minimum(count_rounds(told_late, cols, row_count, a_slots)[0], LANES)
     a_ready, sums = stage([a_blocks] + a_parts, own, sums, items)
-    sums, out = multiply(None, items, a_ready, sums, arrived)
+    sums, rounds = lax.optimization_barrier((sums, rounds))
+    sums, out = finish(None, sums, arrived)
 
     def more(state):
-        return state[0] < rounds[0]
+        return state[0] < rounds
 
     def one_round(state):
         at, sums, _ = state
         base = jnp.reshape(at * CAPACITY, (1,))
         arrived = send_rows(pack(base, told, flat, cols, row_count, a_slots))
-        return at + 1, *multiply(base, items, a_ready, sums, arrived)
+        return at + 1, *finish(base, sums, arrived)
 
     return seen_by_blocks(lax.while_loop(more, one_round, (jnp.int32(1), sums, out))[2])
 

time: 33 us -> 32.5 us (0.985)
  waiting for transfers between devices: 6.36 us -> 4.84 us
  Pallas kernels: 9.8 us -> 10.9 us
  between operations: 0.1 us -> 0.79 us
  loops' own time: 0.68 us -> 0.01 us
    ppermute x12, waiting for transfers between devices: 6.36 us -> 4.84 us  [exchanged(): return lax.ppermute(block, axis, [(i, i ^ distance) for i in range(size)])]
    pallas_call x1 -> x2, Pallas kernels: 2.19 us -> 3.28 us  [the longest x1 2.44 us: multiply(): pl.pallas_call(functools.partial(multiply_kernel, first, chosen), out_sha...]
    another operation x1, loops' own time: 0.68 us -> 0.01 us  [shards(): lax.while_loop(more, one_round, (jnp.int32(1), sums, out))[2]]
    unnamed x12 -> x14, local copies, waits for them, and re-layouts: 1.76 us -> 1.76 us
  transfers between devices with their start and end apart: 12 -> 12, of which waited for: 4 -> 4; matrix products, arithmetic and copies ran while one was open for 0% -> 0% of each run, Pallas kernels for 19% -> 22%
where the time goes in v8:
time: 32.5 us
  starting transfers between devices  14.1 us (43%)
  Pallas kernels  10.9 us (34%)
  waiting for transfers between devices  4.84 us (15%)
  local copies, waits for them, and re-layouts  1.76 us (5%)
  between operations  0.79 us (2%)
    ppermute x12, starting transfers between devices, exchanged(): return lax.ppermute(block, axis, [(i, i ^ distance) for i in range(size)])  14.1 us
    ppermute x12, waiting for transfers between devices, exchanged(): return lax.ppermute(block, axis, [(i, i ^ distance) for i in range(size)])  4.84 us
    pallas_call x1, Pallas kernels, multiply(): pl.pallas_call(functools.partial(multiply_kernel, first, chosen), out_sha...  2.44 us
    pallas_call x1, Pallas kernels, work_list(): pl.pallas_call(functools.partial(list_kernel, cols, a_slots, row_count, p...  1.91 us
    unnamed x14, local copies, waits for them, and re-layouts  1.76 us
    pallas_call x1, Pallas kernels, stage(): pl.pallas_call(functools.partial(stage_kernel, cols), out_shape=(jax.Shap...  1.73 us
    pallas_call x1, Pallas kernels, pack(): pl.pallas_call(functools.partial(pack_kernel, first, peers, cols, a_slots...  1.38 us
    pallas_call x1, Pallas kernels, count_rounds(): pl.pallas_call(functools.partial(rounds_kernel, cols, a_slots, row_count,...  1.35 us
  transfers between devices with their start and end apart: 12, of which 4 were waited for; matrix products, arithmetic and copies ran while one was open for 0% of the time, Pallas kernels for 22%

profile of v8, /device:TPU:0, one launch (start us, length us, event | category | flops | bytes accessed | tf_op | source)
XLA Modules:
  0.0 32.5 jit_solution(5628070963281127178)
XLA Ops:
  0.0 0.5 %collective-permute-start.3 = (s32[2,1,16]{2,1,0:T(1,128)}, s32[2,1,16]{2,1,0:T(1,128)S(1)}, u32[]{:S(2)}, u32[]{:S(2)}) collective-permute-start(s32[2,1,16]{2,1,0:T(1,128)} %param.8), channel_id=1, source_target_pairs={{0,1},{1,0},{2,3},{3,2},{4,5},{5,4},{6,7},{7,6},{8,9},{9,8},{10,11... | collective-permute-start | bytes 392 | tf_op jit(solution)/shard_map/ppermute | solution.py:26
  0.5 2.6 %collective-permute-start.5 = (s32[2,1,16]{2,1,0:T(1,128)}, s32[2,1,16]{2,1,0:T(1,128)S(1)}, u32[]{:S(2)}, u32[]{:S(2)}) collective-permute-start(s32[2,1,16]{2,1,0:T(1,128)} %param.8), channel_id=1, source_target_pairs={{0,3},{1,2},{2,1},{3,0},{4,7},{5,6},{6,5},{7,4},{8,11},{9,10},{10,... | collective-permute-start | bytes 392 | tf_op jit(solution)/shard_map/ppermute | solution.py:26
  3.1 0.0 collective-permute-start.4
  3.1 2.0 %collective-permute-start.10 = (bf16[1,16,4096]{2,1,0:T(8,128)(2,1)}, bf16[1,16,4096]{2,1,0:T(8,128)(2,1)S(1)}, u32[]{:S(2)}, u32[]{:S(2)}) collective-permute-start(bf16[1,16,4096]{2,1,0:T(8,128)(2,1)} %refs_0_.1), channel_id=1, source_target_pairs={{0,2},{1,3},{2,0},{3,1},{4,6},{5,7},{6,4},{7,5},{8,10},{9,11},{10,... | collective-permute-start | bytes 393224 | tf_op jit(solution)/shard_map/ppermute | solution.py:26
  5.1 0.7 %copy-done.5 = s32[16,4]{0,1:T(4,128)S(1)} copy-done((s32[16,4]{0,1:T(4,128)S(1)}, s32[16,4]{0,1:T(4,128)}, u32[]{:S(2)}) %copy-start.5) | copy-done | bytes 280
  5.8 0.0 copy-done.4
  5.8 0.0 copy-done.6
  5.8 0.1 collective-permute-start.6
  5.9 0.0 collective-permute-done.3
  5.9 0.1 collective-permute-start.11
  6.0 0.0 collective-permute-done.5
  6.0 0.8 %collective-permute-done.4 = s32[2,1,16]{2,1,0:T(1,128)S(1)} collective-permute-done((s32[2,1,16]{2,1,0:T(1,128)}, s32[2,1,16]{2,1,0:T(1,128)S(1)}, u32[]{:S(2)}, u32[]{:S(2)}) %collective-permute-start.4) | collective-permute-done | bytes 160 | tf_op jit(solution)/shard_map/ppermute | solution.py:26
  6.9 0.6 %collective-permute-done.6.refs_1_ = bf16[1,16,4096]{2,1,0:T(8,128)(2,1)S(1)} collective-permute-done((bf16[1,16,4096]{2,1,0:T(8,128)(2,1)}, bf16[1,16,4096]{2,1,0:T(8,128)(2,1)S(1)}, u32[]{:S(2)}, u32[]{:S(2)}) %collective-permute-start.6) | collective-permute-done | bytes 131104 | tf_op jit(solution)/shard_map/ppermute | solution.py:26
  7.4 3.6 %collective-permute-start.9 = (s32[16,128]{1,0:T(8,128)S(1)}, s32[16,128]{1,0:T(8,128)S(1)}, u32[]{:S(2)}, u32[]{:S(2)}) collective-permute-start(s32[16,128]{1,0:T(8,128)S(1)} %pad_maximum_fusion.refs_0_), channel_id=1, source_target_pairs={{0,12},{4,8},{8,4},{12,0},{1,13},{5,9},{9,5},{13,1},{2,14},{6,10},... | collective-permute-start | bytes 24584 | tf_op jit(solution)/shard_map/ppermute | solution.py:26
  11.0 0.0 collective-permute-start.8
  11.0 0.8 %collective-permute-start.7 = (s32[16,128]{1,0:T(8,128)S(1)}, s32[16,128]{1,0:T(8,128)S(1)}, u32[]{:S(2)}, u32[]{:S(2)}) collective-permute-start(s32[16,128]{1,0:T(8,128)S(1)} %pad_maximum_fusion.refs_0_), channel_id=1, source_target_pairs={{0,4},{4,0},{8,12},{12,8},{1,5},{5,1},{9,13},{13,9},{2,6},{6,2},{1... | collective-permute-start | bytes 24584 | tf_op jit(solution)/shard_map/ppermute | solution.py:26
  11.8 1.0 %copy-done = bf16[16,4,4096]{2,1,0:T(4,128)(2,1)S(1)} copy-done((bf16[16,4,4096]{2,1,0:T(4,128)(2,1)S(1)}, bf16[16,4,4096]{2,1,0:T(4,128)(2,1)}, u32[]{:S(2)}) %copy-start) | copy-done | bytes 524312
  12.9 1.2 %flatten.1 = (bf16[64,4096]{1,0:T(8,128)(2,1)S(1)}, bf16[2048,128]{1,0:T(8,128)(2,1)S(1)}, f32[16,128,128]{2,1,0:T(8,128)S(1)}) custom-call(bf16[16,128,128]{2,1,0:T(8,128)(2,1)S(1)} %bitcast.20), custom_call_target="tpu_custom_call" | custom-call | flops 1048576 | bytes 8388608 | tf_op jit(solution)/shard_map/flatten/pallas_call | solution.py:86
  14.1 0.0 collective-permute-done.10.refs_2_
  14.1 0.0 collective-permute-done.11.refs_3_
  14.1 0.0 collective-permute-done.9.refs_3_
  14.1 1.4 %collective-permute-done.8.refs_2_ = s32[16,128]{1,0:T(8,128)S(1)} collective-permute-done((s32[16,128]{1,0:T(8,128)S(1)}, s32[16,128]{1,0:T(8,128)S(1)}, u32[]{:S(2)}, u32[]{:S(2)}) %collective-permute-start.8) | collective-permute-done | bytes 8224 | tf_op jit(solution)/shard_map/ppermute | solution.py:26
  15.6 1.4 %pack.2 = (bf16[512,128]{1,0:T(8,128)(2,1)S(1)}, bf16[512,128]{1,0:T(8,128)(2,1)S(1)}, bf16[512,128]{1,0:T(8,128)(2,1)S(1)}) custom-call(s32[16,128]{1,0:T(8,128)S(1)} %pad_maximum_fusion.refs_0_, s32[16,128]{1,0:T(8,128)S(1)} %collective-permute-done.7.refs_1_, s32[16,128]{1,0:T(8,128)S(1)} %collective-permute-done.8.refs_2_, ...), custom_call_target="tpu_custom_call" | custom-call | flops 1048576 | bytes 4194304 | tf_op jit(solution)/shard_map/pack/pallas_call | solution.py:194
  17.0 2.3 %collective-permute-start.12 = (bf16[512,128]{1,0:T(8,128)(2,1)S(1)}, bf16[512,128]{1,0:T(8,128)(2,1)S(1)}, u32[]{:S(2)}, u32[]{:S(2)}) collective-permute-start(bf16[512,128]{1,0:T(8,128)(2,1)S(1)} %get-tuple-element.106), channel_id=1, source_target_pairs={{0,12},{4,8},{8,4},{12,0},{1,13},{5,9},{9,5},{13,1},{2,14},{6,10},... | collective-permute-start | bytes 393224 | tf_op jit(solution)/shard_map/ppermute | solution.py:26
  19.2 0.0 collective-permute-start.13
  19.2 2.2 %collective-permute-start.14 = (bf16[512,128]{1,0:T(8,128)(2,1)S(1)}, bf16[512,128]{1,0:T(8,128)(2,1)S(1)}, u32[]{:S(2)}, u32[]{:S(2)}) collective-permute-start(bf16[512,128]{1,0:T(8,128)(2,1)S(1)} %get-tuple-element.93), channel_id=1, source_target_pairs={{0,4},{4,0},{8,12},{12,8},{1,5},{5,1},{9,13},{13,9},{2,6},{6,2},{1... | collective-permute-start | bytes 393224 | tf_op jit(solution)/shard_map/ppermute | solution.py:26
  21.4 1.4 %count_rounds.1 = s32[1]{0:T(128)} custom-call(s32[16,128]{1,0:T(8,128)S(1)} %pad_maximum_fusion.refs_0_, s32[16,128]{1,0:T(8,128)S(1)} %collective-permute-done.7.refs_1_, s32[16,128]{1,0:T(8,128)S(1)} %collective-permute-done.8.refs_2_, s32[16,128]{1,0:T(8,128)S(1)} %collective-permute-done.9.refs_3_), custom_call_target="tpu_custom_call" | custom-call | flops 1024 | bytes 1024 | tf_op jit(solution)/shard_map/count_rounds/pallas_call | solution.py:324
  22.8 1.9 %work_list.1.refs_5_.refs_0_ = s32[8,128]{1,0:T(8,128)S(1)} custom-call(s32[16,128]{1,0:T(8,128)S(1)} %pad_maximum_fusion.refs_0_, s32[16,128]{1,0:T(8,128)S(1)} %collective-permute-done.7.refs_1_, s32[16,128]{1,0:T(8,128)S(1)} %collective-permute-done.8.refs_2_, s32[16,128]{1,0:T(8,128)S(1)} %collective-permute-done.9.refs_3_), custom_call_target="tpu_custom_call" | custom-call | flops 1024 | bytes 1024 | tf_op jit(solution)/shard_map/work_list/pallas_call | solution.py:275
  24.7 1.7 %stage.1 = (bf16[2048,128]{1,0:T(8,128)(2,1)S(1)}, f32[16,128,128]{2,1,0:T(8,128)S(1)}) custom-call(bf16[1,16,4096]{2,1,0:T(8,128)(2,1)S(1)} %copy-done.1, bf16[1,16,4096]{2,1,0:T(8,128)(2,1)S(1)} %collective-permute-done.6.refs_1_, bf16[1,16,4096]{2,1,0:T(8,128)(2,1)S(1)} %collective-permute-done.10.refs_2_, ...), custom_call_target="tpu_custom_call", output_to_operand_aliasing={{1}: (6, {})} | custom-call | flops 1024 | bytes 1024 | tf_op jit(solution)/shard_map/stage/pallas_call | solution.py:404
  27.1 0.8 %near_products.2.refs_2_ = f32[16,128,128]{2,1,0:T(8,128)S(1)} custom-call(s32[8,128]{1,0:T(8,128)S(1)} %work_list.1.refs_5_.refs_0_, bf16[2048,128]{1,0:T(8,128)(2,1)S(1)} %get-tuple-element.220.refs_1_, f32[16,128,128]{2,1,0:T(8,128)S(1)} %get-tuple-element.105.refs_2_, ...), custom_call_target="tpu_custom_call", output_to_operand_aliasing={{}: (2, {})} | custom-call | flops 1024 | bytes 1024 | tf_op jit(solution)/shard_map/near_products/pallas_call | solution.py:433
  28.0 2.0 %collective-permute-done.13.refs_3_ = bf16[512,128]{1,0:T(8,128)(2,1)S(1)} collective-permute-done((bf16[512,128]{1,0:T(8,128)(2,1)S(1)}, bf16[512,128]{1,0:T(8,128)(2,1)S(1)}, u32[]{:S(2)}, u32[]{:S(2)}) %collective-permute-start.13) | collective-permute-done | bytes 131104 | tf_op jit(solution)/shard_map/ppermute | solution.py:26
  30.0 2.4 %multiply.2 = (f32[16,128,128]{2,1,0:T(8,128)S(1)}, f32[16,128,128]{2,1,0:T(8,128)}) custom-call(s32[8,128]{1,0:T(8,128)S(1)} %work_list.1.refs_5_.refs_0_, bf16[2048,128]{1,0:T(8,128)(2,1)S(1)} %get-tuple-element.220.refs_1_, f32[16,128,128]{2,1,0:T(8,128)S(1)} %near_products.2.refs_2_, ...), custom_call_target="tpu_custom_call", output_to_operand_aliasing={{0}: (2, {})} | custom-call | flops 67108864 | bytes 4194304 | tf_op jit(solution)/shard_map/multiply/pallas_call | solution.py:462
  (16 shorter events, 0.1 us)
Async XLA Ops:
  0.0 5.9 %collective-permute-start.3 = (s32[2,1,16]{2,1,0:T(1,128)}, s32[2,1,16]{2,1,0:T(1,128)S(1)}, u32[]{:S(2)}, u32[]{:S(2)}) collective-permute-start(s32[2,1,16]{2,1,0:T(1,128)} %param.8), channel_id=1, source_target_pairs={{0,1},{1,0},{2,3},{3,2},{4,5},{5,4},{6,7},{7,6},{8,9},{9,8},{10,11... | collective-permute-start | bytes 392 | tf_op jit(solution)/shard_map/ppermute | solution.py:26
  0.5 5.6 %collective-permute-start.5 = (s32[2,1,16]{2,1,0:T(1,128)}, s32[2,1,16]{2,1,0:T(1,128)S(1)}, u32[]{:S(2)}, u32[]{:S(2)}) collective-permute-start(s32[2,1,16]{2,1,0:T(1,128)} %param.8), channel_id=1, source_target_pairs={{0,3},{1,2},{2,1},{3,0},{4,7},{5,6},{6,5},{7,4},{8,11},{9,10},{10,... | collective-permute-start | bytes 392 | tf_op jit(solution)/shard_map/ppermute | solution.py:26
  3.1 3.8 %collective-permute-start.4 = (s32[2,1,16]{2,1,0:T(1,128)}, s32[2,1,16]{2,1,0:T(1,128)S(1)}, u32[]{:S(2)}, u32[]{:S(2)}) collective-permute-start(s32[2,1,16]{2,1,0:T(1,128)} %param.8), channel_id=1, source_target_pairs={{0,2},{1,3},{2,0},{3,1},{4,6},{5,7},{6,4},{7,5},{8,10},{9,11},{10,... | collective-permute-start | bytes 392 | tf_op jit(solution)/shard_map/ppermute | solution.py:26
  3.1 11.1 %collective-permute-start.10 = (bf16[1,16,4096]{2,1,0:T(8,128)(2,1)}, bf16[1,16,4096]{2,1,0:T(8,128)(2,1)S(1)}, u32[]{:S(2)}, u32[]{:S(2)}) collective-permute-start(bf16[1,16,4096]{2,1,0:T(8,128)(2,1)} %refs_0_.1), channel_id=1, source_target_pairs={{0,2},{1,3},{2,0},{3,1},{4,6},{5,7},{6,4},{7,5},{8,10},{9,11},{10,... | collective-permute-start | bytes 393224 | tf_op jit(solution)/shard_map/ppermute | solution.py:26
  5.1 0.7 %copy-start.5 = (s32[16,4]{0,1:T(4,128)S(1)}, s32[16,4]{0,1:T(4,128)}, u32[]{:S(2)}) copy-start(s32[16,4]{0,1:T(4,128)} %param.11) | copy-start | bytes 772
  5.1 0.7 %copy-start.4 = (s32[16,4]{0,1:T(4,128)S(1)}, s32[16,4]{0,1:T(4,128)}, u32[]{:S(2)}) copy-start(s32[16,4]{0,1:T(4,128)} %param.10) | copy-start | bytes 772
  5.1 0.7 %copy-start.6 = (s32[2,1,16]{2,1,0:T(1,128)S(1)}, s32[2,1,16]{2,1,0:T(1,128)}, u32[]{:S(2)}) copy-start(s32[2,1,16]{2,1,0:T(1,128)} %param.8) | copy-start | bytes 388
  5.8 1.6 %collective-permute-start.6 = (bf16[1,16,4096]{2,1,0:T(8,128)(2,1)}, bf16[1,16,4096]{2,1,0:T(8,128)(2,1)S(1)}, u32[]{:S(2)}, u32[]{:S(2)}) collective-permute-start(bf16[1,16,4096]{2,1,0:T(8,128)(2,1)} %refs_0_.1), channel_id=1, source_target_pairs={{0,1},{1,0},{2,3},{3,2},{4,5},{5,4},{6,7},{7,6},{8,9},{9,8},{10,11... | collective-permute-start | bytes 393224 | tf_op jit(solution)/shard_map/ppermute | solution.py:26
  5.9 8.2 %collective-permute-start.11 = (bf16[1,16,4096]{2,1,0:T(8,128)(2,1)}, bf16[1,16,4096]{2,1,0:T(8,128)(2,1)S(1)}, u32[]{:S(2)}, u32[]{:S(2)}) collective-permute-start(bf16[1,16,4096]{2,1,0:T(8,128)(2,1)} %refs_0_.1), channel_id=1, source_target_pairs={{0,3},{1,2},{2,1},{3,0},{4,7},{5,6},{6,5},{7,4},{8,11},{9,10},{10,... | collective-permute-start | bytes 393224 | tf_op jit(solution)/shard_map/ppermute | solution.py:26
  7.4 6.7 %collective-permute-start.9 = (s32[16,128]{1,0:T(8,128)S(1)}, s32[16,128]{1,0:T(8,128)S(1)}, u32[]{:S(2)}, u32[]{:S(2)}) collective-permute-start(s32[16,128]{1,0:T(8,128)S(1)} %pad_maximum_fusion.refs_0_), channel_id=1, source_target_pairs={{0,12},{4,8},{8,4},{12,0},{1,13},{5,9},{9,5},{13,1},{2,14},{6,10},... | collective-permute-start | bytes 24584 | tf_op jit(solution)/shard_map/ppermute | solution.py:26
  11.0 4.5 %collective-permute-start.8 = (s32[16,128]{1,0:T(8,128)S(1)}, s32[16,128]{1,0:T(8,128)S(1)}, u32[]{:S(2)}, u32[]{:S(2)}) collective-permute-start(s32[16,128]{1,0:T(8,128)S(1)} %pad_maximum_fusion.refs_0_), channel_id=1, source_target_pairs={{0,8},{4,12},{8,0},{12,4},{1,9},{5,13},{9,1},{13,5},{2,10},{6,14},... | collective-permute-start | bytes 24584 | tf_op jit(solution)/shard_map/ppermute | solution.py:26
  11.0 4.5 %collective-permute-start.7 = (s32[16,128]{1,0:T(8,128)S(1)}, s32[16,128]{1,0:T(8,128)S(1)}, u32[]{:S(2)}, u32[]{:S(2)}) collective-permute-start(s32[16,128]{1,0:T(8,128)S(1)} %pad_maximum_fusion.refs_0_), channel_id=1, source_target_pairs={{0,4},{4,0},{8,12},{12,8},{1,5},{5,1},{9,13},{13,9},{2,6},{6,2},{1... | collective-permute-start | bytes 24584 | tf_op jit(solution)/shard_map/ppermute | solution.py:26
  11.8 1.0 %copy-start = (bf16[16,4,4096]{2,1,0:T(4,128)(2,1)S(1)}, bf16[16,4,4096]{2,1,0:T(4,128)(2,1)}, u32[]{:S(2)}) copy-start(bf16[16,4,4096]{2,1,0:T(4,128)(2,1)} %param.9) | copy-start | bytes 1572868
  14.1 5.1 %copy-start.2 = (bf16[64,4096]{1,0:T(8,128)(2,1)}, bf16[64,4096]{1,0:T(8,128)(2,1)S(1)}, u32[]{:S(2)}) copy-start(bf16[64,4096]{1,0:T(8,128)(2,1)S(1)} %get-tuple-element.218.refs_4_) | copy-start | bytes 1572868
  15.6 9.1 %copy-start.1 = (bf16[1,16,4096]{2,1,0:T(8,128)(2,1)S(1)}, bf16[1,16,4096]{2,1,0:T(8,128)(2,1)}, u32[]{:S(2)}) copy-start(bf16[1,16,4096]{2,1,0:T(8,128)(2,1)} %refs_0_.1) | copy-start | bytes 393220
  17.0 10.1 %collective-permute-start.12 = (bf16[512,128]{1,0:T(8,128)(2,1)S(1)}, bf16[512,128]{1,0:T(8,128)(2,1)S(1)}, u32[]{:S(2)}, u32[]{:S(2)}) collective-permute-start(bf16[512,128]{1,0:T(8,128)(2,1)S(1)} %get-tuple-element.106), channel_id=1, source_target_pairs={{0,12},{4,8},{8,4},{12,0},{1,13},{5,9},{9,5},{13,1},{2,14},{6,10},... | collective-permute-start | bytes 393224 | tf_op jit(solution)/shard_map/ppermute | solution.py:26
  19.2 10.7 %collective-permute-start.13 = (bf16[512,128]{1,0:T(8,128)(2,1)S(1)}, bf16[512,128]{1,0:T(8,128)(2,1)S(1)}, u32[]{:S(2)}, u32[]{:S(2)}) collective-permute-start(bf16[512,128]{1,0:T(8,128)(2,1)S(1)} %get-tuple-element.107), channel_id=1, source_target_pairs={{0,8},{4,12},{8,0},{12,4},{1,9},{5,13},{9,1},{13,5},{2,10},{6,14},... | collective-permute-start | bytes 393224 | tf_op jit(solution)/shard_map/ppermute | solution.py:26
  19.2 10.7 %collective-permute-start.14 = (bf16[512,128]{1,0:T(8,128)(2,1)S(1)}, bf16[512,128]{1,0:T(8,128)(2,1)S(1)}, u32[]{:S(2)}, u32[]{:S(2)}) collective-permute-start(bf16[512,128]{1,0:T(8,128)(2,1)S(1)} %get-tuple-element.93), channel_id=1, source_target_pairs={{0,4},{4,0},{8,12},{12,8},{1,5},{5,1},{9,13},{13,9},{2,6},{6,2},{1... | collective-permute-start | bytes 393224 | tf_op jit(solution)/shard_map/ppermute | solution.py:26
  27.9 4.5 %copy-start.3 = (bf16[64,4096]{1,0:T(8,128)(2,1)S(1)}, bf16[64,4096]{1,0:T(8,128)(2,1)}, u32[]{:S(2)}) copy-start(bf16[64,4096]{1,0:T(8,128)(2,1)} %copy-done.2) | copy-start | bytes 1572868

commit v9 on v8

--- a/solution.py
+++ b/solution.py
@@ -66,33 +66,25 @@
     return result
 
 
-def flatten_kernel(b_ref, flat, own, sums, wide):
+def flatten_kernel(b_ref, flat, wide):
     row_count = b_ref.shape[0]
     wide[...] = b_ref[...].astype(F32)
     for t in range(ROWS):
         for n in range(SLOTS):
             piece = wide[:, t * SLOTS + n, :].astype(BF16)
             flat[pl.ds(n * row_count, row_count), pl.ds(t * LANES, LANES)] = piece
-    for n in range(SLOTS):
-        for k in range(row_count):
-            block = wide[k, pl.ds(n, ROWS, stride=SLOTS), :].astype(BF16)
-            own[pl.ds((n * row_count + k) * ROWS, ROWS), :] = block
-    sums[...] = jnp.zeros_like(sums)
 
 
 def flatten(b_rows):
     vmem_spec = pl.BlockSpec(memory_space=VMEM)
-    row_count = b_rows.shape[0]
     return pl.pallas_call(
         flatten_kernel,
         out_shape=(
-            jax.ShapeDtypeStruct((row_count * SLOTS, BS * BS), BF16),
-            jax.ShapeDtypeStruct((row_count * SLOTS * ROWS, LANES), BF16),
+            jax.ShapeDtypeStruct((b_rows.shape[0] * SLOTS, BS * BS), BF16),
             jax.ShapeDtypeStruct(b_rows.shape, F32),
         ),
         in_specs=[vmem_spec],
-        out_specs=(vmem_spec,) * 3,
-        scratch_shapes=[VMEM(b_rows.shape, F32)],
+        out_specs=(vmem_spec,) * 2,
         compiler_params=pltpu.CompilerParams(vmem_limit_bytes=24 << 20),
         cost_estimate=pl.CostEstimate(flops=1 << 20, bytes_accessed=8 << 20, transcendentals=0),
         name="flatten",
@@ -377,8 +369,14 @@
 
 
 def stage_kernel(cols, *refs):
-    a_refs, own, items = refs[:cols], refs[cols], refs[cols + 1]
-    a_out, sums, a_wide = refs[cols + 3 :]
+    a_refs, wide, items = refs[:cols], refs[cols], refs[cols + 1]
+    a_out, sums, a_wide, own = refs[cols + 2 :]
+    sums[...] = jnp.zeros_like(sums)
+    row_count = wide.shape[0]
+    for n in range(SLOTS):
+        for k in range(row_count):
+            block = wide[k, pl.ds(n, ROWS, stride=SLOTS), :].astype(BF16)
+            own[pl.ds((n * row_count + k) * ROWS, ROWS), :] = block
     source = iota((LANES, LANES), 0)
     target = iota((LANES, LANES), 1)
     wanted = (target // BS) * BS + 2 * (target % ROWS) + (target // ROWS) % 2
@@ -397,7 +395,7 @@
     add_products(items, a_out, [(0, own)], sums)
 
 
-def stage(a_parts, own, sums, items):
+def stage(a_parts, wide, items):
     cols, slots = len(a_parts), a_parts[0].shape[1]
     vmem_spec = pl.BlockSpec(memory_space=VMEM)
     smem_spec = pl.BlockSpec(memory_space=SMEM)
@@ -405,16 +403,18 @@
         functools.partial(stage_kernel, cols),
         out_shape=(
             jax.ShapeDtypeStruct((cols * slots * ROWS, LANES), BF16),
-            jax.ShapeDtypeStruct(sums.shape, F32),
+            jax.ShapeDtypeStruct(wide.shape, F32),
         ),
-        in_specs=[vmem_spec] * (cols + 1) + [smem_spec] + [vmem_spec],
+        in_specs=[vmem_spec] * (cols + 1) + [smem_spec],
         out_specs=(vmem_spec,) * 2,
-        input_output_aliases={cols + 2: 1},
-        scratch_shapes=[VMEM((cols * slots, ROWS, LANES), F32)],
+        scratch_shapes=[
+            VMEM((cols * slots, ROWS, LANES), F32),
+            VMEM((wide.shape[0] * SLOTS * ROWS, LANES), BF16),
+        ],
         compiler_params=pltpu.CompilerParams(vmem_limit_bytes=40 << 20),
         cost_estimate=pl.CostEstimate(flops=1 << 10, bytes_accessed=1 << 10, transcendentals=0),
         name="stage",
-    )(*a_parts, own, items, sums)
+    )(*a_parts, wide, items)
 
 
 def near_kernel(first, chosen, *refs):
@@ -496,14 +496,14 @@
         far = exchanged(a_blocks, "col", h)
         a_parts += [far, exchanged(a_blocks, "col", h + 1)]
     told = [told] + send_rows([told] * (rows - 1))
-    flat, own, sums = flatten(seen_by_rows(b_blocks))
+    flat, wide = flatten(seen_by_rows(b_blocks))
     flat, *a_parts = lax.optimization_barrier((flat, *a_parts))
     packed = pack(None, told, flat, cols, row_count, a_slots)
     arrived = send_rows(packed)
     told_late = lax.optimization_barrier((told, packed[0]))[0]
     items = work_list(told_late, cols, row_count, a_slots)
     rounds = jnp.minimum(count_rounds(told_late, cols, row_count, a_slots)[0], LANES)
-    a_ready, sums = stage([a_blocks] + a_parts, own, sums, items)
+    a_ready, sums = stage([a_blocks] + a_parts, wide, items)
     sums, rounds = lax.optimization_barrier((sums, rounds))
     sums, out = finish(None, sums, arrived)
 

time: 32.5 us -> 32.6 us (level)
    pallas_call x1, Pallas kernels: 1.73 us -> 2.06 us  [stage(): pl.pallas_call(functools.partial(stage_kernel, cols), out_shape=(jax.Shap...]
where the time goes in v9:
time: 32.6 us; the launch traced here: 32.4 us
  starting transfers between devices  14.1 us (43%)
  Pallas kernels  10.9 us (33%)
  waiting for transfers between devices  4.88 us (15%)
  local copies, waits for them, and re-layouts  1.76 us (5%)
  between operations  0.77 us (2%)
    ppermute x12, starting transfers between devices, exchanged(): return lax.ppermute(block, axis, [(i, i ^ distance) for i in range(size)])  14.1 us
    ppermute x12, waiting for transfers between devices, exchanged(): return lax.ppermute(block, axis, [(i, i ^ distance) for i in range(size)])  4.88 us
    pallas_call x1, Pallas kernels, multiply(): pl.pallas_call(functools.partial(multiply_kernel, first, chosen), out_sha...  2.44 us
    pallas_call x1, Pallas kernels, stage(): pl.pallas_call(functools.partial(stage_kernel, cols), out_shape=(jax.Shap...  2.06 us
    pallas_call x1, Pallas kernels, work_list(): pl.pallas_call(functools.partial(list_kernel, cols, a_slots, row_count, p...  1.91 us
    unnamed x14, local copies, waits for them, and re-layouts  1.76 us
    pallas_call x1, Pallas kernels, pack(): pl.pallas_call(functools.partial(pack_kernel, first, peers, cols, a_slots...  1.38 us
    pallas_call x1, Pallas kernels, count_rounds(): pl.pallas_call(functools.partial(rounds_kernel, cols, a_slots, row_count,...  1.35 us
  transfers between devices with their start and end apart: 12, of which 4 were waited for; matrix products, arithmetic and copies ran while one was open for 0% of the time, Pallas kernels for 22%

profile of v9, /device:TPU:0, one launch (start us, length us, event | category | flops | bytes accessed | tf_op | source)
XLA Modules:
  0.0 32.4 jit_solution(2857405603407148321)
XLA Ops:
  0.0 0.5 %collective-permute-start.3 = (s32[2,1,16]{2,1,0:T(1,128)}, s32[2,1,16]{2,1,0:T(1,128)S(1)}, u32[]{:S(2)}, u32[]{:S(2)}) collective-permute-start(s32[2,1,16]{2,1,0:T(1,128)} %param.8), channel_id=1, source_target_pairs={{0,1},{1,0},{2,3},{3,2},{4,5},{5,4},{6,7},{7,6},{8,9},{9,8},{10,11... | collective-permute-start | bytes 392 | tf_op jit(solution)/shard_map/ppermute | solution.py:26
  0.5 2.6 %collective-permute-start.5 = (s32[2,1,16]{2,1,0:T(1,128)}, s32[2,1,16]{2,1,0:T(1,128)S(1)}, u32[]{:S(2)}, u32[]{:S(2)}) collective-permute-start(s32[2,1,16]{2,1,0:T(1,128)} %param.8), channel_id=1, source_target_pairs={{0,3},{1,2},{2,1},{3,0},{4,7},{5,6},{6,5},{7,4},{8,11},{9,10},{10,... | collective-permute-start | bytes 392 | tf_op jit(solution)/shard_map/ppermute | solution.py:26
  3.1 0.0 collective-permute-start.4
  3.1 2.0 %collective-permute-start.10 = (bf16[1,16,4096]{2,1,0:T(8,128)(2,1)}, bf16[1,16,4096]{2,1,0:T(8,128)(2,1)S(1)}, u32[]{:S(2)}, u32[]{:S(2)}) collective-permute-start(bf16[1,16,4096]{2,1,0:T(8,128)(2,1)} %refs_0_.1), channel_id=1, source_target_pairs={{0,2},{1,3},{2,0},{3,1},{4,6},{5,7},{6,4},{7,5},{8,10},{9,11},{10,... | collective-permute-start | bytes 393224 | tf_op jit(solution)/shard_map/ppermute | solution.py:26
  5.1 0.7 %copy-done.6 = s32[16,4]{0,1:T(4,128)S(1)} copy-done((s32[16,4]{0,1:T(4,128)S(1)}, s32[16,4]{0,1:T(4,128)}, u32[]{:S(2)}) %copy-start.6) | copy-done | bytes 280
  5.8 0.0 copy-done.5
  5.8 0.0 copy-done.7
  5.8 0.1 collective-permute-start.6
  5.9 0.1 collective-permute-start.11
  6.0 0.0 collective-permute-done.5
  6.0 0.8 %collective-permute-done.4 = s32[2,1,16]{2,1,0:T(1,128)S(1)} collective-permute-done((s32[2,1,16]{2,1,0:T(1,128)}, s32[2,1,16]{2,1,0:T(1,128)S(1)}, u32[]{:S(2)}, u32[]{:S(2)}) %collective-permute-start.4) | collective-permute-done | bytes 160 | tf_op jit(solution)/shard_map/ppermute | solution.py:26
  6.9 0.6 %collective-permute-done.6.refs_1_ = bf16[1,16,4096]{2,1,0:T(8,128)(2,1)S(1)} collective-permute-done((bf16[1,16,4096]{2,1,0:T(8,128)(2,1)}, bf16[1,16,4096]{2,1,0:T(8,128)(2,1)S(1)}, u32[]{:S(2)}, u32[]{:S(2)}) %collective-permute-start.6) | collective-permute-done | bytes 131104 | tf_op jit(solution)/shard_map/ppermute | solution.py:26
  7.4 3.6 %collective-permute-start.9 = (s32[16,128]{1,0:T(8,128)S(1)}, s32[16,128]{1,0:T(8,128)S(1)}, u32[]{:S(2)}, u32[]{:S(2)}) collective-permute-start(s32[16,128]{1,0:T(8,128)S(1)} %pad_maximum_fusion.refs_0_), channel_id=1, source_target_pairs={{0,12},{4,8},{8,4},{12,0},{1,13},{5,9},{9,5},{13,1},{2,14},{6,10},... | collective-permute-start | bytes 24584 | tf_op jit(solution)/shard_map/ppermute | solution.py:26
  11.0 0.0 collective-permute-start.8
  11.0 0.8 %collective-permute-start.7 = (s32[16,128]{1,0:T(8,128)S(1)}, s32[16,128]{1,0:T(8,128)S(1)}, u32[]{:S(2)}, u32[]{:S(2)}) collective-permute-start(s32[16,128]{1,0:T(8,128)S(1)} %pad_maximum_fusion.refs_0_), channel_id=1, source_target_pairs={{0,4},{4,0},{8,12},{12,8},{1,5},{5,1},{9,13},{13,9},{2,6},{6,2},{1... | collective-permute-start | bytes 24584 | tf_op jit(solution)/shard_map/ppermute | solution.py:26
  11.8 1.0 %copy-done = bf16[16,4,4096]{2,1,0:T(4,128)(2,1)S(1)} copy-done((bf16[16,4,4096]{2,1,0:T(4,128)(2,1)S(1)}, bf16[16,4,4096]{2,1,0:T(4,128)(2,1)}, u32[]{:S(2)}) %copy-start) | copy-done | bytes 524312
  12.9 1.1 %flatten.1 = (bf16[64,4096]{1,0:T(8,128)(2,1)S(1)}, f32[16,128,128]{2,1,0:T(8,128)S(1)}) custom-call(bf16[16,128,128]{2,1,0:T(8,128)(2,1)S(1)} %bitcast.20), custom_call_target="tpu_custom_call" | custom-call | flops 1048576 | bytes 8388608 | tf_op jit(solution)/shard_map/flatten/pallas_call | solution.py:80
  14.0 0.0 collective-permute-done.10.refs_2_
  14.0 0.0 collective-permute-done.11.refs_3_
  14.0 1.6 %collective-permute-done.8.refs_2_ = s32[16,128]{1,0:T(8,128)S(1)} collective-permute-done((s32[16,128]{1,0:T(8,128)S(1)}, s32[16,128]{1,0:T(8,128)S(1)}, u32[]{:S(2)}, u32[]{:S(2)}) %collective-permute-start.8) | collective-permute-done | bytes 8224 | tf_op jit(solution)/shard_map/ppermute | solution.py:26
  15.6 0.0 collective-permute-done.7.refs_1_
  15.6 1.4 %pack.2 = (bf16[512,128]{1,0:T(8,128)(2,1)S(1)}, bf16[512,128]{1,0:T(8,128)(2,1)S(1)}, bf16[512,128]{1,0:T(8,128)(2,1)S(1)}) custom-call(s32[16,128]{1,0:T(8,128)S(1)} %pad_maximum_fusion.refs_0_, s32[16,128]{1,0:T(8,128)S(1)} %collective-permute-done.7.refs_1_, s32[16,128]{1,0:T(8,128)S(1)} %collective-permute-done.8.refs_2_, ...), custom_call_target="tpu_custom_call" | custom-call | flops 1048576 | bytes 4194304 | tf_op jit(solution)/shard_map/pack/pallas_call | solution.py:186
  17.0 2.1 %collective-permute-start.12 = (bf16[512,128]{1,0:T(8,128)(2,1)S(1)}, bf16[512,128]{1,0:T(8,128)(2,1)S(1)}, u32[]{:S(2)}, u32[]{:S(2)}) collective-permute-start(bf16[512,128]{1,0:T(8,128)(2,1)S(1)} %get-tuple-element.104), channel_id=1, source_target_pairs={{0,12},{4,8},{8,4},{12,0},{1,13},{5,9},{9,5},{13,1},{2,14},{6,10},... | collective-permute-start | bytes 393224 | tf_op jit(solution)/shard_map/ppermute | solution.py:26
  19.1 0.0 collective-permute-start.13
  19.1 2.3 %collective-permute-start.14 = (bf16[512,128]{1,0:T(8,128)(2,1)S(1)}, bf16[512,128]{1,0:T(8,128)(2,1)S(1)}, u32[]{:S(2)}, u32[]{:S(2)}) collective-permute-start(bf16[512,128]{1,0:T(8,128)(2,1)S(1)} %get-tuple-element.92), channel_id=1, source_target_pairs={{0,4},{4,0},{8,12},{12,8},{1,5},{5,1},{9,13},{13,9},{2,6},{6,2},{1... | collective-permute-start | bytes 393224 | tf_op jit(solution)/shard_map/ppermute | solution.py:26
  21.4 1.4 %count_rounds.1 = s32[1]{0:T(128)} custom-call(s32[16,128]{1,0:T(8,128)S(1)} %pad_maximum_fusion.refs_0_, s32[16,128]{1,0:T(8,128)S(1)} %collective-permute-done.7.refs_1_, s32[16,128]{1,0:T(8,128)S(1)} %collective-permute-done.8.refs_2_, s32[16,128]{1,0:T(8,128)S(1)} %collective-permute-done.9.refs_3_), custom_call_target="tpu_custom_call" | custom-call | flops 1024 | bytes 1024 | tf_op jit(solution)/shard_map/count_rounds/pallas_call | solution.py:316
  22.8 1.9 %work_list.1.refs_5_.refs_0_ = s32[8,128]{1,0:T(8,128)S(1)} custom-call(s32[16,128]{1,0:T(8,128)S(1)} %pad_maximum_fusion.refs_0_, s32[16,128]{1,0:T(8,128)S(1)} %collective-permute-done.7.refs_1_, s32[16,128]{1,0:T(8,128)S(1)} %collective-permute-done.8.refs_2_, s32[16,128]{1,0:T(8,128)S(1)} %collective-permute-done.9.refs_3_), custom_call_target="tpu_custom_call" | custom-call | flops 1024 | bytes 1024 | tf_op jit(solution)/shard_map/work_list/pallas_call | solution.py:267
  24.7 2.1 %stage.1 = (bf16[2048,128]{1,0:T(8,128)(2,1)S(1)}, f32[16,128,128]{2,1,0:T(8,128)S(1)}) custom-call(bf16[1,16,4096]{2,1,0:T(8,128)(2,1)S(1)} %copy-done.1, bf16[1,16,4096]{2,1,0:T(8,128)(2,1)S(1)} %collective-permute-done.6.refs_1_, bf16[1,16,4096]{2,1,0:T(8,128)(2,1)S(1)} %collective-permute-done.10.refs_2_, ...), custom_call_target="tpu_custom_call" | custom-call | flops 1024 | bytes 1024 | tf_op jit(solution)/shard_map/stage/pallas_call | solution.py:402
  27.4 0.6 %near_products.2.refs_2_ = f32[16,128,128]{2,1,0:T(8,128)S(1)} custom-call(s32[8,128]{1,0:T(8,128)S(1)} %work_list.1.refs_5_.refs_0_, bf16[2048,128]{1,0:T(8,128)(2,1)S(1)} %get-tuple-element.218.refs_1_, f32[16,128,128]{2,1,0:T(8,128)S(1)} %get-tuple-element.103.refs_2_, ...), custom_call_target="tpu_custom_call", output_to_operand_aliasing={{}: (2, {})} | custom-call | flops 1024 | bytes 1024 | tf_op jit(solution)/shard_map/near_products/pallas_call | solution.py:433
  28.1 1.9 %collective-permute-done.13.refs_3_ = bf16[512,128]{1,0:T(8,128)(2,1)S(1)} collective-permute-done((bf16[512,128]{1,0:T(8,128)(2,1)S(1)}, bf16[512,128]{1,0:T(8,128)(2,1)S(1)}, u32[]{:S(2)}, u32[]{:S(2)}) %collective-permute-start.13) | collective-permute-done | bytes 131104 | tf_op jit(solution)/shard_map/ppermute | solution.py:26
  30.0 0.0 collective-permute-done.14.refs_4_
  30.0 2.4 %multiply.2 = (f32[16,128,128]{2,1,0:T(8,128)S(1)}, f32[16,128,128]{2,1,0:T(8,128)}) custom-call(s32[8,128]{1,0:T(8,128)S(1)} %work_list.1.refs_5_.refs_0_, bf16[2048,128]{1,0:T(8,128)(2,1)S(1)} %get-tuple-element.218.refs_1_, f32[16,128,128]{2,1,0:T(8,128)S(1)} %near_products.2.refs_2_, ...), custom_call_target="tpu_custom_call", output_to_operand_aliasing={{0}: (2, {})} | custom-call | flops 67108864 | bytes 4194304 | tf_op jit(solution)/shard_map/multiply/pallas_call | solution.py:462
  (16 shorter events, 0.1 us)
Async XLA Ops:
  0.0 5.9 %collective-permute-start.3 = (s32[2,1,16]{2,1,0:T(1,128)}, s32[2,1,16]{2,1,0:T(1,128)S(1)}, u32[]{:S(2)}, u32[]{:S(2)}) collective-permute-start(s32[2,1,16]{2,1,0:T(1,128)} %param.8), channel_id=1, source_target_pairs={{0,1},{1,0},{2,3},{3,2},{4,5},{5,4},{6,7},{7,6},{8,9},{9,8},{10,11... | collective-permute-start | bytes 392 | tf_op jit(solution)/shard_map/ppermute | solution.py:26
  0.5 5.6 %collective-permute-start.5 = (s32[2,1,16]{2,1,0:T(1,128)}, s32[2,1,16]{2,1,0:T(1,128)S(1)}, u32[]{:S(2)}, u32[]{:S(2)}) collective-permute-start(s32[2,1,16]{2,1,0:T(1,128)} %param.8), channel_id=1, source_target_pairs={{0,3},{1,2},{2,1},{3,0},{4,7},{5,6},{6,5},{7,4},{8,11},{9,10},{10,... | collective-permute-start | bytes 392 | tf_op jit(solution)/shard_map/ppermute | solution.py:26
  3.1 3.8 %collective-permute-start.4 = (s32[2,1,16]{2,1,0:T(1,128)}, s32[2,1,16]{2,1,0:T(1,128)S(1)}, u32[]{:S(2)}, u32[]{:S(2)}) collective-permute-start(s32[2,1,16]{2,1,0:T(1,128)} %param.8), channel_id=1, source_target_pairs={{0,2},{1,3},{2,0},{3,1},{4,6},{5,7},{6,4},{7,5},{8,10},{9,11},{10,... | collective-permute-start | bytes 392 | tf_op jit(solution)/shard_map/ppermute | solution.py:26
  3.1 10.9 %collective-permute-start.10 = (bf16[1,16,4096]{2,1,0:T(8,128)(2,1)}, bf16[1,16,4096]{2,1,0:T(8,128)(2,1)S(1)}, u32[]{:S(2)}, u32[]{:S(2)}) collective-permute-start(bf16[1,16,4096]{2,1,0:T(8,128)(2,1)} %refs_0_.1), channel_id=1, source_target_pairs={{0,2},{1,3},{2,0},{3,1},{4,6},{5,7},{6,4},{7,5},{8,10},{9,11},{10,... | collective-permute-start | bytes 393224 | tf_op jit(solution)/shard_map/ppermute | solution.py:26
  5.1 0.7 %copy-start.6 = (s32[16,4]{0,1:T(4,128)S(1)}, s32[16,4]{0,1:T(4,128)}, u32[]{:S(2)}) copy-start(s32[16,4]{0,1:T(4,128)} %param.11) | copy-start | bytes 772
  5.1 0.7 %copy-start.5 = (s32[16,4]{0,1:T(4,128)S(1)}, s32[16,4]{0,1:T(4,128)}, u32[]{:S(2)}) copy-start(s32[16,4]{0,1:T(4,128)} %param.10) | copy-start | bytes 772
  5.1 0.7 %copy-start.7 = (s32[2,1,16]{2,1,0:T(1,128)S(1)}, s32[2,1,16]{2,1,0:T(1,128)}, u32[]{:S(2)}) copy-start(s32[2,1,16]{2,1,0:T(1,128)} %param.8) | copy-start | bytes 388
  5.8 1.6 %collective-permute-start.6 = (bf16[1,16,4096]{2,1,0:T(8,128)(2,1)}, bf16[1,16,4096]{2,1,0:T(8,128)(2,1)S(1)}, u32[]{:S(2)}, u32[]{:S(2)}) collective-permute-start(bf16[1,16,4096]{2,1,0:T(8,128)(2,1)} %refs_0_.1), channel_id=1, source_target_pairs={{0,1},{1,0},{2,3},{3,2},{4,5},{5,4},{6,7},{7,6},{8,9},{9,8},{10,11... | collective-permute-start | bytes 393224 | tf_op jit(solution)/shard_map/ppermute | solution.py:26
  5.9 8.1 %collective-permute-start.11 = (bf16[1,16,4096]{2,1,0:T(8,128)(2,1)}, bf16[1,16,4096]{2,1,0:T(8,128)(2,1)S(1)}, u32[]{:S(2)}, u32[]{:S(2)}) collective-permute-start(bf16[1,16,4096]{2,1,0:T(8,128)(2,1)} %refs_0_.1), channel_id=1, source_target_pairs={{0,3},{1,2},{2,1},{3,0},{4,7},{5,6},{6,5},{7,4},{8,11},{9,10},{10,... | collective-permute-start | bytes 393224 | tf_op jit(solution)/shard_map/ppermute | solution.py:26
  7.4 6.6 %collective-permute-start.9 = (s32[16,128]{1,0:T(8,128)S(1)}, s32[16,128]{1,0:T(8,128)S(1)}, u32[]{:S(2)}, u32[]{:S(2)}) collective-permute-start(s32[16,128]{1,0:T(8,128)S(1)} %pad_maximum_fusion.refs_0_), channel_id=1, source_target_pairs={{0,12},{4,8},{8,4},{12,0},{1,13},{5,9},{9,5},{13,1},{2,14},{6,10},... | collective-permute-start | bytes 24584 | tf_op jit(solution)/shard_map/ppermute | solution.py:26
  11.0 4.5 %collective-permute-start.8 = (s32[16,128]{1,0:T(8,128)S(1)}, s32[16,128]{1,0:T(8,128)S(1)}, u32[]{:S(2)}, u32[]{:S(2)}) collective-permute-start(s32[16,128]{1,0:T(8,128)S(1)} %pad_maximum_fusion.refs_0_), channel_id=1, source_target_pairs={{0,8},{4,12},{8,0},{12,4},{1,9},{5,13},{9,1},{13,5},{2,10},{6,14},... | collective-permute-start | bytes 24584 | tf_op jit(solution)/shard_map/ppermute | solution.py:26
  11.0 4.5 %collective-permute-start.7 = (s32[16,128]{1,0:T(8,128)S(1)}, s32[16,128]{1,0:T(8,128)S(1)}, u32[]{:S(2)}, u32[]{:S(2)}) collective-permute-start(s32[16,128]{1,0:T(8,128)S(1)} %pad_maximum_fusion.refs_0_), channel_id=1, source_target_pairs={{0,4},{4,0},{8,12},{12,8},{1,5},{5,1},{9,13},{13,9},{2,6},{6,2},{1... | collective-permute-start | bytes 24584 | tf_op jit(solution)/shard_map/ppermute | solution.py:26
  11.8 1.0 %copy-start = (bf16[16,4,4096]{2,1,0:T(4,128)(2,1)S(1)}, bf16[16,4,4096]{2,1,0:T(4,128)(2,1)}, u32[]{:S(2)}) copy-start(bf16[16,4,4096]{2,1,0:T(4,128)(2,1)} %param.9) | copy-start | bytes 1572868
  14.0 5.2 %copy-start.4 = (bf16[64,4096]{1,0:T(8,128)(2,1)}, bf16[64,4096]{1,0:T(8,128)(2,1)S(1)}, u32[]{:S(2)}) copy-start(bf16[64,4096]{1,0:T(8,128)(2,1)S(1)} %get-tuple-element.216.refs_4_) | copy-start | bytes 1572868
  15.6 9.1 %copy-start.1 = (bf16[1,16,4096]{2,1,0:T(8,128)(2,1)S(1)}, bf16[1,16,4096]{2,1,0:T(8,128)(2,1)}, u32[]{:S(2)}) copy-start(bf16[1,16,4096]{2,1,0:T(8,128)(2,1)} %refs_0_.1) | copy-start | bytes 393220
  17.0 10.4 %collective-permute-start.12 = (bf16[512,128]{1,0:T(8,128)(2,1)S(1)}, bf16[512,128]{1,0:T(8,128)(2,1)S(1)}, u32[]{:S(2)}, u32[]{:S(2)}) collective-permute-start(bf16[512,128]{1,0:T(8,128)(2,1)S(1)} %get-tuple-element.104), channel_id=1, source_target_pairs={{0,12},{4,8},{8,4},{12,0},{1,13},{5,9},{9,5},{13,1},{2,14},{6,10},... | collective-permute-start | bytes 393224 | tf_op jit(solution)/shard_map/ppermute | solution.py:26
  19.1 10.9 %collective-permute-start.13 = (bf16[512,128]{1,0:T(8,128)(2,1)S(1)}, bf16[512,128]{1,0:T(8,128)(2,1)S(1)}, u32[]{:S(2)}, u32[]{:S(2)}) collective-permute-start(bf16[512,128]{1,0:T(8,128)(2,1)S(1)} %get-tuple-element.105), channel_id=1, source_target_pairs={{0,8},{4,12},{8,0},{12,4},{1,9},{5,13},{9,1},{13,5},{2,10},{6,14},... | collective-permute-start | bytes 393224 | tf_op jit(solution)/shard_map/ppermute | solution.py:26
  19.1 10.8 %collective-permute-start.14 = (bf16[512,128]{1,0:T(8,128)(2,1)S(1)}, bf16[512,128]{1,0:T(8,128)(2,1)S(1)}, u32[]{:S(2)}, u32[]{:S(2)}) collective-permute-start(bf16[512,128]{1,0:T(8,128)(2,1)S(1)} %get-tuple-element.92), channel_id=1, source_target_pairs={{0,4},{4,0},{8,12},{12,8},{1,5},{5,1},{9,13},{13,9},{2,6},{6,2},{1... | collective-permute-start | bytes 393224 | tf_op jit(solution)/shard_map/ppermute | solution.py:26
  26.8 3.2 %copy-start.2 = (bf16[2048,128]{1,0:T(8,128)(2,1)}, bf16[2048,128]{1,0:T(8,128)(2,1)S(1)}, u32[]{:S(2)}) copy-start(bf16[2048,128]{1,0:T(8,128)(2,1)S(1)} %get-tuple-element.218.refs_1_) | copy-start | bytes 1572868

commit v10 on v9

--- a/solution.py
+++ b/solution.py
@@ -11,6 +11,7 @@
 BS = 64
 LANES = 128
 ROWS = BS * BS // LANES
+PADDING = 8
 CAPACITY = 16
 UNROLL = 4
 SLOTS = 4
@@ -68,7 +69,7 @@
 
 def flatten_kernel(b_ref, flat, wide):
     row_count = b_ref.shape[0]
-    wide[...] = b_ref[...].astype(F32)
+    wide[:, 0 : SLOTS * ROWS, :] = b_ref[...].astype(F32)
     for t in range(ROWS):
         for n in range(SLOTS):
             piece = wide[:, t * SLOTS + n, :].astype(BF16)
@@ -81,7 +82,7 @@
         flatten_kernel,
         out_shape=(
             jax.ShapeDtypeStruct((b_rows.shape[0] * SLOTS, BS * BS), BF16),
-            jax.ShapeDtypeStruct(b_rows.shape, F32),
+            jax.ShapeDtypeStruct((b_rows.shape[0], SLOTS * ROWS + PADDING, LANES), F32),
         ),
         in_specs=[vmem_spec],
         out_specs=(vmem_spec,) * 2,
@@ -174,7 +175,7 @@
     for d in range(1, peers):
         out = outs[d - 1]
         for x in range(CAPACITY):
-            out[pl.ds(x * ROWS, ROWS), :] = packed[(d - 1) * CAPACITY + x].astype(BF16)
+            out[pl.ds(x * ROWS, ROWS), :] = packed[(d - 1) * CAPACITY + x, 0:ROWS, :].astype(BF16)
 
 
 def pack(base, told, flat, cols, row_count, a_slots):
@@ -190,7 +191,7 @@
         out_specs=[vmem_spec] * (peers - 1),
         scratch_shapes=[
             VMEM(((peers - 1) * CAPACITY, LANES), BF16),
-            VMEM(((peers - 1) * CAPACITY, ROWS, LANES), F32),
+            VMEM(((peers - 1) * CAPACITY, ROWS + PADDING, LANES), F32),
         ],
         compiler_params=pltpu.CompilerParams(vmem_limit_bytes=32 << 20),
         cost_estimate=pl.CostEstimate(flops=1 << 20, bytes_accessed=4 << 20, transcendentals=0),
@@ -391,7 +392,7 @@
         first = (grid_col ^ h) * slots
         for s in range(slots):
             at = pl.multiple_of((first + s) * ROWS, ROWS)
-            a_out[pl.ds(at, ROWS), :] = a_wide[h * slots + s].astype(BF16)
+            a_out[pl.ds(at, ROWS), :] = a_wide[h * slots + s, 0:ROWS, :].astype(BF16)
     add_products(items, a_out, [(0, own)], sums)
 
 
@@ -403,12 +404,12 @@
         functools.partial(stage_kernel, cols),
         out_shape=(
             jax.ShapeDtypeStruct((cols * slots * ROWS, LANES), BF16),
-            jax.ShapeDtypeStruct(wide.shape, F32),
+            jax.ShapeDtypeStruct((wide.shape[0], SLOTS * ROWS, LANES), F32),
         ),
         in_specs=[vmem_spec] * (cols + 1) + [smem_spec],
         out_specs=(vmem_spec,) * 2,
         scratch_shapes=[
-            VMEM((cols * slots, ROWS, LANES), F32),
+            VMEM((cols * slots, ROWS + PADDING, LANES), F32),
             VMEM((wide.shape[0] * SLOTS * ROWS, LANES), BF16),
         ],
         compiler_params=pltpu.CompilerParams(vmem_limit_bytes=40 << 20),

time: 32.6 us -> 32.4 us (level)
  other arithmetic: 0.02 us -> 0.73 us
  local copies, waits for them, and re-layouts: 1.76 us -> 1.06 us
  Pallas kernels: 10.9 us -> 10.5 us
    max x1, other arithmetic: 0.01 us -> 0.72 us  [describe(): jnp.maximum(own, placed(a_parts[0][:, 0, :], 0))]
    unnamed x14 -> x10, local copies, waits for them, and re-layouts: 1.76 us -> 1.06 us
    pallas_call x1, Pallas kernels: 2.06 us -> 1.54 us  [stage(): pl.pallas_call(functools.partial(stage_kernel, cols), out_shape=(jax.Shap...]
    pallas_call x1, Pallas kernels: 0.62 us -> 1.07 us  [near_products(): pl.pallas_call(functools.partial(near_kernel, first, chosen), out_shape=j...]
  transfers between devices with their start and end apart: 12 -> 12, of which waited for: 4 -> 4; matrix products, arithmetic and copies ran while one was open for 0% -> 2% of each run, Pallas kernels for 22% -> 22%
where the time goes in v10:
time: 32.4 us; the launch traced here: 32.2 us
  starting transfers between devices  14.1 us (44%)
  Pallas kernels  10.5 us (32%)
  waiting for transfers between devices  4.92 us (15%)
  local copies, waits for them, and re-layouts  1.06 us (3%)
  between operations  0.79 us (2%)
  other arithmetic  0.73 us (2%)
    ppermute x12, starting transfers between devices, exchanged(): return lax.ppermute(block, axis, [(i, i ^ distance) for i in range(size)])  14.1 us
    ppermute x12, waiting for transfers between devices, exchanged(): return lax.ppermute(block, axis, [(i, i ^ distance) for i in range(size)])  4.92 us
    pallas_call x1, Pallas kernels, multiply(): pl.pallas_call(functools.partial(multiply_kernel, first, chosen), out_sha...  2.16 us
    pallas_call x1, Pallas kernels, work_list(): pl.pallas_call(functools.partial(list_kernel, cols, a_slots, row_count, p...  1.91 us
    pallas_call x1, Pallas kernels, stage(): pl.pallas_call(functools.partial(stage_kernel, cols), out_shape=(jax.Shap...  1.54 us
    pallas_call x1, Pallas kernels, pack(): pl.pallas_call(functools.partial(pack_kernel, first, peers, cols, a_slots...  1.37 us
    pallas_call x1, Pallas kernels, count_rounds(): pl.pallas_call(functools.partial(rounds_kernel, cols, a_slots, row_count,...  1.35 us
    pallas_call x1, Pallas kernels, flatten(): pl.pallas_call(flatten_kernel, out_shape=(jax.ShapeDtypeStruct((b_rows.sh...  1.11 us
  transfers between devices with their start and end apart: 12, of which 4 were waited for; matrix products, arithmetic and copies ran while one was open for 2% of the time, Pallas kernels for 22%

profile of v10, /device:TPU:0, one launch (start us, length us, event | category | flops | bytes accessed | tf_op | source)
XLA Modules:
  0.0 32.2 jit_solution(2948685200173621736)
XLA Ops:
  0.0 0.5 %collective-permute-start.3 = (s32[2,1,16]{2,1,0:T(1,128)}, s32[2,1,16]{2,1,0:T(1,128)S(1)}, u32[]{:S(2)}, u32[]{:S(2)}) collective-permute-start(s32[2,1,16]{2,1,0:T(1,128)} %param.8), channel_id=1, source_target_pairs={{0,1},{1,0},{2,3},{3,2},{4,5},{5,4},{6,7},{7,6},{8,9},{9,8},{10,11... | collective-permute-start | bytes 392 | tf_op jit(solution)/shard_map/ppermute | solution.py:27
  0.5 2.6 %collective-permute-start.5 = (s32[2,1,16]{2,1,0:T(1,128)}, s32[2,1,16]{2,1,0:T(1,128)S(1)}, u32[]{:S(2)}, u32[]{:S(2)}) collective-permute-start(s32[2,1,16]{2,1,0:T(1,128)} %param.8), channel_id=1, source_target_pairs={{0,3},{1,2},{2,1},{3,0},{4,7},{5,6},{6,5},{7,4},{8,11},{9,10},{10,... | collective-permute-start | bytes 392 | tf_op jit(solution)/shard_map/ppermute | solution.py:27
  3.1 0.0 collective-permute-start.4
  3.1 2.0 %collective-permute-start.10 = (bf16[1,16,4096]{2,1,0:T(8,128)(2,1)}, bf16[1,16,4096]{2,1,0:T(8,128)(2,1)S(1)}, u32[]{:S(2)}, u32[]{:S(2)}) collective-permute-start(bf16[1,16,4096]{2,1,0:T(8,128)(2,1)} %refs_0_.1), channel_id=1, source_target_pairs={{0,2},{1,3},{2,0},{3,1},{4,6},{5,7},{6,4},{7,5},{8,10},{9,11},{10,... | collective-permute-start | bytes 393224 | tf_op jit(solution)/shard_map/ppermute | solution.py:27
  5.1 0.7 %pad_maximum_fusion.1 = s32[16,128]{1,0:T(8,128)S(1)} fusion(s32[2,16]{1,0:T(2,128)} %bitcast.26, s32[4,16]{1,0:T(4,128)} %bitcast.21, s32[4,16]{1,0:T(4,128)} %bitcast.22), kind=kLoop, calls=%fused_computation.1 | loop fusion | flops 4096 | bytes 8832 | tf_op jit(solution)/shard_map/max | solution.py:53
  5.8 0.1 collective-permute-start.6
  5.9 0.0 collective-permute-done.3
  5.9 0.2 collective-permute-start.11
  6.0 0.0 collective-permute-done.5
  6.0 0.8 %collective-permute-done.4 = s32[2,1,16]{2,1,0:T(1,128)S(1)} collective-permute-done((s32[2,1,16]{2,1,0:T(1,128)}, s32[2,1,16]{2,1,0:T(1,128)S(1)}, u32[]{:S(2)}, u32[]{:S(2)}) %collective-permute-start.4) | collective-permute-done | bytes 160 | tf_op jit(solution)/shard_map/ppermute | solution.py:27
  6.9 0.6 %collective-permute-done.6.refs_1_ = bf16[1,16,4096]{2,1,0:T(8,128)(2,1)S(1)} collective-permute-done((bf16[1,16,4096]{2,1,0:T(8,128)(2,1)}, bf16[1,16,4096]{2,1,0:T(8,128)(2,1)S(1)}, u32[]{:S(2)}, u32[]{:S(2)}) %collective-permute-start.6) | collective-permute-done | bytes 131104 | tf_op jit(solution)/shard_map/ppermute | solution.py:27
  7.4 3.6 %collective-permute-start.9 = (s32[16,128]{1,0:T(8,128)S(1)}, s32[16,128]{1,0:T(8,128)S(1)}, u32[]{:S(2)}, u32[]{:S(2)}) collective-permute-start(s32[16,128]{1,0:T(8,128)S(1)} %pad_maximum_fusion.refs_0_), channel_id=1, source_target_pairs={{0,12},{4,8},{8,4},{12,0},{1,13},{5,9},{9,5},{13,1},{2,14},{6,10},... | collective-permute-start | bytes 24584 | tf_op jit(solution)/shard_map/ppermute | solution.py:27
  11.0 0.0 collective-permute-start.8
  11.0 0.8 %collective-permute-start.7 = (s32[16,128]{1,0:T(8,128)S(1)}, s32[16,128]{1,0:T(8,128)S(1)}, u32[]{:S(2)}, u32[]{:S(2)}) collective-permute-start(s32[16,128]{1,0:T(8,128)S(1)} %pad_maximum_fusion.refs_0_), channel_id=1, source_target_pairs={{0,4},{4,0},{8,12},{12,8},{1,5},{5,1},{9,13},{13,9},{2,6},{6,2},{1... | collective-permute-start | bytes 24584 | tf_op jit(solution)/shard_map/ppermute | solution.py:27
  11.8 1.0 %copy-done = bf16[16,4,4096]{2,1,0:T(4,128)(2,1)S(1)} copy-done((bf16[16,4,4096]{2,1,0:T(4,128)(2,1)S(1)}, bf16[16,4,4096]{2,1,0:T(4,128)(2,1)}, u32[]{:S(2)}) %copy-start) | copy-done | bytes 524312
  12.9 1.1 %flatten.1 = (bf16[64,4096]{1,0:T(8,128)(2,1)S(1)}, f32[16,136,128]{2,1,0:T(8,128)S(1)}) custom-call(bf16[16,128,128]{2,1,0:T(8,128)(2,1)S(1)} %bitcast.20), custom_call_target="tpu_custom_call" | custom-call | flops 1048576 | bytes 8388608 | tf_op jit(solution)/shard_map/flatten/pallas_call | solution.py:81
  14.0 0.0 collective-permute-done.10.refs_2_
  14.0 0.0 collective-permute-done.11.refs_3_
  14.0 0.0 collective-permute-done.9.refs_3_
  14.0 1.6 %collective-permute-done.8.refs_2_ = s32[16,128]{1,0:T(8,128)S(1)} collective-permute-done((s32[16,128]{1,0:T(8,128)S(1)}, s32[16,128]{1,0:T(8,128)S(1)}, u32[]{:S(2)}, u32[]{:S(2)}) %collective-permute-start.8) | collective-permute-done | bytes 8224 | tf_op jit(solution)/shard_map/ppermute | solution.py:27
  15.6 0.0 collective-permute-done.7.refs_1_
  15.6 1.4 %pack.2 = (bf16[512,128]{1,0:T(8,128)(2,1)S(1)}, bf16[512,128]{1,0:T(8,128)(2,1)S(1)}, bf16[512,128]{1,0:T(8,128)(2,1)S(1)}) custom-call(s32[16,128]{1,0:T(8,128)S(1)} %pad_maximum_fusion.refs_0_, s32[16,128]{1,0:T(8,128)S(1)} %collective-permute-done.7.refs_1_, s32[16,128]{1,0:T(8,128)S(1)} %collective-permute-done.8.refs_2_, ...), custom_call_target="tpu_custom_call" | custom-call | flops 1048576 | bytes 4194304 | tf_op jit(solution)/shard_map/pack/pallas_call | solution.py:187
  17.0 2.1 %collective-permute-start.12 = (bf16[512,128]{1,0:T(8,128)(2,1)S(1)}, bf16[512,128]{1,0:T(8,128)(2,1)S(1)}, u32[]{:S(2)}, u32[]{:S(2)}) collective-permute-start(bf16[512,128]{1,0:T(8,128)(2,1)S(1)} %get-tuple-element.104), channel_id=1, source_target_pairs={{0,12},{4,8},{8,4},{12,0},{1,13},{5,9},{9,5},{13,1},{2,14},{6,10},... | collective-permute-start | bytes 393224 | tf_op jit(solution)/shard_map/ppermute | solution.py:27
  19.1 0.0 collective-permute-start.13
  19.1 2.3 %collective-permute-start.14 = (bf16[512,128]{1,0:T(8,128)(2,1)S(1)}, bf16[512,128]{1,0:T(8,128)(2,1)S(1)}, u32[]{:S(2)}, u32[]{:S(2)}) collective-permute-start(bf16[512,128]{1,0:T(8,128)(2,1)S(1)} %get-tuple-element.92), channel_id=1, source_target_pairs={{0,4},{4,0},{8,12},{12,8},{1,5},{5,1},{9,13},{13,9},{2,6},{6,2},{1... | collective-permute-start | bytes 393224 | tf_op jit(solution)/shard_map/ppermute | solution.py:27
  21.4 1.4 %count_rounds.1 = s32[1]{0:T(128)} custom-call(s32[16,128]{1,0:T(8,128)S(1)} %pad_maximum_fusion.refs_0_, s32[16,128]{1,0:T(8,128)S(1)} %collective-permute-done.7.refs_1_, s32[16,128]{1,0:T(8,128)S(1)} %collective-permute-done.8.refs_2_, s32[16,128]{1,0:T(8,128)S(1)} %collective-permute-done.9.refs_3_), custom_call_target="tpu_custom_call" | custom-call | flops 1024 | bytes 1024 | tf_op jit(solution)/shard_map/count_rounds/pallas_call | solution.py:317
  22.8 1.9 %work_list.1.refs_5_.refs_0_ = s32[8,128]{1,0:T(8,128)S(1)} custom-call(s32[16,128]{1,0:T(8,128)S(1)} %pad_maximum_fusion.refs_0_, s32[16,128]{1,0:T(8,128)S(1)} %collective-permute-done.7.refs_1_, s32[16,128]{1,0:T(8,128)S(1)} %collective-permute-done.8.refs_2_, s32[16,128]{1,0:T(8,128)S(1)} %collective-permute-done.9.refs_3_), custom_call_target="tpu_custom_call" | custom-call | flops 1024 | bytes 1024 | tf_op jit(solution)/shard_map/work_list/pallas_call | solution.py:268
  24.7 1.5 %stage.1 = (bf16[2048,128]{1,0:T(8,128)(2,1)S(1)}, f32[16,128,128]{2,1,0:T(8,128)S(1)}) custom-call(bf16[1,16,4096]{2,1,0:T(8,128)(2,1)S(1)} %copy-done.1, bf16[1,16,4096]{2,1,0:T(8,128)(2,1)S(1)} %collective-permute-done.6.refs_1_, bf16[1,16,4096]{2,1,0:T(8,128)(2,1)S(1)} %collective-permute-done.10.refs_2_, ...), custom_call_target="tpu_custom_call" | custom-call | flops 1024 | bytes 1024 | tf_op jit(solution)/shard_map/stage/pallas_call | solution.py:403
  26.9 0.0 collective-permute-done.12.refs_3_
  26.9 1.1 %near_products.2.refs_2_ = f32[16,128,128]{2,1,0:T(8,128)S(1)} custom-call(s32[8,128]{1,0:T(8,128)S(1)} %work_list.1.refs_5_.refs_0_, bf16[2048,128]{1,0:T(8,128)(2,1)S(1)} %get-tuple-element.218.refs_1_, f32[16,128,128]{2,1,0:T(8,128)S(1)} %get-tuple-element.103.refs_2_, ...), custom_call_target="tpu_custom_call", output_to_operand_aliasing={{}: (2, {})} | custom-call | flops 1024 | bytes 1024 | tf_op jit(solution)/shard_map/near_products/pallas_call | solution.py:434
  28.0 2.0 %collective-permute-done.13.refs_3_ = bf16[512,128]{1,0:T(8,128)(2,1)S(1)} collective-permute-done((bf16[512,128]{1,0:T(8,128)(2,1)S(1)}, bf16[512,128]{1,0:T(8,128)(2,1)S(1)}, u32[]{:S(2)}, u32[]{:S(2)}) %collective-permute-start.13) | collective-permute-done | bytes 131104 | tf_op jit(solution)/shard_map/ppermute | solution.py:27
  30.0 2.2 %multiply.2 = (f32[16,128,128]{2,1,0:T(8,128)S(1)}, f32[16,128,128]{2,1,0:T(8,128)}) custom-call(s32[8,128]{1,0:T(8,128)S(1)} %work_list.1.refs_5_.refs_0_, bf16[2048,128]{1,0:T(8,128)(2,1)S(1)} %get-tuple-element.218.refs_1_, f32[16,128,128]{2,1,0:T(8,128)S(1)} %near_products.2.refs_2_, ...), custom_call_target="tpu_custom_call", output_to_operand_aliasing={{0}: (2, {})} | custom-call | flops 67108864 | bytes 4194304 | tf_op jit(solution)/shard_map/multiply/pallas_call | solution.py:463
  (12 shorter events, 0.0 us)
Async XLA Ops:
  0.0 5.9 %collective-permute-start.3 = (s32[2,1,16]{2,1,0:T(1,128)}, s32[2,1,16]{2,1,0:T(1,128)S(1)}, u32[]{:S(2)}, u32[]{:S(2)}) collective-permute-start(s32[2,1,16]{2,1,0:T(1,128)} %param.8), channel_id=1, source_target_pairs={{0,1},{1,0},{2,3},{3,2},{4,5},{5,4},{6,7},{7,6},{8,9},{9,8},{10,11... | collective-permute-start | bytes 392 | tf_op jit(solution)/shard_map/ppermute | solution.py:27
  0.5 5.6 %collective-permute-start.5 = (s32[2,1,16]{2,1,0:T(1,128)}, s32[2,1,16]{2,1,0:T(1,128)S(1)}, u32[]{:S(2)}, u32[]{:S(2)}) collective-permute-start(s32[2,1,16]{2,1,0:T(1,128)} %param.8), channel_id=1, source_target_pairs={{0,3},{1,2},{2,1},{3,0},{4,7},{5,6},{6,5},{7,4},{8,11},{9,10},{10,... | collective-permute-start | bytes 392 | tf_op jit(solution)/shard_map/ppermute | solution.py:27
  3.1 3.8 %collective-permute-start.4 = (s32[2,1,16]{2,1,0:T(1,128)}, s32[2,1,16]{2,1,0:T(1,128)S(1)}, u32[]{:S(2)}, u32[]{:S(2)}) collective-permute-start(s32[2,1,16]{2,1,0:T(1,128)} %param.8), channel_id=1, source_target_pairs={{0,2},{1,3},{2,0},{3,1},{4,6},{5,7},{6,4},{7,5},{8,10},{9,11},{10,... | collective-permute-start | bytes 392 | tf_op jit(solution)/shard_map/ppermute | solution.py:27
  3.1 10.9 %collective-permute-start.10 = (bf16[1,16,4096]{2,1,0:T(8,128)(2,1)}, bf16[1,16,4096]{2,1,0:T(8,128)(2,1)S(1)}, u32[]{:S(2)}, u32[]{:S(2)}) collective-permute-start(bf16[1,16,4096]{2,1,0:T(8,128)(2,1)} %refs_0_.1), channel_id=1, source_target_pairs={{0,2},{1,3},{2,0},{3,1},{4,6},{5,7},{6,4},{7,5},{8,10},{9,11},{10,... | collective-permute-start | bytes 393224 | tf_op jit(solution)/shard_map/ppermute | solution.py:27
  5.8 1.6 %collective-permute-start.6 = (bf16[1,16,4096]{2,1,0:T(8,128)(2,1)}, bf16[1,16,4096]{2,1,0:T(8,128)(2,1)S(1)}, u32[]{:S(2)}, u32[]{:S(2)}) collective-permute-start(bf16[1,16,4096]{2,1,0:T(8,128)(2,1)} %refs_0_.1), channel_id=1, source_target_pairs={{0,1},{1,0},{2,3},{3,2},{4,5},{5,4},{6,7},{7,6},{8,9},{9,8},{10,11... | collective-permute-start | bytes 393224 | tf_op jit(solution)/shard_map/ppermute | solution.py:27
  5.9 8.1 %collective-permute-start.11 = (bf16[1,16,4096]{2,1,0:T(8,128)(2,1)}, bf16[1,16,4096]{2,1,0:T(8,128)(2,1)S(1)}, u32[]{:S(2)}, u32[]{:S(2)}) collective-permute-start(bf16[1,16,4096]{2,1,0:T(8,128)(2,1)} %refs_0_.1), channel_id=1, source_target_pairs={{0,3},{1,2},{2,1},{3,0},{4,7},{5,6},{6,5},{7,4},{8,11},{9,10},{10,... | collective-permute-start | bytes 393224 | tf_op jit(solution)/shard_map/ppermute | solution.py:27
  7.4 6.6 %collective-permute-start.9 = (s32[16,128]{1,0:T(8,128)S(1)}, s32[16,128]{1,0:T(8,128)S(1)}, u32[]{:S(2)}, u32[]{:S(2)}) collective-permute-start(s32[16,128]{1,0:T(8,128)S(1)} %pad_maximum_fusion.refs_0_), channel_id=1, source_target_pairs={{0,12},{4,8},{8,4},{12,0},{1,13},{5,9},{9,5},{13,1},{2,14},{6,10},... | collective-permute-start | bytes 24584 | tf_op jit(solution)/shard_map/ppermute | solution.py:27
  11.0 4.5 %collective-permute-start.8 = (s32[16,128]{1,0:T(8,128)S(1)}, s32[16,128]{1,0:T(8,128)S(1)}, u32[]{:S(2)}, u32[]{:S(2)}) collective-permute-start(s32[16,128]{1,0:T(8,128)S(1)} %pad_maximum_fusion.refs_0_), channel_id=1, source_target_pairs={{0,8},{4,12},{8,0},{12,4},{1,9},{5,13},{9,1},{13,5},{2,10},{6,14},... | collective-permute-start | bytes 24584 | tf_op jit(solution)/shard_map/ppermute | solution.py:27
  11.0 4.5 %collective-permute-start.7 = (s32[16,128]{1,0:T(8,128)S(1)}, s32[16,128]{1,0:T(8,128)S(1)}, u32[]{:S(2)}, u32[]{:S(2)}) collective-permute-start(s32[16,128]{1,0:T(8,128)S(1)} %pad_maximum_fusion.refs_0_), channel_id=1, source_target_pairs={{0,4},{4,0},{8,12},{12,8},{1,5},{5,1},{9,13},{13,9},{2,6},{6,2},{1... | collective-permute-start | bytes 24584 | tf_op jit(solution)/shard_map/ppermute | solution.py:27
  11.8 1.0 %copy-start = (bf16[16,4,4096]{2,1,0:T(4,128)(2,1)S(1)}, bf16[16,4,4096]{2,1,0:T(4,128)(2,1)}, u32[]{:S(2)}) copy-start(bf16[16,4,4096]{2,1,0:T(4,128)(2,1)} %param.9) | copy-start | bytes 1572868
  12.9 11.8 %copy-start.1 = (bf16[1,16,4096]{2,1,0:T(8,128)(2,1)S(1)}, bf16[1,16,4096]{2,1,0:T(8,128)(2,1)}, u32[]{:S(2)}) copy-start(bf16[1,16,4096]{2,1,0:T(8,128)(2,1)} %refs_0_.1) | copy-start | bytes 393220
  14.0 5.2 %copy-start.4 = (bf16[64,4096]{1,0:T(8,128)(2,1)}, bf16[64,4096]{1,0:T(8,128)(2,1)S(1)}, u32[]{:S(2)}) copy-start(bf16[64,4096]{1,0:T(8,128)(2,1)S(1)} %get-tuple-element.216.refs_4_) | copy-start | bytes 1572868
  17.0 9.9 %collective-permute-start.12 = (bf16[512,128]{1,0:T(8,128)(2,1)S(1)}, bf16[512,128]{1,0:T(8,128)(2,1)S(1)}, u32[]{:S(2)}, u32[]{:S(2)}) collective-permute-start(bf16[512,128]{1,0:T(8,128)(2,1)S(1)} %get-tuple-element.104), channel_id=1, source_target_pairs={{0,12},{4,8},{8,4},{12,0},{1,13},{5,9},{9,5},{13,1},{2,14},{6,10},... | collective-permute-start | bytes 393224 | tf_op jit(solution)/shard_map/ppermute | solution.py:27
  19.1 10.9 %collective-permute-start.13 = (bf16[512,128]{1,0:T(8,128)(2,1)S(1)}, bf16[512,128]{1,0:T(8,128)(2,1)S(1)}, u32[]{:S(2)}, u32[]{:S(2)}) collective-permute-start(bf16[512,128]{1,0:T(8,128)(2,1)S(1)} %get-tuple-element.105), channel_id=1, source_target_pairs={{0,8},{4,12},{8,0},{12,4},{1,9},{5,13},{9,1},{13,5},{2,10},{6,14},... | collective-permute-start | bytes 393224 | tf_op jit(solution)/shard_map/ppermute | solution.py:27
  19.1 10.8 %collective-permute-start.14 = (bf16[512,128]{1,0:T(8,128)(2,1)S(1)}, bf16[512,128]{1,0:T(8,128)(2,1)S(1)}, u32[]{:S(2)}, u32[]{:S(2)}) collective-permute-start(bf16[512,128]{1,0:T(8,128)(2,1)S(1)} %get-tuple-element.92), channel_id=1, source_target_pairs={{0,4},{4,0},{8,12},{12,8},{1,5},{5,1},{9,13},{13,9},{2,6},{6,2},{1... | collective-permute-start | bytes 393224 | tf_op jit(solution)/shard_map/ppermute | solution.py:27
  26.2 3.7 %copy-start.2 = (bf16[2048,128]{1,0:T(8,128)(2,1)}, bf16[2048,128]{1,0:T(8,128)(2,1)S(1)}, u32[]{:S(2)}) copy-start(bf16[2048,128]{1,0:T(8,128)(2,1)S(1)} %get-tuple-element.218.refs_1_) | copy-start | bytes 1572868
  28.0 4.2 %copy-start.5 = (bf16[64,4096]{1,0:T(8,128)(2,1)S(1)}, bf16[64,4096]{1,0:T(8,128)(2,1)}, u32[]{:S(2)}) copy-start(bf16[64,4096]{1,0:T(8,128)(2,1)} %copy-done.4) | copy-start | bytes 1572868

commit v11 on v10

--- a/solution.py
+++ b/solution.py
@@ -11,6 +11,8 @@
 BS = 64
 LANES = 128
 ROWS = BS * BS // LANES
+GROUP = 16
+PIECES = 4
 PADDING = 8
 CAPACITY = 16
 UNROLL = 4
@@ -65,31 +67,6 @@
         moved = pltpu.roll(rows, n * row_count, 1)[n : n + 1]
         result = jnp.where(lane // row_count == n, moved, result)
     return result
-
-
-def flatten_kernel(b_ref, flat, wide):
-    row_count = b_ref.shape[0]
-    wide[:, 0 : SLOTS * ROWS, :] = b_ref[...].astype(F32)
-    for t in range(ROWS):
-        for n in range(SLOTS):
-            piece = wide[:, t * SLOTS + n, :].astype(BF16)
-            flat[pl.ds(n * row_count, row_count), pl.ds(t * LANES, LANES)] = piece
-
-
-def flatten(b_rows):
-    vmem_spec = pl.BlockSpec(memory_space=VMEM)
-    return pl.pallas_call(
-        flatten_kernel,
-        out_shape=(
-            jax.ShapeDtypeStruct((b_rows.shape[0] * SLOTS, BS * BS), BF16),
-            jax.ShapeDtypeStruct((b_rows.shape[0], SLOTS * ROWS + PADDING, LANES), F32),
-        ),
-        in_specs=[vmem_spec],
-        out_specs=(vmem_spec,) * 2,
-        compiler_params=pltpu.CompilerParams(vmem_limit_bytes=24 << 20),
-        cost_estimate=pl.CostEstimate(flops=1 << 20, bytes_accessed=8 << 20, transcendentals=0),
-        name="flatten",
-    )(b_rows)
 
 
 def iota(shape, axis):
@@ -151,9 +128,11 @@
     refs = list(refs)
     base = 0 if first else refs.pop(0)[0]
     told = refs[:peers]
-    flat = refs[peers]
+    b_any = refs[peers]
     outs = refs[peers + 1 : 2 * peers]
-    picks, packed = refs[2 * peers :]
+    b_ref, picks, packed, sem = refs[2 * peers :]
+    loading = pltpu.make_async_copy(b_any, b_ref, sem.at[0])
+    loading.start()
     grid_row = lax.axis_index("row")
     per_col = peers // cols
     offered = offers(told[0], cols, row_count)
@@ -166,19 +145,28 @@
         place = jnp.where(needed > 0.5, places(needed), -1.0).astype(I32)
         pick = (place == iota((CAPACITY, LANES), 0) + base).astype(BF16)
         picks[pl.ds((d - 1) * CAPACITY, CAPACITY), :] = pick
-    pick = picks[...][:, : flat.shape[0]]
-    for t in range(0, ROWS, 2):
-        both = flat[:, pl.ds(t * LANES, 2 * LANES)]
-        both = jnp.dot(pick, both, preferred_element_type=F32)
-        packed[:, t, :] = both[:, :LANES]
-        packed[:, t + 1, :] = both[:, LANES:]
+    steps = GROUP // SLOTS
+    count = row_count * GROUP
+    lane = iota((LANES, count), 1)
+    spread = iota((LANES, count), 0) == lane % SLOTS * row_count + lane // GROUP
+    spread = jnp.dot(picks[...], spread.astype(BF16), preferred_element_type=F32)
+    lane = iota(spread.shape, 1)
+    wanted = [jnp.where(lane // SLOTS % steps == t, spread, 0.0) for t in range(steps)]
+    wanted = jnp.concatenate(wanted, axis=0).astype(BF16)
+    total = spread.shape[0]
+    loading.wait()
+    for at in range(0, ROWS, steps):
+        rows = b_ref[:, at * SLOTS : (at + steps) * SLOTS, :].reshape(count, LANES)
+        found = jnp.dot(wanted, rows, preferred_element_type=F32)
+        for t in range(steps):
+            packed[:, at + t, :] = found[t * total : (t + 1) * total]
     for d in range(1, peers):
         out = outs[d - 1]
         for x in range(CAPACITY):
             out[pl.ds(x * ROWS, ROWS), :] = packed[(d - 1) * CAPACITY + x, 0:ROWS, :].astype(BF16)
 
 
-def pack(base, told, flat, cols, row_count, a_slots):
+def pack(base, told, b_rows, cols, row_count, a_slots):
     first = base is None
     peers = len(told)
     smem_spec = pl.BlockSpec(memory_space=SMEM)
@@ -187,16 +175,20 @@
     return pl.pallas_call(
         functools.partial(pack_kernel, first, peers, cols, a_slots, row_count),
         out_shape=[jax.ShapeDtypeStruct((CAPACITY * ROWS, LANES), BF16)] * (peers - 1),
-        in_specs=[smem_spec] * len(given) + [vmem_spec] * (peers + 1),
+        in_specs=[smem_spec] * len(given)
+        + [vmem_spec] * peers
+        + [pl.BlockSpec(memory_space=pl.ANY)],
         out_specs=[vmem_spec] * (peers - 1),
         scratch_shapes=[
+            VMEM(b_rows.shape, BF16),
             VMEM(((peers - 1) * CAPACITY, LANES), BF16),
             VMEM(((peers - 1) * CAPACITY, ROWS + PADDING, LANES), F32),
+            pltpu.SemaphoreType.DMA((1,)),
         ],
         compiler_params=pltpu.CompilerParams(vmem_limit_bytes=32 << 20),
         cost_estimate=pl.CostEstimate(flops=1 << 20, bytes_accessed=4 << 20, transcendentals=0),
         name="pack",
-    )(*given, *told, flat)
+    )(*given, *told, b_rows)
 
 
 def list_kernel(cols, a_slots, row_count, peers, *refs):
@@ -370,8 +362,9 @@
 
 
 def stage_kernel(cols, *refs):
-    a_refs, wide, items = refs[:cols], refs[cols], refs[cols + 1]
-    a_out, sums, a_wide, own = refs[cols + 2 :]
+    a_refs, b_ref, items = refs[:cols], refs[cols], refs[cols + 1]
+    a_out, sums, a_wide, wide, own = refs[cols + 2 :]
+    wide[...] = b_ref[...].astype(F32)
     sums[...] = jnp.zeros_like(sums)
     row_count = wide.shape[0]
     for n in range(SLOTS):
@@ -396,7 +389,7 @@
     add_products(items, a_out, [(0, own)], sums)
 
 
-def stage(a_parts, wide, items):
+def stage(a_parts, b_rows, items):
     cols, slots = len(a_parts), a_parts[0].shape[1]
     vmem_spec = pl.BlockSpec(memory_space=VMEM)
     smem_spec = pl.BlockSpec(memory_space=SMEM)
@@ -404,18 +397,19 @@
         functools.partial(stage_kernel, cols),
         out_shape=(
             jax.ShapeDtypeStruct((cols * slots * ROWS, LANES), BF16),
-            jax.ShapeDtypeStruct((wide.shape[0], SLOTS * ROWS, LANES), F32),
+            jax.ShapeDtypeStruct(b_rows.shape, F32),
         ),
         in_specs=[vmem_spec] * (cols + 1) + [smem_spec],
         out_specs=(vmem_spec,) * 2,
         scratch_shapes=[
             VMEM((cols * slots, ROWS + PADDING, LANES), F32),
-            VMEM((wide.shape[0] * SLOTS * ROWS, LANES), BF16),
+            VMEM(b_rows.shape, F32),
+            VMEM((b_rows.shape[0] * SLOTS * ROWS, LANES), BF16),
         ],
         compiler_params=pltpu.CompilerParams(vmem_limit_bytes=40 << 20),
         cost_estimate=pl.CostEstimate(flops=1 << 10, bytes_accessed=1 << 10, transcendentals=0),
         name="stage",
-    )(*a_parts, wide, items)
+    )(*a_parts, b_rows, items)
 
 
 def near_kernel(first, chosen, *refs):
@@ -450,9 +444,15 @@
     b_refs = refs[3 : 3 + len(chosen)]
     sums, out, sem = refs[3 + len(chosen) :]
     add_products(items, a_ref, list(zip(chosen, b_refs)), sums, window=base)
-    copy = pltpu.make_async_copy(sums, out, sem.at[0])
-    copy.start()
-    copy.wait()
+    part = out.shape[0] // PIECES
+    copies = [
+        pltpu.make_async_copy(sums.at[pl.ds(p * part, part)], out.at[pl.ds(p * part, part)], sem.at[p])
+        for p in range(PIECES)
+    ]
+    for copy in copies:
+        copy.start()
+    for copy in copies:
+        copy.wait()
 
 
 def multiply(base, chosen, items, a_ready, sums, b_parts):
@@ -466,7 +466,7 @@
         in_specs=[smem_spec] * (len(given) + 1) + [vmem_spec] * (2 + len(chosen)),
         out_specs=[vmem_spec, pl.BlockSpec(memory_space=pl.ANY)],
         input_output_aliases={len(given) + 2: 0},
-        scratch_shapes=[pltpu.SemaphoreType.DMA((1,))],
+        scratch_shapes=[pltpu.SemaphoreType.DMA((PIECES,))],
         compiler_params=pltpu.CompilerParams(vmem_limit_bytes=32 << 20),
         cost_estimate=pl.CostEstimate(flops=1 << 26, bytes_accessed=4 << 20, transcendentals=0),
         name="multiply",
@@ -497,14 +497,14 @@
         far = exchanged(a_blocks, "col", h)
         a_parts += [far, exchanged(a_blocks, "col", h + 1)]
     told = [told] + send_rows([told] * (rows - 1))
-    flat, wide = flatten(seen_by_rows(b_blocks))
-    flat, *a_parts = lax.optimization_barrier((flat, *a_parts))
-    packed = pack(None, told, flat, cols, row_count, a_slots)
+    b_rows = seen_by_rows(b_blocks)
+    *a_parts, b_rows = lax.optimization_barrier((*a_parts, b_rows))
+    packed = pack(None, told, b_rows, cols, row_count, a_slots)
     arrived = send_rows(packed)
     told_late = lax.optimization_barrier((told, packed[0]))[0]
     items = work_list(told_late, cols, row_count, a_slots)
     rounds = jnp.minimum(count_rounds(told_late, cols, row_count, a_slots)[0], LANES)
-    a_ready, sums = stage([a_blocks] + a_parts, wide, items)
+    a_ready, sums = stage([a_blocks] + a_parts, b_rows, items)
     sums, rounds = lax.optimization_barrier((sums, rounds))
     sums, out = finish(None, sums, arrived)
 
@@ -514,7 +514,7 @@
     def one_round(state):
         at, sums, _ = state
         base = jnp.reshape(at * CAPACITY, (1,))
-        arrived = send_rows(pack(base, told, flat, cols, row_count, a_slots))
+        arrived = send_rows(pack(base, told, b_rows, cols, row_count, a_slots))
         return at + 1, *finish(base, sums, arrived)
 
     return seen_by_blocks(lax.while_loop(more, one_round, (jnp.int32(1), sums, out))[2])

time: 32.4 us -> 33 us (1.019)
  waiting for transfers between devices: 4.92 us -> 6.82 us
  local copies, waits for them, and re-layouts: 1.06 us -> 0.01 us
    ppermute x12, waiting for transfers between devices: 4.92 us -> 6.82 us  [exchanged(): return lax.ppermute(block, axis, [(i, i ^ distance) for i in range(size)])]
    pallas_call x1 -> x0, Pallas kernels: 1.11 us -> none  [flatten(): pl.pallas_call(flatten_kernel, out_shape=(jax.ShapeDtypeStruct((b_rows.sh...]
    unnamed x10 -> x4, local copies, waits for them, and re-layouts: 1.06 us -> 0.01 us
    pallas_call x1, Pallas kernels: 1.54 us -> 2.05 us  [stage(): pl.pallas_call(functools.partial(stage_kernel, cols), out_shape=(jax.Shap...]
    pallas_call x1, Pallas kernels: 1.37 us -> 1.78 us  [pack(): pl.pallas_call(functools.partial(pack_kernel, first, peers, cols, a_slots...]
  transfers between devices with their start and end apart: 12 -> 12, of which waited for: 4 -> 5; matrix products, arithmetic and copies ran while one was open for 2% -> 2% of each run, Pallas kernels for 22% -> 19%
where the time goes in v11:
time: 33 us; the launch traced here: 32.9 us
  starting transfers between devices  14.1 us (43%)
  Pallas kernels  10.4 us (32%)
  waiting for transfers between devices  6.82 us (21%)
  between operations  0.74 us (2%)
  other arithmetic  0.73 us (2%)
    ppermute x12, starting transfers between devices, exchanged(): return lax.ppermute(block, axis, [(i, i ^ distance) for i in range(size)])  14.1 us
    ppermute x12, waiting for transfers between devices, exchanged(): return lax.ppermute(block, axis, [(i, i ^ distance) for i in range(size)])  6.82 us
    pallas_call x1, Pallas kernels, multiply(): pl.pallas_call(functools.partial(multiply_kernel, first, chosen), out_sha...  2.46 us
    pallas_call x1, Pallas kernels, stage(): pl.pallas_call(functools.partial(stage_kernel, cols), out_shape=(jax.Shap...  2.05 us
    pallas_call x1, Pallas kernels, work_list(): pl.pallas_call(functools.partial(list_kernel, cols, a_slots, row_count, p...  1.91 us
    pallas_call x1, Pallas kernels, pack(): pl.pallas_call(functools.partial(pack_kernel, first, peers, cols, a_slots...  1.78 us
    pallas_call x1, Pallas kernels, count_rounds(): pl.pallas_call(functools.partial(rounds_kernel, cols, a_slots, row_count,...  1.35 us
    pallas_call x1, Pallas kernels, near_products(): pl.pallas_call(functools.partial(near_kernel, first, chosen), out_shape=j...  0.84 us
  transfers between devices with their start and end apart: 12, of which 5 were waited for; matrix products, arithmetic and copies ran while one was open for 2% of the time, Pallas kernels for 19%

profile of v11, /device:TPU:0, one launch (start us, length us, event | category | flops | bytes accessed | tf_op | source)
XLA Modules:
  0.0 32.9 jit_solution(13226917784457022166)
XLA Ops:
  0.0 0.5 %collective-permute-start.3 = (s32[2,1,16]{2,1,0:T(1,128)}, s32[2,1,16]{2,1,0:T(1,128)S(1)}, u32[]{:S(2)}, u32[]{:S(2)}) collective-permute-start(s32[2,1,16]{2,1,0:T(1,128)} %param.8), channel_id=1, source_target_pairs={{0,1},{1,0},{2,3},{3,2},{4,5},{5,4},{6,7},{7,6},{8,9},{9,8},{10,11... | collective-permute-start | bytes 392 | tf_op jit(solution)/shard_map/ppermute | solution.py:29
  0.5 2.6 %collective-permute-start.5 = (s32[2,1,16]{2,1,0:T(1,128)}, s32[2,1,16]{2,1,0:T(1,128)S(1)}, u32[]{:S(2)}, u32[]{:S(2)}) collective-permute-start(s32[2,1,16]{2,1,0:T(1,128)} %param.8), channel_id=1, source_target_pairs={{0,3},{1,2},{2,1},{3,0},{4,7},{5,6},{6,5},{7,4},{8,11},{9,10},{10,... | collective-permute-start | bytes 392 | tf_op jit(solution)/shard_map/ppermute | solution.py:29
  3.1 0.1 collective-permute-start.4
  3.1 2.0 %collective-permute-start.10 = (bf16[1,16,4096]{2,1,0:T(8,128)(2,1)}, bf16[1,16,4096]{2,1,0:T(8,128)(2,1)S(1)}, u32[]{:S(2)}, u32[]{:S(2)}) collective-permute-start(bf16[1,16,4096]{2,1,0:T(8,128)(2,1)} %refs_0_.1), channel_id=1, source_target_pairs={{0,2},{1,3},{2,0},{3,1},{4,6},{5,7},{6,4},{7,5},{8,10},{9,11},{10,... | collective-permute-start | bytes 393224 | tf_op jit(solution)/shard_map/ppermute | solution.py:29
  5.1 0.7 %pad_maximum_fusion.1 = s32[16,128]{1,0:T(8,128)S(1)} fusion(s32[2,16]{1,0:T(2,128)} %bitcast.28, s32[4,16]{1,0:T(4,128)} %bitcast.23, s32[4,16]{1,0:T(4,128)} %bitcast.24), kind=kLoop, calls=%fused_computation.1 | loop fusion | flops 4096 | bytes 8832 | tf_op jit(solution)/shard_map/max | solution.py:55
  5.8 0.1 collective-permute-start.6
  5.9 0.0 collective-permute-done.3
  5.9 0.2 collective-permute-start.11
  6.1 0.0 collective-permute-done.5
  6.1 0.8 %collective-permute-done.4 = s32[2,1,16]{2,1,0:T(1,128)S(1)} collective-permute-done((s32[2,1,16]{2,1,0:T(1,128)}, s32[2,1,16]{2,1,0:T(1,128)S(1)}, u32[]{:S(2)}, u32[]{:S(2)}) %collective-permute-start.4) | collective-permute-done | bytes 160 | tf_op jit(solution)/shard_map/ppermute | solution.py:29
  6.9 0.6 %collective-permute-done.6.refs_1_ = bf16[1,16,4096]{2,1,0:T(8,128)(2,1)S(1)} collective-permute-done((bf16[1,16,4096]{2,1,0:T(8,128)(2,1)}, bf16[1,16,4096]{2,1,0:T(8,128)(2,1)S(1)}, u32[]{:S(2)}, u32[]{:S(2)}) %collective-permute-start.6) | collective-permute-done | bytes 131104 | tf_op jit(solution)/shard_map/ppermute | solution.py:29
  7.4 3.6 %collective-permute-start.9 = (s32[16,128]{1,0:T(8,128)S(1)}, s32[16,128]{1,0:T(8,128)S(1)}, u32[]{:S(2)}, u32[]{:S(2)}) collective-permute-start(s32[16,128]{1,0:T(8,128)S(1)} %pad_maximum_fusion.refs_0_), channel_id=1, source_target_pairs={{0,12},{4,8},{8,4},{12,0},{1,13},{5,9},{9,5},{13,1},{2,14},{6,10},... | collective-permute-start | bytes 24584 | tf_op jit(solution)/shard_map/ppermute | solution.py:29
  11.0 0.0 collective-permute-start.8
  11.0 0.8 %collective-permute-start.7 = (s32[16,128]{1,0:T(8,128)S(1)}, s32[16,128]{1,0:T(8,128)S(1)}, u32[]{:S(2)}, u32[]{:S(2)}) collective-permute-start(s32[16,128]{1,0:T(8,128)S(1)} %pad_maximum_fusion.refs_0_), channel_id=1, source_target_pairs={{0,4},{4,0},{8,12},{12,8},{1,5},{5,1},{9,13},{13,9},{2,6},{6,2},{1... | collective-permute-start | bytes 24584 | tf_op jit(solution)/shard_map/ppermute | solution.py:29
  11.8 0.0 collective-permute-done.10.refs_2_
  11.8 0.0 collective-permute-done.11.refs_3_
  11.8 1.1 %collective-permute-done.9.refs_3_ = s32[16,128]{1,0:T(8,128)S(1)} collective-permute-done((s32[16,128]{1,0:T(8,128)S(1)}, s32[16,128]{1,0:T(8,128)S(1)}, u32[]{:S(2)}, u32[]{:S(2)}) %collective-permute-start.9) | collective-permute-done | bytes 8224 | tf_op jit(solution)/shard_map/ppermute | solution.py:29
  12.9 2.7 %collective-permute-done.8.refs_2_ = s32[16,128]{1,0:T(8,128)S(1)} collective-permute-done((s32[16,128]{1,0:T(8,128)S(1)}, s32[16,128]{1,0:T(8,128)S(1)}, u32[]{:S(2)}, u32[]{:S(2)}) %collective-permute-start.8) | collective-permute-done | bytes 8224 | tf_op jit(solution)/shard_map/ppermute | solution.py:29
  15.6 0.0 collective-permute-done.7.refs_1_
  15.6 1.8 %pack.2 = (bf16[512,128]{1,0:T(8,128)(2,1)S(1)}, bf16[512,128]{1,0:T(8,128)(2,1)S(1)}, bf16[512,128]{1,0:T(8,128)(2,1)S(1)}) custom-call(s32[16,128]{1,0:T(8,128)S(1)} %pad_maximum_fusion.refs_0_, s32[16,128]{1,0:T(8,128)S(1)} %collective-permute-done.7.refs_1_, s32[16,128]{1,0:T(8,128)S(1)} %collective-permute-done.8.refs_2_, ...), custom_call_target="tpu_custom_call" | custom-call | flops 1048576 | bytes 4194304 | tf_op jit(solution)/shard_map/pack/pallas_call | solution.py:175
  17.4 1.5 %collective-permute-start.12 = (bf16[512,128]{1,0:T(8,128)(2,1)S(1)}, bf16[512,128]{1,0:T(8,128)(2,1)S(1)}, u32[]{:S(2)}, u32[]{:S(2)}) collective-permute-start(bf16[512,128]{1,0:T(8,128)(2,1)S(1)} %get-tuple-element.100), channel_id=1, source_target_pairs={{0,12},{4,8},{8,4},{12,0},{1,13},{5,9},{9,5},{13,1},{2,14},{6,10},... | collective-permute-start | bytes 393224 | tf_op jit(solution)/shard_map/ppermute | solution.py:29
  18.9 0.6 %collective-permute-start.13 = (bf16[512,128]{1,0:T(8,128)(2,1)S(1)}, bf16[512,128]{1,0:T(8,128)(2,1)S(1)}, u32[]{:S(2)}, u32[]{:S(2)}) collective-permute-start(bf16[512,128]{1,0:T(8,128)(2,1)S(1)} %get-tuple-element.101), channel_id=1, source_target_pairs={{0,8},{4,12},{8,0},{12,4},{1,9},{5,13},{9,1},{13,5},{2,10},{6,14},... | collective-permute-start | bytes 393224 | tf_op jit(solution)/shard_map/ppermute | solution.py:29
  19.5 2.3 %collective-permute-start.14 = (bf16[512,128]{1,0:T(8,128)(2,1)S(1)}, bf16[512,128]{1,0:T(8,128)(2,1)S(1)}, u32[]{:S(2)}, u32[]{:S(2)}) collective-permute-start(bf16[512,128]{1,0:T(8,128)(2,1)S(1)} %get-tuple-element.89), channel_id=1, source_target_pairs={{0,4},{4,0},{8,12},{12,8},{1,5},{5,1},{9,13},{13,9},{2,6},{6,2},{1... | collective-permute-start | bytes 393224 | tf_op jit(solution)/shard_map/ppermute | solution.py:29
  21.8 1.4 %count_rounds.1 = s32[1]{0:T(128)} custom-call(s32[16,128]{1,0:T(8,128)S(1)} %pad_maximum_fusion.refs_0_, s32[16,128]{1,0:T(8,128)S(1)} %collective-permute-done.7.refs_1_, s32[16,128]{1,0:T(8,128)S(1)} %collective-permute-done.8.refs_2_, s32[16,128]{1,0:T(8,128)S(1)} %collective-permute-done.9.refs_3_), custom_call_target="tpu_custom_call" | custom-call | flops 1024 | bytes 1024 | tf_op jit(solution)/shard_map/count_rounds/pallas_call | solution.py:309
  23.2 1.9 %work_list.1.refs_5_.refs_0_ = s32[8,128]{1,0:T(8,128)S(1)} custom-call(s32[16,128]{1,0:T(8,128)S(1)} %pad_maximum_fusion.refs_0_, s32[16,128]{1,0:T(8,128)S(1)} %collective-permute-done.7.refs_1_, s32[16,128]{1,0:T(8,128)S(1)} %collective-permute-done.8.refs_2_, s32[16,128]{1,0:T(8,128)S(1)} %collective-permute-done.9.refs_3_), custom_call_target="tpu_custom_call" | custom-call | flops 1024 | bytes 1024 | tf_op jit(solution)/shard_map/work_list/pallas_call | solution.py:260
  25.1 0.0 copy-done
  25.1 2.1 %stage.1 = (bf16[2048,128]{1,0:T(8,128)(2,1)S(1)}, f32[16,128,128]{2,1,0:T(8,128)S(1)}) custom-call(bf16[1,16,4096]{2,1,0:T(8,128)(2,1)S(1)} %copy-done, bf16[1,16,4096]{2,1,0:T(8,128)(2,1)S(1)} %collective-permute-done.6.refs_1_, bf16[1,16,4096]{2,1,0:T(8,128)(2,1)S(1)} %collective-permute-done.10.refs_2_, ...), custom_call_target="tpu_custom_call" | custom-call | flops 1024 | bytes 1024 | tf_op jit(solution)/shard_map/stage/pallas_call | solution.py:396
  27.8 0.0 collective-permute-done.12.refs_3_
  27.8 0.8 %near_products.2.refs_2_ = f32[16,128,128]{2,1,0:T(8,128)S(1)} custom-call(s32[8,128]{1,0:T(8,128)S(1)} %work_list.1.refs_5_.refs_0_, bf16[2048,128]{1,0:T(8,128)(2,1)S(1)} %get-tuple-element.214.refs_1_, f32[16,128,128]{2,1,0:T(8,128)S(1)} %get-tuple-element.99.refs_2_, ...), custom_call_target="tpu_custom_call", output_to_operand_aliasing={{}: (2, {})} | custom-call | flops 1024 | bytes 1024 | tf_op jit(solution)/shard_map/near_products/pallas_call | solution.py:428
  28.7 1.7 %collective-permute-done.13.refs_3_ = bf16[512,128]{1,0:T(8,128)(2,1)S(1)} collective-permute-done((bf16[512,128]{1,0:T(8,128)(2,1)S(1)}, bf16[512,128]{1,0:T(8,128)(2,1)S(1)}, u32[]{:S(2)}, u32[]{:S(2)}) %collective-permute-start.13) | collective-permute-done | bytes 131104 | tf_op jit(solution)/shard_map/ppermute | solution.py:29
  30.4 0.0 collective-permute-done.14.refs_4_
  30.4 2.5 %multiply.2 = (f32[16,128,128]{2,1,0:T(8,128)S(1)}, f32[16,128,128]{2,1,0:T(8,128)}) custom-call(s32[8,128]{1,0:T(8,128)S(1)} %work_list.1.refs_5_.refs_0_, bf16[2048,128]{1,0:T(8,128)(2,1)S(1)} %get-tuple-element.214.refs_1_, f32[16,128,128]{2,1,0:T(8,128)S(1)} %near_products.2.refs_2_, ...), custom_call_target="tpu_custom_call", output_to_operand_aliasing={{0}: (2, {})} | custom-call | flops 67108864 | bytes 4194304 | tf_op jit(solution)/shard_map/multiply/pallas_call | solution.py:463
  (5 shorter events, 0.0 us)
Async XLA Ops:
  0.0 25.1 %copy-start.1 = (bf16[16,4,4096]{2,1,0:T(4,128)(2,1)S(1)}, bf16[16,4,4096]{2,1,0:T(4,128)(2,1)}, u32[]{:S(2)}) copy-start(bf16[16,4,4096]{2,1,0:T(4,128)(2,1)} %param.9) | copy-start | bytes 1572868
  0.0 5.9 %collective-permute-start.3 = (s32[2,1,16]{2,1,0:T(1,128)}, s32[2,1,16]{2,1,0:T(1,128)S(1)}, u32[]{:S(2)}, u32[]{:S(2)}) collective-permute-start(s32[2,1,16]{2,1,0:T(1,128)} %param.8), channel_id=1, source_target_pairs={{0,1},{1,0},{2,3},{3,2},{4,5},{5,4},{6,7},{7,6},{8,9},{9,8},{10,11... | collective-permute-start | bytes 392 | tf_op jit(solution)/shard_map/ppermute | solution.py:29
  0.5 5.6 %collective-permute-start.5 = (s32[2,1,16]{2,1,0:T(1,128)}, s32[2,1,16]{2,1,0:T(1,128)S(1)}, u32[]{:S(2)}, u32[]{:S(2)}) collective-permute-start(s32[2,1,16]{2,1,0:T(1,128)} %param.8), channel_id=1, source_target_pairs={{0,3},{1,2},{2,1},{3,0},{4,7},{5,6},{6,5},{7,4},{8,11},{9,10},{10,... | collective-permute-start | bytes 392 | tf_op jit(solution)/shard_map/ppermute | solution.py:29
  3.1 3.8 %collective-permute-start.4 = (s32[2,1,16]{2,1,0:T(1,128)}, s32[2,1,16]{2,1,0:T(1,128)S(1)}, u32[]{:S(2)}, u32[]{:S(2)}) collective-permute-start(s32[2,1,16]{2,1,0:T(1,128)} %param.8), channel_id=1, source_target_pairs={{0,2},{1,3},{2,0},{3,1},{4,6},{5,7},{6,4},{7,5},{8,10},{9,11},{10,... | collective-permute-start | bytes 392 | tf_op jit(solution)/shard_map/ppermute | solution.py:29
  3.1 8.7 %collective-permute-start.10 = (bf16[1,16,4096]{2,1,0:T(8,128)(2,1)}, bf16[1,16,4096]{2,1,0:T(8,128)(2,1)S(1)}, u32[]{:S(2)}, u32[]{:S(2)}) collective-permute-start(bf16[1,16,4096]{2,1,0:T(8,128)(2,1)} %refs_0_.1), channel_id=1, source_target_pairs={{0,2},{1,3},{2,0},{3,1},{4,6},{5,7},{6,4},{7,5},{8,10},{9,11},{10,... | collective-permute-start | bytes 393224 | tf_op jit(solution)/shard_map/ppermute | solution.py:29
  5.8 1.6 %collective-permute-start.6 = (bf16[1,16,4096]{2,1,0:T(8,128)(2,1)}, bf16[1,16,4096]{2,1,0:T(8,128)(2,1)S(1)}, u32[]{:S(2)}, u32[]{:S(2)}) collective-permute-start(bf16[1,16,4096]{2,1,0:T(8,128)(2,1)} %refs_0_.1), channel_id=1, source_target_pairs={{0,1},{1,0},{2,3},{3,2},{4,5},{5,4},{6,7},{7,6},{8,9},{9,8},{10,11... | collective-permute-start | bytes 393224 | tf_op jit(solution)/shard_map/ppermute | solution.py:29
  5.9 5.9 %collective-permute-start.11 = (bf16[1,16,4096]{2,1,0:T(8,128)(2,1)}, bf16[1,16,4096]{2,1,0:T(8,128)(2,1)S(1)}, u32[]{:S(2)}, u32[]{:S(2)}) collective-permute-start(bf16[1,16,4096]{2,1,0:T(8,128)(2,1)} %refs_0_.1), channel_id=1, source_target_pairs={{0,3},{1,2},{2,1},{3,0},{4,7},{5,6},{6,5},{7,4},{8,11},{9,10},{10,... | collective-permute-start | bytes 393224 | tf_op jit(solution)/shard_map/ppermute | solution.py:29
  7.4 5.4 %collective-permute-start.9 = (s32[16,128]{1,0:T(8,128)S(1)}, s32[16,128]{1,0:T(8,128)S(1)}, u32[]{:S(2)}, u32[]{:S(2)}) collective-permute-start(s32[16,128]{1,0:T(8,128)S(1)} %pad_maximum_fusion.refs_0_), channel_id=1, source_target_pairs={{0,12},{4,8},{8,4},{12,0},{1,13},{5,9},{9,5},{13,1},{2,14},{6,10},... | collective-permute-start | bytes 24584 | tf_op jit(solution)/shard_map/ppermute | solution.py:29
  11.0 4.5 %collective-permute-start.8 = (s32[16,128]{1,0:T(8,128)S(1)}, s32[16,128]{1,0:T(8,128)S(1)}, u32[]{:S(2)}, u32[]{:S(2)}) collective-permute-start(s32[16,128]{1,0:T(8,128)S(1)} %pad_maximum_fusion.refs_0_), channel_id=1, source_target_pairs={{0,8},{4,12},{8,0},{12,4},{1,9},{5,13},{9,1},{13,5},{2,10},{6,14},... | collective-permute-start | bytes 24584 | tf_op jit(solution)/shard_map/ppermute | solution.py:29
  11.0 4.5 %collective-permute-start.7 = (s32[16,128]{1,0:T(8,128)S(1)}, s32[16,128]{1,0:T(8,128)S(1)}, u32[]{:S(2)}, u32[]{:S(2)}) collective-permute-start(s32[16,128]{1,0:T(8,128)S(1)} %pad_maximum_fusion.refs_0_), channel_id=1, source_target_pairs={{0,4},{4,0},{8,12},{12,8},{1,5},{5,1},{9,13},{13,9},{2,6},{6,2},{1... | collective-permute-start | bytes 24584 | tf_op jit(solution)/shard_map/ppermute | solution.py:29
  15.6 9.5 %copy-start = (bf16[1,16,4096]{2,1,0:T(8,128)(2,1)S(1)}, bf16[1,16,4096]{2,1,0:T(8,128)(2,1)}, u32[]{:S(2)}) copy-start(bf16[1,16,4096]{2,1,0:T(8,128)(2,1)} %refs_0_.1) | copy-start | bytes 393220
  17.4 10.5 %collective-permute-start.12 = (bf16[512,128]{1,0:T(8,128)(2,1)S(1)}, bf16[512,128]{1,0:T(8,128)(2,1)S(1)}, u32[]{:S(2)}, u32[]{:S(2)}) collective-permute-start(bf16[512,128]{1,0:T(8,128)(2,1)S(1)} %get-tuple-element.100), channel_id=1, source_target_pairs={{0,12},{4,8},{8,4},{12,0},{1,13},{5,9},{9,5},{13,1},{2,14},{6,10},... | collective-permute-start | bytes 393224 | tf_op jit(solution)/shard_map/ppermute | solution.py:29
  18.9 11.5 %collective-permute-start.13 = (bf16[512,128]{1,0:T(8,128)(2,1)S(1)}, bf16[512,128]{1,0:T(8,128)(2,1)S(1)}, u32[]{:S(2)}, u32[]{:S(2)}) collective-permute-start(bf16[512,128]{1,0:T(8,128)(2,1)S(1)} %get-tuple-element.101), channel_id=1, source_target_pairs={{0,8},{4,12},{8,0},{12,4},{1,9},{5,13},{9,1},{13,5},{2,10},{6,14},... | collective-permute-start | bytes 393224 | tf_op jit(solution)/shard_map/ppermute | solution.py:29
  19.5 10.8 %collective-permute-start.14 = (bf16[512,128]{1,0:T(8,128)(2,1)S(1)}, bf16[512,128]{1,0:T(8,128)(2,1)S(1)}, u32[]{:S(2)}, u32[]{:S(2)}) collective-permute-start(bf16[512,128]{1,0:T(8,128)(2,1)S(1)} %get-tuple-element.89), channel_id=1, source_target_pairs={{0,4},{4,0},{8,12},{12,8},{1,5},{5,1},{9,13},{13,9},{2,6},{6,2},{1... | collective-permute-start | bytes 393224 | tf_op jit(solution)/shard_map/ppermute | solution.py:29

commit v12 on v11

--- a/solution.py
+++ b/solution.py
@@ -124,71 +124,73 @@
     return jnp.dot(many, before, preferred_element_type=F32)[0:1]
 
 
-def pack_kernel(first, peers, cols, a_slots, row_count, *refs):
+def pack_kernel(first, load, chosen, peers, cols, a_slots, row_count, *refs):
     refs = list(refs)
     base = 0 if first else refs.pop(0)[0]
-    told = refs[:peers]
-    b_any = refs[peers]
-    outs = refs[peers + 1 : 2 * peers]
-    b_ref, picks, packed, sem = refs[2 * peers :]
-    loading = pltpu.make_async_copy(b_any, b_ref, sem.at[0])
-    loading.start()
+    count = len(chosen)
+    told, refs = refs[: count + 1], refs[count + 1 :]
+    b_ref, outs, refs = refs[0], refs[1 : count + 1], refs[count + 1 :]
+    if load:
+        b_any, b_ref, sem = b_ref, refs.pop(), refs.pop()
+        loading = pltpu.make_async_copy(b_any, b_ref, sem.at[0])
+        loading.start()
+    picks, packed = refs
     grid_row = lax.axis_index("row")
     per_col = peers // cols
     offered = offers(told[0], cols, row_count)
     first_slot = grid_row % per_col * a_slots if per_col > 1 else 0
-    for d in range(1, peers):
+    for at in range(count):
         pairs, _, _ = matches(
-            told[d], offered, grid_row // per_col, cols, row_count, first_slot, a_slots
+            told[at + 1], offered, grid_row // per_col, cols, row_count, first_slot, a_slots
         )
         needed = jnp.max(pairs, axis=0, keepdims=True)
         place = jnp.where(needed > 0.5, places(needed), -1.0).astype(I32)
         pick = (place == iota((CAPACITY, LANES), 0) + base).astype(BF16)
-        picks[pl.ds((d - 1) * CAPACITY, CAPACITY), :] = pick
+        picks[pl.ds(at * CAPACITY, CAPACITY), :] = pick
     steps = GROUP // SLOTS
-    count = row_count * GROUP
-    lane = iota((LANES, count), 1)
-    spread = iota((LANES, count), 0) == lane % SLOTS * row_count + lane // GROUP
+    depth = row_count * GROUP
+    lane = iota((LANES, depth), 1)
+    spread = iota((LANES, depth), 0) == lane % SLOTS * row_count + lane // GROUP
     spread = jnp.dot(picks[...], spread.astype(BF16), preferred_element_type=F32)
     lane = iota(spread.shape, 1)
     wanted = [jnp.where(lane // SLOTS % steps == t, spread, 0.0) for t in range(steps)]
     wanted = jnp.concatenate(wanted, axis=0).astype(BF16)
     total = spread.shape[0]
-    loading.wait()
+    if load:
+        loading.wait()
     for at in range(0, ROWS, steps):
-        rows = b_ref[:, at * SLOTS : (at + steps) * SLOTS, :].reshape(count, LANES)
+        rows = b_ref[:, at * SLOTS : (at + steps) * SLOTS, :].reshape(depth, LANES)
         found = jnp.dot(wanted, rows, preferred_element_type=F32)
         for t in range(steps):
             packed[:, at + t, :] = found[t * total : (t + 1) * total]
-    for d in range(1, peers):
-        out = outs[d - 1]
+    for at in range(count):
         for x in range(CAPACITY):
-            out[pl.ds(x * ROWS, ROWS), :] = packed[(d - 1) * CAPACITY + x, 0:ROWS, :].astype(BF16)
-
-
-def pack(base, told, b_rows, cols, row_count, a_slots):
+            block = packed[at * CAPACITY + x, 0:ROWS, :].astype(BF16)
+            outs[at][pl.ds(x * ROWS, ROWS), :] = block
+
+
+def pack(base, load, chosen, told, b_rows, cols, row_count, a_slots):
     first = base is None
     peers = len(told)
     smem_spec = pl.BlockSpec(memory_space=SMEM)
     vmem_spec = pl.BlockSpec(memory_space=VMEM)
     given = [] if first else [base]
+    message = jax.ShapeDtypeStruct((CAPACITY * ROWS, LANES), BF16)
+    loaded = [pltpu.SemaphoreType.DMA((1,)), VMEM(b_rows.shape, BF16)] if load else []
+    held = len(chosen) * CAPACITY
     return pl.pallas_call(
-        functools.partial(pack_kernel, first, peers, cols, a_slots, row_count),
-        out_shape=[jax.ShapeDtypeStruct((CAPACITY * ROWS, LANES), BF16)] * (peers - 1),
+        functools.partial(pack_kernel, first, load, chosen, peers, cols, a_slots, row_count),
+        out_shape=[message] * len(chosen),
         in_specs=[smem_spec] * len(given)
-        + [vmem_spec] * peers
-        + [pl.BlockSpec(memory_space=pl.ANY)],
-        out_specs=[vmem_spec] * (peers - 1),
-        scratch_shapes=[
-            VMEM(b_rows.shape, BF16),
-            VMEM(((peers - 1) * CAPACITY, LANES), BF16),
-            VMEM(((peers - 1) * CAPACITY, ROWS + PADDING, LANES), F32),
-            pltpu.SemaphoreType.DMA((1,)),
-        ],
+        + [vmem_spec] * (len(chosen) + 1)
+        + [pl.BlockSpec(memory_space=pl.ANY) if load else vmem_spec],
+        out_specs=[vmem_spec] * len(chosen),
+        scratch_shapes=[VMEM((held, LANES), BF16), VMEM((held, ROWS + PADDING, LANES), F32)]
+        + loaded,
         compiler_params=pltpu.CompilerParams(vmem_limit_bytes=32 << 20),
         cost_estimate=pl.CostEstimate(flops=1 << 20, bytes_accessed=4 << 20, transcendentals=0),
         name="pack",
-    )(*given, *told, b_rows)
+    )(*given, told[0], *[told[d] for d in chosen], b_rows)
 
 
 def list_kernel(cols, a_slots, row_count, peers, *refs):
@@ -497,10 +499,14 @@
         far = exchanged(a_blocks, "col", h)
         a_parts += [far, exchanged(a_blocks, "col", h + 1)]
     told = [told] + send_rows([told] * (rows - 1))
+    far = rows - 1
+    others = list(range(1, far))
     b_rows = seen_by_rows(b_blocks)
+    message = pack(None, True, [far], told, b_rows, cols, row_count, a_slots)[0]
+    arrived_far = exchanged(message, "row", far)
     *a_parts, b_rows = lax.optimization_barrier((*a_parts, b_rows))
-    packed = pack(None, told, b_rows, cols, row_count, a_slots)
-    arrived = send_rows(packed)
+    packed = pack(None, False, others, told, b_rows, cols, row_count, a_slots)
+    arrived = [exchanged(packed[d - 1], "row", d) for d in others[::-1]][::-1] + [arrived_far]
     told_late = lax.optimization_barrier((told, packed[0]))[0]
     items = work_list(told_late, cols, row_count, a_slots)
     rounds = jnp.minimum(count_rounds(told_late, cols, row_count, a_slots)[0], LANES)
@@ -514,7 +520,9 @@
     def one_round(state):
         at, sums, _ = state
         base = jnp.reshape(at * CAPACITY, (1,))
-        arrived = send_rows(pack(base, told, b_rows, cols, row_count, a_slots))
+        arrived = send_rows(
+            pack(base, False, list(range(1, rows)), told, b_rows, cols, row_count, a_slots)
+        )
         return at + 1, *finish(base, sums, arrived)
 
     return seen_by_blocks(lax.while_loop(more, one_round, (jnp.int32(1), sums, out))[2])

time: 33 us -> 30.6 us (0.927)
  waiting for transfers between devices: 6.82 us -> 3.15 us
  Pallas kernels: 10.4 us -> 11.7 us
    ppermute x12, waiting for transfers between devices: 6.82 us -> 3.15 us  [exchanged(): return lax.ppermute(block, axis, [(i, i ^ distance) for i in range(size)])]
    pallas_call x1 -> x2, Pallas kernels: 1.78 us -> 2.63 us  [pack(): pl.pallas_call(functools.partial(pack_kernel, first, load, chosen, peers,...]
  transfers between devices with their start and end apart: 12 -> 12, of which waited for: 5 -> 4; matrix products, arithmetic and copies ran while one was open for 2% -> 2% of each run, Pallas kernels for 19% -> 30%
where the time goes in v12:
time: 30.6 us
  starting transfers between devices  14.2 us (46%)
  Pallas kernels  11.7 us (38%)
  waiting for transfers between devices  3.15 us (10%)
  between operations  0.76 us (2%)
  other arithmetic  0.73 us (2%)
    ppermute x12, starting transfers between devices, exchanged(): return lax.ppermute(block, axis, [(i, i ^ distance) for i in range(size)])  14.2 us
    ppermute x12, waiting for transfers between devices, exchanged(): return lax.ppermute(block, axis, [(i, i ^ distance) for i in range(size)])  3.15 us
    pallas_call x2, Pallas kernels, pack(): pl.pallas_call(functools.partial(pack_kernel, first, load, chosen, peers,...  2.63 us
    pallas_call x1, Pallas kernels, multiply(): pl.pallas_call(functools.partial(multiply_kernel, first, chosen), out_sha...  2.46 us
    pallas_call x1, Pallas kernels, stage(): pl.pallas_call(functools.partial(stage_kernel, cols), out_shape=(jax.Shap...  2.28 us
    pallas_call x1, Pallas kernels, work_list(): pl.pallas_call(functools.partial(list_kernel, cols, a_slots, row_count, p...  1.91 us
    pallas_call x1, Pallas kernels, count_rounds(): pl.pallas_call(functools.partial(rounds_kernel, cols, a_slots, row_count,...  1.35 us
    pallas_call x1, Pallas kernels, near_products(): pl.pallas_call(functools.partial(near_kernel, first, chosen), out_shape=j...  1.07 us
  transfers between devices with their start and end apart: 12, of which 4 were waited for; matrix products, arithmetic and copies ran while one was open for 2% of the time, Pallas kernels for 30%

profile of v12, /device:TPU:0, one launch (start us, length us, event | category | flops | bytes accessed | tf_op | source)
XLA Modules:
  0.0 30.6 jit_solution(15591206218391039994)
XLA Ops:
  0.0 0.5 %collective-permute-start.3 = (s32[2,1,16]{2,1,0:T(1,128)}, s32[2,1,16]{2,1,0:T(1,128)S(1)}, u32[]{:S(2)}, u32[]{:S(2)}) collective-permute-start(s32[2,1,16]{2,1,0:T(1,128)} %param.8), channel_id=1, source_target_pairs={{0,1},{1,0},{2,3},{3,2},{4,5},{5,4},{6,7},{7,6},{8,9},{9,8},{10,11... | collective-permute-start | bytes 392 | tf_op jit(solution)/shard_map/ppermute | solution.py:29
  0.5 2.6 %collective-permute-start.5 = (s32[2,1,16]{2,1,0:T(1,128)}, s32[2,1,16]{2,1,0:T(1,128)S(1)}, u32[]{:S(2)}, u32[]{:S(2)}) collective-permute-start(s32[2,1,16]{2,1,0:T(1,128)} %param.8), channel_id=1, source_target_pairs={{0,3},{1,2},{2,1},{3,0},{4,7},{5,6},{6,5},{7,4},{8,11},{9,10},{10,... | collective-permute-start | bytes 392 | tf_op jit(solution)/shard_map/ppermute | solution.py:29
  3.1 0.1 collective-permute-start.4
  3.1 2.0 %collective-permute-start.10 = (bf16[1,16,4096]{2,1,0:T(8,128)(2,1)}, bf16[1,16,4096]{2,1,0:T(8,128)(2,1)S(1)}, u32[]{:S(2)}, u32[]{:S(2)}) collective-permute-start(bf16[1,16,4096]{2,1,0:T(8,128)(2,1)} %refs_0_.1), channel_id=1, source_target_pairs={{0,2},{1,3},{2,0},{3,1},{4,6},{5,7},{6,4},{7,5},{8,10},{9,11},{10,... | collective-permute-start | bytes 393224 | tf_op jit(solution)/shard_map/ppermute | solution.py:29
  5.1 0.7 %pad_maximum_fusion.1 = s32[16,128]{1,0:T(8,128)S(1)} fusion(s32[2,16]{1,0:T(2,128)} %bitcast.29, s32[4,16]{1,0:T(4,128)} %bitcast.24, s32[4,16]{1,0:T(4,128)} %bitcast.25), kind=kLoop, calls=%fused_computation.1 | loop fusion | flops 4096 | bytes 8832 | tf_op jit(solution)/shard_map/max | solution.py:55
  5.8 0.1 collective-permute-start.6
  5.9 0.0 collective-permute-done.3
  5.9 0.2 collective-permute-start.11
  6.1 0.0 collective-permute-done.5
  6.1 0.8 %collective-permute-done.4 = s32[2,1,16]{2,1,0:T(1,128)S(1)} collective-permute-done((s32[2,1,16]{2,1,0:T(1,128)}, s32[2,1,16]{2,1,0:T(1,128)S(1)}, u32[]{:S(2)}, u32[]{:S(2)}) %collective-permute-start.4) | collective-permute-done | bytes 160 | tf_op jit(solution)/shard_map/ppermute | solution.py:29
  6.9 0.6 %collective-permute-done.6.refs_1_ = bf16[1,16,4096]{2,1,0:T(8,128)(2,1)S(1)} collective-permute-done((bf16[1,16,4096]{2,1,0:T(8,128)(2,1)}, bf16[1,16,4096]{2,1,0:T(8,128)(2,1)S(1)}, u32[]{:S(2)}, u32[]{:S(2)}) %collective-permute-start.6) | collective-permute-done | bytes 131104 | tf_op jit(solution)/shard_map/ppermute | solution.py:29
  7.4 3.6 %collective-permute-start.9 = (s32[16,128]{1,0:T(8,128)S(1)}, s32[16,128]{1,0:T(8,128)S(1)}, u32[]{:S(2)}, u32[]{:S(2)}) collective-permute-start(s32[16,128]{1,0:T(8,128)S(1)} %pad_maximum_fusion.refs_0_), channel_id=1, source_target_pairs={{0,12},{4,8},{8,4},{12,0},{1,13},{5,9},{9,5},{13,1},{2,14},{6,10},... | collective-permute-start | bytes 24584 | tf_op jit(solution)/shard_map/ppermute | solution.py:29
  11.0 0.0 collective-permute-start.8
  11.0 0.8 %collective-permute-start.7 = (s32[16,128]{1,0:T(8,128)S(1)}, s32[16,128]{1,0:T(8,128)S(1)}, u32[]{:S(2)}, u32[]{:S(2)}) collective-permute-start(s32[16,128]{1,0:T(8,128)S(1)} %pad_maximum_fusion.refs_0_), channel_id=1, source_target_pairs={{0,4},{4,0},{8,12},{12,8},{1,5},{5,1},{9,13},{13,9},{2,6},{6,2},{1... | collective-permute-start | bytes 24584 | tf_op jit(solution)/shard_map/ppermute | solution.py:29
  11.8 0.0 collective-permute-done.10.refs_2_
  11.8 0.0 collective-permute-done.11.refs_3_
  11.8 1.1 %collective-permute-done.9.refs_3_.refs_1_ = s32[16,128]{1,0:T(8,128)S(1)} collective-permute-done((s32[16,128]{1,0:T(8,128)S(1)}, s32[16,128]{1,0:T(8,128)S(1)}, u32[]{:S(2)}, u32[]{:S(2)}) %collective-permute-start.9) | collective-permute-done | bytes 8224 | tf_op jit(solution)/shard_map/ppermute | solution.py:29
  12.9 1.4 %pack.4 = bf16[512,128]{1,0:T(8,128)(2,1)S(1)} custom-call(s32[16,128]{1,0:T(8,128)S(1)} %pad_maximum_fusion.refs_0_, s32[16,128]{1,0:T(8,128)S(1)} %collective-permute-done.9.refs_3_.refs_1_, bf16[16,128,128]{2,1,0:T(8,128)(2,1)} %bitcast.20), custom_call_target="tpu_custom_call" | custom-call | flops 1048576 | bytes 4194304 | tf_op jit(solution)/shard_map/pack/pallas_call | solution.py:181
  14.3 3.7 %collective-permute-start.12 = (bf16[512,128]{1,0:T(8,128)(2,1)S(1)}, bf16[512,128]{1,0:T(8,128)(2,1)S(1)}, u32[]{:S(2)}, u32[]{:S(2)}) collective-permute-start(bf16[512,128]{1,0:T(8,128)(2,1)S(1)} %pack.4), channel_id=1, source_target_pairs={{0,12},{4,8},{8,4},{12,0},{1,13},{5,9},{9,5},{13,1},{2,14},{6,10},... | collective-permute-start | bytes 393224 | tf_op jit(solution)/shard_map/ppermute | solution.py:29
  17.9 0.0 collective-permute-done.8.refs_2_
  17.9 0.0 collective-permute-done.7.refs_1_
  17.9 0.0 copy-start
  17.9 1.3 %pack.3 = (bf16[512,128]{1,0:T(8,128)(2,1)S(1)}, bf16[512,128]{1,0:T(8,128)(2,1)S(1)}) custom-call(s32[16,128]{1,0:T(8,128)S(1)} %pad_maximum_fusion.refs_0_, s32[16,128]{1,0:T(8,128)S(1)} %collective-permute-done.7.refs_1_, s32[16,128]{1,0:T(8,128)S(1)} %collective-permute-done.8.refs_2_, bf16[16,128,128]{2,1,0:T(8,128)(2,1)S(1)} %bitcast.21), custom_call_target="tpu_custom_call" | custom-call | flops 1048576 | bytes 4194304 | tf_op jit(solution)/shard_map/pack/pallas_call | solution.py:181
  19.2 0.1 collective-permute-start.13
  19.3 0.8 %collective-permute-start.14 = (bf16[512,128]{1,0:T(8,128)(2,1)S(1)}, bf16[512,128]{1,0:T(8,128)(2,1)S(1)}, u32[]{:S(2)}, u32[]{:S(2)}) collective-permute-start(bf16[512,128]{1,0:T(8,128)(2,1)S(1)} %get-tuple-element.88), channel_id=1, source_target_pairs={{0,4},{4,0},{8,12},{12,8},{1,5},{5,1},{9,13},{13,9},{2,6},{6,2},{1... | collective-permute-start | bytes 393224 | tf_op jit(solution)/shard_map/ppermute | solution.py:29
  20.1 1.4 %count_rounds.1 = s32[1]{0:T(128)} custom-call(s32[16,128]{1,0:T(8,128)S(1)} %pad_maximum_fusion.refs_0_, s32[16,128]{1,0:T(8,128)S(1)} %collective-permute-done.7.refs_1_, s32[16,128]{1,0:T(8,128)S(1)} %collective-permute-done.8.refs_2_, s32[16,128]{1,0:T(8,128)S(1)} %collective-permute-done.9.refs_3_.refs_1_), custom_call_target="tpu_custom_call" | custom-call | flops 1024 | bytes 1024 | tf_op jit(solution)/shard_map/count_rounds/pallas_call | solution.py:311
  21.4 1.9 %work_list.1.refs_5_.refs_0_ = s32[8,128]{1,0:T(8,128)S(1)} custom-call(s32[16,128]{1,0:T(8,128)S(1)} %pad_maximum_fusion.refs_0_, s32[16,128]{1,0:T(8,128)S(1)} %collective-permute-done.7.refs_1_, s32[16,128]{1,0:T(8,128)S(1)} %collective-permute-done.8.refs_2_, s32[16,128]{1,0:T(8,128)S(1)} %collective-permute-done.9.refs_3_.refs_1_), custom_call_target="tpu_custom_call" | custom-call | flops 1024 | bytes 1024 | tf_op jit(solution)/shard_map/work_list/pallas_call | solution.py:262
  23.3 2.3 %stage.1 = (bf16[2048,128]{1,0:T(8,128)(2,1)S(1)}, f32[16,128,128]{2,1,0:T(8,128)S(1)}) custom-call(bf16[1,16,4096]{2,1,0:T(8,128)(2,1)S(1)} %copy-done, bf16[1,16,4096]{2,1,0:T(8,128)(2,1)S(1)} %collective-permute-done.6.refs_1_, bf16[1,16,4096]{2,1,0:T(8,128)(2,1)S(1)} %collective-permute-done.10.refs_2_, ...), custom_call_target="tpu_custom_call" | custom-call | flops 1024 | bytes 1024 | tf_op jit(solution)/shard_map/stage/pallas_call | solution.py:398
  26.3 1.1 %near_products.2.refs_2_ = f32[16,128,128]{2,1,0:T(8,128)S(1)} custom-call(s32[8,128]{1,0:T(8,128)S(1)} %work_list.1.refs_5_.refs_0_, bf16[2048,128]{1,0:T(8,128)(2,1)S(1)} %get-tuple-element.212.refs_1_, f32[16,128,128]{2,1,0:T(8,128)S(1)} %get-tuple-element.98.refs_2_, ...), custom_call_target="tpu_custom_call", output_to_operand_aliasing={{}: (2, {})} | custom-call | flops 1024 | bytes 1024 | tf_op jit(solution)/shard_map/near_products/pallas_call | solution.py:430
  27.4 0.7 %collective-permute-done.13.refs_3_ = bf16[512,128]{1,0:T(8,128)(2,1)S(1)} collective-permute-done((bf16[512,128]{1,0:T(8,128)(2,1)S(1)}, bf16[512,128]{1,0:T(8,128)(2,1)S(1)}, u32[]{:S(2)}, u32[]{:S(2)}) %collective-permute-start.13) | collective-permute-done | bytes 131104 | tf_op jit(solution)/shard_map/ppermute | solution.py:29
  28.1 0.0 collective-permute-done.14.refs_4_
  28.1 2.5 %multiply.2 = (f32[16,128,128]{2,1,0:T(8,128)S(1)}, f32[16,128,128]{2,1,0:T(8,128)}) custom-call(s32[8,128]{1,0:T(8,128)S(1)} %work_list.1.refs_5_.refs_0_, bf16[2048,128]{1,0:T(8,128)(2,1)S(1)} %get-tuple-element.212.refs_1_, f32[16,128,128]{2,1,0:T(8,128)S(1)} %near_products.2.refs_2_, ...), custom_call_target="tpu_custom_call", output_to_operand_aliasing={{0}: (2, {})} | custom-call | flops 67108864 | bytes 4194304 | tf_op jit(solution)/shard_map/multiply/pallas_call | solution.py:465
  (6 shorter events, 0.0 us)
Async XLA Ops:
  0.0 17.9 %copy-start.1 = (bf16[16,4,4096]{2,1,0:T(4,128)(2,1)S(1)}, bf16[16,4,4096]{2,1,0:T(4,128)(2,1)}, u32[]{:S(2)}) copy-start(bf16[16,4,4096]{2,1,0:T(4,128)(2,1)} %param.9) | copy-start | bytes 1572868
  0.0 5.9 %collective-permute-start.3 = (s32[2,1,16]{2,1,0:T(1,128)}, s32[2,1,16]{2,1,0:T(1,128)S(1)}, u32[]{:S(2)}, u32[]{:S(2)}) collective-permute-start(s32[2,1,16]{2,1,0:T(1,128)} %param.8), channel_id=1, source_target_pairs={{0,1},{1,0},{2,3},{3,2},{4,5},{5,4},{6,7},{7,6},{8,9},{9,8},{10,11... | collective-permute-start | bytes 392 | tf_op jit(solution)/shard_map/ppermute | solution.py:29
  0.5 5.6 %collective-permute-start.5 = (s32[2,1,16]{2,1,0:T(1,128)}, s32[2,1,16]{2,1,0:T(1,128)S(1)}, u32[]{:S(2)}, u32[]{:S(2)}) collective-permute-start(s32[2,1,16]{2,1,0:T(1,128)} %param.8), channel_id=1, source_target_pairs={{0,3},{1,2},{2,1},{3,0},{4,7},{5,6},{6,5},{7,4},{8,11},{9,10},{10,... | collective-permute-start | bytes 392 | tf_op jit(solution)/shard_map/ppermute | solution.py:29
  3.1 3.8 %collective-permute-start.4 = (s32[2,1,16]{2,1,0:T(1,128)}, s32[2,1,16]{2,1,0:T(1,128)S(1)}, u32[]{:S(2)}, u32[]{:S(2)}) collective-permute-start(s32[2,1,16]{2,1,0:T(1,128)} %param.8), channel_id=1, source_target_pairs={{0,2},{1,3},{2,0},{3,1},{4,6},{5,7},{6,4},{7,5},{8,10},{9,11},{10,... | collective-permute-start | bytes 392 | tf_op jit(solution)/shard_map/ppermute | solution.py:29
  3.1 8.7 %collective-permute-start.10 = (bf16[1,16,4096]{2,1,0:T(8,128)(2,1)}, bf16[1,16,4096]{2,1,0:T(8,128)(2,1)S(1)}, u32[]{:S(2)}, u32[]{:S(2)}) collective-permute-start(bf16[1,16,4096]{2,1,0:T(8,128)(2,1)} %refs_0_.1), channel_id=1, source_target_pairs={{0,2},{1,3},{2,0},{3,1},{4,6},{5,7},{6,4},{7,5},{8,10},{9,11},{10,... | collective-permute-start | bytes 393224 | tf_op jit(solution)/shard_map/ppermute | solution.py:29
  5.8 1.6 %collective-permute-start.6 = (bf16[1,16,4096]{2,1,0:T(8,128)(2,1)}, bf16[1,16,4096]{2,1,0:T(8,128)(2,1)S(1)}, u32[]{:S(2)}, u32[]{:S(2)}) collective-permute-start(bf16[1,16,4096]{2,1,0:T(8,128)(2,1)} %refs_0_.1), channel_id=1, source_target_pairs={{0,1},{1,0},{2,3},{3,2},{4,5},{5,4},{6,7},{7,6},{8,9},{9,8},{10,11... | collective-permute-start | bytes 393224 | tf_op jit(solution)/shard_map/ppermute | solution.py:29
  5.9 5.9 %collective-permute-start.11 = (bf16[1,16,4096]{2,1,0:T(8,128)(2,1)}, bf16[1,16,4096]{2,1,0:T(8,128)(2,1)S(1)}, u32[]{:S(2)}, u32[]{:S(2)}) collective-permute-start(bf16[1,16,4096]{2,1,0:T(8,128)(2,1)} %refs_0_.1), channel_id=1, source_target_pairs={{0,3},{1,2},{2,1},{3,0},{4,7},{5,6},{6,5},{7,4},{8,11},{9,10},{10,... | collective-permute-start | bytes 393224 | tf_op jit(solution)/shard_map/ppermute | solution.py:29
  7.4 5.4 %collective-permute-start.9 = (s32[16,128]{1,0:T(8,128)S(1)}, s32[16,128]{1,0:T(8,128)S(1)}, u32[]{:S(2)}, u32[]{:S(2)}) collective-permute-start(s32[16,128]{1,0:T(8,128)S(1)} %pad_maximum_fusion.refs_0_), channel_id=1, source_target_pairs={{0,12},{4,8},{8,4},{12,0},{1,13},{5,9},{9,5},{13,1},{2,14},{6,10},... | collective-permute-start | bytes 24584 | tf_op jit(solution)/shard_map/ppermute | solution.py:29
  11.0 6.9 %collective-permute-start.8 = (s32[16,128]{1,0:T(8,128)S(1)}, s32[16,128]{1,0:T(8,128)S(1)}, u32[]{:S(2)}, u32[]{:S(2)}) collective-permute-start(s32[16,128]{1,0:T(8,128)S(1)} %pad_maximum_fusion.refs_0_), channel_id=1, source_target_pairs={{0,8},{4,12},{8,0},{12,4},{1,9},{5,13},{9,1},{13,5},{2,10},{6,14},... | collective-permute-start | bytes 24584 | tf_op jit(solution)/shard_map/ppermute | solution.py:29
  11.0 6.9 %collective-permute-start.7 = (s32[16,128]{1,0:T(8,128)S(1)}, s32[16,128]{1,0:T(8,128)S(1)}, u32[]{:S(2)}, u32[]{:S(2)}) collective-permute-start(s32[16,128]{1,0:T(8,128)S(1)} %pad_maximum_fusion.refs_0_), channel_id=1, source_target_pairs={{0,4},{4,0},{8,12},{12,8},{1,5},{5,1},{9,13},{13,9},{2,6},{6,2},{1... | collective-permute-start | bytes 24584 | tf_op jit(solution)/shard_map/ppermute | solution.py:29
  14.3 12.0 %collective-permute-start.12 = (bf16[512,128]{1,0:T(8,128)(2,1)S(1)}, bf16[512,128]{1,0:T(8,128)(2,1)S(1)}, u32[]{:S(2)}, u32[]{:S(2)}) collective-permute-start(bf16[512,128]{1,0:T(8,128)(2,1)S(1)} %pack.4), channel_id=1, source_target_pairs={{0,12},{4,8},{8,4},{12,0},{1,13},{5,9},{9,5},{13,1},{2,14},{6,10},... | collective-permute-start | bytes 393224 | tf_op jit(solution)/shard_map/ppermute | solution.py:29
  17.9 5.4 %copy-start = (bf16[1,16,4096]{2,1,0:T(8,128)(2,1)S(1)}, bf16[1,16,4096]{2,1,0:T(8,128)(2,1)}, u32[]{:S(2)}) copy-start(bf16[1,16,4096]{2,1,0:T(8,128)(2,1)} %refs_0_.1) | copy-start | bytes 393220
  19.2 8.9 %collective-permute-start.13 = (bf16[512,128]{1,0:T(8,128)(2,1)S(1)}, bf16[512,128]{1,0:T(8,128)(2,1)S(1)}, u32[]{:S(2)}, u32[]{:S(2)}) collective-permute-start(bf16[512,128]{1,0:T(8,128)(2,1)S(1)} %get-tuple-element.99), channel_id=1, source_target_pairs={{0,8},{4,12},{8,0},{12,4},{1,9},{5,13},{9,1},{13,5},{2,10},{6,14},... | collective-permute-start | bytes 393224 | tf_op jit(solution)/shard_map/ppermute | solution.py:29
  19.3 8.8 %collective-permute-start.14 = (bf16[512,128]{1,0:T(8,128)(2,1)S(1)}, bf16[512,128]{1,0:T(8,128)(2,1)S(1)}, u32[]{:S(2)}, u32[]{:S(2)}) collective-permute-start(bf16[512,128]{1,0:T(8,128)(2,1)S(1)} %get-tuple-element.88), channel_id=1, source_target_pairs={{0,4},{4,0},{8,12},{12,8},{1,5},{5,1},{9,13},{13,9},{2,6},{6,2},{1... | collective-permute-start | bytes 393224 | tf_op jit(solution)/shard_map/ppermute | solution.py:29

commit v13 on v12

--- a/solution.py
+++ b/solution.py
@@ -257,18 +257,6 @@
         items[pl.ds(d, 1), :] = jnp.where(lane == LANES - 1, total, word)
 
 
-def work_list(told, cols, row_count, a_slots):
-    peers = len(told)
-    return pl.pallas_call(
-        functools.partial(list_kernel, cols, a_slots, row_count, peers),
-        out_shape=jax.ShapeDtypeStruct((-(-peers // 8) * 8, LANES), I32),
-        in_specs=[pl.BlockSpec(memory_space=VMEM)] * peers,
-        out_specs=pl.BlockSpec(memory_space=VMEM),
-        cost_estimate=pl.CostEstimate(flops=1 << 10, bytes_accessed=1 << 10, transcendentals=0),
-        name="work_list",
-    )(*told)
-
-
 def rounds_kernel(cols, a_slots, row_count, peers, *refs):
     told_refs, rounds, told = refs[:peers], refs[peers], refs[peers + 1]
     for d, ref in enumerate(told_refs):
@@ -306,16 +294,25 @@
     rounds[0] = (jnp.max(most).astype(I32) + CAPACITY - 1) // CAPACITY
 
 
-def count_rounds(told, cols, row_count, a_slots):
+def plan_kernel(cols, a_slots, row_count, peers, *refs):
+    told, (items, rounds, scratch) = refs[:peers], refs[peers:]
+    list_kernel(cols, a_slots, row_count, peers, *told, items)
+    rounds_kernel(cols, a_slots, row_count, peers, *told, rounds, scratch)
+
+
+def plan(told, cols, row_count, a_slots):
     peers = len(told)
     return pl.pallas_call(
-        functools.partial(rounds_kernel, cols, a_slots, row_count, peers),
-        out_shape=jax.ShapeDtypeStruct((1,), I32),
+        functools.partial(plan_kernel, cols, a_slots, row_count, peers),
+        out_shape=(
+            jax.ShapeDtypeStruct((-(-peers // 8) * 8, LANES), I32),
+            jax.ShapeDtypeStruct((1,), I32),
+        ),
         in_specs=[pl.BlockSpec(memory_space=VMEM)] * peers,
-        out_specs=pl.BlockSpec(memory_space=SMEM),
+        out_specs=(pl.BlockSpec(memory_space=VMEM), pl.BlockSpec(memory_space=SMEM)),
         scratch_shapes=[VMEM((peers,) + told[0].shape, I32)],
         cost_estimate=pl.CostEstimate(flops=1 << 10, bytes_accessed=1 << 10, transcendentals=0),
-        name="count_rounds",
+        name="plan",
     )(*told)
 
 
@@ -499,17 +496,16 @@
         far = exchanged(a_blocks, "col", h)
         a_parts += [far, exchanged(a_blocks, "col", h + 1)]
     told = [told] + send_rows([told] * (rows - 1))
-    far = rows - 1
-    others = list(range(1, far))
     b_rows = seen_by_rows(b_blocks)
-    message = pack(None, True, [far], told, b_rows, cols, row_count, a_slots)[0]
-    arrived_far = exchanged(message, "row", far)
-    *a_parts, b_rows = lax.optimization_barrier((*a_parts, b_rows))
-    packed = pack(None, False, others, told, b_rows, cols, row_count, a_slots)
-    arrived = [exchanged(packed[d - 1], "row", d) for d in others[::-1]][::-1] + [arrived_far]
-    told_late = lax.optimization_barrier((told, packed[0]))[0]
-    items = work_list(told_late, cols, row_count, a_slots)
-    rounds = jnp.minimum(count_rounds(told_late, cols, row_count, a_slots)[0], LANES)
+    arrived = []
+    for d in range(rows - 1, 0, -1):
+        message = pack(None, d == rows - 1, [d], told, b_rows, cols, row_count, a_slots)[0]
+        arrived.insert(0, exchanged(message, "row", d))
+        if d == rows - 1:
+            *a_parts, b_rows = lax.optimization_barrier((*a_parts, b_rows))
+    told_late = lax.optimization_barrier((told, message))[0]
+    items, rounds = plan(told_late, cols, row_count, a_slots)
+    rounds = jnp.minimum(rounds[0], LANES)
     a_ready, sums = stage([a_blocks] + a_parts, b_rows, items)
     sums, rounds = lax.optimization_barrier((sums, rounds))
     sums, out = finish(None, sums, arrived)

time: 30.6 us -> 30.6 us (level)
    pallas_call x1, Pallas kernels: 2.28 us -> 1.61 us  [stage(): pl.pallas_call(functools.partial(stage_kernel, cols), out_shape=(jax.Shap...]
    pallas_call x2 -> x3, Pallas kernels: 2.63 us -> 3.12 us  [pack(): pl.pallas_call(functools.partial(pack_kernel, first, load, chosen, peers,...]
    pallas_call x2 -> x1, Pallas kernels: 3.26 us -> 3.22 us  [plan(): pl.pallas_call(functools.partial(plan_kernel, cols, a_slots, row_count, p...]
  transfers between devices with their start and end apart: 12 -> 12, of which waited for: 4 -> 4; matrix products, arithmetic and copies ran while one was open for 2% -> 2% of each run, Pallas kernels for 30% -> 31%
where the time goes in v13:
time: 30.6 us; the launch traced here: 30.3 us
  starting transfers between devices  14.3 us (47%)
  Pallas kernels  11.4 us (37%)
  waiting for transfers between devices  3.08 us (10%)
  between operations  0.77 us (3%)
  other arithmetic  0.73 us (2%)
    ppermute x12, starting transfers between devices, exchanged(): return lax.ppermute(block, axis, [(i, i ^ distance) for i in range(size)])  14.3 us
    pallas_call x1, Pallas kernels, plan(): pl.pallas_call(functools.partial(plan_kernel, cols, a_slots, row_count, p...  3.22 us
    pallas_call x3, Pallas kernels, pack(): pl.pallas_call(functools.partial(pack_kernel, first, load, chosen, peers,...  3.12 us
    ppermute x12, waiting for transfers between devices, exchanged(): return lax.ppermute(block, axis, [(i, i ^ distance) for i in range(size)])  3.08 us
    pallas_call x1, Pallas kernels, multiply(): pl.pallas_call(functools.partial(multiply_kernel, first, chosen), out_sha...  2.18 us
    pallas_call x1, Pallas kernels, stage(): pl.pallas_call(functools.partial(stage_kernel, cols), out_shape=(jax.Shap...  1.61 us
    pallas_call x1, Pallas kernels, near_products(): pl.pallas_call(functools.partial(near_kernel, first, chosen), out_shape=j...  1.3 us
    max x1, other arithmetic, describe(): jnp.maximum(own, placed(a_parts[0][:, 0, :], 0))  0.72 us
  transfers between devices with their start and end apart: 12, of which 4 were waited for; matrix products, arithmetic and copies ran while one was open for 2% of the time, Pallas kernels for 31%

profile of v13, /device:TPU:0, one launch (start us, length us, event | category | flops | bytes accessed | tf_op | source)
XLA Modules:
  0.0 30.3 jit_solution(2457675751629683526)
XLA Ops:
  0.0 0.5 %collective-permute-start.3 = (s32[2,1,16]{2,1,0:T(1,128)}, s32[2,1,16]{2,1,0:T(1,128)S(1)}, u32[]{:S(2)}, u32[]{:S(2)}) collective-permute-start(s32[2,1,16]{2,1,0:T(1,128)} %param.8), channel_id=1, source_target_pairs={{0,1},{1,0},{2,3},{3,2},{4,5},{5,4},{6,7},{7,6},{8,9},{9,8},{10,11... | collective-permute-start | bytes 392 | tf_op jit(solution)/shard_map/ppermute | solution.py:29
  0.5 2.6 %collective-permute-start.5 = (s32[2,1,16]{2,1,0:T(1,128)}, s32[2,1,16]{2,1,0:T(1,128)S(1)}, u32[]{:S(2)}, u32[]{:S(2)}) collective-permute-start(s32[2,1,16]{2,1,0:T(1,128)} %param.8), channel_id=1, source_target_pairs={{0,3},{1,2},{2,1},{3,0},{4,7},{5,6},{6,5},{7,4},{8,11},{9,10},{10,... | collective-permute-start | bytes 392 | tf_op jit(solution)/shard_map/ppermute | solution.py:29
  3.1 0.1 collective-permute-start.4
  3.1 2.0 %collective-permute-start.10 = (bf16[1,16,4096]{2,1,0:T(8,128)(2,1)}, bf16[1,16,4096]{2,1,0:T(8,128)(2,1)S(1)}, u32[]{:S(2)}, u32[]{:S(2)}) collective-permute-start(bf16[1,16,4096]{2,1,0:T(8,128)(2,1)} %refs_0_.1), channel_id=1, source_target_pairs={{0,2},{1,3},{2,0},{3,1},{4,6},{5,7},{6,4},{7,5},{8,10},{9,11},{10,... | collective-permute-start | bytes 393224 | tf_op jit(solution)/shard_map/ppermute | solution.py:29
  5.1 0.7 %pad_maximum_fusion.1 = s32[16,128]{1,0:T(8,128)S(1)} fusion(s32[2,16]{1,0:T(2,128)} %bitcast.30, s32[4,16]{1,0:T(4,128)} %bitcast.25, s32[4,16]{1,0:T(4,128)} %bitcast.26), kind=kLoop, calls=%fused_computation.1 | loop fusion | flops 4096 | bytes 8832 | tf_op jit(solution)/shard_map/max | solution.py:55
  5.8 0.1 collective-permute-start.6
  5.9 0.0 collective-permute-done.3
  5.9 0.2 collective-permute-start.11
  6.1 0.0 collective-permute-done.5
  6.1 0.8 %collective-permute-done.4 = s32[2,1,16]{2,1,0:T(1,128)S(1)} collective-permute-done((s32[2,1,16]{2,1,0:T(1,128)}, s32[2,1,16]{2,1,0:T(1,128)S(1)}, u32[]{:S(2)}, u32[]{:S(2)}) %collective-permute-start.4) | collective-permute-done | bytes 160 | tf_op jit(solution)/shard_map/ppermute | solution.py:29
  6.9 0.6 %collective-permute-done.6.refs_1_ = bf16[1,16,4096]{2,1,0:T(8,128)(2,1)S(1)} collective-permute-done((bf16[1,16,4096]{2,1,0:T(8,128)(2,1)}, bf16[1,16,4096]{2,1,0:T(8,128)(2,1)S(1)}, u32[]{:S(2)}, u32[]{:S(2)}) %collective-permute-start.6) | collective-permute-done | bytes 131104 | tf_op jit(solution)/shard_map/ppermute | solution.py:29
  7.4 3.6 %collective-permute-start.9 = (s32[16,128]{1,0:T(8,128)S(1)}, s32[16,128]{1,0:T(8,128)S(1)}, u32[]{:S(2)}, u32[]{:S(2)}) collective-permute-start(s32[16,128]{1,0:T(8,128)S(1)} %pad_maximum_fusion.refs_0_), channel_id=1, source_target_pairs={{0,12},{4,8},{8,4},{12,0},{1,13},{5,9},{9,5},{13,1},{2,14},{6,10},... | collective-permute-start | bytes 24584 | tf_op jit(solution)/shard_map/ppermute | solution.py:29
  11.0 0.0 collective-permute-start.8
  11.0 0.8 %collective-permute-start.7 = (s32[16,128]{1,0:T(8,128)S(1)}, s32[16,128]{1,0:T(8,128)S(1)}, u32[]{:S(2)}, u32[]{:S(2)}) collective-permute-start(s32[16,128]{1,0:T(8,128)S(1)} %pad_maximum_fusion.refs_0_), channel_id=1, source_target_pairs={{0,4},{4,0},{8,12},{12,8},{1,5},{5,1},{9,13},{13,9},{2,6},{6,2},{1... | collective-permute-start | bytes 24584 | tf_op jit(solution)/shard_map/ppermute | solution.py:29
  11.8 0.0 collective-permute-done.10.refs_2_
  11.8 0.0 collective-permute-done.11.refs_3_
  11.8 1.1 %collective-permute-done.9.refs_3_.refs_1_ = s32[16,128]{1,0:T(8,128)S(1)} collective-permute-done((s32[16,128]{1,0:T(8,128)S(1)}, s32[16,128]{1,0:T(8,128)S(1)}, u32[]{:S(2)}, u32[]{:S(2)}) %collective-permute-start.9) | collective-permute-done | bytes 8224 | tf_op jit(solution)/shard_map/ppermute | solution.py:29
  12.9 1.4 %pack.5 = bf16[512,128]{1,0:T(8,128)(2,1)S(1)} custom-call(s32[16,128]{1,0:T(8,128)S(1)} %pad_maximum_fusion.refs_0_, s32[16,128]{1,0:T(8,128)S(1)} %collective-permute-done.9.refs_3_.refs_1_, bf16[16,128,128]{2,1,0:T(8,128)(2,1)} %bitcast.20), custom_call_target="tpu_custom_call" | custom-call | flops 1048576 | bytes 4194304 | tf_op jit(solution)/shard_map/pack/pallas_call | solution.py:181
  14.3 3.7 %collective-permute-start.12 = (bf16[512,128]{1,0:T(8,128)(2,1)S(1)}, bf16[512,128]{1,0:T(8,128)(2,1)S(1)}, u32[]{:S(2)}, u32[]{:S(2)}) collective-permute-start(bf16[512,128]{1,0:T(8,128)(2,1)S(1)} %pack.5), channel_id=1, source_target_pairs={{0,12},{4,8},{8,4},{12,0},{1,13},{5,9},{9,5},{13,1},{2,14},{6,10},... | collective-permute-start | bytes 393224 | tf_op jit(solution)/shard_map/ppermute | solution.py:29
  17.9 0.0 collective-permute-done.8.refs_2_.refs_1_
  17.9 0.9 %pack.6 = bf16[512,128]{1,0:T(8,128)(2,1)S(1)} custom-call(s32[16,128]{1,0:T(8,128)S(1)} %pad_maximum_fusion.refs_0_, s32[16,128]{1,0:T(8,128)S(1)} %collective-permute-done.8.refs_2_.refs_1_, bf16[16,128,128]{2,1,0:T(8,128)(2,1)S(1)} %bitcast.21), custom_call_target="tpu_custom_call" | custom-call | flops 1048576 | bytes 4194304 | tf_op jit(solution)/shard_map/pack/pallas_call | solution.py:181
  18.8 0.0 copy-start
  18.8 0.1 collective-permute-start.13
  18.9 0.9 %pack.4 = bf16[512,128]{1,0:T(8,128)(2,1)S(1)} custom-call(s32[16,128]{1,0:T(8,128)S(1)} %pad_maximum_fusion.refs_0_, s32[16,128]{1,0:T(8,128)S(1)} %collective-permute-done.7.refs_1_, bf16[16,128,128]{2,1,0:T(8,128)(2,1)S(1)} %bitcast.22), custom_call_target="tpu_custom_call" | custom-call | flops 1048576 | bytes 4194304 | tf_op jit(solution)/shard_map/pack/pallas_call | solution.py:181
  19.8 0.8 %collective-permute-start.14 = (bf16[512,128]{1,0:T(8,128)(2,1)S(1)}, bf16[512,128]{1,0:T(8,128)(2,1)S(1)}, u32[]{:S(2)}, u32[]{:S(2)}) collective-permute-start(bf16[512,128]{1,0:T(8,128)(2,1)S(1)} %pack.4), channel_id=1, source_target_pairs={{0,4},{4,0},{8,12},{12,8},{1,5},{5,1},{9,13},{13,9},{2,6},{6,2},{1... | collective-permute-start | bytes 393224 | tf_op jit(solution)/shard_map/ppermute | solution.py:29
  20.6 3.2 %plan.1 = (s32[8,128]{1,0:T(8,128)S(1)}, s32[1]{0:T(128)}) custom-call(s32[16,128]{1,0:T(8,128)S(1)} %pad_maximum_fusion.refs_0_, s32[16,128]{1,0:T(8,128)S(1)} %collective-permute-done.7.refs_1_, s32[16,128]{1,0:T(8,128)S(1)} %collective-permute-done.8.refs_2_.refs_1_, s32[16,128]{1,0:T(8,128)S(1)} %collective-permute-done.9.refs_3_.refs_1_), custom_call_target="tpu_custom_call" | custom-call | flops 1024 | bytes 1024 | tf_op jit(solution)/shard_map/plan/pallas_call | solution.py:305
  23.8 1.6 %stage.1 = (bf16[2048,128]{1,0:T(8,128)(2,1)S(1)}, f32[16,128,128]{2,1,0:T(8,128)S(1)}) custom-call(bf16[1,16,4096]{2,1,0:T(8,128)(2,1)S(1)} %copy-done, bf16[1,16,4096]{2,1,0:T(8,128)(2,1)S(1)} %collective-permute-done.6.refs_1_, bf16[1,16,4096]{2,1,0:T(8,128)(2,1)S(1)} %collective-permute-done.10.refs_2_, ...), custom_call_target="tpu_custom_call" | custom-call | flops 1024 | bytes 1024 | tf_op jit(solution)/shard_map/stage/pallas_call | solution.py:395
  26.1 0.0 collective-permute-done.12.refs_3_
  26.1 1.3 %near_products.2.refs_2_ = f32[16,128,128]{2,1,0:T(8,128)S(1)} custom-call(s32[8,128]{1,0:T(8,128)S(1)} %get-tuple-element.211.refs_5_.refs_0_, bf16[2048,128]{1,0:T(8,128)(2,1)S(1)} %get-tuple-element.212.refs_1_, f32[16,128,128]{2,1,0:T(8,128)S(1)} %get-tuple-element.99.refs_2_, ...), custom_call_target="tpu_custom_call", output_to_operand_aliasing={{}: (2, {})} | custom-call | flops 1024 | bytes 1024 | tf_op jit(solution)/shard_map/near_products/pallas_call | solution.py:427
  27.4 0.6 %collective-permute-done.13.refs_3_ = bf16[512,128]{1,0:T(8,128)(2,1)S(1)} collective-permute-done((bf16[512,128]{1,0:T(8,128)(2,1)S(1)}, bf16[512,128]{1,0:T(8,128)(2,1)S(1)}, u32[]{:S(2)}, u32[]{:S(2)}) %collective-permute-start.13) | collective-permute-done | bytes 131104 | tf_op jit(solution)/shard_map/ppermute | solution.py:29
  28.1 0.0 collective-permute-done.14.refs_4_
  28.1 2.2 %multiply.2 = (f32[16,128,128]{2,1,0:T(8,128)S(1)}, f32[16,128,128]{2,1,0:T(8,128)}) custom-call(s32[8,128]{1,0:T(8,128)S(1)} %get-tuple-element.211.refs_5_.refs_0_, bf16[2048,128]{1,0:T(8,128)(2,1)S(1)} %get-tuple-element.212.refs_1_, f32[16,128,128]{2,1,0:T(8,128)S(1)} %near_products.2.refs_2_, ...), custom_call_target="tpu_custom_call", output_to_operand_aliasing={{0}: (2, {})} | custom-call | flops 67108864 | bytes 4194304 | tf_op jit(solution)/shard_map/multiply/pallas_call | solution.py:462
  (6 shorter events, 0.0 us)
Async XLA Ops:
  0.0 17.9 %copy-start.1 = (bf16[16,4,4096]{2,1,0:T(4,128)(2,1)S(1)}, bf16[16,4,4096]{2,1,0:T(4,128)(2,1)}, u32[]{:S(2)}) copy-start(bf16[16,4,4096]{2,1,0:T(4,128)(2,1)} %param.9) | copy-start | bytes 1572868
  0.0 5.9 %collective-permute-start.3 = (s32[2,1,16]{2,1,0:T(1,128)}, s32[2,1,16]{2,1,0:T(1,128)S(1)}, u32[]{:S(2)}, u32[]{:S(2)}) collective-permute-start(s32[2,1,16]{2,1,0:T(1,128)} %param.8), channel_id=1, source_target_pairs={{0,1},{1,0},{2,3},{3,2},{4,5},{5,4},{6,7},{7,6},{8,9},{9,8},{10,11... | collective-permute-start | bytes 392 | tf_op jit(solution)/shard_map/ppermute | solution.py:29
  0.5 5.6 %collective-permute-start.5 = (s32[2,1,16]{2,1,0:T(1,128)}, s32[2,1,16]{2,1,0:T(1,128)S(1)}, u32[]{:S(2)}, u32[]{:S(2)}) collective-permute-start(s32[2,1,16]{2,1,0:T(1,128)} %param.8), channel_id=1, source_target_pairs={{0,3},{1,2},{2,1},{3,0},{4,7},{5,6},{6,5},{7,4},{8,11},{9,10},{10,... | collective-permute-start | bytes 392 | tf_op jit(solution)/shard_map/ppermute | solution.py:29
  3.1 3.8 %collective-permute-start.4 = (s32[2,1,16]{2,1,0:T(1,128)}, s32[2,1,16]{2,1,0:T(1,128)S(1)}, u32[]{:S(2)}, u32[]{:S(2)}) collective-permute-start(s32[2,1,16]{2,1,0:T(1,128)} %param.8), channel_id=1, source_target_pairs={{0,2},{1,3},{2,0},{3,1},{4,6},{5,7},{6,4},{7,5},{8,10},{9,11},{10,... | collective-permute-start | bytes 392 | tf_op jit(solution)/shard_map/ppermute | solution.py:29
  3.1 8.7 %collective-permute-start.10 = (bf16[1,16,4096]{2,1,0:T(8,128)(2,1)}, bf16[1,16,4096]{2,1,0:T(8,128)(2,1)S(1)}, u32[]{:S(2)}, u32[]{:S(2)}) collective-permute-start(bf16[1,16,4096]{2,1,0:T(8,128)(2,1)} %refs_0_.1), channel_id=1, source_target_pairs={{0,2},{1,3},{2,0},{3,1},{4,6},{5,7},{6,4},{7,5},{8,10},{9,11},{10,... | collective-permute-start | bytes 393224 | tf_op jit(solution)/shard_map/ppermute | solution.py:29
  5.8 1.6 %collective-permute-start.6 = (bf16[1,16,4096]{2,1,0:T(8,128)(2,1)}, bf16[1,16,4096]{2,1,0:T(8,128)(2,1)S(1)}, u32[]{:S(2)}, u32[]{:S(2)}) collective-permute-start(bf16[1,16,4096]{2,1,0:T(8,128)(2,1)} %refs_0_.1), channel_id=1, source_target_pairs={{0,1},{1,0},{2,3},{3,2},{4,5},{5,4},{6,7},{7,6},{8,9},{9,8},{10,11... | collective-permute-start | bytes 393224 | tf_op jit(solution)/shard_map/ppermute | solution.py:29
  5.9 5.9 %collective-permute-start.11 = (bf16[1,16,4096]{2,1,0:T(8,128)(2,1)}, bf16[1,16,4096]{2,1,0:T(8,128)(2,1)S(1)}, u32[]{:S(2)}, u32[]{:S(2)}) collective-permute-start(bf16[1,16,4096]{2,1,0:T(8,128)(2,1)} %refs_0_.1), channel_id=1, source_target_pairs={{0,3},{1,2},{2,1},{3,0},{4,7},{5,6},{6,5},{7,4},{8,11},{9,10},{10,... | collective-permute-start | bytes 393224 | tf_op jit(solution)/shard_map/ppermute | solution.py:29
  7.4 5.4 %collective-permute-start.9 = (s32[16,128]{1,0:T(8,128)S(1)}, s32[16,128]{1,0:T(8,128)S(1)}, u32[]{:S(2)}, u32[]{:S(2)}) collective-permute-start(s32[16,128]{1,0:T(8,128)S(1)} %pad_maximum_fusion.refs_0_), channel_id=1, source_target_pairs={{0,12},{4,8},{8,4},{12,0},{1,13},{5,9},{9,5},{13,1},{2,14},{6,10},... | collective-permute-start | bytes 24584 | tf_op jit(solution)/shard_map/ppermute | solution.py:29
  11.0 6.9 %collective-permute-start.8 = (s32[16,128]{1,0:T(8,128)S(1)}, s32[16,128]{1,0:T(8,128)S(1)}, u32[]{:S(2)}, u32[]{:S(2)}) collective-permute-start(s32[16,128]{1,0:T(8,128)S(1)} %pad_maximum_fusion.refs_0_), channel_id=1, source_target_pairs={{0,8},{4,12},{8,0},{12,4},{1,9},{5,13},{9,1},{13,5},{2,10},{6,14},... | collective-permute-start | bytes 24584 | tf_op jit(solution)/shard_map/ppermute | solution.py:29
  11.0 7.9 %collective-permute-start.7 = (s32[16,128]{1,0:T(8,128)S(1)}, s32[16,128]{1,0:T(8,128)S(1)}, u32[]{:S(2)}, u32[]{:S(2)}) collective-permute-start(s32[16,128]{1,0:T(8,128)S(1)} %pad_maximum_fusion.refs_0_), channel_id=1, source_target_pairs={{0,4},{4,0},{8,12},{12,8},{1,5},{5,1},{9,13},{13,9},{2,6},{6,2},{1... | collective-permute-start | bytes 24584 | tf_op jit(solution)/shard_map/ppermute | solution.py:29
  14.3 11.9 %collective-permute-start.12 = (bf16[512,128]{1,0:T(8,128)(2,1)S(1)}, bf16[512,128]{1,0:T(8,128)(2,1)S(1)}, u32[]{:S(2)}, u32[]{:S(2)}) collective-permute-start(bf16[512,128]{1,0:T(8,128)(2,1)S(1)} %pack.5), channel_id=1, source_target_pairs={{0,12},{4,8},{8,4},{12,0},{1,13},{5,9},{9,5},{13,1},{2,14},{6,10},... | collective-permute-start | bytes 393224 | tf_op jit(solution)/shard_map/ppermute | solution.py:29
  18.8 5.0 %copy-start = (bf16[1,16,4096]{2,1,0:T(8,128)(2,1)S(1)}, bf16[1,16,4096]{2,1,0:T(8,128)(2,1)}, u32[]{:S(2)}) copy-start(bf16[1,16,4096]{2,1,0:T(8,128)(2,1)} %refs_0_.1) | copy-start | bytes 393220
  18.8 9.3 %collective-permute-start.13 = (bf16[512,128]{1,0:T(8,128)(2,1)S(1)}, bf16[512,128]{1,0:T(8,128)(2,1)S(1)}, u32[]{:S(2)}, u32[]{:S(2)}) collective-permute-start(bf16[512,128]{1,0:T(8,128)(2,1)S(1)} %pack.6), channel_id=1, source_target_pairs={{0,8},{4,12},{8,0},{12,4},{1,9},{5,13},{9,1},{13,5},{2,10},{6,14},... | collective-permute-start | bytes 393224 | tf_op jit(solution)/shard_map/ppermute | solution.py:29
  19.8 8.3 %collective-permute-start.14 = (bf16[512,128]{1,0:T(8,128)(2,1)S(1)}, bf16[512,128]{1,0:T(8,128)(2,1)S(1)}, u32[]{:S(2)}, u32[]{:S(2)}) collective-permute-start(bf16[512,128]{1,0:T(8,128)(2,1)S(1)} %pack.4), channel_id=1, source_target_pairs={{0,4},{4,0},{8,12},{12,8},{1,5},{5,1},{9,13},{13,9},{2,6},{6,2},{1... | collective-permute-start | bytes 393224 | tf_op jit(solution)/shard_map/ppermute | solution.py:29

commit v14 on v13

--- a/solution.py
+++ b/solution.py
@@ -204,6 +204,7 @@
     before = (iota((LANES, LANES), 0) < iota((LANES, LANES), 1)).astype(BF16)
     below = (iota((blocks, blocks), 1) < iota((blocks, blocks), 0)).astype(BF16)
     same_slot = spot // row_count == iota((blocks, LANES), 1) // a_slots
+    most = jnp.zeros((1, 1), F32)
     for d in range(peers):
         group = grid_row ^ d
         holder = group // per_col
@@ -239,6 +240,7 @@
             needed = jnp.max(pairs, axis=1, keepdims=True)
             many = jnp.broadcast_to(needed, (blocks, LANES)).astype(BF16)
             place = jnp.dot(below, many, preferred_element_type=F32)
+            most = jnp.maximum(most, jnp.sum(needed, axis=0, keepdims=True))
         hit = jnp.sum(pairs, axis=0, keepdims=True)
         place = jnp.sum(pairs * place, axis=0, keepdims=True)
         out = jnp.sum(pairs * both[blocks:], axis=0, keepdims=True)
@@ -255,9 +257,10 @@
         word = (a_slot * 64 + listed[1:2]) * 64 + listed[2:3]
         total = jnp.sum(hit, axis=1, keepdims=True).astype(I32)
         items[pl.ds(d, 1), :] = jnp.where(lane == LANES - 1, total, word)
-
-
-def rounds_kernel(cols, a_slots, row_count, peers, *refs):
+    return most
+
+
+def rounds_kernel(cols, a_slots, row_count, peers, most, *refs):
     told_refs, rounds, told = refs[:peers], refs[peers], refs[peers + 1]
     for d, ref in enumerate(told_refs):
         told[d, :, :] = ref[...]
@@ -280,24 +283,23 @@
         needed = jnp.max(pairs, axis=0, keepdims=True)
         return jnp.maximum(most, jnp.sum(needed, axis=1, keepdims=True))
 
-    most = jnp.zeros((1, 1), F32)
     if peers <= 4:
-        for receiver in range(peers):
+        for receiver in range(1, peers):
             for d in range(1, peers):
                 most = one_pair(receiver, d, most)
     else:
 
         def step(at, most):
-            return one_pair(at // (peers - 1), at % (peers - 1) + 1, most)
-
-        most = lax.fori_loop(0, peers * (peers - 1), step, most)
+            return one_pair(at // (peers - 1) + 1, at % (peers - 1) + 1, most)
+
+        most = lax.fori_loop(0, (peers - 1) * (peers - 1), step, most)
     rounds[0] = (jnp.max(most).astype(I32) + CAPACITY - 1) // CAPACITY
 
 
 def plan_kernel(cols, a_slots, row_count, peers, *refs):
     told, (items, rounds, scratch) = refs[:peers], refs[peers:]
-    list_kernel(cols, a_slots, row_count, peers, *told, items)
-    rounds_kernel(cols, a_slots, row_count, peers, *told, rounds, scratch)
+    most = list_kernel(cols, a_slots, row_count, peers, *told, items)
+    rounds_kernel(cols, a_slots, row_count, peers, most, *told, rounds, scratch)
 
 
 def plan(told, cols, row_count, a_slots):
@@ -316,11 +318,15 @@
     )(*told)
 
 
+def packed_loader(b_ref):
+    return lambda place: b_ref[pl.ds(pl.multiple_of(place * ROWS, ROWS), ROWS), :]
+
+
 def add_products(items, a_ref, peer_refs, sums, window=None):
     low = iota((ROWS, LANES), 1) < BS
     nothing = jnp.zeros((ROWS, LANES), BF16)
 
-    def add_one(word, used, b_ref):
+    def add_one(word, used, load):
         word = jnp.where(used, word, 0)
         place = word & 63
         target = (word >> 6) & 63
@@ -329,8 +335,7 @@
             used = used & (place >= 0) & (place < CAPACITY)
             place = jnp.where(used, place, 0)
         a_at = pl.multiple_of((word >> 12) * ROWS, ROWS)
-        b_at = pl.multiple_of(place * ROWS, ROWS)
-        block = jnp.where(used, b_ref[pl.ds(b_at, ROWS), :], nothing)
+        block = jnp.where(used, load(place), nothing)
         turned = jnp.concatenate([block[:, BS:], block[:, :BS]], axis=1)
         right = jnp.concatenate(
             [
@@ -352,9 +357,9 @@
 
         def some_items(step, carry, chosen=chosen, totals=totals, width=width):
             for u in range(width):
-                for (d, b_ref), total in zip(chosen, totals):
+                for (d, load), total in zip(chosen, totals):
                     y = step * width + u
-                    add_one(items[d, y], y < total, b_ref)
+                    add_one(items[d, y], y < total, load)
             return carry
 
         lax.fori_loop(0, (longest + width - 1) // width, some_items, 0)
@@ -362,14 +367,15 @@
 
 def stage_kernel(cols, *refs):
     a_refs, b_ref, items = refs[:cols], refs[cols], refs[cols + 1]
-    a_out, sums, a_wide, wide, own = refs[cols + 2 :]
+    a_out, sums, a_wide, wide = refs[cols + 2 :]
     wide[...] = b_ref[...].astype(F32)
     sums[...] = jnp.zeros_like(sums)
     row_count = wide.shape[0]
-    for n in range(SLOTS):
-        for k in range(row_count):
-            block = wide[k, pl.ds(n, ROWS, stride=SLOTS), :].astype(BF16)
-            own[pl.ds((n * row_count + k) * ROWS, ROWS), :] = block
+
+    def load_own(place):
+        at = pl.ds(place // row_count, ROWS, stride=SLOTS)
+        return wide[place % row_count, at, :].astype(BF16)
+
     source = iota((LANES, LANES), 0)
     target = iota((LANES, LANES), 1)
     wanted = (target // BS) * BS + 2 * (target % ROWS) + (target // ROWS) % 2
@@ -385,7 +391,7 @@
         for s in range(slots):
             at = pl.multiple_of((first + s) * ROWS, ROWS)
             a_out[pl.ds(at, ROWS), :] = a_wide[h * slots + s, 0:ROWS, :].astype(BF16)
-    add_products(items, a_out, [(0, own)], sums)
+    add_products(items, a_out, [(0, load_own)], sums)
 
 
 def stage(a_parts, b_rows, items):
@@ -403,7 +409,6 @@
         scratch_shapes=[
             VMEM((cols * slots, ROWS + PADDING, LANES), F32),
             VMEM(b_rows.shape, F32),
-            VMEM((b_rows.shape[0] * SLOTS * ROWS, LANES), BF16),
         ],
         compiler_params=pltpu.CompilerParams(vmem_limit_bytes=40 << 20),
         cost_estimate=pl.CostEstimate(flops=1 << 10, bytes_accessed=1 << 10, transcendentals=0),
@@ -416,7 +421,7 @@
     base = 0 if first else refs.pop(0)[0]
     items, a_ref = refs[:2]
     b_refs, sums = refs[3:-1], refs[-1]
-    add_products(items, a_ref, list(zip(chosen, b_refs)), sums, window=base)
+    add_products(items, a_ref, list(zip(chosen, map(packed_loader, b_refs))), sums, window=base)
 
 
 def near_products(base, chosen, items, a_ready, sums, b_parts):
@@ -442,7 +447,7 @@
     items, a_ref = refs[:2]
     b_refs = refs[3 : 3 + len(chosen)]
     sums, out, sem = refs[3 + len(chosen) :]
-    add_products(items, a_ref, list(zip(chosen, b_refs)), sums, window=base)
+    add_products(items, a_ref, list(zip(chosen, map(packed_loader, b_refs))), sums, window=base)
     part = out.shape[0] // PIECES
     copies = [
         pltpu.make_async_copy(sums.at[pl.ds(p * part, part)], out.at[pl.ds(p * part, part)], sem.at[p])

time: 30.6 us -> 30.6 us (level)
  waiting for transfers between devices: 3.08 us -> 3.4 us
    pallas_call x1, Pallas kernels: 1.3 us -> 0.84 us  [near_products(): pl.pallas_call(functools.partial(near_kernel, first, chosen), out_shape=j...]
    ppermute x12, waiting for transfers between devices: 3.08 us -> 3.4 us  [exchanged(): return lax.ppermute(block, axis, [(i, i ^ distance) for i in range(size)])]
  transfers between devices with their start and end apart: 12 -> 12, of which waited for: 4 -> 4; matrix products, arithmetic and copies ran while one was open for 2% -> 2% of each run, Pallas kernels for 31% -> 29%
where the time goes in v14:
time: 30.6 us; the launch traced here: 30.3 us
  starting transfers between devices  14.3 us (47%)
  Pallas kernels  11.1 us (36%)
  waiting for transfers between devices  3.4 us (11%)
  between operations  0.77 us (3%)
  other arithmetic  0.73 us (2%)
    ppermute x12, starting transfers between devices, exchanged(): return lax.ppermute(block, axis, [(i, i ^ distance) for i in range(size)])  14.3 us
    ppermute x12, waiting for transfers between devices, exchanged(): return lax.ppermute(block, axis, [(i, i ^ distance) for i in range(size)])  3.4 us
    pallas_call x1, Pallas kernels, plan(): pl.pallas_call(functools.partial(plan_kernel, cols, a_slots, row_count, p...  3.18 us
    pallas_call x3, Pallas kernels, pack(): pl.pallas_call(functools.partial(pack_kernel, first, load, chosen, peers,...  3.12 us
    pallas_call x1, Pallas kernels, multiply(): pl.pallas_call(functools.partial(multiply_kernel, first, chosen), out_sha...  2.18 us
    pallas_call x1, Pallas kernels, stage(): pl.pallas_call(functools.partial(stage_kernel, cols), out_shape=(jax.Shap...  1.78 us
    pallas_call x1, Pallas kernels, near_products(): pl.pallas_call(functools.partial(near_kernel, first, chosen), out_shape=j...  0.84 us
    max x1, other arithmetic, describe(): jnp.maximum(own, placed(a_parts[0][:, 0, :], 0))  0.72 us
  transfers between devices with their start and end apart: 12, of which 4 were waited for; matrix products, arithmetic and copies ran while one was open for 2% of the time, Pallas kernels for 29%

profile of v14, /device:TPU:0, one launch (start us, length us, event | category | flops | bytes accessed | tf_op | source)
XLA Modules:
  0.0 30.3 jit_solution(1050753734453654566)
XLA Ops:
  0.0 0.5 %collective-permute-start.3 = (s32[2,1,16]{2,1,0:T(1,128)}, s32[2,1,16]{2,1,0:T(1,128)S(1)}, u32[]{:S(2)}, u32[]{:S(2)}) collective-permute-start(s32[2,1,16]{2,1,0:T(1,128)} %param.8), channel_id=1, source_target_pairs={{0,1},{1,0},{2,3},{3,2},{4,5},{5,4},{6,7},{7,6},{8,9},{9,8},{10,11... | collective-permute-start | bytes 392 | tf_op jit(solution)/shard_map/ppermute | solution.py:29
  0.5 2.6 %collective-permute-start.5 = (s32[2,1,16]{2,1,0:T(1,128)}, s32[2,1,16]{2,1,0:T(1,128)S(1)}, u32[]{:S(2)}, u32[]{:S(2)}) collective-permute-start(s32[2,1,16]{2,1,0:T(1,128)} %param.8), channel_id=1, source_target_pairs={{0,3},{1,2},{2,1},{3,0},{4,7},{5,6},{6,5},{7,4},{8,11},{9,10},{10,... | collective-permute-start | bytes 392 | tf_op jit(solution)/shard_map/ppermute | solution.py:29
  3.1 0.1 collective-permute-start.4
  3.1 2.0 %collective-permute-start.10 = (bf16[1,16,4096]{2,1,0:T(8,128)(2,1)}, bf16[1,16,4096]{2,1,0:T(8,128)(2,1)S(1)}, u32[]{:S(2)}, u32[]{:S(2)}) collective-permute-start(bf16[1,16,4096]{2,1,0:T(8,128)(2,1)} %refs_0_.1), channel_id=1, source_target_pairs={{0,2},{1,3},{2,0},{3,1},{4,6},{5,7},{6,4},{7,5},{8,10},{9,11},{10,... | collective-permute-start | bytes 393224 | tf_op jit(solution)/shard_map/ppermute | solution.py:29
  5.1 0.7 %pad_maximum_fusion.1 = s32[16,128]{1,0:T(8,128)S(1)} fusion(s32[2,16]{1,0:T(2,128)} %bitcast.30, s32[4,16]{1,0:T(4,128)} %bitcast.25, s32[4,16]{1,0:T(4,128)} %bitcast.26), kind=kLoop, calls=%fused_computation.1 | loop fusion | flops 4096 | bytes 8832 | tf_op jit(solution)/shard_map/max | solution.py:55
  5.8 0.1 collective-permute-start.6
  5.9 0.0 collective-permute-done.3
  5.9 0.2 collective-permute-start.11
  6.1 0.0 collective-permute-done.5
  6.1 0.8 %collective-permute-done.4 = s32[2,1,16]{2,1,0:T(1,128)S(1)} collective-permute-done((s32[2,1,16]{2,1,0:T(1,128)}, s32[2,1,16]{2,1,0:T(1,128)S(1)}, u32[]{:S(2)}, u32[]{:S(2)}) %collective-permute-start.4) | collective-permute-done | bytes 160 | tf_op jit(solution)/shard_map/ppermute | solution.py:29
  6.9 0.6 %collective-permute-done.6.refs_1_ = bf16[1,16,4096]{2,1,0:T(8,128)(2,1)S(1)} collective-permute-done((bf16[1,16,4096]{2,1,0:T(8,128)(2,1)}, bf16[1,16,4096]{2,1,0:T(8,128)(2,1)S(1)}, u32[]{:S(2)}, u32[]{:S(2)}) %collective-permute-start.6) | collective-permute-done | bytes 131104 | tf_op jit(solution)/shard_map/ppermute | solution.py:29
  7.4 3.6 %collective-permute-start.9 = (s32[16,128]{1,0:T(8,128)S(1)}, s32[16,128]{1,0:T(8,128)S(1)}, u32[]{:S(2)}, u32[]{:S(2)}) collective-permute-start(s32[16,128]{1,0:T(8,128)S(1)} %pad_maximum_fusion.refs_0_), channel_id=1, source_target_pairs={{0,12},{4,8},{8,4},{12,0},{1,13},{5,9},{9,5},{13,1},{2,14},{6,10},... | collective-permute-start | bytes 24584 | tf_op jit(solution)/shard_map/ppermute | solution.py:29
  11.0 0.0 collective-permute-start.8
  11.0 0.8 %collective-permute-start.7 = (s32[16,128]{1,0:T(8,128)S(1)}, s32[16,128]{1,0:T(8,128)S(1)}, u32[]{:S(2)}, u32[]{:S(2)}) collective-permute-start(s32[16,128]{1,0:T(8,128)S(1)} %pad_maximum_fusion.refs_0_), channel_id=1, source_target_pairs={{0,4},{4,0},{8,12},{12,8},{1,5},{5,1},{9,13},{13,9},{2,6},{6,2},{1... | collective-permute-start | bytes 24584 | tf_op jit(solution)/shard_map/ppermute | solution.py:29
  11.8 0.0 collective-permute-done.10.refs_2_
  11.8 0.0 collective-permute-done.11.refs_3_
  11.8 1.1 %collective-permute-done.9.refs_3_.refs_1_ = s32[16,128]{1,0:T(8,128)S(1)} collective-permute-done((s32[16,128]{1,0:T(8,128)S(1)}, s32[16,128]{1,0:T(8,128)S(1)}, u32[]{:S(2)}, u32[]{:S(2)}) %collective-permute-start.9) | collective-permute-done | bytes 8224 | tf_op jit(solution)/shard_map/ppermute | solution.py:29
  12.9 1.4 %pack.5 = bf16[512,128]{1,0:T(8,128)(2,1)S(1)} custom-call(s32[16,128]{1,0:T(8,128)S(1)} %pad_maximum_fusion.refs_0_, s32[16,128]{1,0:T(8,128)S(1)} %collective-permute-done.9.refs_3_.refs_1_, bf16[16,128,128]{2,1,0:T(8,128)(2,1)} %bitcast.20), custom_call_target="tpu_custom_call" | custom-call | flops 1048576 | bytes 4194304 | tf_op jit(solution)/shard_map/pack/pallas_call | solution.py:181
  14.3 3.7 %collective-permute-start.12 = (bf16[512,128]{1,0:T(8,128)(2,1)S(1)}, bf16[512,128]{1,0:T(8,128)(2,1)S(1)}, u32[]{:S(2)}, u32[]{:S(2)}) collective-permute-start(bf16[512,128]{1,0:T(8,128)(2,1)S(1)} %pack.5), channel_id=1, source_target_pairs={{0,12},{4,8},{8,4},{12,0},{1,13},{5,9},{9,5},{13,1},{2,14},{6,10},... | collective-permute-start | bytes 393224 | tf_op jit(solution)/shard_map/ppermute | solution.py:29
  17.9 0.9 %pack.6 = bf16[512,128]{1,0:T(8,128)(2,1)S(1)} custom-call(s32[16,128]{1,0:T(8,128)S(1)} %pad_maximum_fusion.refs_0_, s32[16,128]{1,0:T(8,128)S(1)} %collective-permute-done.8.refs_2_.refs_1_, bf16[16,128,128]{2,1,0:T(8,128)(2,1)S(1)} %bitcast.21), custom_call_target="tpu_custom_call" | custom-call | flops 1048576 | bytes 4194304 | tf_op jit(solution)/shard_map/pack/pallas_call | solution.py:181
  18.8 0.0 copy-start
  18.8 0.1 collective-permute-start.13
  18.9 0.0 collective-permute-done.7.refs_1_
  18.9 0.9 %pack.4 = bf16[512,128]{1,0:T(8,128)(2,1)S(1)} custom-call(s32[16,128]{1,0:T(8,128)S(1)} %pad_maximum_fusion.refs_0_, s32[16,128]{1,0:T(8,128)S(1)} %collective-permute-done.7.refs_1_, bf16[16,128,128]{2,1,0:T(8,128)(2,1)S(1)} %bitcast.22), custom_call_target="tpu_custom_call" | custom-call | flops 1048576 | bytes 4194304 | tf_op jit(solution)/shard_map/pack/pallas_call | solution.py:181
  19.8 0.8 %collective-permute-start.14 = (bf16[512,128]{1,0:T(8,128)(2,1)S(1)}, bf16[512,128]{1,0:T(8,128)(2,1)S(1)}, u32[]{:S(2)}, u32[]{:S(2)}) collective-permute-start(bf16[512,128]{1,0:T(8,128)(2,1)S(1)} %pack.4), channel_id=1, source_target_pairs={{0,4},{4,0},{8,12},{12,8},{1,5},{5,1},{9,13},{13,9},{2,6},{6,2},{1... | collective-permute-start | bytes 393224 | tf_op jit(solution)/shard_map/ppermute | solution.py:29
  20.6 3.2 %plan.1 = (s32[8,128]{1,0:T(8,128)S(1)}, s32[1]{0:T(128)}) custom-call(s32[16,128]{1,0:T(8,128)S(1)} %pad_maximum_fusion.refs_0_, s32[16,128]{1,0:T(8,128)S(1)} %collective-permute-done.7.refs_1_, s32[16,128]{1,0:T(8,128)S(1)} %collective-permute-done.8.refs_2_.refs_1_, s32[16,128]{1,0:T(8,128)S(1)} %collective-permute-done.9.refs_3_.refs_1_), custom_call_target="tpu_custom_call" | custom-call | flops 1024 | bytes 1024 | tf_op jit(solution)/shard_map/plan/pallas_call | solution.py:307
  23.8 1.8 %stage.1 = (bf16[2048,128]{1,0:T(8,128)(2,1)S(1)}, f32[16,128,128]{2,1,0:T(8,128)S(1)}) custom-call(bf16[1,16,4096]{2,1,0:T(8,128)(2,1)S(1)} %copy-done, bf16[1,16,4096]{2,1,0:T(8,128)(2,1)S(1)} %collective-permute-done.6.refs_1_, bf16[1,16,4096]{2,1,0:T(8,128)(2,1)S(1)} %collective-permute-done.10.refs_2_, ...), custom_call_target="tpu_custom_call" | custom-call | flops 1024 | bytes 1024 | tf_op jit(solution)/shard_map/stage/pallas_call | solution.py:401
  26.3 0.0 collective-permute-done.12.refs_3_
  26.3 0.8 %near_products.2.refs_2_ = f32[16,128,128]{2,1,0:T(8,128)S(1)} custom-call(s32[8,128]{1,0:T(8,128)S(1)} %get-tuple-element.211.refs_5_.refs_0_, bf16[2048,128]{1,0:T(8,128)(2,1)S(1)} %get-tuple-element.212.refs_1_, f32[16,128,128]{2,1,0:T(8,128)S(1)} %get-tuple-element.99.refs_2_, ...), custom_call_target="tpu_custom_call", output_to_operand_aliasing={{}: (2, {})} | custom-call | flops 1024 | bytes 1024 | tf_op jit(solution)/shard_map/near_products/pallas_call | solution.py:432
  27.1 1.0 %collective-permute-done.13.refs_3_ = bf16[512,128]{1,0:T(8,128)(2,1)S(1)} collective-permute-done((bf16[512,128]{1,0:T(8,128)(2,1)S(1)}, bf16[512,128]{1,0:T(8,128)(2,1)S(1)}, u32[]{:S(2)}, u32[]{:S(2)}) %collective-permute-start.13) | collective-permute-done | bytes 131104 | tf_op jit(solution)/shard_map/ppermute | solution.py:29
  28.1 0.0 collective-permute-done.14.refs_4_
  28.1 2.2 %multiply.2 = (f32[16,128,128]{2,1,0:T(8,128)S(1)}, f32[16,128,128]{2,1,0:T(8,128)}) custom-call(s32[8,128]{1,0:T(8,128)S(1)} %get-tuple-element.211.refs_5_.refs_0_, bf16[2048,128]{1,0:T(8,128)(2,1)S(1)} %get-tuple-element.212.refs_1_, f32[16,128,128]{2,1,0:T(8,128)S(1)} %near_products.2.refs_2_, ...), custom_call_target="tpu_custom_call", output_to_operand_aliasing={{0}: (2, {})} | custom-call | flops 67108864 | bytes 4194304 | tf_op jit(solution)/shard_map/multiply/pallas_call | solution.py:467
  (6 shorter events, 0.0 us)
Async XLA Ops:
  0.0 17.9 %copy-start.1 = (bf16[16,4,4096]{2,1,0:T(4,128)(2,1)S(1)}, bf16[16,4,4096]{2,1,0:T(4,128)(2,1)}, u32[]{:S(2)}) copy-start(bf16[16,4,4096]{2,1,0:T(4,128)(2,1)} %param.9) | copy-start | bytes 1572868
  0.0 5.9 %collective-permute-start.3 = (s32[2,1,16]{2,1,0:T(1,128)}, s32[2,1,16]{2,1,0:T(1,128)S(1)}, u32[]{:S(2)}, u32[]{:S(2)}) collective-permute-start(s32[2,1,16]{2,1,0:T(1,128)} %param.8), channel_id=1, source_target_pairs={{0,1},{1,0},{2,3},{3,2},{4,5},{5,4},{6,7},{7,6},{8,9},{9,8},{10,11... | collective-permute-start | bytes 392 | tf_op jit(solution)/shard_map/ppermute | solution.py:29
  0.5 5.6 %collective-permute-start.5 = (s32[2,1,16]{2,1,0:T(1,128)}, s32[2,1,16]{2,1,0:T(1,128)S(1)}, u32[]{:S(2)}, u32[]{:S(2)}) collective-permute-start(s32[2,1,16]{2,1,0:T(1,128)} %param.8), channel_id=1, source_target_pairs={{0,3},{1,2},{2,1},{3,0},{4,7},{5,6},{6,5},{7,4},{8,11},{9,10},{10,... | collective-permute-start | bytes 392 | tf_op jit(solution)/shard_map/ppermute | solution.py:29
  3.1 3.8 %collective-permute-start.4 = (s32[2,1,16]{2,1,0:T(1,128)}, s32[2,1,16]{2,1,0:T(1,128)S(1)}, u32[]{:S(2)}, u32[]{:S(2)}) collective-permute-start(s32[2,1,16]{2,1,0:T(1,128)} %param.8), channel_id=1, source_target_pairs={{0,2},{1,3},{2,0},{3,1},{4,6},{5,7},{6,4},{7,5},{8,10},{9,11},{10,... | collective-permute-start | bytes 392 | tf_op jit(solution)/shard_map/ppermute | solution.py:29
  3.1 8.7 %collective-permute-start.10 = (bf16[1,16,4096]{2,1,0:T(8,128)(2,1)}, bf16[1,16,4096]{2,1,0:T(8,128)(2,1)S(1)}, u32[]{:S(2)}, u32[]{:S(2)}) collective-permute-start(bf16[1,16,4096]{2,1,0:T(8,128)(2,1)} %refs_0_.1), channel_id=1, source_target_pairs={{0,2},{1,3},{2,0},{3,1},{4,6},{5,7},{6,4},{7,5},{8,10},{9,11},{10,... | collective-permute-start | bytes 393224 | tf_op jit(solution)/shard_map/ppermute | solution.py:29
  5.8 1.6 %collective-permute-start.6 = (bf16[1,16,4096]{2,1,0:T(8,128)(2,1)}, bf16[1,16,4096]{2,1,0:T(8,128)(2,1)S(1)}, u32[]{:S(2)}, u32[]{:S(2)}) collective-permute-start(bf16[1,16,4096]{2,1,0:T(8,128)(2,1)} %refs_0_.1), channel_id=1, source_target_pairs={{0,1},{1,0},{2,3},{3,2},{4,5},{5,4},{6,7},{7,6},{8,9},{9,8},{10,11... | collective-permute-start | bytes 393224 | tf_op jit(solution)/shard_map/ppermute | solution.py:29
  5.9 5.9 %collective-permute-start.11 = (bf16[1,16,4096]{2,1,0:T(8,128)(2,1)}, bf16[1,16,4096]{2,1,0:T(8,128)(2,1)S(1)}, u32[]{:S(2)}, u32[]{:S(2)}) collective-permute-start(bf16[1,16,4096]{2,1,0:T(8,128)(2,1)} %refs_0_.1), channel_id=1, source_target_pairs={{0,3},{1,2},{2,1},{3,0},{4,7},{5,6},{6,5},{7,4},{8,11},{9,10},{10,... | collective-permute-start | bytes 393224 | tf_op jit(solution)/shard_map/ppermute | solution.py:29
  7.4 5.4 %collective-permute-start.9 = (s32[16,128]{1,0:T(8,128)S(1)}, s32[16,128]{1,0:T(8,128)S(1)}, u32[]{:S(2)}, u32[]{:S(2)}) collective-permute-start(s32[16,128]{1,0:T(8,128)S(1)} %pad_maximum_fusion.refs_0_), channel_id=1, source_target_pairs={{0,12},{4,8},{8,4},{12,0},{1,13},{5,9},{9,5},{13,1},{2,14},{6,10},... | collective-permute-start | bytes 24584 | tf_op jit(solution)/shard_map/ppermute | solution.py:29
  11.0 6.9 %collective-permute-start.8 = (s32[16,128]{1,0:T(8,128)S(1)}, s32[16,128]{1,0:T(8,128)S(1)}, u32[]{:S(2)}, u32[]{:S(2)}) collective-permute-start(s32[16,128]{1,0:T(8,128)S(1)} %pad_maximum_fusion.refs_0_), channel_id=1, source_target_pairs={{0,8},{4,12},{8,0},{12,4},{1,9},{5,13},{9,1},{13,5},{2,10},{6,14},... | collective-permute-start | bytes 24584 | tf_op jit(solution)/shard_map/ppermute | solution.py:29
  11.0 7.9 %collective-permute-start.7 = (s32[16,128]{1,0:T(8,128)S(1)}, s32[16,128]{1,0:T(8,128)S(1)}, u32[]{:S(2)}, u32[]{:S(2)}) collective-permute-start(s32[16,128]{1,0:T(8,128)S(1)} %pad_maximum_fusion.refs_0_), channel_id=1, source_target_pairs={{0,4},{4,0},{8,12},{12,8},{1,5},{5,1},{9,13},{13,9},{2,6},{6,2},{1... | collective-permute-start | bytes 24584 | tf_op jit(solution)/shard_map/ppermute | solution.py:29
  14.3 12.0 %collective-permute-start.12 = (bf16[512,128]{1,0:T(8,128)(2,1)S(1)}, bf16[512,128]{1,0:T(8,128)(2,1)S(1)}, u32[]{:S(2)}, u32[]{:S(2)}) collective-permute-start(bf16[512,128]{1,0:T(8,128)(2,1)S(1)} %pack.5), channel_id=1, source_target_pairs={{0,12},{4,8},{8,4},{12,0},{1,13},{5,9},{9,5},{13,1},{2,14},{6,10},... | collective-permute-start | bytes 393224 | tf_op jit(solution)/shard_map/ppermute | solution.py:29
  18.8 5.0 %copy-start = (bf16[1,16,4096]{2,1,0:T(8,128)(2,1)S(1)}, bf16[1,16,4096]{2,1,0:T(8,128)(2,1)}, u32[]{:S(2)}) copy-start(bf16[1,16,4096]{2,1,0:T(8,128)(2,1)} %refs_0_.1) | copy-start | bytes 393220
  18.8 9.3 %collective-permute-start.13 = (bf16[512,128]{1,0:T(8,128)(2,1)S(1)}, bf16[512,128]{1,0:T(8,128)(2,1)S(1)}, u32[]{:S(2)}, u32[]{:S(2)}) collective-permute-start(bf16[512,128]{1,0:T(8,128)(2,1)S(1)} %pack.6), channel_id=1, source_target_pairs={{0,8},{4,12},{8,0},{12,4},{1,9},{5,13},{9,1},{13,5},{2,10},{6,14},... | collective-permute-start | bytes 393224 | tf_op jit(solution)/shard_map/ppermute | solution.py:29
  19.8 8.3 %collective-permute-start.14 = (bf16[512,128]{1,0:T(8,128)(2,1)S(1)}, bf16[512,128]{1,0:T(8,128)(2,1)S(1)}, u32[]{:S(2)}, u32[]{:S(2)}) collective-permute-start(bf16[512,128]{1,0:T(8,128)(2,1)S(1)} %pack.4), channel_id=1, source_target_pairs={{0,4},{4,0},{8,12},{12,8},{1,5},{5,1},{9,13},{13,9},{2,6},{6,2},{1... | collective-permute-start | bytes 393224 | tf_op jit(solution)/shard_map/ppermute | solution.py:29

commit v15 on v14

--- a/solution.py
+++ b/solution.py
@@ -132,8 +132,14 @@
     b_ref, outs, refs = refs[0], refs[1 : count + 1], refs[count + 1 :]
     if load:
         b_any, b_ref, sem = b_ref, refs.pop(), refs.pop()
-        loading = pltpu.make_async_copy(b_any, b_ref, sem.at[0])
-        loading.start()
+        loading = [
+            pltpu.make_async_copy(
+                b_any.at[:, pl.ds(at, GROUP), :], b_ref.at[:, pl.ds(at, GROUP), :], sem.at[at // GROUP]
+            )
+            for at in range(0, SLOTS * ROWS, GROUP)
+        ]
+        for copy in loading:
+            copy.start()
     picks, packed = refs
     grid_row = lax.axis_index("row")
     per_col = peers // cols
@@ -156,9 +162,9 @@
     wanted = [jnp.where(lane // SLOTS % steps == t, spread, 0.0) for t in range(steps)]
     wanted = jnp.concatenate(wanted, axis=0).astype(BF16)
     total = spread.shape[0]
-    if load:
-        loading.wait()
     for at in range(0, ROWS, steps):
+        if load:
+            loading[at // steps].wait()
         rows = b_ref[:, at * SLOTS : (at + steps) * SLOTS, :].reshape(depth, LANES)
         found = jnp.dot(wanted, rows, preferred_element_type=F32)
         for t in range(steps):
@@ -176,7 +182,7 @@
     vmem_spec = pl.BlockSpec(memory_space=VMEM)
     given = [] if first else [base]
     message = jax.ShapeDtypeStruct((CAPACITY * ROWS, LANES), BF16)
-    loaded = [pltpu.SemaphoreType.DMA((1,)), VMEM(b_rows.shape, BF16)] if load else []
+    loaded = [pltpu.SemaphoreType.DMA((SLOTS * ROWS // GROUP,)), VMEM(b_rows.shape, BF16)] if load else []
     held = len(chosen) * CAPACITY
     return pl.pallas_call(
         functools.partial(pack_kernel, first, load, chosen, peers, cols, a_slots, row_count),

time: 30.6 us -> 31.4 us (1.026)
  Pallas kernels: 11.1 us -> 13 us
  waiting for transfers between devices: 3.4 us -> 2.43 us
    ppermute x12, waiting for transfers between devices: 3.4 us -> 2.43 us  [exchanged(): return lax.ppermute(block, axis, [(i, i ^ distance) for i in range(size)])]
    pallas_call x3, Pallas kernels: 3.12 us -> 3.92 us  [pack(): pl.pallas_call(functools.partial(pack_kernel, first, load, chosen, peers,...]
    pallas_call x1, Pallas kernels: 1.78 us -> 2.47 us  [stage(): pl.pallas_call(functools.partial(stage_kernel, cols), out_shape=(jax.Shap...]
    pallas_call x1, Pallas kernels: 0.84 us -> 1.3 us  [near_products(): pl.pallas_call(functools.partial(near_kernel, first, chosen), out_shape=j...]
  transfers between devices with their start and end apart: 12 -> 12, of which waited for: 4 -> 3; matrix products, arithmetic and copies ran while one was open for 2% -> 2% of each run, Pallas kernels for 29% -> 35%
where the time goes in v15:
time: 31.4 us; the launch traced here: 31.3 us
  starting transfers between devices  14.3 us (46%)
  Pallas kernels  13 us (41%)
  waiting for transfers between devices  2.43 us (8%)
  between operations  0.79 us (3%)
  other arithmetic  0.73 us (2%)
    ppermute x12, starting transfers between devices, exchanged(): return lax.ppermute(block, axis, [(i, i ^ distance) for i in range(size)])  14.3 us
    pallas_call x3, Pallas kernels, pack(): pl.pallas_call(functools.partial(pack_kernel, first, load, chosen, peers,...  3.92 us
    pallas_call x1, Pallas kernels, plan(): pl.pallas_call(functools.partial(plan_kernel, cols, a_slots, row_count, p...  3.18 us
    pallas_call x1, Pallas kernels, stage(): pl.pallas_call(functools.partial(stage_kernel, cols), out_shape=(jax.Shap...  2.47 us
    ppermute x12, waiting for transfers between devices, exchanged(): return lax.ppermute(block, axis, [(i, i ^ distance) for i in range(size)])  2.43 us
    pallas_call x1, Pallas kernels, multiply(): pl.pallas_call(functools.partial(multiply_kernel, first, chosen), out_sha...  2.18 us
    pallas_call x1, Pallas kernels, near_products(): pl.pallas_call(functools.partial(near_kernel, first, chosen), out_shape=j...  1.3 us
    max x1, other arithmetic, describe(): jnp.maximum(own, placed(a_parts[0][:, 0, :], 0))  0.72 us
  transfers between devices with their start and end apart: 12, of which 3 were waited for; matrix products, arithmetic and copies ran while one was open for 2% of the time, Pallas kernels for 35%

profile of v15, /device:TPU:0, one launch (start us, length us, event | category | flops | bytes accessed | tf_op | source)
XLA Modules:
  0.0 31.3 jit_solution(8970746566915744527)
XLA Ops:
  0.0 0.5 %collective-permute-start.3 = (s32[2,1,16]{2,1,0:T(1,128)}, s32[2,1,16]{2,1,0:T(1,128)S(1)}, u32[]{:S(2)}, u32[]{:S(2)}) collective-permute-start(s32[2,1,16]{2,1,0:T(1,128)} %param.8), channel_id=1, source_target_pairs={{0,1},{1,0},{2,3},{3,2},{4,5},{5,4},{6,7},{7,6},{8,9},{9,8},{10,11... | collective-permute-start | bytes 392 | tf_op jit(solution)/shard_map/ppermute | solution.py:29
  0.5 2.6 %collective-permute-start.5 = (s32[2,1,16]{2,1,0:T(1,128)}, s32[2,1,16]{2,1,0:T(1,128)S(1)}, u32[]{:S(2)}, u32[]{:S(2)}) collective-permute-start(s32[2,1,16]{2,1,0:T(1,128)} %param.8), channel_id=1, source_target_pairs={{0,3},{1,2},{2,1},{3,0},{4,7},{5,6},{6,5},{7,4},{8,11},{9,10},{10,... | collective-permute-start | bytes 392 | tf_op jit(solution)/shard_map/ppermute | solution.py:29
  3.1 0.1 collective-permute-start.4
  3.1 2.0 %collective-permute-start.10 = (bf16[1,16,4096]{2,1,0:T(8,128)(2,1)}, bf16[1,16,4096]{2,1,0:T(8,128)(2,1)S(1)}, u32[]{:S(2)}, u32[]{:S(2)}) collective-permute-start(bf16[1,16,4096]{2,1,0:T(8,128)(2,1)} %refs_0_.1), channel_id=1, source_target_pairs={{0,2},{1,3},{2,0},{3,1},{4,6},{5,7},{6,4},{7,5},{8,10},{9,11},{10,... | collective-permute-start | bytes 393224 | tf_op jit(solution)/shard_map/ppermute | solution.py:29
  5.1 0.7 %pad_maximum_fusion.1 = s32[16,128]{1,0:T(8,128)S(1)} fusion(s32[2,16]{1,0:T(2,128)} %bitcast.30, s32[4,16]{1,0:T(4,128)} %bitcast.25, s32[4,16]{1,0:T(4,128)} %bitcast.26), kind=kLoop, calls=%fused_computation.1 | loop fusion | flops 4096 | bytes 8832 | tf_op jit(solution)/shard_map/max | solution.py:55
  5.8 0.1 collective-permute-start.6
  5.9 0.0 collective-permute-done.3
  5.9 0.2 collective-permute-start.11
  6.1 0.0 collective-permute-done.5
  6.1 0.8 %collective-permute-done.4 = s32[2,1,16]{2,1,0:T(1,128)S(1)} collective-permute-done((s32[2,1,16]{2,1,0:T(1,128)}, s32[2,1,16]{2,1,0:T(1,128)S(1)}, u32[]{:S(2)}, u32[]{:S(2)}) %collective-permute-start.4) | collective-permute-done | bytes 160 | tf_op jit(solution)/shard_map/ppermute | solution.py:29
  6.9 0.6 %collective-permute-done.6.refs_1_ = bf16[1,16,4096]{2,1,0:T(8,128)(2,1)S(1)} collective-permute-done((bf16[1,16,4096]{2,1,0:T(8,128)(2,1)}, bf16[1,16,4096]{2,1,0:T(8,128)(2,1)S(1)}, u32[]{:S(2)}, u32[]{:S(2)}) %collective-permute-start.6) | collective-permute-done | bytes 131104 | tf_op jit(solution)/shard_map/ppermute | solution.py:29
  7.4 3.6 %collective-permute-start.9 = (s32[16,128]{1,0:T(8,128)S(1)}, s32[16,128]{1,0:T(8,128)S(1)}, u32[]{:S(2)}, u32[]{:S(2)}) collective-permute-start(s32[16,128]{1,0:T(8,128)S(1)} %pad_maximum_fusion.refs_0_), channel_id=1, source_target_pairs={{0,12},{4,8},{8,4},{12,0},{1,13},{5,9},{9,5},{13,1},{2,14},{6,10},... | collective-permute-start | bytes 24584 | tf_op jit(solution)/shard_map/ppermute | solution.py:29
  11.0 0.0 collective-permute-start.8
  11.0 0.8 %collective-permute-start.7 = (s32[16,128]{1,0:T(8,128)S(1)}, s32[16,128]{1,0:T(8,128)S(1)}, u32[]{:S(2)}, u32[]{:S(2)}) collective-permute-start(s32[16,128]{1,0:T(8,128)S(1)} %pad_maximum_fusion.refs_0_), channel_id=1, source_target_pairs={{0,4},{4,0},{8,12},{12,8},{1,5},{5,1},{9,13},{13,9},{2,6},{6,2},{1... | collective-permute-start | bytes 24584 | tf_op jit(solution)/shard_map/ppermute | solution.py:29
  11.8 0.0 collective-permute-done.10.refs_2_
  11.8 0.0 collective-permute-done.11.refs_3_
  11.8 1.1 %collective-permute-done.9.refs_3_.refs_1_ = s32[16,128]{1,0:T(8,128)S(1)} collective-permute-done((s32[16,128]{1,0:T(8,128)S(1)}, s32[16,128]{1,0:T(8,128)S(1)}, u32[]{:S(2)}, u32[]{:S(2)}) %collective-permute-start.9) | collective-permute-done | bytes 8224 | tf_op jit(solution)/shard_map/ppermute | solution.py:29
  12.9 2.2 %pack.5 = bf16[512,128]{1,0:T(8,128)(2,1)S(1)} custom-call(s32[16,128]{1,0:T(8,128)S(1)} %pad_maximum_fusion.refs_0_, s32[16,128]{1,0:T(8,128)S(1)} %collective-permute-done.9.refs_3_.refs_1_, bf16[16,128,128]{2,1,0:T(8,128)(2,1)} %bitcast.20), custom_call_target="tpu_custom_call" | custom-call | flops 1048576 | bytes 4194304 | tf_op jit(solution)/shard_map/pack/pallas_call | solution.py:187
  15.1 3.7 %collective-permute-start.12 = (bf16[512,128]{1,0:T(8,128)(2,1)S(1)}, bf16[512,128]{1,0:T(8,128)(2,1)S(1)}, u32[]{:S(2)}, u32[]{:S(2)}) collective-permute-start(bf16[512,128]{1,0:T(8,128)(2,1)S(1)} %pack.5), channel_id=1, source_target_pairs={{0,12},{4,8},{8,4},{12,0},{1,13},{5,9},{9,5},{13,1},{2,14},{6,10},... | collective-permute-start | bytes 393224 | tf_op jit(solution)/shard_map/ppermute | solution.py:29
  18.7 0.0 collective-permute-done.8.refs_2_.refs_1_
  18.7 0.9 %pack.6 = bf16[512,128]{1,0:T(8,128)(2,1)S(1)} custom-call(s32[16,128]{1,0:T(8,128)S(1)} %pad_maximum_fusion.refs_0_, s32[16,128]{1,0:T(8,128)S(1)} %collective-permute-done.8.refs_2_.refs_1_, bf16[16,128,128]{2,1,0:T(8,128)(2,1)S(1)} %bitcast.21), custom_call_target="tpu_custom_call" | custom-call | flops 1048576 | bytes 4194304 | tf_op jit(solution)/shard_map/pack/pallas_call | solution.py:187
  19.6 0.0 copy-start
  19.6 0.1 collective-permute-start.13
  19.7 0.0 collective-permute-done.7.refs_1_
  19.7 0.9 %pack.4 = bf16[512,128]{1,0:T(8,128)(2,1)S(1)} custom-call(s32[16,128]{1,0:T(8,128)S(1)} %pad_maximum_fusion.refs_0_, s32[16,128]{1,0:T(8,128)S(1)} %collective-permute-done.7.refs_1_, bf16[16,128,128]{2,1,0:T(8,128)(2,1)S(1)} %bitcast.22), custom_call_target="tpu_custom_call" | custom-call | flops 1048576 | bytes 4194304 | tf_op jit(solution)/shard_map/pack/pallas_call | solution.py:187
  20.6 0.8 %collective-permute-start.14 = (bf16[512,128]{1,0:T(8,128)(2,1)S(1)}, bf16[512,128]{1,0:T(8,128)(2,1)S(1)}, u32[]{:S(2)}, u32[]{:S(2)}) collective-permute-start(bf16[512,128]{1,0:T(8,128)(2,1)S(1)} %pack.4), channel_id=1, source_target_pairs={{0,4},{4,0},{8,12},{12,8},{1,5},{5,1},{9,13},{13,9},{2,6},{6,2},{1... | collective-permute-start | bytes 393224 | tf_op jit(solution)/shard_map/ppermute | solution.py:29
  21.4 3.2 %plan.1 = (s32[8,128]{1,0:T(8,128)S(1)}, s32[1]{0:T(128)}) custom-call(s32[16,128]{1,0:T(8,128)S(1)} %pad_maximum_fusion.refs_0_, s32[16,128]{1,0:T(8,128)S(1)} %collective-permute-done.7.refs_1_, s32[16,128]{1,0:T(8,128)S(1)} %collective-permute-done.8.refs_2_.refs_1_, s32[16,128]{1,0:T(8,128)S(1)} %collective-permute-done.9.refs_3_.refs_1_), custom_call_target="tpu_custom_call" | custom-call | flops 1024 | bytes 1024 | tf_op jit(solution)/shard_map/plan/pallas_call | solution.py:313
  24.6 2.5 %stage.1 = (bf16[2048,128]{1,0:T(8,128)(2,1)S(1)}, f32[16,128,128]{2,1,0:T(8,128)S(1)}) custom-call(bf16[1,16,4096]{2,1,0:T(8,128)(2,1)S(1)} %copy-done, bf16[1,16,4096]{2,1,0:T(8,128)(2,1)S(1)} %collective-permute-done.6.refs_1_, bf16[1,16,4096]{2,1,0:T(8,128)(2,1)S(1)} %collective-permute-done.10.refs_2_, ...), custom_call_target="tpu_custom_call" | custom-call | flops 1024 | bytes 1024 | tf_op jit(solution)/shard_map/stage/pallas_call | solution.py:407
  27.7 0.0 collective-permute-done.12.refs_3_
  27.8 1.3 %near_products.2.refs_2_ = f32[16,128,128]{2,1,0:T(8,128)S(1)} custom-call(s32[8,128]{1,0:T(8,128)S(1)} %get-tuple-element.211.refs_5_.refs_0_, bf16[2048,128]{1,0:T(8,128)(2,1)S(1)} %get-tuple-element.212.refs_1_, f32[16,128,128]{2,1,0:T(8,128)S(1)} %get-tuple-element.99.refs_2_, ...), custom_call_target="tpu_custom_call", output_to_operand_aliasing={{}: (2, {})} | custom-call | flops 1024 | bytes 1024 | tf_op jit(solution)/shard_map/near_products/pallas_call | solution.py:438
  29.1 0.0 collective-permute-done.13.refs_3_
  29.1 2.2 %multiply.2 = (f32[16,128,128]{2,1,0:T(8,128)S(1)}, f32[16,128,128]{2,1,0:T(8,128)}) custom-call(s32[8,128]{1,0:T(8,128)S(1)} %get-tuple-element.211.refs_5_.refs_0_, bf16[2048,128]{1,0:T(8,128)(2,1)S(1)} %get-tuple-element.212.refs_1_, f32[16,128,128]{2,1,0:T(8,128)S(1)} %near_products.2.refs_2_, ...), custom_call_target="tpu_custom_call", output_to_operand_aliasing={{0}: (2, {})} | custom-call | flops 67108864 | bytes 4194304 | tf_op jit(solution)/shard_map/multiply/pallas_call | solution.py:473
  (6 shorter events, 0.0 us)
Async XLA Ops:
  0.0 18.7 %copy-start.1 = (bf16[16,4,4096]{2,1,0:T(4,128)(2,1)S(1)}, bf16[16,4,4096]{2,1,0:T(4,128)(2,1)}, u32[]{:S(2)}) copy-start(bf16[16,4,4096]{2,1,0:T(4,128)(2,1)} %param.9) | copy-start | bytes 1572868
  0.0 5.9 %collective-permute-start.3 = (s32[2,1,16]{2,1,0:T(1,128)}, s32[2,1,16]{2,1,0:T(1,128)S(1)}, u32[]{:S(2)}, u32[]{:S(2)}) collective-permute-start(s32[2,1,16]{2,1,0:T(1,128)} %param.8), channel_id=1, source_target_pairs={{0,1},{1,0},{2,3},{3,2},{4,5},{5,4},{6,7},{7,6},{8,9},{9,8},{10,11... | collective-permute-start | bytes 392 | tf_op jit(solution)/shard_map/ppermute | solution.py:29
  0.5 5.6 %collective-permute-start.5 = (s32[2,1,16]{2,1,0:T(1,128)}, s32[2,1,16]{2,1,0:T(1,128)S(1)}, u32[]{:S(2)}, u32[]{:S(2)}) collective-permute-start(s32[2,1,16]{2,1,0:T(1,128)} %param.8), channel_id=1, source_target_pairs={{0,3},{1,2},{2,1},{3,0},{4,7},{5,6},{6,5},{7,4},{8,11},{9,10},{10,... | collective-permute-start | bytes 392 | tf_op jit(solution)/shard_map/ppermute | solution.py:29
  3.1 3.8 %collective-permute-start.4 = (s32[2,1,16]{2,1,0:T(1,128)}, s32[2,1,16]{2,1,0:T(1,128)S(1)}, u32[]{:S(2)}, u32[]{:S(2)}) collective-permute-start(s32[2,1,16]{2,1,0:T(1,128)} %param.8), channel_id=1, source_target_pairs={{0,2},{1,3},{2,0},{3,1},{4,6},{5,7},{6,4},{7,5},{8,10},{9,11},{10,... | collective-permute-start | bytes 392 | tf_op jit(solution)/shard_map/ppermute | solution.py:29
  3.1 8.7 %collective-permute-start.10 = (bf16[1,16,4096]{2,1,0:T(8,128)(2,1)}, bf16[1,16,4096]{2,1,0:T(8,128)(2,1)S(1)}, u32[]{:S(2)}, u32[]{:S(2)}) collective-permute-start(bf16[1,16,4096]{2,1,0:T(8,128)(2,1)} %refs_0_.1), channel_id=1, source_target_pairs={{0,2},{1,3},{2,0},{3,1},{4,6},{5,7},{6,4},{7,5},{8,10},{9,11},{10,... | collective-permute-start | bytes 393224 | tf_op jit(solution)/shard_map/ppermute | solution.py:29
  5.8 1.6 %collective-permute-start.6 = (bf16[1,16,4096]{2,1,0:T(8,128)(2,1)}, bf16[1,16,4096]{2,1,0:T(8,128)(2,1)S(1)}, u32[]{:S(2)}, u32[]{:S(2)}) collective-permute-start(bf16[1,16,4096]{2,1,0:T(8,128)(2,1)} %refs_0_.1), channel_id=1, source_target_pairs={{0,1},{1,0},{2,3},{3,2},{4,5},{5,4},{6,7},{7,6},{8,9},{9,8},{10,11... | collective-permute-start | bytes 393224 | tf_op jit(solution)/shard_map/ppermute | solution.py:29
  5.9 5.9 %collective-permute-start.11 = (bf16[1,16,4096]{2,1,0:T(8,128)(2,1)}, bf16[1,16,4096]{2,1,0:T(8,128)(2,1)S(1)}, u32[]{:S(2)}, u32[]{:S(2)}) collective-permute-start(bf16[1,16,4096]{2,1,0:T(8,128)(2,1)} %refs_0_.1), channel_id=1, source_target_pairs={{0,3},{1,2},{2,1},{3,0},{4,7},{5,6},{6,5},{7,4},{8,11},{9,10},{10,... | collective-permute-start | bytes 393224 | tf_op jit(solution)/shard_map/ppermute | solution.py:29
  7.4 5.4 %collective-permute-start.9 = (s32[16,128]{1,0:T(8,128)S(1)}, s32[16,128]{1,0:T(8,128)S(1)}, u32[]{:S(2)}, u32[]{:S(2)}) collective-permute-start(s32[16,128]{1,0:T(8,128)S(1)} %pad_maximum_fusion.refs_0_), channel_id=1, source_target_pairs={{0,12},{4,8},{8,4},{12,0},{1,13},{5,9},{9,5},{13,1},{2,14},{6,10},... | collective-permute-start | bytes 24584 | tf_op jit(solution)/shard_map/ppermute | solution.py:29
  11.0 7.7 %collective-permute-start.8 = (s32[16,128]{1,0:T(8,128)S(1)}, s32[16,128]{1,0:T(8,128)S(1)}, u32[]{:S(2)}, u32[]{:S(2)}) collective-permute-start(s32[16,128]{1,0:T(8,128)S(1)} %pad_maximum_fusion.refs_0_), channel_id=1, source_target_pairs={{0,8},{4,12},{8,0},{12,4},{1,9},{5,13},{9,1},{13,5},{2,10},{6,14},... | collective-permute-start | bytes 24584 | tf_op jit(solution)/shard_map/ppermute | solution.py:29
  11.0 8.7 %collective-permute-start.7 = (s32[16,128]{1,0:T(8,128)S(1)}, s32[16,128]{1,0:T(8,128)S(1)}, u32[]{:S(2)}, u32[]{:S(2)}) collective-permute-start(s32[16,128]{1,0:T(8,128)S(1)} %pad_maximum_fusion.refs_0_), channel_id=1, source_target_pairs={{0,4},{4,0},{8,12},{12,8},{1,5},{5,1},{9,13},{13,9},{2,6},{6,2},{1... | collective-permute-start | bytes 24584 | tf_op jit(solution)/shard_map/ppermute | solution.py:29
  15.1 12.7 %collective-permute-start.12 = (bf16[512,128]{1,0:T(8,128)(2,1)S(1)}, bf16[512,128]{1,0:T(8,128)(2,1)S(1)}, u32[]{:S(2)}, u32[]{:S(2)}) collective-permute-start(bf16[512,128]{1,0:T(8,128)(2,1)S(1)} %pack.5), channel_id=1, source_target_pairs={{0,12},{4,8},{8,4},{12,0},{1,13},{5,9},{9,5},{13,1},{2,14},{6,10},... | collective-permute-start | bytes 393224 | tf_op jit(solution)/shard_map/ppermute | solution.py:29
  19.6 5.0 %copy-start = (bf16[1,16,4096]{2,1,0:T(8,128)(2,1)S(1)}, bf16[1,16,4096]{2,1,0:T(8,128)(2,1)}, u32[]{:S(2)}) copy-start(bf16[1,16,4096]{2,1,0:T(8,128)(2,1)} %refs_0_.1) | copy-start | bytes 393220
  19.6 9.4 %collective-permute-start.13 = (bf16[512,128]{1,0:T(8,128)(2,1)S(1)}, bf16[512,128]{1,0:T(8,128)(2,1)S(1)}, u32[]{:S(2)}, u32[]{:S(2)}) collective-permute-start(bf16[512,128]{1,0:T(8,128)(2,1)S(1)} %pack.6), channel_id=1, source_target_pairs={{0,8},{4,12},{8,0},{12,4},{1,9},{5,13},{9,1},{13,5},{2,10},{6,14},... | collective-permute-start | bytes 393224 | tf_op jit(solution)/shard_map/ppermute | solution.py:29
  20.6 8.5 %collective-permute-start.14 = (bf16[512,128]{1,0:T(8,128)(2,1)S(1)}, bf16[512,128]{1,0:T(8,128)(2,1)S(1)}, u32[]{:S(2)}, u32[]{:S(2)}) collective-permute-start(bf16[512,128]{1,0:T(8,128)(2,1)S(1)} %pack.4), channel_id=1, source_target_pairs={{0,4},{4,0},{8,12},{12,8},{1,5},{5,1},{9,13},{13,9},{2,6},{6,2},{1... | collective-permute-start | bytes 393224 | tf_op jit(solution)/shard_map/ppermute | solution.py:29
